TPU v7x, 32 devices: a whole 2x2x4 slice. The times are simulated.
32 devices in a mesh: dp: 8 (over z, y), tensor: 4 (over x, core).
Axes of the slice: x: 2, y: 2, z: 4, core: 2. Of those that a mesh axis runs over, the one named last changes fastest.
Arguments:
- block_input: bfloat16 [2, 8192, 1024], P(None, ('dp', 'tensor')), may hold values from -6 to 6
- cotangent: bfloat16 [2, 8192, 1024], P(None, ('dp', 'tensor')), may hold values from -6 to 6
- routes: int32 [2, 8192, 8], P(None, 'dp'), may hold values from 0 to 31, all different within a row; in each aligned block of 1024 rows (0 to 1023, 1024 to 2047, ..., all dimensions but the last counted through in order) at most 288 rows name the same one
- gate_weights: float32 [2, 8192, 8], P(None, 'dp'), may hold values from 0.2 to 0.6
- w_query: bfloat16 [1024, 1024], P('dp', 'tensor'), may hold values from -0.1875 to 0.1875
- w_key: bfloat16 [1024, 512], P('dp', 'tensor'), may hold values from -0.1875 to 0.1875
- w_value: bfloat16 [1024, 512], P('dp', 'tensor'), may hold values from -0.1875 to 0.1875
- w_out: bfloat16 [1024, 1024], P('tensor', 'dp'), may hold values from -1.5 to 1.5
- w_gate_up: bfloat16 [32, 1024, 2, 512], P(None, 'dp', None, 'tensor'), may hold values from -0.1875 to 0.1875
- w_down: bfloat16 [32, 512, 1024], P(None, 'tensor', 'dp'), may hold values from -0.25 to 0.25
- norm_attn: float32 [1024], replicated, may hold values from 0.1 to 1.9
- norm_moe: float32 [1024], replicated, may hold values from 0.1 to 1.9
Outputs:
- block_output: bfloat16 [2, 8192, 1024], P(None, ('dp', 'tensor'))
- input_grad: float32 [2, 8192, 1024], P(None, ('dp', 'tensor'))
- grad_query: float32 [1024, 1024], P('dp', 'tensor')
- grad_key: float32 [1024, 512], P('dp', 'tensor')
- grad_value: float32 [1024, 512], P('dp', 'tensor')
- grad_out: float32 [1024, 1024], P('tensor', 'dp')
- grad_gate_up: float32 [32, 1024, 2, 512], P(None, 'dp', None, 'tensor')
- grad_down: float32 [32, 512, 1024], P(None, 'tensor', 'dp')
- grad_norm_attn: float32 [1024], replicated
- grad_norm_moe: float32 [1024], replicated
Inputs may be any that keep to these rules, and one draw needn't show every extreme that they name: Each token names 8 different experts. In each group of 1024 rows of one micro-batch, no expert is named by more than 288 routes, a bound that some block reaches.
All inputs are finite; a program needn't handle non-finite values.
Results may differ from a plain program's by a relative error of at most 0.013.
Values may be sent and summed in bfloat16 or wider, within the bound.
No kernel may reach another device: no remote copies, remote signals or barrier semaphores. Data moves between devices by JAX's collectives and lax.ppermute only.
A program may use at most 448 MiB of HBM per device.

v0:
```python
import math

import jax
import jax.numpy as jnp
from jax import lax
from jax.sharding import PartitionSpec as P

HD = 64
E = 32
TOPK = 8
PROMPT = 512
CONT = 512
CAP = 288


EPSILON = 1e-06
BF = jnp.bfloat16
FP = jnp.float32


def dot_rows(left, right):
    return lax.dot_general(left, right, (((0,), (0,)), ((), ())), preferred_element_type=FP)


def dot_cols(left, right):
    return lax.dot_general(left, right, (((1,), (1,)), ((), ())), preferred_element_type=FP)


def row_norm(in_rows, gain_vec):
    row_scale = lax.rsqrt(jnp.mean(in_rows * in_rows, axis=-1, keepdims=True) + EPSILON)
    return (in_rows * row_scale * gain_vec, row_scale)


def norm_back(in_rows, row_scale, gain_vec, grad_in):
    weighted = grad_in * gain_vec
    inner = jnp.mean(weighted * in_rows, axis=-1, keepdims=True)
    returned = row_scale * weighted - in_rows * row_scale * row_scale * row_scale * inner
    gain_part = jnp.sum(grad_in * in_rows * row_scale, axis=0)
    return (returned, gain_part)


def fetch_weights(w_query, w_key, w_value, w_out, w_gate_up, w_down):
    return (
        lax.all_gather(w_query, "dp", axis=0, tiled=True),
        lax.all_gather(w_key, "dp", axis=0, tiled=True),
        lax.all_gather(w_value, "dp", axis=0, tiled=True),
        lax.all_gather(w_out, "dp", axis=1, tiled=True),
        lax.all_gather(w_gate_up, "dp", axis=1, tiled=True),
        lax.all_gather(w_down, "dp", axis=2, tiled=True),
    )


def reduce_grads(grad_set):
    grad_query, grad_key, grad_value, grad_out, grad_pair, grad_down = grad_set
    return (
        lax.psum_scatter(grad_query, "dp", scatter_dimension=0, tiled=True),
        lax.psum_scatter(grad_key, "dp", scatter_dimension=0, tiled=True),
        lax.psum_scatter(grad_value, "dp", scatter_dimension=0, tiled=True),
        lax.psum_scatter(grad_out, "dp", scatter_dimension=1, tiled=True),
        lax.psum_scatter(grad_pair, "dp", scatter_dimension=1, tiled=True),
        lax.psum_scatter(grad_down, "dp", scatter_dimension=2, tiled=True),
    )


def add_sets(left_set, right_set):
    if left_set is None:
        return right_set
    return tuple((left_term + right_term for left_term, right_term in zip(left_set, right_set)))


def slot_tables(route_rows, gate_rows):
    flat_routes = route_rows.reshape(-1)
    expert_ids = jnp.arange(E, dtype=jnp.int32)
    onehot = (flat_routes[:, None] == expert_ids[None, :]).astype(jnp.int32)
    before = jnp.cumsum(onehot, axis=0) - onehot
    slot_place = jnp.sum(before * onehot, axis=1)
    slot_index = flat_routes * CAP + slot_place
    token_index = jnp.arange(flat_routes.shape[0], dtype=jnp.int32) // TOPK
    source = jnp.zeros((E * CAP,), jnp.int32).at[slot_index].set(token_index)
    filled = jnp.zeros((E * CAP,), FP).at[slot_index].set(1.0)
    weight = jnp.zeros((E * CAP,), FP).at[slot_index].set(gate_rows.reshape(-1))
    return (source, filled, weight)


def segment_plan():
    plan = [(0, PROMPT, 0)]
    plan.append((PROMPT, CONT, PROMPT))
    return plan


def segment_keys(keys_all, values_all, start_row, length, prefix):
    if prefix > 0:
        key_set = jnp.concatenate(
            [keys_all[:prefix], keys_all[start_row : start_row + length]], axis=0
        )
        value_set = jnp.concatenate(
            [values_all[:prefix], values_all[start_row : start_row + length]], axis=0
        )
        return (key_set, value_set)
    return (keys_all[start_row : start_row + length], values_all[start_row : start_row + length])


def add_key_grads(grad_sums, grad_parts, start_row, length, prefix):
    if prefix > 0:
        return tuple(
            (
                grad_sum.at[:prefix]
                .add(grad_part[:prefix])
                .at[start_row : start_row + length]
                .add(grad_part[prefix:])
                for grad_sum, grad_part in zip(grad_sums, grad_parts)
            )
        )
    return tuple(
        (
            grad_sum.at[start_row : start_row + length].add(grad_part)
            for grad_sum, grad_part in zip(grad_sums, grad_parts)
        )
    )


def mask_scores(query_blk, key_set, prefix, score_scale):
    scores = (
        jnp.einsum("bgrd,lgd->grbl", query_blk, key_set, preferred_element_type=FP) * score_scale
    )
    row_pos = lax.broadcasted_iota(jnp.int32, scores.shape, 2)
    col_pos = lax.broadcasted_iota(jnp.int32, scores.shape, 3)
    allowed = (col_pos < prefix) | (col_pos - prefix <= row_pos)
    return jnp.where(allowed, scores, -1e30)


def attention_forward(query, keys_all, values_all, score_scale):
    outputs = []
    saved = []
    for start_row, length, prefix in segment_plan():
        key_set, value_set = segment_keys(keys_all, values_all, start_row, length, prefix)
        block_rows = min(512, length)
        query_blk = query[start_row : start_row + block_rows]
        scores = mask_scores(query_blk, key_set, prefix, score_scale)
        row_max = jnp.max(scores, axis=-1, keepdims=True)
        exponent = jnp.exp(scores - row_max)
        row_total = jnp.sum(exponent, axis=-1, keepdims=True)
        attn_probs = (exponent / row_total).astype(BF)
        outputs.append(
            jnp.einsum("grbl,lgd->bgrd", attn_probs, value_set, preferred_element_type=FP)
        )
        saved.append(row_max + jnp.log(row_total))
    return (jnp.concatenate(outputs, axis=0), saved)


def attention_backward(query, keys_all, values_all, head_grad, saved, score_scale):
    query_parts = []
    key_grads = (jnp.zeros(keys_all.shape, FP), jnp.zeros(values_all.shape, FP))
    counter = 0
    for start_row, length, prefix in segment_plan():
        key_set, value_set = segment_keys(keys_all, values_all, start_row, length, prefix)
        block_rows = min(512, length)
        query_blk = query[start_row : start_row + block_rows]
        grad_blk = head_grad[start_row : start_row + block_rows]
        scores = mask_scores(query_blk, key_set, prefix, score_scale)
        attn_probs = jnp.exp(scores - saved[counter])
        counter += 1
        prob_grad = jnp.einsum("bgrd,lgd->grbl", grad_blk, value_set, preferred_element_type=FP)
        inner = jnp.sum(attn_probs * prob_grad, axis=-1, keepdims=True)
        score_grad = (attn_probs * (prob_grad - inner)).astype(BF)
        query_parts.append(
            jnp.einsum("grbl,lgd->bgrd", score_grad, key_set, preferred_element_type=FP)
            * score_scale
        )
        key_part = (
            jnp.einsum("grbl,bgrd->lgd", score_grad, query_blk, preferred_element_type=FP)
            * score_scale
        )
        value_part = jnp.einsum(
            "grbl,bgrd->lgd", attn_probs.astype(BF), grad_blk, preferred_element_type=FP
        )
        key_grads = add_key_grads(key_grads, (key_part, value_part), start_row, length, prefix)
    return (jnp.concatenate(query_parts, axis=0), key_grads[0], key_grads[1])


def gather_slots(moe_in, source_block, fill_block, capacity):
    picked = jnp.where(fill_block[:, None] > 0, moe_in[source_block], jnp.zeros((), BF))
    return picked.reshape(-1, capacity, moe_in.shape[1])


def expert_items(pair_mat, down_mat, source, filled, weight):
    expert_count, model_width, pair_width = pair_mat.shape
    per_block = min(4, expert_count)
    block_count = expert_count // per_block
    items = (
        pair_mat.reshape(block_count, per_block, model_width, pair_width),
        down_mat.reshape(block_count, per_block, pair_width // 2, model_width),
        source.reshape(block_count, -1),
        filled.reshape(block_count, -1),
        weight.reshape(block_count, -1),
    )
    return (items, source.shape[0] // expert_count, pair_width // 2)


def expert_forward(moe_in, source, filled, weight, pair_mat, down_mat):
    items, capacity, hidden_local = expert_items(pair_mat, down_mat, source, filled, weight)

    def one_block(mixed_sum, block_items):
        pair_block, down_block, source_block, fill_block, weight_block = block_items
        expert_in = gather_slots(moe_in, source_block, fill_block, capacity)
        pair_out = jnp.einsum("ecd,edf->ecf", expert_in, pair_block, preferred_element_type=FP)
        gate_pre = pair_out[..., :hidden_local]
        up_pre = pair_out[..., hidden_local:]
        hidden = (gate_pre * jax.nn.sigmoid(gate_pre) * up_pre).astype(BF)
        expert_out = jnp.einsum("ecf,efd->ecd", hidden, down_block, preferred_element_type=FP)
        flat_out = expert_out.reshape(-1, moe_in.shape[1]) * weight_block[:, None]
        mixed_sum = mixed_sum + jax.ops.segment_sum(
            flat_out, source_block, num_segments=moe_in.shape[0]
        )
        return (mixed_sum, pair_out)

    return lax.scan(one_block, jnp.zeros(moe_in.shape, FP), items)


def expert_backward(moe_in, moe_grad, source, filled, weight, pair_mat, down_mat, pair_saved):
    items, capacity, hidden_local = expert_items(pair_mat, down_mat, source, filled, weight)

    def one_block(in_grad_sum, block_items):
        pair_block, down_block, source_block, fill_block, weight_block, pair_out = block_items
        expert_in = gather_slots(moe_in, source_block, fill_block, capacity)
        gate_pre = pair_out[..., :hidden_local]
        up_pre = pair_out[..., hidden_local:]
        sigmoid_gate = jax.nn.sigmoid(gate_pre)
        hidden = (gate_pre * sigmoid_gate * up_pre).astype(BF)
        slot_grad = (moe_grad[source_block].astype(FP) * weight_block[:, None]).astype(BF)
        slot_grad = slot_grad.reshape(-1, capacity, moe_in.shape[1])
        down_grad = jnp.einsum("ecf,ecd->efd", hidden, slot_grad, preferred_element_type=FP)
        hidden_grad = jnp.einsum("ecd,efd->ecf", slot_grad, down_block, preferred_element_type=FP)
        gate_grad = hidden_grad * up_pre * sigmoid_gate * (1.0 + gate_pre * (1.0 - sigmoid_gate))
        up_grad = hidden_grad * gate_pre * sigmoid_gate
        pair_grad = jnp.concatenate([gate_grad, up_grad], axis=-1).astype(BF)
        pair_weight_grad = jnp.einsum(
            "ecd,ecf->edf", expert_in, pair_grad, preferred_element_type=FP
        )
        slot_in_grad = jnp.einsum("ecf,edf->ecd", pair_grad, pair_block, preferred_element_type=FP)
        in_grad_sum = in_grad_sum + jax.ops.segment_sum(
            slot_in_grad.reshape(-1, moe_in.shape[1]), source_block, num_segments=moe_in.shape[0]
        )
        return (in_grad_sum, (pair_weight_grad, down_grad))

    return lax.scan(one_block, jnp.zeros(moe_in.shape, FP), items + (pair_saved,))


def on_device(
    block_input,
    cotangent,
    routes,
    gate_weights,
    w_query,
    w_key,
    w_value,
    w_out,
    w_gate_up,
    w_down,
    norm_attn,
    norm_moe,
):
    score_scale = 1.0 / math.sqrt(HD)
    micro_count = block_input.shape[0]
    heads_local = w_query.shape[1] // HD
    kv_local = w_key.shape[1] // HD
    head_ratio = heads_local // kv_local
    q_width = heads_local * HD
    kv_width = kv_local * HD
    outputs = []
    input_grads = []
    grad_shards = None
    gain_attn_total = jnp.zeros(norm_attn.shape, FP)
    gain_moe_total = jnp.zeros(norm_moe.shape, FP)
    for micro_index in range(micro_count):
        full_weights = fetch_weights(w_query, w_key, w_value, w_out, w_gate_up, w_down)
        query_full, key_full, value_full, out_full, pair_full, down_full = full_weights
        w_project = jnp.concatenate([query_full, key_full, value_full], axis=1)
        expert_count, model_width = (pair_full.shape[0], pair_full.shape[1])
        hidden_local = pair_full.shape[3]
        pair_mat = pair_full.reshape(expert_count, model_width, 2 * hidden_local)
        in_rows = block_input[micro_index].astype(FP)
        normed_attn, scale_attn = row_norm(in_rows, norm_attn)
        attn_in = lax.all_gather(normed_attn.astype(BF), "tensor", axis=0, tiled=True)
        projected = jnp.dot(attn_in, w_project, preferred_element_type=FP).astype(BF)
        query = projected[:, :q_width].reshape(-1, kv_local, head_ratio, HD)
        keys_all = projected[:, q_width : q_width + kv_width].reshape(-1, kv_local, HD)
        values_all = projected[:, q_width + kv_width :].reshape(-1, kv_local, HD)
        attn_raw, saved = attention_forward(query, keys_all, values_all, score_scale)
        head_out = attn_raw.astype(BF).reshape(-1, q_width)
        branch = lax.psum_scatter(
            jnp.dot(head_out, out_full, preferred_element_type=FP),
            "tensor",
            scatter_dimension=0,
            tiled=True,
        )
        middle = in_rows + branch
        normed_moe, scale_moe = row_norm(middle, norm_moe)
        moe_in = lax.all_gather(normed_moe.astype(BF), "tensor", axis=0, tiled=True)
        source, filled, weight = slot_tables(routes[micro_index], gate_weights[micro_index])
        mixed_part, pair_saved = expert_forward(moe_in, source, filled, weight, pair_mat, down_full)
        mixed_out = lax.psum_scatter(
            mixed_part.astype(jnp.bfloat16), "tensor", scatter_dimension=0, tiled=True
        ).astype(jnp.float32)
        outputs.append((middle + mixed_out).astype(BF))
        out_grad = cotangent[micro_index].astype(FP)
        moe_grad = lax.all_gather(out_grad.astype(BF), "tensor", axis=0, tiled=True)
        moe_in_part, (pair_weight_grad, down_grad) = expert_backward(
            moe_in, moe_grad, source, filled, weight, pair_mat, down_full, pair_saved
        )
        moe_in_grad = lax.psum_scatter(moe_in_part, "tensor", scatter_dimension=0, tiled=True)
        middle_back, gain_moe_part = norm_back(middle, scale_moe, norm_moe, moe_in_grad)
        middle_grad = out_grad + middle_back
        attn_grad = lax.all_gather(middle_grad.astype(BF), "tensor", axis=0, tiled=True)
        out_weight_grad = dot_rows(head_out, attn_grad)
        head_grad = dot_cols(attn_grad, out_full).astype(BF).reshape(-1, kv_local, head_ratio, HD)
        query_grad, key_grad, value_grad = attention_backward(
            query, keys_all, values_all, head_grad, saved, score_scale
        )
        project_grad = jnp.concatenate(
            [
                query_grad.reshape(-1, q_width),
                key_grad.reshape(-1, kv_width),
                value_grad.reshape(-1, kv_width),
            ],
            axis=1,
        ).astype(BF)
        project_weight_grad = dot_rows(attn_in, project_grad)
        attn_in_grad = lax.psum_scatter(
            dot_cols(project_grad, w_project), "tensor", scatter_dimension=0, tiled=True
        )
        in_back, gain_attn_part = norm_back(in_rows, scale_attn, norm_attn, attn_in_grad)
        input_grads.append(middle_grad + in_back)
        gain_attn_total = gain_attn_total + gain_attn_part
        gain_moe_total = gain_moe_total + gain_moe_part
        grad_set = (
            project_weight_grad[:, :q_width],
            project_weight_grad[:, q_width : q_width + kv_width],
            project_weight_grad[:, q_width + kv_width :],
            out_weight_grad,
            pair_weight_grad.reshape(expert_count, model_width, 2, hidden_local),
            down_grad.reshape(expert_count, hidden_local, model_width),
        )
        grad_shards = add_sets(grad_shards, reduce_grads(grad_set))
    gain_attn_grad, gain_moe_grad = lax.psum((gain_attn_total, gain_moe_total), ("dp", "tensor"))
    shard_query, shard_key, shard_value, shard_out, shard_pair, shard_down = grad_shards
    return (
        jnp.stack(outputs),
        jnp.stack(input_grads),
        shard_query,
        shard_key,
        shard_value,
        shard_out,
        shard_pair,
        shard_down,
        gain_attn_grad,
        gain_moe_grad,
    )


def solution(mesh):
    return jax.shard_map(
        on_device,
        mesh=mesh,
        in_specs=(
            P(None, ("dp", "tensor"), None),
            P(None, ("dp", "tensor"), None),
            P(None, "dp", None),
            P(None, "dp", None),
            P("dp", "tensor"),
            P("dp", "tensor"),
            P("dp", "tensor"),
            P("tensor", "dp"),
            P(None, "dp", None, "tensor"),
            P(None, "tensor", "dp"),
            P(),
            P(),
        ),
        out_specs=(
            P(None, ("dp", "tensor"), None),
            P(None, ("dp", "tensor"), None),
            P("dp", "tensor"),
            P("dp", "tensor"),
            P("dp", "tensor"),
            P("tensor", "dp"),
            P(None, "dp", None, "tensor"),
            P(None, "tensor", "dp"),
            P(),
            P(),
        ),
        check_vma=False,
    )
```

profile of v0, /device:TPU:0, one launch (start us, length us, event | category | flops | bytes accessed | tf_op | source)
XLA Modules:
  0.0 3441.1 jit_solution(18161191929021835460)
XLA Ops:
  13.0 32.7 all_gather.50
  45.7 30.8 all_gather.51
  104.1 31.2 all_gather.49
  195.2 47.1 %reduce-scatter.19.cloned.1.call-done = f32[256,1024]{1,0:T(8,128)} async-done(((f32[1024,1024]{1,0:T(8,128)}), f32[256,1024]{1,0:T(8,128)}) %reduce-scatter.19.cloned.1.call-update) | async-done | bytes 1048592 | tf_op jit(solution)/shard_map/reduce_scatter | solution.py:291
  355.6 42.0 %all-gather.17.cloned.1.call-done = bf16[32,1024,2,128]{3,2,1,0:T(2,128)(2,1)} async-done(((bf16[32,128,2,128]{3,2,1,0:T(2,128)(2,1)}), bf16[32,1024,2,128]{3,2,1,0:T(2,128)(2,1)}) %all-gather.17.cloned.1.call-update) | async-done | bytes 16777232 | tf_op jit(solution)/shard_map/all_gather | solution.py:48
  424.8 97.9 %all-gather.19.cloned.1.call-done = bf16[32,128,1024]{2,1,0:T(8,128)(2,1)} async-done(((bf16[32,128,128]{2,1,0:T(8,128)(2,1)}), bf16[32,128,1024]{2,1,0:T(8,128)(2,1)}) %all-gather.19.cloned.1.call-update) | async-done | bytes 8388624 | tf_op jit(solution)/shard_map/all_gather | solution.py:49
  552.7 262.2 %while.64 = (s32[]{:T(128)}, f32[1024,1024]{1,0:T(8,128)}, f32[8,4,288,256]{3,2,1,0:T(8,128)}, s32[8,1152]{1,0:T(8,128)S(1)}, f32[8,1152]{1,0:T(8,128)S(1)}, /*i...) while((s32[]{:T(128)}, f32[1024,1024]{1,0:T(8,128)}, ...), condition=%wide.region_15.16_spmd, body=%wide.region_13.15_spmd.sunk | while | flops 910400000 | bytes 42138752 | solution.py:217
  836.6 397.6 %while.66 = (s32[]{:T(128)}, f32[1024,1024]{1,0:T(8,128)}, f32[8,4,1024,256]{2,3,1,0:T(8,128)}, f32[8,4,128,1024]{3,2,1,0:T(8,128)}, s32[8,1152]{1,0:T(8,128)S(1...) while((s32[]{:T(128)}, f32[1024,1024]{1,0:T(8,128)}, ...), condition=%wide.region_36.37_spmd, body=%wide.region_34.36_spmd.sunk | while | flops 1826544128 | bytes 65552692 | solution.py:246
  1235.0 44.1 %reduce-scatter.23.cloned.1.call-done = f32[256,1024]{1,0:T(8,128)} async-done(((f32[1024,1024]{1,0:T(8,128)}), f32[256,1024]{1,0:T(8,128)}) %reduce-scatter.23.cloned.1.call-update) | async-done | bytes 1048592 | tf_op jit(solution)/shard_map/reduce_scatter | solution.py:311
  1358.1 30.8 scatter_custom_fusion.8
  1396.3 262.7 %while.65 = (s32[]{:T(128)}, f32[1024,1024]{1,0:T(8,128)}, f32[8,4,288,256]{3,2,1,0:T(8,128)}, s32[8,1152]{1,0:T(8,128)S(1)}, f32[8,1152]{1,0:T(8,128)S(1)}, /*i...) while((s32[]{:T(128)}, f32[1024,1024]{1,0:T(8,128)}, ...), condition=%wide.region_32.33_spmd, body=%wide.region_30.32_spmd.sunk | while | flops 910400000 | bytes 42138752 | solution.py:217
  1680.8 397.6 %while.67 = (s32[]{:T(128)}, f32[1024,1024]{1,0:T(8,128)}, f32[8,4,1024,256]{2,3,1,0:T(8,128)}, f32[8,4,128,1024]{3,2,1,0:T(8,128)}, s32[8,1152]{1,0:T(8,128)S(1...) while((s32[]{:T(128)}, f32[1024,1024]{1,0:T(8,128)}, ...), condition=%wide.region_45.46_spmd, body=%wide.region_43.45_spmd.sunk | while | flops 1826544128 | bytes 65552692 | solution.py:246
  2087.6 35.4 %reduce-scatter.27.cloned.1.call-done = f32[256,1024]{1,0:T(8,128)} async-done(((f32[1024,1024]{1,0:T(8,128)}), f32[256,1024]{1,0:T(8,128)}) %reduce-scatter.27.cloned.1.call-update) | async-done | bytes 1048592 | tf_op jit(solution)/shard_map/reduce_scatter | solution.py:311
  2125.2 32.4 reduce-scatter.17.cloned.1.call-done
  2157.6 34.6 %reduce-scatter.21.cloned.1.call-done = bf16[256,1024]{1,0:T(8,128)(2,1)} async-done(((bf16[1024,1024]{1,0:T(8,128)(2,1)}), bf16[256,1024]{1,0:T(8,128)(2,1)}) %reduce-scatter.21.cloned.1.call-update) | async-done | bytes 524304 | tf_op jit(solution)/shard_map/reduce_scatter | solution.py:302
  2269.7 34.5 %add.422 = f32[8,4,1024,256]{2,3,1,0:T(8,128)} add(f32[8,4,1024,256]{2,3,1,0:T(8,128)} %get-tuple-element.384, f32[8,4,1024,256]{2,3,1,0:T(8,128)} %get-tuple-element.385) | non-fusion elementwise | flops 8388608 | bytes 100663296 | tf_op jit(solution)/shard_map/add | solution.py:68
  2304.2 34.2 copy.113
  2376.5 44.7 %all-reduce.4 = (f32[1024]{0:T(1024)}, f32[1024]{0:T(1024)}) all-reduce(f32[1024]{0:T(1024)S(1)} %add.414, f32[1024]{0:T(1024)S(1)} %add.415), channel_id=1, replica_groups=mesh['dp'=8,'tensor'=4] {'dp','tensor'}, use_global_device_ids=true, to_apply=%region_66.67 | all-reduce | flops 2048 | bytes 16384 | tf_op jit(solution)/shard_map/psum | solution.py:345
  2425.1 458.8 %reduce-scatter.39.cloned.1.call-done = f32[32,128,2,128]{3,0,2,1:T(8,128)} async-done(((f32[32,1024,2,128]{3,0,2,1:T(8,128)}), f32[32,128,2,128]{3,0,2,1:T(8,128)}) %reduce-scatter.39.cloned.1.call-update) | async-done | bytes 4194320 | tf_op jit(solution)/shard_map/reduce_scatter | solution.py:60
  2891.4 57.3 %reduce-scatter.35.cloned.1.call-done = f32[128,128]{1,0:T(8,128)} async-done(((f32[1024,128]{1,0:T(8,128)}), f32[128,128]{1,0:T(8,128)}) %reduce-scatter.35.cloned.1.call-update) | async-done | bytes 65552 | tf_op jit(solution)/shard_map/reduce_scatter | solution.py:58
  2948.7 65.2 %reduce-scatter.33.cloned.1.call-done = f32[128,128]{1,0:T(8,128)} async-done(((f32[1024,128]{1,0:T(8,128)}), f32[128,128]{1,0:T(8,128)}) %reduce-scatter.33.cloned.1.call-update) | async-done | bytes 65552 | tf_op jit(solution)/shard_map/reduce_scatter | solution.py:57
  3013.9 66.9 %reduce-scatter.37.cloned.1.call-done = f32[256,128]{1,0:T(8,128)} async-done(((f32[256,1024]{1,0:T(8,128)}), f32[256,128]{1,0:T(8,128)}) %reduce-scatter.37.cloned.1.call-update) | async-done | bytes 131088 | tf_op jit(solution)/shard_map/reduce_scatter | solution.py:59
  3080.7 66.7 %reduce-scatter.31.cloned.1.call-done = f32[128,256]{1,0:T(8,128)} async-done(((f32[1024,256]{1,0:T(8,128)}), f32[128,256]{1,0:T(8,128)}) %reduce-scatter.31.cloned.1.call-update) | async-done | bytes 131088 | tf_op jit(solution)/shard_map/reduce_scatter | solution.py:56
  3147.4 286.0 %reduce-scatter.41.cloned.1.call-done = f32[32,128,128]{2,1,0:T(8,128)} async-done(((f32[32,128,1024]{2,1,0:T(8,128)}), f32[32,128,128]{2,1,0:T(8,128)}) %reduce-scatter.41.cloned.1.call-update) | async-done | bytes 2097168 | tf_op jit(solution)/shard_map/reduce_scatter | solution.py:61
  (1022 shorter events, 1847.9 us)
Async XLA Ops:
  8.1 127.5 %all-gather.13.cloned.1.call-start = ((), (), s32[]{:S(2)}) async-start(), calls=%async_computation.14 | async-start | bytes 2621440 | tf_op jit(solution)/shard_map/all_gather | solution.py:284
  12.2 140.0 %all-gather.21.cloned.1.call-start = ((), (), s32[]{:S(2)}) async-start(), calls=%async_computation.20 | async-start | bytes 2621440 | tf_op jit(solution)/shard_map/all_gather | solution.py:284
  12.9 182.3 %reduce-scatter.15.cloned.1.call-start = ((), (), s32[]{:S(2)}) async-start(), calls=%async_computation.15 | async-start | bytes 5242880 | tf_op jit(solution)/shard_map/reduce_scatter | solution.py:291
  151.7 90.7 %reduce-scatter.19.cloned.1.call-start = ((), (), s32[]{:S(2)}) async-start(), calls=%async_computation.21 | async-start | bytes 5242880 | tf_op jit(solution)/shard_map/reduce_scatter | solution.py:291
  168.0 229.6 %all-gather.17.cloned.1.call-start = ((), (), s32[]{:S(2)}) async-start(), calls=%async_computation.17 | async-start | bytes 18874368 | tf_op jit(solution)/shard_map/all_gather | solution.py:48
  168.6 354.1 %all-gather.19.cloned.1.call-start = ((), (), s32[]{:S(2)}) async-start(), calls=%async_computation.18 | async-start | bytes 9437184 | tf_op jit(solution)/shard_map/all_gather | solution.py:49
  169.2 376.2 %all-gather.15.cloned.1.call-start = ((), (), s32[]{:S(2)}) async-start(), calls=%async_computation.16 | async-start | bytes 2621440 | tf_op jit(solution)/shard_map/all_gather | solution.py:299
  247.6 567.3 %all-gather.29.cloned.1.call-start = ((), (), s32[]{:S(2)}) async-start(), calls=%async_computation.30 | async-start | bytes 2621440 | tf_op jit(solution)/shard_map/all_gather | solution.py:307
  248.8 1030.3 %reduce-scatter.23.cloned.1.call-start = ((), (), s32[]{:S(2)}) async-start(), calls=%async_computation.24 | async-start | bytes 5242880 | tf_op jit(solution)/shard_map/reduce_scatter | solution.py:311
  1234.4 154.7 %all-gather.23.cloned.1.call-start = ((), (), s32[]{:S(2)}) async-start(), calls=%async_computation.22 | async-start | bytes 2621440 | tf_op jit(solution)/shard_map/all_gather | solution.py:299
  1282.0 377.0 %all-gather.31.cloned.1.call-start = ((), (), s32[]{:S(2)}) async-start(), calls=%async_computation.31 | async-start | bytes 2621440 | tf_op jit(solution)/shard_map/all_gather | solution.py:307
  1282.8 840.3 %reduce-scatter.27.cloned.1.call-start = ((), (), s32[]{:S(2)}) async-start(), calls=%async_computation.27 | async-start | bytes 5242880 | tf_op jit(solution)/shard_map/reduce_scatter | solution.py:311
  2078.4 79.2 %reduce-scatter.17.cloned.1.call-start = ((), (), s32[]{:S(2)}) async-start(), calls=%async_computation.19 | async-start | bytes 2621440 | tf_op jit(solution)/shard_map/reduce_scatter | solution.py:302
  2082.3 109.8 %reduce-scatter.21.cloned.1.call-start = ((), (), s32[]{:S(2)}) async-start(), calls=%async_computation.23 | async-start | bytes 2621440 | tf_op jit(solution)/shard_map/reduce_scatter | solution.py:302
  2087.2 132.6 %all-gather.25.cloned.1.call-start = ((), (), s32[]{:S(2)}) async-start(), calls=%async_computation.25 | async-start | bytes 2621440 | tf_op jit(solution)/shard_map/all_gather | solution.py:314
  2197.2 47.2 %all-gather.27.cloned.1.call-start = ((), (), s32[]{:S(2)}) async-start(), calls=%async_computation.28 | async-start | bytes 2621440 | tf_op jit(solution)/shard_map/all_gather | solution.py:314
  2197.9 176.3 %reduce-scatter.25.cloned.1.call-start = ((), (), s32[]{:S(2)}) async-start(), calls=%async_computation.26 | async-start | bytes 5242880 | tf_op jit(solution)/shard_map/reduce_scatter | solution.py:329
  2240.2 134.1 %reduce-scatter.29.cloned.1.call-start = ((), (), s32[]{:S(2)}) async-start(), calls=%async_computation.29 | async-start | bytes 5242880 | tf_op jit(solution)/shard_map/reduce_scatter | solution.py:329
  2269.6 614.3 %reduce-scatter.39.cloned.1.call-start = ((), (), s32[]{:S(2)}) async-start(), calls=%async_computation.36 | async-start | bytes 37748736 | tf_op jit(solution)/shard_map/reduce_scatter | solution.py:60
  2338.5 610.2 %reduce-scatter.35.cloned.1.call-start = ((), (), s32[]{:S(2)}) async-start(), calls=%async_computation.34 | async-start | bytes 589824 | tf_op jit(solution)/shard_map/reduce_scatter | solution.py:58
  2346.3 667.6 %reduce-scatter.33.cloned.1.call-start = ((), (), s32[]{:S(2)}) async-start(), calls=%async_computation.33 | async-start | bytes 589824 | tf_op jit(solution)/shard_map/reduce_scatter | solution.py:57
  2346.9 733.9 %reduce-scatter.37.cloned.1.call-start = ((), (), s32[]{:S(2)}) async-start(), calls=%async_computation.35 | async-start | bytes 1179648 | tf_op jit(solution)/shard_map/reduce_scatter | solution.py:59
  2351.2 796.2 %reduce-scatter.31.cloned.1.call-start = ((), (), s32[]{:S(2)}) async-start(), calls=%async_computation.32 | async-start | bytes 1179648 | tf_op jit(solution)/shard_map/reduce_scatter | solution.py:56
  2353.7 1079.7 %reduce-scatter.41.cloned.1.call-start = ((), (), s32[]{:S(2)}) async-start(), calls=%async_computation.37 | async-start | bytes 18874368 | tf_op jit(solution)/shard_map/reduce_scatter | solution.py:61
  (193 other events, 2538.9 us)
Sparse Core Ops, SparseCore 0:
  12.3 25.2 all-gather.12
  39.7 22.5 all-gather.20
  151.8 43.4 reduce-scatter.14
  197.8 44.5 reduce-scatter.18
  1234.5 44.5 reduce-scatter.22
  1282.2 22.5 all-gather.22
  1306.4 22.5 all-gather.30
  2078.5 44.4 reduce-scatter.26
  2126.2 31.4 reduce-scatter.16
  2160.7 31.3 reduce-scatter.20
  2240.3 44.4 reduce-scatter.24
  2287.4 44.4 reduce-scatter.28
  2338.6 545.2 reduce-scatter.38
  2887.7 60.9 reduce-scatter.34
  2952.8 60.9 reduce-scatter.32
  3017.7 62.9 reduce-scatter.36
  3084.9 62.4 reduce-scatter.30
  3151.6 281.7 reduce-scatter.40
Sparse Core Ops, SparseCore 1:
  170.7 226.9 all-gather.16
  399.5 123.1 all-gather.18
  524.7 20.6 all-gather.14
  547.5 22.4 all-gather.28
  2197.3 22.4 all-gather.24
  2222.0 22.4 all-gather.26
where the time goes:
time: 3450 us; the launch traced here: 3440 us
  waiting for transfers between devices  1410 us (41%)
  other arithmetic  771 us (22%)
  local copies, waits for them, and re-layouts  666 us (19%)
  matrix products  402 us (12%)
  blocking collectives  167 us (5%)
    reduce_scatter x1, waiting for transfers between devices, reduce_grads(): lax.psum_scatter(grad_pair, 'dp', scatter_dimension=1, tiled=True)  459 us
    scatter-add x16, other arithmetic, one_block(): jax.ops.segment_sum(flat_out, source_block, num_segments=moe_in.shape[0])  301 us
    scatter-add x16, other arithmetic, one_block(): jax.ops.segment_sum(slot_in_grad.reshape(-1, moe_in.shape[1]), source_blo...  301 us
    reduce_scatter x1, waiting for transfers between devices, reduce_grads(): lax.psum_scatter(grad_down, 'dp', scatter_dimension=2, tiled=True)  286 us
    gather x32, local copies, waits for them, and re-layouts, gather_slots(): moe_in[source_block]  160 us
    gather x16, local copies, waits for them, and re-layouts, one_block(): moe_grad[source_block].astype(FP) * weight_block[:, None]  135 us
    all_gather x1, waiting for transfers between devices, fetch_weights(): lax.all_gather(w_down, 'dp', axis=2, tiled=True)  97.9 us
    reduce_scatter x2, waiting for transfers between devices, on_device(): lax.psum_scatter(moe_in_part, 'tensor', scatter_dimension=0, tiled=True)  79.5 us
  transfers between devices with their start and end apart: 24, of which 17 were waited for; matrix products, arithmetic and copies ran while one was open for 28% of the time, Pallas kernels for 0%

commit v1 on v0

v1 whole, which is shorter than its diff:
```python
import functools
import math

import jax
import jax.numpy as jnp
from jax import lax
from jax.experimental import pallas as pl
from jax.experimental.pallas import tpu as pltpu
from jax.sharding import Mesh
from jax.sharding import PartitionSpec as P

HD = 64
E = 32
PROMPT = 512
CONT = 512
CHUNKS = 4

EPSILON = 1e-06
BF = jnp.bfloat16
FP = jnp.float32


def dot_nn(left, right):
    return lax.dot_general(left, right, (((1,), (0,)), ((), ())), preferred_element_type=FP)


def dot_tn(left, right):
    return lax.dot_general(left, right, (((0,), (0,)), ((), ())), preferred_element_type=FP)


def dot_nt(left, right):
    return lax.dot_general(left, right, (((1,), (1,)), ((), ())), preferred_element_type=FP)


def row_norm(in_rows, gain_vec):
    row_scale = lax.rsqrt(jnp.mean(in_rows * in_rows, axis=-1, keepdims=True) + EPSILON)
    return (in_rows * row_scale * gain_vec, row_scale)


def norm_back(in_rows, row_scale, gain_vec, grad_in):
    weighted = grad_in * gain_vec
    inner = jnp.mean(weighted * in_rows, axis=-1, keepdims=True)
    returned = row_scale * weighted - in_rows * row_scale * row_scale * row_scale * inner
    gain_part = jnp.sum(grad_in * in_rows * row_scale, axis=0)
    return (returned, gain_part)


def swap(value, axis):
    return lax.ppermute(value, axis, [(0, 1), (1, 0)])


def in_order(mine, other, axis, dim):
    first = lax.axis_index(axis) == 0
    return jnp.stack([jnp.where(first, mine, other), jnp.where(first, other, mine)], axis=dim)


def gather_rows(rows):
    pair = in_order(rows, swap(rows, "x"), "x", -3)
    whole = in_order(pair, swap(pair, "c"), "c", -3)
    return whole.reshape(*rows.shape[:-2], 4 * rows.shape[-2], rows.shape[-1])


def scatter_rows(partial):
    rows, width = partial.shape
    parts = partial.reshape(2, 2, rows // 4, width)
    core, chip = lax.axis_index("c"), lax.axis_index("x")
    sent = lax.dynamic_index_in_dim(parts, 1 - core, 1, False).astype(BF)
    kept = lax.dynamic_index_in_dim(parts, core, 1, False).astype(FP)
    half = kept + swap(sent, "c").astype(FP)
    sent = lax.dynamic_index_in_dim(half, 1 - chip, 0, False).astype(BF)
    kept = lax.dynamic_index_in_dim(half, chip, 0, False)
    return kept + swap(sent, "x").astype(FP)


def gather_dp(shard, depth):
    turn_up = [(i, (i + 1) % depth) for i in range(depth)]
    turn_down = [(i, (i - 1) % depth) for i in range(depth)]
    before, after = [], []
    piece = shard
    for _ in range(depth // 2):
        piece = lax.ppermute(piece, "z", turn_up)
        before.append(piece)
    piece = shard
    for _ in range((depth - 1) // 2):
        piece = lax.ppermute(piece, "z", turn_down)
        after.append(piece)
    line = before[::-1] + [shard] + after
    place = lax.axis_index("z")
    start = lax.rem(depth + len(before) - place, depth)
    column = lax.dynamic_slice_in_dim(jnp.stack(line + line), start, depth, 0)
    return in_order(column, swap(column, "y"), "y", 1).reshape(-1, shard.shape[-1])


def scatter_dp(partial, depth):
    blocks = partial.reshape(depth, 2, -1, partial.shape[-1])
    mine = lax.axis_index("y")
    sent = lax.dynamic_index_in_dim(blocks, 1 - mine, 1, False).astype(BF)
    kept = lax.dynamic_index_in_dim(blocks, mine, 1, False)
    column = (kept + swap(sent, "y").astype(FP)).astype(BF)
    return lax.psum_scatter(column, "z", scatter_dimension=0, tiled=False)


def moe_kernel(first, side_ref, x_ref, g_ref, gate_ref, mine_ref, other_ref, *rest):
    if first:
        mixed_ref, back_ref, gmine_ref, gother_ref, w_scr, acc = rest
    else:
        mixed_in, back_in, mixed_ref, back_ref, gmine_ref, gother_ref, w_scr, acc = rest
    step = pl.program_id(0)
    depth, pairs, blk, width = mine_ref.shape
    half = width // 3
    side = side_ref[0]

    def spot(z, y):
        return pl.ds(pl.multiple_of((z * 2 + y) * blk, blk), blk)

    @pl.when(step == 0)
    def _():
        for p in range(pairs):
            for z in range(depth):
                w_scr[p, spot(z, side), :] = mine_ref[z, p]
                w_scr[p, spot(z, 1 - side), :] = other_ref[z, p]
        acc[...] = jnp.zeros_like(acc)

    x = x_ref[...]
    g = g_ref[...]
    hidden_local = half // 2
    mixed = None
    back = None
    for p in range(pairs):
        weights = w_scr.at[p]
        pre = dot_nn(x, weights[:, : 2 * half])
        out_back = dot_nn(g, weights[:, 2 * half :])
        gate = pre[:, :half]
        up = pre[:, half:]
        sig = 0.5 + 0.5 * jnp.tanh(0.5 * gate)
        share = jnp.concatenate(
            [
                jnp.broadcast_to(gate_ref[:, i : i + 1], (x.shape[0], hidden_local))
                for i in (2 * p, 2 * p + 1)
            ],
            axis=1,
        )
        silu = gate * sig
        hidden = (share * (silu * up)).astype(BF)
        hidden_grad = share * out_back
        gate_grad = (hidden_grad * up * sig * (1.0 + gate * (1.0 - sig))).astype(BF)
        up_grad = (hidden_grad * silu).astype(BF)
        pair_grad = jnp.concatenate([gate_grad, up_grad], axis=1)
        mixed_p = dot_nt(hidden, weights[:, 2 * half :])
        back_p = dot_nt(pair_grad, weights[:, : 2 * half])
        mixed = mixed_p if mixed is None else mixed + mixed_p
        back = back_p if back is None else back + back_p
        acc[p, :, : 2 * half] += dot_tn(x, pair_grad)
        acc[p, :, 2 * half :] += dot_tn(g, hidden)
    if first:
        mixed_ref[...] = mixed
        back_ref[...] = back
    else:
        mixed_ref[...] = mixed_in[...] + mixed
        back_ref[...] = back_in[...] + back

    @pl.when(step == pl.num_programs(0) - 1)
    def _():
        for p in range(pairs):
            for z in range(depth):
                gmine_ref[z, p] = acc[p, spot(z, side), :].astype(BF)
                gother_ref[z, p] = acc[p, spot(z, 1 - side), :].astype(BF)


def moe_chunk(side, x, g, gates, mine, other, sums):
    rows, model_width = x.shape
    tile = 256
    pairs, width = mine.shape[1], mine.shape[3]
    once = pl.Buffered(1)
    row = pl.BlockSpec((tile, model_width), lambda i, s: (i, 0))
    gate_spec = pl.BlockSpec((tile, gates.shape[1]), lambda i, s: (i, 0))
    whole = pl.BlockSpec(mine.shape, lambda i, s: (0, 0, 0, 0), pipeline_mode=once)
    first = sums is None
    operands = [side, x, g, gates, mine, other] + ([] if first else list(sums))
    return pl.pallas_call(
        functools.partial(moe_kernel, first),
        grid_spec=pltpu.PrefetchScalarGridSpec(
            num_scalar_prefetch=1,
            grid=(rows // tile,),
            in_specs=[row, row, gate_spec, whole, whole] + ([] if first else [row, row]),
            out_specs=[row, row, whole, whole],
            scratch_shapes=[
                pltpu.VMEM((pairs, model_width, width), BF),
                pltpu.VMEM((pairs, model_width, width), FP),
            ],
        ),
        out_shape=[jax.ShapeDtypeStruct((rows, model_width), FP)] * 2
        + [jax.ShapeDtypeStruct(mine.shape, BF)] * 2,
        input_output_aliases={} if first else {6: 0, 7: 1},
        compiler_params=pltpu.CompilerParams(vmem_limit_bytes=60 << 20),
        cost_estimate=pl.CostEstimate(
            flops=6 * rows * model_width * pairs * width,
            bytes_accessed=48 << 20,
            transcendentals=rows * pairs * width // 3,
        ),
    )(*operands)


def pack_experts(w_gate_up, w_down):
    blk, hidden_local = w_gate_up.shape[1], w_gate_up.shape[3]
    gate_up = w_gate_up.reshape(E // 2, 2, blk, 2, hidden_local).transpose(0, 2, 3, 1, 4)
    down = w_down.reshape(E // 2, 2, hidden_local, blk).transpose(0, 3, 1, 2)
    return jnp.concatenate(
        [gate_up.reshape(E // 2, blk, -1), down.reshape(E // 2, blk, -1)], axis=-1
    )


def unpack_experts(packed):
    pairs, blk, width = packed.shape
    hidden_local = width // 6
    packed = packed.astype(FP)
    gate_up = packed[:, :, : 4 * hidden_local].reshape(pairs, blk, 2, 2, hidden_local)
    down = packed[:, :, 4 * hidden_local :].reshape(pairs, blk, 2, hidden_local)
    return (
        gate_up.transpose(0, 3, 1, 2, 4).reshape(2 * pairs, blk, 2, hidden_local),
        down.transpose(0, 2, 3, 1).reshape(2 * pairs, hidden_local, blk),
    )


def mask_scores(query_blk, key_set, prefix, score_scale):
    scores = (
        jnp.einsum("bgrd,lgd->grbl", query_blk, key_set, preferred_element_type=FP) * score_scale
    )
    row_pos = lax.broadcasted_iota(jnp.int32, scores.shape, 2)
    col_pos = lax.broadcasted_iota(jnp.int32, scores.shape, 3)
    allowed = (col_pos < prefix) | (col_pos - prefix <= row_pos)
    return jnp.where(allowed, scores, -1e30)


def segments(rows):
    return ((0, PROMPT, 0), (PROMPT, rows - PROMPT, PROMPT))


def attention_forward(query, keys_all, values_all, score_scale):
    outputs = []
    saved = []
    for start_row, length, prefix in segments(query.shape[0]):
        key_set, value_set = keys_all[: start_row + length], values_all[: start_row + length]
        query_blk = query[start_row : start_row + length]
        scores = mask_scores(query_blk, key_set, prefix, score_scale)
        row_max = jnp.max(scores, axis=-1, keepdims=True)
        exponent = jnp.exp(scores - row_max)
        row_total = jnp.sum(exponent, axis=-1, keepdims=True)
        attn_probs = (exponent / row_total).astype(BF)
        outputs.append(
            jnp.einsum("grbl,lgd->bgrd", attn_probs, value_set, preferred_element_type=FP)
        )
        saved.append(row_max + jnp.log(row_total))
    return (jnp.concatenate(outputs, axis=0), saved)


def attention_backward(query, keys_all, values_all, head_grad, saved, score_scale):
    query_parts = []
    key_grad = jnp.zeros(keys_all.shape, FP)
    value_grad = jnp.zeros(values_all.shape, FP)
    for (start_row, length, prefix), saved_part in zip(segments(query.shape[0]), saved):
        stop = start_row + length
        key_set, value_set = keys_all[:stop], values_all[:stop]
        query_blk = query[start_row:stop]
        grad_blk = head_grad[start_row:stop]
        scores = mask_scores(query_blk, key_set, prefix, score_scale)
        attn_probs = jnp.exp(scores - saved_part)
        prob_grad = jnp.einsum("bgrd,lgd->grbl", grad_blk, value_set, preferred_element_type=FP)
        inner = jnp.sum(attn_probs * prob_grad, axis=-1, keepdims=True)
        score_grad = (attn_probs * (prob_grad - inner)).astype(BF)
        query_parts.append(
            jnp.einsum("grbl,lgd->bgrd", score_grad, key_set, preferred_element_type=FP)
            * score_scale
        )
        key_part = (
            jnp.einsum("grbl,bgrd->lgd", score_grad, query_blk, preferred_element_type=FP)
            * score_scale
        )
        value_part = jnp.einsum(
            "grbl,bgrd->lgd", attn_probs.astype(BF), grad_blk, preferred_element_type=FP
        )
        key_grad = key_grad.at[:stop].add(key_part)
        value_grad = value_grad.at[:stop].add(value_part)
    return (jnp.concatenate(query_parts, axis=0), key_grad, value_grad)


def on_device(
    block_input,
    cotangent,
    routes,
    gate_weights,
    w_query,
    w_key,
    w_value,
    w_out,
    w_gate_up,
    w_down,
    norm_attn,
    norm_moe,
):
    score_scale = 1.0 / math.sqrt(HD)
    depth = lax.axis_size("z")
    micro_count, rows_local, model_width = block_input.shape
    kv_local = w_key.shape[1] // HD
    q_width, kv_width = w_query.shape[1], w_key.shape[1]
    head_ratio = q_width // kv_width
    proj_width = q_width + 2 * kv_width
    side = lax.axis_index("y").astype(jnp.int32).reshape(1)

    packed_attn = jnp.concatenate([w_query, w_key, w_value, w_out.T], axis=1)
    attn_full = gather_dp(packed_attn, depth)
    w_project, out_t = attn_full[:, :proj_width], attn_full[:, proj_width:]
    packed = pack_experts(w_gate_up, w_down)
    per_chunk = packed.shape[0] // CHUNKS
    chunk_weights = []
    for chunk in range(CHUNKS):
        mine = lax.all_gather(packed[chunk * per_chunk : (chunk + 1) * per_chunk], "z", axis=0)
        chunk_weights.append((mine, swap(mine, "y")))

    in_rows = block_input.astype(FP)
    normed_attn, scale_attn = row_norm(in_rows, norm_attn)
    normed_attn = normed_attn.astype(BF)
    attn_in, projections, saved_all, heads_all = [], [], [], []
    middles = []
    for m in range(micro_count):
        attn_in.append(gather_rows(normed_attn[m]))
        projected = dot_nn(attn_in[m], w_project).astype(BF)
        query = projected[:, :q_width].reshape(-1, kv_local, head_ratio, HD)
        keys_all = projected[:, q_width : q_width + kv_width].reshape(-1, kv_local, HD)
        values_all = projected[:, q_width + kv_width :].reshape(-1, kv_local, HD)
        attn_raw, saved = attention_forward(query, keys_all, values_all, score_scale)
        head_out = attn_raw.astype(BF).reshape(-1, q_width)
        projections.append((query, keys_all, values_all))
        saved_all.append(saved)
        heads_all.append(head_out)
        middles.append(in_rows[m] + scatter_rows(dot_nt(head_out, out_t)))
    middle = jnp.stack(middles)
    normed_moe, scale_moe = row_norm(middle, norm_moe)
    moe_in = jnp.concatenate([gather_rows(normed_moe[m].astype(BF)) for m in range(micro_count)])
    moe_grad = gather_rows(cotangent).reshape(-1, model_width)

    expert_ids = jnp.arange(E, dtype=jnp.int32)
    gates = jnp.sum(
        jnp.where(routes[..., None] == expert_ids, gate_weights[..., None], 0.0), axis=2
    ).reshape(-1, CHUNKS, 2 * per_chunk)
    sums = None
    shards = []
    for chunk in range(CHUNKS):
        mine, other = chunk_weights[chunk]
        *sums, grad_mine, grad_other = moe_chunk(
            side, moe_in, moe_grad, gates[:, chunk], mine, other, sums
        )
        column = (grad_mine.astype(FP) + swap(grad_other, "y").astype(FP)).astype(BF)
        shards.append(lax.psum_scatter(column, "z", scatter_dimension=0, tiled=False))
    mixed, moe_back = (s.reshape(micro_count, -1, model_width) for s in sums)
    shard_pair, shard_down = unpack_experts(jnp.concatenate(shards))

    out_grad = cotangent.astype(FP)
    outputs, input_grads = [], []
    gain_attn_total = jnp.zeros(norm_attn.shape, FP)
    gain_moe_total = jnp.zeros(norm_moe.shape, FP)
    attn_grad_total = None
    for m in range(micro_count):
        moe_in_grad = scatter_rows(moe_back[m])
        middle_back, gain_moe_part = norm_back(middle[m], scale_moe[m], norm_moe, moe_in_grad)
        middle_grad = out_grad[m] + middle_back
        attn_grad = gather_rows(middle_grad.astype(BF))
        out_weight_grad = dot_tn(attn_grad, heads_all[m])
        head_grad = dot_nn(attn_grad, out_t).astype(BF).reshape(-1, kv_local, head_ratio, HD)
        query_grad, key_grad, value_grad = attention_backward(
            *projections[m], head_grad, saved_all[m], score_scale
        )
        project_grad = jnp.concatenate(
            [
                query_grad.reshape(-1, q_width),
                key_grad.reshape(-1, kv_width),
                value_grad.reshape(-1, kv_width),
            ],
            axis=1,
        ).astype(BF)
        weight_grad = jnp.concatenate([dot_tn(attn_in[m], project_grad), out_weight_grad], axis=1)
        attn_grad_total = weight_grad if m == 0 else attn_grad_total + weight_grad
        attn_in_grad = scatter_rows(dot_nt(project_grad, w_project))
        in_back, gain_attn_part = norm_back(in_rows[m], scale_attn[m], norm_attn, attn_in_grad)
        input_grads.append(middle_grad + in_back)
        outputs.append((middle[m] + scatter_rows(mixed[m])).astype(BF))
        gain_attn_total = gain_attn_total + gain_attn_part
        gain_moe_total = gain_moe_total + gain_moe_part
    attn_shard = scatter_dp(attn_grad_total, depth).astype(FP)
    gain_attn_grad, gain_moe_grad = lax.psum(
        (gain_attn_total, gain_moe_total), ("z", "y", "x", "c")
    )
    return (
        jnp.stack(outputs),
        jnp.stack(input_grads),
        attn_shard[:, :q_width],
        attn_shard[:, q_width : q_width + kv_width],
        attn_shard[:, q_width + kv_width : proj_width],
        attn_shard[:, proj_width:].T,
        shard_pair,
        shard_down,
        gain_attn_grad,
        gain_moe_grad,
    )


def solution(mesh):
    dp, tensor = mesh.shape["dp"], mesh.shape["tensor"]
    fine = Mesh(mesh.devices.reshape(dp // 2, 2, tensor // 2, 2), ("z", "y", "x", "c"))
    dp_axes, tensor_axes = ("z", "y"), ("x", "c")
    rows = P(None, dp_axes + tensor_axes, None)
    return jax.shard_map(
        on_device,
        mesh=fine,
        in_specs=(
            rows,
            rows,
            P(None, dp_axes, None),
            P(None, dp_axes, None),
            P(dp_axes, tensor_axes),
            P(dp_axes, tensor_axes),
            P(dp_axes, tensor_axes),
            P(tensor_axes, dp_axes),
            P(None, dp_axes, None, tensor_axes),
            P(None, tensor_axes, dp_axes),
            P(),
            P(),
        ),
        out_specs=(
            rows,
            rows,
            P(dp_axes, tensor_axes),
            P(dp_axes, tensor_axes),
            P(dp_axes, tensor_axes),
            P(tensor_axes, dp_axes),
            P(None, dp_axes, None, tensor_axes),
            P(None, tensor_axes, dp_axes),
            P(),
            P(),
        ),
        check_vma=False,
    )
```

time: 3450 us -> 1040 us (0.30)
  waiting for transfers between devices: 1410 us -> 449 us
  other arithmetic: 771 us -> 84.8 us
  local copies, waits for them, and re-layouts: 666 us -> 121 us
  matrix products: 402 us -> 59.4 us
  Pallas kernels: 0 us -> 224 us
  blocking collectives: 167 us -> 41.9 us
  starting transfers between devices: 2.88 us -> 39.4 us
    reduce_scatter x14 -> x5, waiting for transfers between devices: 1220 us -> 0.04 us  [the longest x4 0.03 us: on_device(): lax.psum_scatter(column, 'z', scatter_dimension=0, tiled=False)]
    scatter-add x40 -> x0, other arithmetic: 602 us -> none  [the longest x16 301 us: one_block(): jax.ops.segment_sum(flat_out, source_block, num_segments=moe_in.shape[0])]
    ppermute x0 -> x43, waiting for transfers between devices: none -> 376 us  [the longest x40 361 us: swap(): return lax.ppermute(value, axis, [(0, 1), (1, 0)])]
    dot_general x108 -> x12, matrix products: 371 us -> 17.9 us  [the longest x4 9.71 us: dot_tn(): lax.dot_general(left, right, (((0,), (0,)), ((), ())), preferred_element_...]
    gather x48 -> x0, local copies, waits for them, and re-layouts: 296 us -> none  [the longest x32 160 us: gather_slots(): moe_in[source_block]]
    pallas_call x0 -> x4, Pallas kernels: none -> 224 us  [moe_chunk(): pl.pallas_call(functools.partial(moe_kernel, first), grid_spec=pltpu.Pref...]
    scatter x6 -> x0, local copies, waits for them, and re-layouts: 184 us -> none  [the longest x2 61.5 us: slot_tables(): filled = jnp.zeros((E * CAP,), FP).at[slot_index].set(1.0)]
    all_gather x4 -> x0, blocking collectives: 122 us -> none  [the longest x1 32.7 us: fetch_weights(): lax.all_gather(w_key, 'dp', axis=0, tiled=True)]
  transfers between devices with their start and end apart: 24 -> 52, of which waited for: 17 -> 24; matrix products, arithmetic and copies ran while one was open for 28% -> 19% of each run, Pallas kernels for 0% -> 16%
where the time goes in v1:
time: 1040 us
  waiting for transfers between devices  449 us (43%)
  Pallas kernels  224 us (22%)
  local copies, waits for them, and re-layouts  121 us (12%)
  other arithmetic  84.8 us (8%)
  matrix products  59.4 us (6%)
  blocking collectives  41.9 us (4%)
  starting transfers between devices  39.4 us (4%)
  between operations  16.5 us (2%)
    ppermute x40, waiting for transfers between devices, swap(): return lax.ppermute(value, axis, [(0, 1), (1, 0)])  361 us
    pallas_call x4, Pallas kernels, moe_chunk(): pl.pallas_call(functools.partial(moe_kernel, first), grid_spec=pltpu.Pref...  224 us
    all_gather x4, waiting for transfers between devices, on_device(): lax.all_gather(packed[chunk * per_chunk:(chunk + 1) * per_chunk], 'z', ax...  71.9 us
    psum x1, blocking collectives, on_device(): lax.psum((gain_attn_total, gain_moe_total), ('z', 'y', 'x', 'c'))  41.9 us
    ppermute x40, starting transfers between devices, swap(): return lax.ppermute(value, axis, [(0, 1), (1, 0)])  33.7 us
    unnamed x298, local copies, waits for them, and re-layouts  30.3 us
    another operation x27, other arithmetic, in_order(): jnp.stack([jnp.where(first, mine, other), jnp.where(first, other, mine)],...  27.2 us
  transfers between devices with their start and end apart: 52, of which 24 were waited for; matrix products, arithmetic and copies ran while one was open for 19% of the time, Pallas kernels for 16%

profile of v1, /device:TPU:0, one launch (start us, length us, event | category | flops | bytes accessed | tf_op | source)
XLA Modules:
  0.0 1035.9 jit_solution(11890033114070008870)
XLA Ops:
  39.1 10.0 collective-permute-done.3
  52.3 8.6 collective-permute-done.8
  124.5 17.3 %collective-permute-done.16 = bf16[2,256,1024]{2,1,0:T(8,128)(2,1)} collective-permute-done((bf16[2,256,1024]{2,1,0:T(8,128)(2,1)}, bf16[2,256,1024]{2,1,0:T(8,128)(2,1)}, u32[]{:S(2)}, u32[]{:S(2)}) %collective-permute-start.16) | collective-permute-done | bytes 1048608 | tf_op jit(solution)/shard_map/ppermute | solution.py:49
  153.0 10.4 %collective-permute-done.7 = bf16[256,1024]{1,0:T(8,128)(2,1)} collective-permute-done((bf16[256,1024]{1,0:T(8,128)(2,1)}, bf16[256,1024]{1,0:T(8,128)(2,1)}, u32[]{:S(2)}, u32[]{:S(2)}) %collective-permute-start.7) | collective-permute-done | bytes 524320 | tf_op jit(solution)/shard_map/ppermute | solution.py:49
  170.8 11.1 %collective-permute-done.12 = bf16[256,1024]{1,0:T(8,128)(2,1)S(1)} collective-permute-done((bf16[256,1024]{1,0:T(8,128)(2,1)}, bf16[256,1024]{1,0:T(8,128)(2,1)S(1)}, u32[]{:S(2)}, u32[]{:S(2)}) %collective-permute-start.12) | collective-permute-done | bytes 524320 | tf_op jit(solution)/shard_map/ppermute | solution.py:49
  182.7 8.8 collective-permute-done.14
  213.3 9.8 all-gather.11.cloned.1.call-done
  224.5 62.1 %all-gather.9.cloned.1.call-done = bf16[16,128,768]{2,1,0:T(8,128)(2,1)} async-done(((bf16[4,128,768]{2,1,0:T(8,128)(2,1)}), bf16[16,128,768]{2,1,0:T(8,128)(2,1)}) %all-gather.9.cloned.1.call-update) | async-done | bytes 3145744 | tf_op jit(solution)/shard_map/all_gather | solution.py:317
  292.2 55.2 %shard_map.215 = (f32[2048,1024]{1,0:T(8,128)}, f32[2048,1024]{1,0:T(8,128)}, bf16[4,4,128,768]{3,2,1,0:T(8,128)(2,1)}, bf16[4,4,128,768]{3,2,1,0:T(8,128)(2,1)}) custom-call(s32[1]{0:T(128)} %bitcast.42.side_ref, bf16[2048,1024]{1,0:T(8,128)(2,1)} %pad_maximum_fusion.x_ref, bf16[2048,1024]{1,0:T(8,128)(2,1)} %bitcast.651, f32[2048,8]{1,0:T(8,128)} %bitcast.697, ...), custom_call_target="tpu_custom_call" | custom-call | flops 38654705664 | bytes 50331648 | tf_op jit(solution)/shard_map/pallas_call | solution.py:180
  347.4 56.1 %shard_map.216 = (f32[2048,1024]{1,0:T(8,128)}, f32[2048,1024]{1,0:T(8,128)}, bf16[4,4,128,768]{3,2,1,0:T(8,128)(2,1)}, bf16[4,4,128,768]{3,2,1,0:T(8,128)(2,1)}) custom-call(s32[1]{0:T(128)} %bitcast.42.side_ref, bf16[2048,1024]{1,0:T(8,128)(2,1)} %pad_maximum_fusion.x_ref, ...), custom_call_target="tpu_custom_call", output_to_operand_aliasing={{0}: (6, {}), {1}: (7, {})} | custom-call | flops 38654705664 | bytes 50331648 | tf_op jit(solution)/shard_map/pallas_call | solution.py:180
  403.4 56.3 %shard_map.217 = (f32[2048,1024]{1,0:T(8,128)}, f32[2048,1024]{1,0:T(8,128)}, bf16[4,4,128,768]{3,2,1,0:T(8,128)(2,1)}, bf16[4,4,128,768]{3,2,1,0:T(8,128)(2,1)}) custom-call(s32[1]{0:T(128)} %bitcast.42.side_ref, bf16[2048,1024]{1,0:T(8,128)(2,1)} %pad_maximum_fusion.x_ref, ...), custom_call_target="tpu_custom_call", output_to_operand_aliasing={{0}: (6, {}), {1}: (7, {})} | custom-call | flops 38654705664 | bytes 50331648 | tf_op jit(solution)/shard_map/pallas_call | solution.py:180
  459.7 56.3 %shard_map.218 = (f32[2048,1024]{1,0:T(8,128)}, f32[2048,1024]{1,0:T(8,128)}, bf16[4,4,128,768]{3,2,1,0:T(8,128)(2,1)}, bf16[4,4,128,768]{3,2,1,0:T(8,128)(2,1)}) custom-call(s32[1]{0:T(128)} %bitcast.42.side_ref, bf16[2048,1024]{1,0:T(8,128)(2,1)} %pad_maximum_fusion.x_ref, ...), custom_call_target="tpu_custom_call", output_to_operand_aliasing={{0}: (6, {}), {1}: (7, {})} | custom-call | flops 38654705664 | bytes 50331648 | tf_op jit(solution)/shard_map/pallas_call | solution.py:180
  533.0 8.9 collective-permute-done.33
  541.8 11.2 %collective-permute-done.27 = bf16[256,1024]{1,0:T(8,128)(2,1)S(1)} collective-permute-done((bf16[256,1024]{1,0:T(8,128)(2,1)S(1)}, bf16[256,1024]{1,0:T(8,128)(2,1)S(1)}, u32[]{:S(2)}, u32[]{:S(2)}) %collective-permute-start.27) | collective-permute-done | bytes 524320 | tf_op jit(solution)/shard_map/ppermute | solution.py:49
  553.9 10.4 %collective-permute-done.23 = bf16[256,1024]{1,0:T(8,128)(2,1)S(1)} collective-permute-done((bf16[256,1024]{1,0:T(8,128)(2,1)S(1)}, bf16[256,1024]{1,0:T(8,128)(2,1)S(1)}, u32[]{:S(2)}, u32[]{:S(2)}) %collective-permute-start.23) | collective-permute-done | bytes 524320 | tf_op jit(solution)/shard_map/ppermute | solution.py:49
  564.3 10.3 collective-permute-done.25
  579.5 12.8 %collective-permute-done.34 = bf16[256,1024]{1,0:T(8,128)(2,1)} collective-permute-done((bf16[256,1024]{1,0:T(8,128)(2,1)S(1)}, bf16[256,1024]{1,0:T(8,128)(2,1)}, u32[]{:S(2)}, u32[]{:S(2)}) %collective-permute-start.34) | collective-permute-done | bytes 524320 | tf_op jit(solution)/shard_map/ppermute | solution.py:49
  677.1 18.6 %collective-permute-done.38 = bf16[4,128,768]{2,1,0:T(8,128)(2,1)} collective-permute-done((bf16[4,128,768]{2,1,0:T(8,128)(2,1)}, bf16[4,128,768]{2,1,0:T(8,128)(2,1)}, u32[]{:S(2)}, u32[]{:S(2)}) %collective-permute-start.38) | collective-permute-done | bytes 786464 | tf_op jit(solution)/shard_map/ppermute | solution.py:49
  705.2 68.2 %collective-permute-done.41 = bf16[4,4,128,768]{3,2,1,0:T(8,128)(2,1)S(1)} collective-permute-done((bf16[4,4,128,768]{3,2,1,0:T(8,128)(2,1)}, bf16[4,4,128,768]{3,2,1,0:T(8,128)(2,1)S(1)}, u32[]{:S(2)}, u32[]{:S(2)}) %collective-permute-start.41) | collective-permute-done | bytes 3145760 | tf_op jit(solution)/shard_map/ppermute | solution.py:49
  777.7 67.4 %collective-permute-done.42 = bf16[4,4,128,768]{3,2,1,0:T(8,128)(2,1)S(1)} collective-permute-done((bf16[4,4,128,768]{3,2,1,0:T(8,128)(2,1)}, bf16[4,4,128,768]{3,2,1,0:T(8,128)(2,1)S(1)}, u32[]{:S(2)}, u32[]{:S(2)}) %collective-permute-start.42) | collective-permute-done | bytes 3145760 | tf_op jit(solution)/shard_map/ppermute | solution.py:49
  849.4 66.6 %collective-permute-done.39 = bf16[4,4,128,768]{3,2,1,0:T(8,128)(2,1)S(1)} collective-permute-done((bf16[4,4,128,768]{3,2,1,0:T(8,128)(2,1)}, bf16[4,4,128,768]{3,2,1,0:T(8,128)(2,1)S(1)}, u32[]{:S(2)}, u32[]{:S(2)}) %collective-permute-start.39) | collective-permute-done | bytes 3145760 | tf_op jit(solution)/shard_map/ppermute | solution.py:49
  929.4 10.6 %collective-permute-done.37 = bf16[256,1024]{1,0:T(8,128)(2,1)S(1)} collective-permute-done((bf16[256,1024]{1,0:T(8,128)(2,1)S(1)}, bf16[256,1024]{1,0:T(8,128)(2,1)S(1)}, u32[]{:S(2)}, u32[]{:S(2)}) %collective-permute-start.37) | collective-permute-done | bytes 524320 | tf_op jit(solution)/shard_map/ppermute | solution.py:49
  940.0 10.4 %collective-permute-done.31 = bf16[256,1024]{1,0:T(8,128)(2,1)S(1)} collective-permute-done((bf16[256,1024]{1,0:T(8,128)(2,1)S(1)}, bf16[256,1024]{1,0:T(8,128)(2,1)S(1)}, u32[]{:S(2)}, u32[]{:S(2)}) %collective-permute-start.31) | collective-permute-done | bytes 524320 | tf_op jit(solution)/shard_map/ppermute | solution.py:49
  951.2 41.9 %all-reduce.4 = (f32[1024]{0:T(1024)}, f32[1024]{0:T(1024)}) all-reduce(f32[1024]{0:T(1024)S(1)} %add.342, f32[1024]{0:T(1024)S(1)} %add.343), channel_id=1, replica_groups=mesh['z'=4,'y'=2,'x'=2,'c'=2] {'z','y','x','c'}, use_global_device_ids=true, to_apply=%region_26.27 | all-reduce | flops 2048 | bytes 16384 | tf_op jit(solution)/shard_map/psum | solution.py:390
  (588 shorter events, 320.3 us)
Async XLA Ops:
  7.2 161.7 %all-gather.15.cloned.1.call-start = ((), (), s32[]{:S(2)}) async-start(), calls=%async_computation.13 | async-start | bytes 3932160 | tf_op jit(solution)/shard_map/all_gather | solution.py:317
  24.0 188.1 %all-gather.13.cloned.1.call-start = ((), (), s32[]{:S(2)}) async-start(), calls=%async_computation.12 | async-start | bytes 3932160 | tf_op jit(solution)/shard_map/all_gather | solution.py:317
  24.7 198.3 %all-gather.11.cloned.1.call-start = ((), (), s32[]{:S(2)}) async-start(), calls=%async_computation.11 | async-start | bytes 3932160 | tf_op jit(solution)/shard_map/all_gather | solution.py:317
  64.2 222.5 %all-gather.9.cloned.1.call-start = ((), (), s32[]{:S(2)}) async-start(), calls=%async_computation.10 | async-start | bytes 3932160 | tf_op jit(solution)/shard_map/all_gather | solution.py:317
  115.4 26.3 %collective-permute-start.16 = (bf16[2,256,1024]{2,1,0:T(8,128)(2,1)}, bf16[2,256,1024]{2,1,0:T(8,128)(2,1)}, u32[]{:S(2)}, u32[]{:S(2)}) collective-permute-start(bf16[2,256,1024]{2,1,0:T(8,128)(2,1)} %param.37), channel_id=1, source_target_pairs={{0,2},{2,0},{1,3},{3,1},{4,6},{6,4},{5,7},{7,5},{8,10},{10,8},{9,1... | collective-permute-start | bytes 3145736 | tf_op jit(solution)/shard_map/ppermute | solution.py:49
  116.6 880.9 %reduce-scatter.6.cloned.1.call-start = ((), (), s32[]{:S(2)}) async-start(), calls=%async_computation.5 | async-start | bytes 983040 | tf_op jit(solution)/shard_map/reduce_scatter | solution.py:100
  120.2 32.8 %collective-permute-start.11 = (bf16[256,1024]{1,0:T(8,128)(2,1)}, bf16[256,1024]{1,0:T(8,128)(2,1)}, u32[]{:S(2)}, u32[]{:S(2)}) collective-permute-start(bf16[256,1024]{1,0:T(8,128)(2,1)} %fusion.110), channel_id=1, source_target_pairs={{0,2},{2,0},{1,3},{3,1},{4,6},{6,4},{5,7},{7,5},{8,10},{10,8},{9,1... | collective-permute-start | bytes 1572872 | tf_op jit(solution)/shard_map/ppermute | solution.py:49
  123.0 40.3 %collective-permute-start.7 = (bf16[256,1024]{1,0:T(8,128)(2,1)}, bf16[256,1024]{1,0:T(8,128)(2,1)}, u32[]{:S(2)}, u32[]{:S(2)}) collective-permute-start(bf16[256,1024]{1,0:T(8,128)(2,1)} %fusion.109), channel_id=1, source_target_pairs={{0,2},{2,0},{1,3},{3,1},{4,6},{6,4},{5,7},{7,5},{8,10},{10,8},{9,1... | collective-permute-start | bytes 1572872 | tf_op jit(solution)/shard_map/ppermute | solution.py:49
  146.7 56.5 %collective-permute-start.17 = (bf16[2,2,256,1024]{3,2,0,1:T(8,128)(2,1)}, bf16[2,2,256,1024]{3,2,0,1:T(8,128)(2,1)}, u32[]{:S(2)}, u32[]{:S(2)}) collective-permute-start(bf16[2,2,256,1024]{3,2,0,1:T(8,128)(2,1)} %pad_maximum_fusion.7), channel_id=1, source_target_pairs={{0,1},{1,0},{2,3},{3,2},{4,5},{5,4},{6,7},{7,6},{8,9},{9,8},{10,11... | collective-permute-start | bytes 6291464 | tf_op jit(solution)/shard_map/ppermute | solution.py:49
  168.9 123.3 %collective-permute-start.21 = (bf16[4,4,128,768]{3,2,1,0:T(8,128)(2,1)}, bf16[4,4,128,768]{3,2,1,0:T(8,128)(2,1)}, u32[]{:S(2)}, u32[]{:S(2)}) collective-permute-start(bf16[4,4,128,768]{3,2,1,0:T(8,128)(2,1)} %bitcast.737), channel_id=1, source_target_pairs={{0,4},{4,0},{1,5},{5,1},{2,6},{6,2},{3,7},{7,3},{8,12},{12,8},{9,1... | collective-permute-start | bytes 9437192 | tf_op jit(solution)/shard_map/ppermute | solution.py:49
  212.0 135.3 %collective-permute-start.20 = (bf16[4,4,128,768]{3,2,1,0:T(8,128)(2,1)}, bf16[4,4,128,768]{3,2,1,0:T(8,128)(2,1)}, u32[]{:S(2)}, u32[]{:S(2)}) collective-permute-start(bf16[4,4,128,768]{3,2,1,0:T(8,128)(2,1)} %bitcast.735), channel_id=1, source_target_pairs={{0,4},{4,0},{1,5},{5,1},{2,6},{6,2},{3,7},{7,3},{8,12},{12,8},{9,1... | collective-permute-start | bytes 9437192 | tf_op jit(solution)/shard_map/ppermute | solution.py:49
  223.0 180.4 %collective-permute-start.19 = (bf16[4,4,128,768]{3,2,1,0:T(8,128)(2,1)}, bf16[4,4,128,768]{3,2,1,0:T(8,128)(2,1)}, u32[]{:S(2)}, u32[]{:S(2)}) collective-permute-start(bf16[4,4,128,768]{3,2,1,0:T(8,128)(2,1)} %bitcast.739), channel_id=1, source_target_pairs={{0,4},{4,0},{1,5},{5,1},{2,6},{6,2},{3,7},{7,3},{8,12},{12,8},{9,1... | collective-permute-start | bytes 9437192 | tf_op jit(solution)/shard_map/ppermute | solution.py:49
  286.7 173.0 %collective-permute-start.18 = (bf16[4,4,128,768]{3,2,1,0:T(8,128)(2,1)}, bf16[4,4,128,768]{3,2,1,0:T(8,128)(2,1)}, u32[]{:S(2)}, u32[]{:S(2)}) collective-permute-start(bf16[4,4,128,768]{3,2,1,0:T(8,128)(2,1)} %bitcast.741), channel_id=1, source_target_pairs={{0,4},{4,0},{1,5},{5,1},{2,6},{6,2},{3,7},{7,3},{8,12},{12,8},{9,1... | collective-permute-start | bytes 9437192 | tf_op jit(solution)/shard_map/ppermute | solution.py:49
  529.1 24.0 %collective-permute-start.27 = (bf16[256,1024]{1,0:T(8,128)(2,1)S(1)}, bf16[256,1024]{1,0:T(8,128)(2,1)S(1)}, u32[]{:S(2)}, u32[]{:S(2)}) collective-permute-start(bf16[256,1024]{1,0:T(8,128)(2,1)S(1)} %fusion.113), channel_id=1, source_target_pairs={{0,2},{2,0},{1,3},{3,1},{4,6},{6,4},{5,7},{7,5},{8,10},{10,8},{9,1... | collective-permute-start | bytes 1572872 | tf_op jit(solution)/shard_map/ppermute | solution.py:49
  530.3 34.0 %collective-permute-start.23 = (bf16[256,1024]{1,0:T(8,128)(2,1)S(1)}, bf16[256,1024]{1,0:T(8,128)(2,1)S(1)}, u32[]{:S(2)}, u32[]{:S(2)}) collective-permute-start(bf16[256,1024]{1,0:T(8,128)(2,1)S(1)} %fusion.111), channel_id=1, source_target_pairs={{0,2},{2,0},{1,3},{3,1},{4,6},{6,4},{5,7},{7,5},{8,10},{10,8},{9,1... | collective-permute-start | bytes 1572872 | tf_op jit(solution)/shard_map/ppermute | solution.py:49
  532.3 42.3 %collective-permute-start.25 = (bf16[256,1024]{1,0:T(8,128)(2,1)S(1)}, bf16[256,1024]{1,0:T(8,128)(2,1)S(1)}, u32[]{:S(2)}, u32[]{:S(2)}) collective-permute-start(bf16[256,1024]{1,0:T(8,128)(2,1)S(1)} %fusion.112), channel_id=1, source_target_pairs={{0,2},{2,0},{1,3},{3,1},{4,6},{6,4},{5,7},{7,5},{8,10},{10,8},{9,1... | collective-permute-start | bytes 1572872 | tf_op jit(solution)/shard_map/ppermute | solution.py:49
  601.8 96.2 %collective-permute-start.40 = (bf16[4,4,128,768]{3,2,1,0:T(8,128)(2,1)}, bf16[4,4,128,768]{3,2,1,0:T(8,128)(2,1)}, u32[]{:S(2)}, u32[]{:S(2)}) collective-permute-start(bf16[4,4,128,768]{3,2,1,0:T(8,128)(2,1)} %get-tuple-element.165), channel_id=1, source_target_pairs={{0,4},{4,0},{1,5},{5,1},{2,6},{6,2},{3,7},{7,3},{8,12},{12,8},{9,1... | collective-permute-start | bytes 9437192 | tf_op jit(solution)/shard_map/ppermute | solution.py:49
  697.9 302.6 %reduce-scatter.10.cloned.1.call-start = ((), (), s32[]{:S(2)}) async-start(), calls=%async_computation.7 | async-start | bytes 3932160 | tf_op jit(solution)/shard_map/reduce_scatter | solution.py:354
  703.7 296.9 %reduce-scatter.12.cloned.1.call-start = ((), (), s32[]{:S(2)}) async-start(), calls=%async_computation.8 | async-start | bytes 3932160 | tf_op jit(solution)/shard_map/reduce_scatter | solution.py:354
  703.7 69.8 %collective-permute-start.41 = (bf16[4,4,128,768]{3,2,1,0:T(8,128)(2,1)}, bf16[4,4,128,768]{3,2,1,0:T(8,128)(2,1)S(1)}, u32[]{:S(2)}, u32[]{:S(2)}) collective-permute-start(bf16[4,4,128,768]{3,2,1,0:T(8,128)(2,1)} %get-tuple-element.167), channel_id=1, source_target_pairs={{0,4},{4,0},{1,5},{5,1},{2,6},{6,2},{3,7},{7,3},{8,12},{12,8},{9,1... | collective-permute-start | bytes 9437192 | tf_op jit(solution)/shard_map/ppermute | solution.py:49
  776.1 224.4 %reduce-scatter.14.cloned.1.call-start = ((), (), s32[]{:S(2)}) async-start(), calls=%async_computation.9 | async-start | bytes 3932160 | tf_op jit(solution)/shard_map/reduce_scatter | solution.py:354
  776.2 68.9 %collective-permute-start.42 = (bf16[4,4,128,768]{3,2,1,0:T(8,128)(2,1)}, bf16[4,4,128,768]{3,2,1,0:T(8,128)(2,1)S(1)}, u32[]{:S(2)}, u32[]{:S(2)}) collective-permute-start(bf16[4,4,128,768]{3,2,1,0:T(8,128)(2,1)} %get-tuple-element.169), channel_id=1, source_target_pairs={{0,4},{4,0},{1,5},{5,1},{2,6},{6,2},{3,7},{7,3},{8,12},{12,8},{9,1... | collective-permute-start | bytes 9437192 | tf_op jit(solution)/shard_map/ppermute | solution.py:49
  847.8 152.7 %reduce-scatter.8.cloned.1.call-start = ((), (), s32[]{:S(2)}) async-start(), calls=%async_computation.6 | async-start | bytes 3932160 | tf_op jit(solution)/shard_map/reduce_scatter | solution.py:354
  847.9 68.1 %collective-permute-start.39 = (bf16[4,4,128,768]{3,2,1,0:T(8,128)(2,1)}, bf16[4,4,128,768]{3,2,1,0:T(8,128)(2,1)S(1)}, u32[]{:S(2)}, u32[]{:S(2)}) collective-permute-start(bf16[4,4,128,768]{3,2,1,0:T(8,128)(2,1)} %get-tuple-element.163), channel_id=1, source_target_pairs={{0,4},{4,0},{1,5},{5,1},{2,6},{6,2},{3,7},{7,3},{8,12},{12,8},{9,1... | collective-permute-start | bytes 9437192 | tf_op jit(solution)/shard_map/ppermute | solution.py:49
  (170 other events, 1449.4 us)
Sparse Core Ops, SparseCore 0:
  24.1 70.8 all-gather.14
  96.5 62.6 all-gather.12
  160.9 62.1 all-gather.10
  224.5 62.1 all-gather.8
  698.0 21.9 reduce-scatter.5
  722.2 59.4 reduce-scatter.9
  784.0 60.2 reduce-scatter.11
  847.9 59.5 reduce-scatter.13
  918.8 59.5 reduce-scatter.7

commit v2 on v1

v2 whole, which is shorter than its diff:
```python
import functools

import jax
import jax.numpy as jnp
from jax import lax
from jax.experimental import pallas as pl
from jax.experimental.pallas import tpu as pltpu
from jax.sharding import Mesh
from jax.sharding import PartitionSpec as P

HD = 64
E = 32
CHUNKS = 4

EPSILON = 1e-06
BF = jnp.bfloat16
FP = jnp.float32


def dot_nn(left, right):
    return lax.dot_general(left, right, (((1,), (0,)), ((), ())), preferred_element_type=FP)


def dot_tn(left, right):
    return lax.dot_general(left, right, (((0,), (0,)), ((), ())), preferred_element_type=FP)


def dot_nt(left, right):
    return lax.dot_general(left, right, (((1,), (1,)), ((), ())), preferred_element_type=FP)


def row_norm(in_rows, gain_vec):
    row_scale = lax.rsqrt(jnp.mean(in_rows * in_rows, axis=-1, keepdims=True) + EPSILON)
    return (in_rows * row_scale * gain_vec, row_scale)


def norm_back(in_rows, row_scale, gain_vec, grad_in):
    weighted = grad_in * gain_vec
    inner = jnp.mean(weighted * in_rows, axis=-1, keepdims=True)
    returned = row_scale * weighted - in_rows * row_scale * row_scale * row_scale * inner
    gain_part = jnp.sum(grad_in * in_rows * row_scale, axis=0)
    return (returned, gain_part)


def swap(value, axis):
    return lax.ppermute(value, axis, [(0, 1), (1, 0)])


def in_order(mine, other, axis, dim):
    first = lax.axis_index(axis) == 0
    return jnp.stack([jnp.where(first, mine, other), jnp.where(first, other, mine)], axis=dim)


def gather_rows(rows):
    pair = in_order(rows, swap(rows, "x"), "x", 0)
    whole = in_order(pair, swap(pair, "c"), "c", 1)
    return whole.reshape(4 * rows.shape[0], rows.shape[1])


def gather_pair(rows):
    both = jnp.stack([rows, swap(rows, "y")])
    pair = in_order(both, swap(both, "x"), "x", 1)
    whole = in_order(pair, swap(pair, "c"), "c", 2)
    return whole.reshape(8 * rows.shape[0], rows.shape[1])


def scatter_rows(kept, sent):
    half = (kept + swap(sent, "c").astype(FP)).reshape(2, -1, kept.shape[-1])
    chip = lax.axis_index("x")
    sent = lax.dynamic_index_in_dim(half, 1 - chip, 0, False).astype(BF)
    kept = lax.dynamic_index_in_dim(half, chip, 0, False)
    return kept + swap(sent, "x").astype(FP)


def scatter_pair(kept, sent):
    half = (kept + swap(sent, "c").astype(FP)).reshape(2, 2, -1, kept.shape[-1])
    chip = lax.axis_index("x")
    sent = lax.dynamic_index_in_dim(half, 1 - chip, 1, False).astype(BF)
    kept = lax.dynamic_index_in_dim(half, chip, 1, False)
    both = kept + swap(sent, "x").astype(FP)
    return both[0] + swap(both[1].astype(BF), "y").astype(FP)


def turns(depth):
    up = [(i, (i + 1) % depth) for i in range(depth)]
    down = [(i, (i - 1) % depth) for i in range(depth)]
    return up, down


def gather_dp(shard, depth):
    turn_up, turn_down = turns(depth)
    before, after = [], []
    piece = shard
    for _ in range(depth // 2):
        piece = lax.ppermute(piece, "z", turn_up)
        before.append(piece)
    piece = shard
    for _ in range((depth - 1) // 2):
        piece = lax.ppermute(piece, "z", turn_down)
        after.append(piece)
    line = before[::-1] + [shard] + after
    place = lax.axis_index("z")
    start = lax.rem(depth + len(before) - place, depth)
    column = lax.dynamic_slice_in_dim(jnp.stack(line + line), start, depth, 0)
    return in_order(column, swap(column, "y"), "y", 1).reshape(-1, shard.shape[-1])


def scatter_dp(partial, depth):
    blocks = partial.reshape(depth, 2, -1, partial.shape[-1])
    mine = lax.axis_index("y")
    sent = lax.dynamic_index_in_dim(blocks, 1 - mine, 1, False).astype(BF)
    kept = lax.dynamic_index_in_dim(blocks, mine, 1, False)
    column = kept + swap(sent, "y").astype(FP)
    place = lax.axis_index("z")

    def owned(distance):
        return lax.dynamic_index_in_dim(column, lax.rem(place + distance, depth), 0, False)

    turn_up, turn_down = turns(depth)
    total = owned(0)
    for turn, sign, steps in ((turn_up, 1, depth // 2), (turn_down, -1, (depth - 1) // 2)):
        carried = None
        for distance in range(steps, 0, -1):
            block = owned(depth + sign * distance)
            carried = block if carried is None else block + carried
            carried = lax.ppermute(carried.astype(BF), "z", turn).astype(FP)
        if carried is not None:
            total = total + carried
    return total


def sum_all(value, depth):
    for axis in ("c", "x", "y"):
        value = value + swap(value, axis)
    reach = 1
    while reach < depth:
        pairs = [(i, i ^ reach) for i in range(depth)]
        value = value + lax.ppermute(value, "z", pairs)
        reach *= 2
    return value


def moe_kernel(first, last, column, core_ref, x_ref, g_ref, gate_ref, w_ref, *rest):
    rest = list(rest)
    sums_in = [] if first else [rest.pop(0), rest.pop(0)]
    acc = rest.pop()
    grads_ref = rest.pop()
    sums_out = rest
    step = pl.program_id(0)
    blocks, pairs, blk, width = w_ref.shape
    model_width = blocks * blk
    half = width // 3
    hidden_local = half // 2

    @pl.when(step == 0)
    def _():
        acc[...] = jnp.zeros_like(acc)

    x = x_ref[...]
    g = g_ref[...]
    totals = [None, None]
    for p in range(pairs):
        weights = w_ref[:, p].reshape(model_width, width)
        pre = dot_nn(x, weights[:, : 2 * half])
        out_back = dot_nn(g, weights[:, 2 * half :])
        gate = pre[:, :half]
        up = pre[:, half:]
        sig = 0.5 + 0.5 * jnp.tanh(0.5 * gate)
        share = jnp.concatenate(
            [
                jnp.broadcast_to(gate_ref[:, i : i + 1], (x.shape[0], hidden_local))
                for i in (column + 2 * p, column + 2 * p + 1)
            ],
            axis=1,
        )
        silu = gate * sig
        hidden = (share * (silu * up)).astype(BF)
        hidden_grad = share * out_back
        gate_grad = (hidden_grad * up * (sig + silu * (1.0 - sig))).astype(BF)
        up_grad = (hidden_grad * silu).astype(BF)
        pair_grad = jnp.concatenate([gate_grad, up_grad], axis=1)
        terms = (
            dot_nt(hidden, weights[:, 2 * half :]),
            dot_nt(pair_grad, weights[:, : 2 * half]),
        )
        totals = [t if s is None else s + t for s, t in zip(totals, terms)]
        acc[p, :, : 2 * half] += dot_tn(x, pair_grad)
        acc[p, :, 2 * half :] += dot_tn(g, hidden)
    if not first:
        totals = [s[...] + t for s, t in zip(sums_in, totals)]
    if last:
        rows = x.shape[0] // 2
        for kept_ref, sent_ref, total in zip(sums_out[::2], sums_out[1::2], totals):

            @pl.when(core_ref[0] == 0)
            def _():
                kept_ref[...] = total[:rows]
                sent_ref[...] = total[rows:].astype(BF)

            @pl.when(core_ref[0] == 1)
            def _():
                kept_ref[...] = total[rows:]
                sent_ref[...] = total[:rows].astype(BF)
    else:
        for out_ref, total in zip(sums_out, totals):
            out_ref[...] = total

    @pl.when(step == pl.num_programs(0) - 1)
    def _():
        for p in range(pairs):
            grads_ref[:, p] = acc[p].reshape(blocks, blk, width).astype(BF)


def moe_chunk(core, x, g, gates, weights, sums, column, last):
    rows, model_width = x.shape
    tile = 512
    blocks, pairs, blk, width = weights.shape
    once = pl.Buffered(1)
    row = pl.BlockSpec((tile, model_width), lambda i, s: (i, 0))
    half = pl.BlockSpec((tile // 2, model_width), lambda i, s: (i, 0))
    gate_spec = pl.BlockSpec((tile, gates.shape[1]), lambda i, s: (i, 0))
    whole = pl.BlockSpec(weights.shape, lambda i, s: (0, 0, 0, 0), pipeline_mode=once)
    first = sums is None
    operands = [core, x, g, gates, weights] + ([] if first else list(sums))
    if last:
        out_specs = [half] * 4
        outs = [jax.ShapeDtypeStruct((rows // 2, model_width), t) for t in (FP, BF, FP, BF)]
    else:
        out_specs = [row] * 2
        outs = [jax.ShapeDtypeStruct((rows, model_width), FP)] * 2
    *sums, grads = pl.pallas_call(
        functools.partial(moe_kernel, first, last, column),
        grid_spec=pltpu.PrefetchScalarGridSpec(
            num_scalar_prefetch=1,
            grid=(rows // tile,),
            in_specs=[row, row, gate_spec, whole] + ([] if first else [row, row]),
            out_specs=out_specs + [whole],
            scratch_shapes=[pltpu.VMEM((pairs, model_width, width), FP)],
        ),
        out_shape=outs + [jax.ShapeDtypeStruct(weights.shape, BF)],
        input_output_aliases={} if first or last else {5: 0, 6: 1},
        compiler_params=pltpu.CompilerParams(vmem_limit_bytes=60 << 20),
        cost_estimate=pl.CostEstimate(
            flops=6 * rows * model_width * pairs * width,
            bytes_accessed=90 << 20,
            transcendentals=rows * pairs * width // 3,
        ),
    )(*operands)
    return sums, grads


def pack_experts(w_gate_up, w_down):
    blk, hidden_local = w_gate_up.shape[1], w_gate_up.shape[3]
    gate_up = w_gate_up.reshape(E // 2, 2, blk, 2, hidden_local).transpose(0, 2, 3, 1, 4)
    down = w_down.reshape(E // 2, 2, hidden_local, blk).transpose(0, 3, 1, 2)
    return jnp.concatenate(
        [gate_up.reshape(E // 2, blk, -1), down.reshape(E // 2, blk, -1)], axis=-1
    )


def unpack_experts(packed):
    pairs, blk, width = packed.shape
    hidden_local = width // 6
    packed = packed.astype(FP)
    gate_up = packed[:, :, : 4 * hidden_local].reshape(pairs, blk, 2, 2, hidden_local)
    down = packed[:, :, 4 * hidden_local :].reshape(pairs, blk, 2, hidden_local)
    return (
        gate_up.transpose(0, 3, 1, 2, 4).reshape(2 * pairs, blk, 2, hidden_local),
        down.transpose(0, 2, 3, 1).reshape(2 * pairs, hidden_local, blk),
    )


def split_rows(core_ref, kept_ref, sent_ref, value):
    rows = value.shape[0] // 4
    for x in range(2):
        here = pl.ds(x * rows, rows)
        even, odd = value[2 * x * rows : (2 * x + 1) * rows], value[(2 * x + 1) * rows : (2 * x + 2) * rows]

        @pl.when(core_ref[0] == 0)
        def _():
            kept_ref[here, :] = even
            sent_ref[here, :] = odd.astype(BF)

        @pl.when(core_ref[0] == 1)
        def _():
            kept_ref[here, :] = odd
            sent_ref[here, :] = even.astype(BF)


def attn_forward_kernel(kv_local, core_ref, x_ref, wp_ref, wo_ref, qkv_ref, heads_ref, kept_ref, sent_ref):
    rows = x_ref.shape[0]
    ratio = heads_ref.shape[1] // HD // kv_local
    q_width = kv_local * ratio * HD
    tile = min(256, rows)
    qkv_ref[...] = dot_nn(x_ref[...], wp_ref[...]).astype(BF)
    for kv in range(kv_local):
        keys = qkv_ref[:, q_width + kv * HD : q_width + (kv + 1) * HD]
        values = qkv_ref[:, q_width + (kv_local + kv) * HD : q_width + (kv_local + kv + 1) * HD]
        for start in range(0, rows, tile):
            stop = start + tile
            cols = [slice((kv * ratio + r) * HD, (kv * ratio + r + 1) * HD) for r in range(ratio)]
            query = jnp.concatenate([qkv_ref[start:stop, c] for c in cols], axis=0) * BF(HD**-0.5)
            near = dot_nt(query, keys[start:stop])
            row_pos = lax.broadcasted_iota(jnp.int32, near.shape, 0) & (tile - 1)
            col_pos = lax.broadcasted_iota(jnp.int32, near.shape, 1)
            scores = jnp.where(col_pos <= row_pos, near, -1e30)
            if start:
                scores = jnp.concatenate([dot_nt(query, keys[:start]), scores], axis=1)
            exponent = jnp.exp(scores - jnp.max(scores, axis=-1, keepdims=True))
            total = jnp.sum(exponent, axis=-1, keepdims=True)
            probs = (exponent * (1.0 / total)).astype(BF)
            out = dot_nn(probs, values[:stop]).astype(BF)
            for r, c in enumerate(cols):
                heads_ref[start:stop, c] = out[r * tile : (r + 1) * tile]
    split_rows(core_ref, kept_ref, sent_ref, dot_nt(heads_ref[...], wo_ref[...]))


def attn_backward_kernel(
    kv_local, first, core_ref, dy_ref, x_ref, qkv_ref, heads_ref, wp_ref, wo_ref, *rest
):
    rest = list(rest)
    earlier_ref = None if first else rest.pop(0)
    grads_ref, kept_ref, sent_ref, head_grad_ref, proj_grad_ref, key_acc, value_acc = rest
    rows = x_ref.shape[0]
    ratio = heads_ref.shape[1] // HD // kv_local
    q_width = kv_local * ratio * HD
    proj_width = q_width + 2 * kv_local * HD
    tile = min(256, rows)
    scale = BF(HD**-0.5)
    head_grad_ref[...] = dot_nn(dy_ref[...], wo_ref[...]).astype(BF)
    for kv in range(kv_local):
        key_cols = slice(q_width + kv * HD, q_width + (kv + 1) * HD)
        value_cols = slice(q_width + (kv_local + kv) * HD, q_width + (kv_local + kv + 1) * HD)
        keys = qkv_ref[:, key_cols]
        values = qkv_ref[:, value_cols]
        key_acc[...] = jnp.zeros_like(key_acc)
        value_acc[...] = jnp.zeros_like(value_acc)
        for start in range(0, rows, tile):
            stop = start + tile
            cols = [slice((kv * ratio + r) * HD, (kv * ratio + r + 1) * HD) for r in range(ratio)]
            query = jnp.concatenate([qkv_ref[start:stop, c] for c in cols], axis=0) * scale
            out_grad = jnp.concatenate([head_grad_ref[start:stop, c] for c in cols], axis=0)
            near = dot_nt(keys[start:stop], query)
            key_pos = lax.broadcasted_iota(jnp.int32, near.shape, 0)
            row_pos = lax.broadcasted_iota(jnp.int32, near.shape, 1) & (tile - 1)
            scores = jnp.where(key_pos <= row_pos, near, -1e30)
            if start:
                scores = jnp.concatenate([dot_nt(keys[:start], query), scores], axis=0)
            exponent = jnp.exp(scores - jnp.max(scores, axis=0, keepdims=True))
            probs = exponent * (1.0 / jnp.sum(exponent, axis=0, keepdims=True))
            prob_grad = dot_nt(values[:stop], out_grad)
            inner = jnp.sum(probs * prob_grad, axis=0, keepdims=True)
            score_grad = (probs * (prob_grad - inner)).astype(BF)
            value_acc[:stop] += dot_nn(probs.astype(BF), out_grad)
            key_acc[:stop] += dot_nn(score_grad, query)
            query_grad = (dot_tn(score_grad, keys[:stop]) * (HD**-0.5)).astype(BF)
            for r, c in enumerate(cols):
                proj_grad_ref[start:stop, c] = query_grad[r * tile : (r + 1) * tile]
        proj_grad_ref[:, key_cols] = key_acc[...].astype(BF)
        proj_grad_ref[:, value_cols] = value_acc[...].astype(BF)
    proj_grad = proj_grad_ref[...]
    split_rows(core_ref, kept_ref, sent_ref, dot_nt(proj_grad, wp_ref[...]))
    proj_part = dot_tn(x_ref[...], proj_grad)
    out_part = dot_tn(dy_ref[...], heads_ref[...])
    if first:
        grads_ref[:, :proj_width] = proj_part
        grads_ref[:, proj_width:] = out_part
    else:
        grads_ref[:, :proj_width] = earlier_ref[:, :proj_width] + proj_part
        grads_ref[:, proj_width:] = earlier_ref[:, proj_width:] + out_part


SMEM = pl.BlockSpec(memory_space=pltpu.SMEM)
VMEM = pl.BlockSpec(memory_space=pltpu.VMEM)


def attn_forward(core, x, w_project, out_t, kv_local):
    rows, model_width = x.shape
    heads_width = out_t.shape[1]
    return pl.pallas_call(
        functools.partial(attn_forward_kernel, kv_local),
        in_specs=[SMEM, VMEM, VMEM, VMEM],
        out_specs=[VMEM] * 4,
        out_shape=[
            jax.ShapeDtypeStruct((rows, w_project.shape[1]), BF),
            jax.ShapeDtypeStruct((rows, heads_width), BF),
            jax.ShapeDtypeStruct((rows // 2, model_width), FP),
            jax.ShapeDtypeStruct((rows // 2, model_width), BF),
        ],
        compiler_params=pltpu.CompilerParams(vmem_limit_bytes=56 << 20),
        cost_estimate=pl.CostEstimate(
            flops=14 << 30, bytes_accessed=10 << 20, transcendentals=3 << 20
        ),
    )(core, x, w_project, out_t)


def attn_backward(core, dy, x, qkv, heads, w_project, out_t, earlier, kv_local):
    rows, model_width = x.shape
    width = w_project.shape[1] + out_t.shape[1]
    first = earlier is None
    operands = [core, dy, x, qkv, heads, w_project, out_t] + ([] if first else [earlier])
    return pl.pallas_call(
        functools.partial(attn_backward_kernel, kv_local, first),
        in_specs=[SMEM] + [VMEM] * (len(operands) - 1),
        out_specs=[VMEM] * 3,
        out_shape=[
            jax.ShapeDtypeStruct((model_width, width), FP),
            jax.ShapeDtypeStruct((rows // 2, model_width), FP),
            jax.ShapeDtypeStruct((rows // 2, model_width), BF),
        ],
        scratch_shapes=[
            pltpu.VMEM(heads.shape, BF),
            pltpu.VMEM(qkv.shape, BF),
            pltpu.VMEM((rows, HD), FP),
            pltpu.VMEM((rows, HD), FP),
        ],
        compiler_params=pltpu.CompilerParams(vmem_limit_bytes=56 << 20),
        cost_estimate=pl.CostEstimate(
            flops=30 << 30, bytes_accessed=16 << 20, transcendentals=3 << 20
        ),
    )(*operands)


def on_device(
    block_input,
    cotangent,
    routes,
    gate_weights,
    w_query,
    w_key,
    w_value,
    w_out,
    w_gate_up,
    w_down,
    norm_attn,
    norm_moe,
):
    depth = lax.axis_size("z")
    micro_count, rows_local, model_width = block_input.shape
    kv_local = w_key.shape[1] // HD
    q_width, kv_width = w_query.shape[1], w_key.shape[1]
    proj_width = q_width + 2 * kv_width
    side = lax.axis_index("y")
    core = lax.axis_index("c").astype(jnp.int32).reshape(1)

    packed_attn = jnp.concatenate([w_query, w_key, w_value, w_out.T], axis=1)
    packed = pack_experts(w_gate_up, w_down)
    packed = packed.reshape(2, packed.shape[0] // 2, *packed.shape[1:])
    mine = lax.dynamic_index_in_dim(packed, side, 0, False)
    theirs = lax.dynamic_index_in_dim(packed, 1 - side, 0, False)
    per_chunk = mine.shape[0] // CHUNKS
    chunk_weights = []
    for chunk in range(CHUNKS):
        part = slice(chunk * per_chunk, (chunk + 1) * per_chunk)
        shard = in_order(mine[part], swap(theirs[part], "y"), "y", 0)
        if chunk:
            shard, _ = lax.optimization_barrier((shard, chunk_weights[-1][:1, :1, :8]))
        whole = lax.all_gather(shard, "z", axis=0)
        chunk_weights.append(whole.reshape(-1, *whole.shape[2:]))
    attn_full = gather_dp(packed_attn, depth)
    w_project, out_t = attn_full[:, :proj_width], attn_full[:, proj_width:]

    in_rows = block_input.astype(FP)
    normed_attn, scale_attn = row_norm(in_rows, norm_attn)
    normed_attn = normed_attn.astype(BF)
    attn_in, saved, middle, scale_moe, moe_in = [], [], [], [], []
    for m in range(micro_count):
        attn_in.append(gather_rows(normed_attn[m]))
        qkv, heads, kept, sent = attn_forward(core, attn_in[m], w_project, out_t, kv_local)
        saved.append((qkv, heads))
        middle.append(in_rows[m] + scatter_rows(kept, sent))
        normed_moe, scale = row_norm(middle[m], norm_moe)
        scale_moe.append(scale)
        moe_in.append(gather_pair(normed_moe.astype(BF)))
    moe_in = jnp.concatenate(moe_in)
    moe_grad = jnp.concatenate([gather_pair(cotangent[m]) for m in range(micro_count)])

    expert_ids = jnp.arange(E, dtype=jnp.int32)[:, None, None, None]
    gates = jnp.sum(jnp.where(routes == expert_ids, gate_weights, 0.0), axis=3)
    gates = gates.reshape(2, E // 2, micro_count, -1)
    gates = jnp.stack(
        [
            lax.dynamic_index_in_dim(gates, side, 0, False),
            swap(lax.dynamic_index_in_dim(gates, 1 - side, 0, False), "y"),
        ]
    )
    gates = gates.transpose(2, 0, 3, 1).reshape(-1, E // 2)

    sums = None
    shards = []
    for chunk in range(CHUNKS):
        sums, grads = moe_chunk(
            core,
            moe_in,
            moe_grad,
            gates,
            chunk_weights[chunk],
            sums,
            2 * per_chunk * chunk,
            chunk == CHUNKS - 1,
        )
        grads = grads.reshape(depth, 2, *grads.shape[1:])
        grads = lax.psum_scatter(grads, "z", scatter_dimension=0, tiled=False)
        kept = lax.dynamic_index_in_dim(grads, side, 0, False)
        sent = lax.dynamic_index_in_dim(grads, 1 - side, 0, False)
        shards.append(in_order(kept, swap(sent, "y"), "y", 0))
    packed_grads = jnp.concatenate(shards, axis=1)
    shard_pair, shard_down = unpack_experts(packed_grads.reshape(-1, *packed_grads.shape[2:]))
    mixed_kept, mixed_sent, back_kept, back_sent = (
        s.reshape(micro_count, 2, -1, model_width) for s in sums
    )

    out_grad = cotangent.astype(FP)
    outputs, input_grads = [], []
    gains = jnp.zeros((2, model_width), FP)
    attn_grads = None
    for m in range(micro_count):
        moe_in_grad = scatter_pair(back_kept[m], back_sent[m])
        middle_back, gain_moe = norm_back(middle[m], scale_moe[m], norm_moe, moe_in_grad)
        middle_grad = out_grad[m] + middle_back
        branch_grad = gather_rows(middle_grad.astype(BF))
        attn_grads, kept, sent = attn_backward(
            core, branch_grad, attn_in[m], *saved[m], w_project, out_t, attn_grads, kv_local
        )
        attn_in_grad = scatter_rows(kept, sent)
        in_back, gain_attn = norm_back(in_rows[m], scale_attn[m], norm_attn, attn_in_grad)
        input_grads.append(middle_grad + in_back)
        gains = gains + jnp.stack([gain_attn, gain_moe])
    for m in range(micro_count):
        outputs.append((middle[m] + scatter_pair(mixed_kept[m], mixed_sent[m])).astype(BF))
    attn_shard = scatter_dp(attn_grads, depth)
    gains = sum_all(gains.reshape(16, -1), depth).reshape(2, model_width)
    return (
        jnp.stack(outputs),
        jnp.stack(input_grads),
        attn_shard[:, :q_width],
        attn_shard[:, q_width : q_width + kv_width],
        attn_shard[:, q_width + kv_width : proj_width],
        attn_shard[:, proj_width:].T,
        shard_pair,
        shard_down,
        gains[0],
        gains[1],
    )


def solution(mesh):
    dp, tensor = mesh.shape["dp"], mesh.shape["tensor"]
    fine = Mesh(mesh.devices.reshape(dp // 2, 2, tensor // 2, 2), ("z", "y", "x", "c"))
    dp_axes, tensor_axes = ("z", "y"), ("x", "c")
    rows = P(None, dp_axes + tensor_axes, None)
    return jax.shard_map(
        on_device,
        mesh=fine,
        in_specs=(
            rows,
            rows,
            P(None, dp_axes, None),
            P(None, dp_axes, None),
            P(dp_axes, tensor_axes),
            P(dp_axes, tensor_axes),
            P(dp_axes, tensor_axes),
            P(tensor_axes, dp_axes),
            P(None, dp_axes, None, tensor_axes),
            P(None, tensor_axes, dp_axes),
            P(),
            P(),
        ),
        out_specs=(
            rows,
            rows,
            P(dp_axes, tensor_axes),
            P(dp_axes, tensor_axes),
            P(dp_axes, tensor_axes),
            P(tensor_axes, dp_axes),
            P(None, dp_axes, None, tensor_axes),
            P(None, tensor_axes, dp_axes),
            P(),
            P(),
        ),
        check_vma=False,
    )
```

time: 1040 us -> 891 us (0.86)
  waiting for transfers between devices: 449 us -> 308 us
  Pallas kernels: 224 us -> 287 us
  matrix products: 59.4 us -> 0 us
  blocking collectives: 41.9 us -> 0 us
  other arithmetic: 84.8 us -> 107 us
  starting transfers between devices: 39.4 us -> 58.4 us
  local copies, waits for them, and re-layouts: 121 us -> 108 us
    all_gather x4, waiting for transfers between devices: 71.9 us -> 0.06 us  [on_device(): whole = lax.all_gather(shard, 'z', axis=0)]
    ppermute x40 -> x54, waiting for transfers between devices: 361 us -> 291 us  [swap(): return lax.ppermute(value, axis, [(0, 1), (1, 0)])]
    pallas_call x4 -> x8, Pallas kernels: 224 us -> 287 us  [the longest x4 220 us: moe_chunk(): pl.pallas_call(functools.partial(moe_kernel, first, last, column), grid_s...]
    dot_general x36 -> x0, matrix products: 59.4 us -> none  [the longest x4 9.92 us: attention_backward(): jnp.einsum('grbl,bgrd->lgd', attn_probs.astype(BF), grad_blk, preferred_e...]
    psum x1 -> x0, blocking collectives: 41.9 us -> none  [on_device(): lax.psum((gain_attn_total, gain_moe_total), ('z', 'y', 'x', 'c'))]
    convert_element_type x13 -> x4, other arithmetic: 29 us -> 3.14 us  [the longest x1 2.62 us: on_device(): branch_grad = gather_rows(middle_grad.astype(BF))]
    unnamed x298 -> x157, local copies, waits for them, and re-layouts: 30.3 us -> 12.8 us
    another operation x27 -> x40, other arithmetic: 27.2 us -> 43.3 us  [in_order(): jnp.stack([jnp.where(first, mine, other), jnp.where(first, other, mine)],...]
  transfers between devices with their start and end apart: 52 -> 70, of which waited for: 24 -> 30; matrix products, arithmetic and copies ran while one was open for 19% -> 21% of each run, Pallas kernels for 16% -> 32%
where the time goes in v2:
time: 891 us; the launch traced here: 884 us
  waiting for transfers between devices  308 us (35%)
  Pallas kernels  287 us (32%)
  local copies, waits for them, and re-layouts  108 us (12%)
  other arithmetic  107 us (12%)
  starting transfers between devices  58.4 us (7%)
  between operations  15.7 us (2%)
    ppermute x54, waiting for transfers between devices, swap(): return lax.ppermute(value, axis, [(0, 1), (1, 0)])  291 us
    pallas_call x4, Pallas kernels, moe_chunk(): pl.pallas_call(functools.partial(moe_kernel, first, last, column), grid_s...  220 us
    ppermute x54, starting transfers between devices, swap(): return lax.ppermute(value, axis, [(0, 1), (1, 0)])  45.1 us
    another operation x40, other arithmetic, in_order(): jnp.stack([jnp.where(first, mine, other), jnp.where(first, other, mine)],...  43.3 us
    pallas_call x2, Pallas kernels, attn_backward(): pl.pallas_call(functools.partial(attn_backward_kernel, kv_local, first),...  42.9 us
    pallas_call x2, Pallas kernels, attn_forward(): pl.pallas_call(functools.partial(attn_forward_kernel, kv_local), in_specs...  24.3 us
  transfers between devices with their start and end apart: 70, of which 30 were waited for; matrix products, arithmetic and copies ran while one was open for 21% of the time, Pallas kernels for 32%

profile of v2, /device:TPU:0, one launch (start us, length us, event | category | flops | bytes accessed | tf_op | source)
XLA Modules:
  0.0 883.6 jit_solution(13870086293785648752)
XLA Ops:
  37.8 8.5 collective-permute-done.26
  46.3 8.4 collective-permute-done.27
  79.5 8.5 collective-permute-done.3
  118.9 12.2 %shard_map.196 = (bf16[1024,512]{1,0:T(8,128)(2,1)}, bf16[1024,256]{1,0:T(8,128)(2,1)}, f32[512,1024]{1,0:T(8,128)}, bf16[512,1024]{1,0:T(8,128)(2,1)}) custom-call(s32[1]{0:T(128)} %bitcast.1.core_ref, bf16[1024,1024]{1,0:T(8,128)(2,1)} %bitcast.487, bf16[1024,512]{1,0:T(8,128)(2,1)} %slice.231.wp_ref, bf16[1024,256]{1,0:T(8,128)(2,1)} %slice.232.wo_ref), custom_call_target="tpu_custom_call" | custom-call | flops 15032385536 | bytes 10485760 | tf_op jit(solution)/shard_map/pallas_call | solution.py:380
  134.3 12.0 %shard_map.195 = (bf16[1024,512]{1,0:T(8,128)(2,1)}, bf16[1024,256]{1,0:T(8,128)(2,1)}, f32[512,1024]{1,0:T(8,128)}, bf16[512,1024]{1,0:T(8,128)(2,1)}) custom-call(s32[1]{0:T(128)} %bitcast.1.core_ref, bf16[1024,1024]{1,0:T(8,128)(2,1)} %bitcast.489, bf16[1024,512]{1,0:T(8,128)(2,1)} %slice.231.wp_ref, bf16[1024,256]{1,0:T(8,128)(2,1)} %slice.232.wo_ref), custom_call_target="tpu_custom_call" | custom-call | flops 15032385536 | bytes 10485760 | tf_op jit(solution)/shard_map/pallas_call | solution.py:380
  164.7 13.1 %collective-permute-done.19 = bf16[2,256,1024]{2,1,0:T(8,128)(2,1)} collective-permute-done((bf16[2,256,1024]{2,1,0:T(8,128)(2,1)}, bf16[2,256,1024]{2,1,0:T(8,128)(2,1)}, u32[]{:S(2)}, u32[]{:S(2)}) %collective-permute-start.19) | collective-permute-done | bytes 1048608 | tf_op jit(solution)/shard_map/ppermute | solution.py:46
  179.6 9.5 %collective-permute-done.14 = bf16[256,1024]{1,0:T(8,128)(2,1)} collective-permute-done((bf16[256,1024]{1,0:T(8,128)(2,1)}, bf16[256,1024]{1,0:T(8,128)(2,1)}, u32[]{:S(2)}, u32[]{:S(2)}) %collective-permute-start.14) | collective-permute-done | bytes 524320 | tf_op jit(solution)/shard_map/ppermute | solution.py:46
  189.1 11.2 %collective-permute-done.7 = bf16[256,1024]{1,0:T(8,128)(2,1)} collective-permute-done((bf16[256,1024]{1,0:T(8,128)(2,1)}, bf16[256,1024]{1,0:T(8,128)(2,1)}, u32[]{:S(2)}, u32[]{:S(2)}) %collective-permute-start.7) | collective-permute-done | bytes 524320 | tf_op jit(solution)/shard_map/ppermute | solution.py:46
  206.1 15.3 %collective-permute-done.22 = bf16[2,256,1024]{2,1,0:T(8,128)(2,1)S(1)} collective-permute-done((bf16[2,256,1024]{2,1,0:T(8,128)(2,1)S(1)}, bf16[2,256,1024]{2,1,0:T(8,128)(2,1)S(1)}, u32[]{:S(2)}, u32[]{:S(2)}) %collective-permute-start.22) | collective-permute-done | bytes 1048608 | tf_op jit(solution)/shard_map/ppermute | solution.py:46
  228.9 21.4 %collective-permute-done.9 = bf16[2,256,1024]{2,1,0:T(8,128)(2,1)S(1)} collective-permute-done((bf16[2,256,1024]{2,1,0:T(8,128)(2,1)S(1)}, bf16[2,256,1024]{2,1,0:T(8,128)(2,1)S(1)}, u32[]{:S(2)}, u32[]{:S(2)}) %collective-permute-start.9) | collective-permute-done | bytes 1048608 | tf_op jit(solution)/shard_map/ppermute | solution.py:46
  250.3 22.1 %collective-permute-done.16 = bf16[2,256,1024]{2,1,0:T(8,128)(2,1)S(1)} collective-permute-done((bf16[2,256,1024]{2,1,0:T(8,128)(2,1)S(1)}, bf16[2,256,1024]{2,1,0:T(8,128)(2,1)S(1)}, u32[]{:S(2)}, u32[]{:S(2)}) %collective-permute-start.16) | collective-permute-done | bytes 1048608 | tf_op jit(solution)/shard_map/ppermute | solution.py:46
  318.8 53.1 %shard_map.197 = (f32[4096,1024]{1,0:T(8,128)}, f32[4096,1024]{1,0:T(8,128)}, bf16[8,2,128,768]{3,2,1,0:T(8,128)(2,1)}) custom-call(s32[1]{0:T(128)} %bitcast.1.core_ref, bf16[4096,1024]{1,0:T(8,128)(2,1)} %pad_maximum_fusion.x_ref, bf16[4096,1024]{1,0:T(8,128)(2,1)} %pad_maximum_fusion.1.g_ref, f32[4096,16]{1,0:T(8,128)} %bitcast.482, ...), custom_call_target="tpu_custom_call" | custom-call | flops 38654705664 | bytes 94371840 | tf_op jit(solution)/shard_map/pallas_call | solution.py:231
  371.9 54.8 %shard_map.198 = (f32[4096,1024]{1,0:T(8,128)}, f32[4096,1024]{1,0:T(8,128)}, bf16[8,2,128,768]{3,2,1,0:T(8,128)(2,1)}) custom-call(s32[1]{0:T(128)} %bitcast.1.core_ref, bf16[4096,1024]{1,0:T(8,128)(2,1)} %pad_maximum_fusion.x_ref, bf16[4096,1024]{1,0:T(8,128)(2,1)} %pad_maximum_fusion.1.g_ref, ...), custom_call_target="tpu_custom_call", output_to_operand_aliasing={{0}: (5, {}), {1}: (6, {})} | custom-call | flops 38654705664 | bytes 94371840 | tf_op jit(solution)/shard_map/pallas_call | solution.py:231
  426.8 55.2 %shard_map.199 = (f32[4096,1024]{1,0:T(8,128)}, f32[4096,1024]{1,0:T(8,128)}, bf16[8,2,128,768]{3,2,1,0:T(8,128)(2,1)}) custom-call(s32[1]{0:T(128)} %bitcast.1.core_ref, bf16[4096,1024]{1,0:T(8,128)(2,1)} %pad_maximum_fusion.x_ref, bf16[4096,1024]{1,0:T(8,128)(2,1)} %pad_maximum_fusion.1.g_ref, ...), custom_call_target="tpu_custom_call", output_to_operand_aliasing={{0}: (5, {}), {1}: (6, {})} | custom-call | flops 38654705664 | bytes 94371840 | tf_op jit(solution)/shard_map/pallas_call | solution.py:231
  482.1 56.7 %shard_map.200 = (f32[2048,1024]{1,0:T(8,128)}, bf16[2048,1024]{1,0:T(8,128)(2,1)}, f32[2048,1024]{1,0:T(8,128)}, bf16[2048,1024]{1,0:T(8,128)(2,1)}, bf16[8,2,128,768]{3,2,1,0:T(8,128)(2,1)}) custom-call(s32[1]{0:T(128)} %bitcast.1.core_ref, bf16[4096,1024]{1,0:T(8,128)(2,1)} %pad_maximum_fusion.x_ref, bf16[4096,1024]{1,0:T(8,128)(2,1)} %pad_maximum_fusion.1.g_ref, ...), custom_call_target="tpu_custom_call" | custom-call | flops 38654705664 | bytes 94371840 | tf_op jit(solution)/shard_map/pallas_call | solution.py:231
  574.0 13.0 %collective-permute-done.30 = bf16[2,256,1024]{2,1,0:T(8,128)(2,1)S(1)} collective-permute-done((bf16[2,256,1024]{2,1,0:T(8,128)(2,1)S(1)}, bf16[2,256,1024]{2,1,0:T(8,128)(2,1)S(1)}, u32[]{:S(2)}, u32[]{:S(2)}) %collective-permute-start.30) | collective-permute-done | bytes 1048608 | tf_op jit(solution)/shard_map/ppermute | solution.py:46
  588.8 43.1 %collective-permute-done.43 = bf16[2,256,1024]{2,1,0:T(8,128)(2,1)S(1)} collective-permute-done((bf16[2,256,1024]{2,1,0:T(8,128)(2,1)S(1)}, bf16[2,256,1024]{2,1,0:T(8,128)(2,1)S(1)}, u32[]{:S(2)}, u32[]{:S(2)}) %collective-permute-start.43) | collective-permute-done | bytes 1048608 | tf_op jit(solution)/shard_map/ppermute | solution.py:46
  633.9 19.7 %collective-permute-done.36 = bf16[2,256,1024]{2,1,0:T(8,128)(2,1)S(1)} collective-permute-done((bf16[2,256,1024]{2,1,0:T(8,128)(2,1)S(1)}, bf16[2,256,1024]{2,1,0:T(8,128)(2,1)S(1)}, u32[]{:S(2)}, u32[]{:S(2)}) %collective-permute-start.36) | collective-permute-done | bytes 1048608 | tf_op jit(solution)/shard_map/ppermute | solution.py:46
  656.6 12.4 %collective-permute-done.37 = bf16[256,1024]{1,0:T(8,128)(2,1)S(1)} collective-permute-done((bf16[256,1024]{1,0:T(8,128)(2,1)S(1)}, bf16[256,1024]{1,0:T(8,128)(2,1)S(1)}, u32[]{:S(2)}, u32[]{:S(2)}) %collective-permute-start.37) | collective-permute-done | bytes 524320 | tf_op jit(solution)/shard_map/ppermute | solution.py:46
  669.8 8.6 collective-permute-done.34
  683.2 12.8 %collective-permute-done.45 = bf16[256,1024]{1,0:T(8,128)(2,1)S(1)} collective-permute-done((bf16[256,1024]{1,0:T(8,128)(2,1)S(1)}, bf16[256,1024]{1,0:T(8,128)(2,1)S(1)}, u32[]{:S(2)}, u32[]{:S(2)}) %collective-permute-start.45) | collective-permute-done | bytes 524320 | tf_op jit(solution)/shard_map/ppermute | solution.py:46
  710.7 21.3 %shard_map.201 = (f32[1024,768]{1,0:T(8,128)}, f32[512,1024]{1,0:T(8,128)}, bf16[512,1024]{1,0:T(8,128)(2,1)}) custom-call(s32[1]{0:T(128)} %bitcast.1.core_ref, bf16[1024,1024]{1,0:T(8,128)(2,1)} %bitcast.493, bf16[1024,1024]{1,0:T(8,128)(2,1)} %bitcast.490, bf16[1024,512]{1,0:T(8,128)(2,1)} %get-tuple-element.52.qkv_ref, ...), custom_call_target="tpu_custom_call" | custom-call | flops 32212254720 | bytes 16777216 | tf_op jit(solution)/shard_map/pallas_call | solution.py:402
  732.0 21.5 %shard_map.202 = (f32[1024,768]{1,0:T(8,128)}, f32[512,1024]{1,0:T(8,128)}, bf16[512,1024]{1,0:T(8,128)(2,1)}) custom-call(s32[1]{0:T(128)} %bitcast.1.core_ref, bf16[1024,1024]{1,0:T(8,128)(2,1)} %bitcast.492, bf16[1024,1024]{1,0:T(8,128)(2,1)} %bitcast.488, bf16[1024,512]{1,0:T(8,128)(2,1)} %get-tuple-element.56.qkv_ref, ...), custom_call_target="tpu_custom_call" | custom-call | flops 32212254720 | bytes 16777216 | tf_op jit(solution)/shard_map/pallas_call | solution.py:402
  758.9 17.6 %collective-permute-done.49 = bf16[4,128,768]{1,2,0:T(8,128)(2,1)} collective-permute-done((bf16[4,128,768]{1,2,0:T(8,128)(2,1)}, bf16[4,128,768]{1,2,0:T(8,128)(2,1)}, u32[]{:S(2)}, u32[]{:S(2)}) %collective-permute-start.49) | collective-permute-done | bytes 786464 | tf_op jit(solution)/shard_map/ppermute | solution.py:46
  (442 shorter events, 335.6 us)
Async XLA Ops:
  7.2 311.6 %all-gather.15.cloned.1.call-start = ((), (), s32[]{:S(2)}) async-start(), calls=%async_computation.11 | async-start | bytes 3932160 | tf_op jit(solution)/shard_map/all_gather | solution.py:458
  29.7 32.7 %collective-permute-start.28 = (bf16[2,128,768]{2,1,0:T(8,128)(2,1)}, bf16[2,128,768]{2,1,0:T(8,128)(2,1)}, u32[]{:S(2)}, u32[]{:S(2)}) collective-permute-start(bf16[2,128,768]{2,1,0:T(8,128)(2,1)} %get-tuple-element.154), channel_id=1, source_target_pairs={{0,4},{4,0},{1,5},{5,1},{2,6},{6,2},{3,7},{7,3},{8,12},{12,8},{9,1... | collective-permute-start | bytes 1179656 | tf_op jit(solution)/shard_map/ppermute | solution.py:46
  66.1 305.7 %all-gather.13.cloned.1.call-start = ((), (), s32[]{:S(2)}) async-start(), calls=%async_computation.10 | async-start | bytes 3932160 | tf_op jit(solution)/shard_map/all_gather | solution.py:458
  104.3 44.9 %collective-permute-start.18 = (bf16[256,1024]{1,0:T(8,128)(2,1)}, bf16[256,1024]{1,0:T(8,128)(2,1)}, u32[]{:S(2)}, u32[]{:S(2)}) collective-permute-start(bf16[256,1024]{1,0:T(8,128)(2,1)} %get-tuple-element.203), channel_id=1, source_target_pairs={{0,4},{4,0},{1,5},{5,1},{2,6},{6,2},{3,7},{7,3},{8,12},{12,8},{9,1... | collective-permute-start | bytes 1572872 | tf_op jit(solution)/shard_map/ppermute | solution.py:46
  106.5 320.2 %all-gather.11.cloned.1.call-start = ((), (), s32[]{:S(2)}) async-start(), calls=%async_computation.9 | async-start | bytes 3932160 | tf_op jit(solution)/shard_map/all_gather | solution.py:458
  148.7 333.4 %all-gather.9.cloned.1.call-start = ((), (), s32[]{:S(2)}) async-start(), calls=%async_computation.8 | async-start | bytes 3932160 | tf_op jit(solution)/shard_map/all_gather | solution.py:458
  155.5 33.6 %collective-permute-start.14 = (bf16[256,1024]{1,0:T(8,128)(2,1)}, bf16[256,1024]{1,0:T(8,128)(2,1)}, u32[]{:S(2)}, u32[]{:S(2)}) collective-permute-start(bf16[256,1024]{1,0:T(8,128)(2,1)} %fusion.17), channel_id=1, source_target_pairs={{0,2},{2,0},{1,3},{3,1},{4,6},{6,4},{5,7},{7,5},{8,10},{10,8},{9,1... | collective-permute-start | bytes 1572872 | tf_op jit(solution)/shard_map/ppermute | solution.py:46
  160.3 40.1 %collective-permute-start.7 = (bf16[256,1024]{1,0:T(8,128)(2,1)}, bf16[256,1024]{1,0:T(8,128)(2,1)}, u32[]{:S(2)}, u32[]{:S(2)}) collective-permute-start(bf16[256,1024]{1,0:T(8,128)(2,1)} %fusion.16), channel_id=1, source_target_pairs={{0,2},{2,0},{1,3},{3,1},{4,6},{6,4},{5,7},{7,5},{8,10},{10,8},{9,1... | collective-permute-start | bytes 1572872 | tf_op jit(solution)/shard_map/ppermute | solution.py:46
  163.8 57.6 %collective-permute-start.22 = (bf16[2,256,1024]{2,1,0:T(8,128)(2,1)S(1)}, bf16[2,256,1024]{2,1,0:T(8,128)(2,1)S(1)}, u32[]{:S(2)}, u32[]{:S(2)}) collective-permute-start(bf16[2,256,1024]{2,1,0:T(8,128)(2,1)S(1)} %pad_maximum_fusion.21), channel_id=1, source_target_pairs={{0,2},{2,0},{1,3},{3,1},{4,6},{6,4},{5,7},{7,5},{8,10},{10,8},{9,1... | collective-permute-start | bytes 3145736 | tf_op jit(solution)/shard_map/ppermute | solution.py:46
  205.1 80.3 %collective-permute-start.20 = (bf16[2,2,256,1024]{3,2,0,1:T(8,128)(2,1)}, bf16[2,2,256,1024]{3,2,0,1:T(8,128)(2,1)}, u32[]{:S(2)}, u32[]{:S(2)}) collective-permute-start(bf16[2,2,256,1024]{3,2,0,1:T(8,128)(2,1)} %pad_maximum_fusion.10), channel_id=1, source_target_pairs={{0,1},{1,0},{2,3},{3,2},{4,5},{5,4},{6,7},{7,6},{8,9},{9,8},{10,11... | collective-permute-start | bytes 6291464 | tf_op jit(solution)/shard_map/ppermute | solution.py:46
  224.1 61.3 %collective-permute-start.23 = (bf16[2,2,256,1024]{3,2,0,1:T(8,128)(2,1)}, bf16[2,2,256,1024]{3,2,0,1:T(8,128)(2,1)}, u32[]{:S(2)}, u32[]{:S(2)}) collective-permute-start(bf16[2,2,256,1024]{3,2,0,1:T(8,128)(2,1)} %pad_maximum_fusion.11), channel_id=1, source_target_pairs={{0,1},{1,0},{2,3},{3,2},{4,5},{5,4},{6,7},{7,6},{8,9},{9,8},{10,11... | collective-permute-start | bytes 6291464 | tf_op jit(solution)/shard_map/ppermute | solution.py:46
  225.6 46.7 %collective-permute-start.16 = (bf16[2,256,1024]{2,1,0:T(8,128)(2,1)S(1)}, bf16[2,256,1024]{2,1,0:T(8,128)(2,1)S(1)}, u32[]{:S(2)}, u32[]{:S(2)}) collective-permute-start(bf16[2,256,1024]{2,1,0:T(8,128)(2,1)S(1)} %pad_maximum_fusion.19), channel_id=1, source_target_pairs={{0,2},{2,0},{1,3},{3,1},{4,6},{6,4},{5,7},{7,5},{8,10},{10,8},{9,1... | collective-permute-start | bytes 3145736 | tf_op jit(solution)/shard_map/ppermute | solution.py:46
  227.5 48.5 %collective-permute-start.24 = (f32[16,2,1024]{2,0,1:T(8,128)S(1)}, f32[16,2,1024]{2,0,1:T(8,128)S(1)}, u32[]{:S(2)}, u32[]{:S(2)}) collective-permute-start(f32[16,2,1024]{2,0,1:T(8,128)S(1)} %get-tuple-element.215), channel_id=1, source_target_pairs={{0,4},{4,0},{1,5},{5,1},{2,6},{6,2},{3,7},{7,3},{8,12},{12,8},{9,1... | collective-permute-start | bytes 393224 | tf_op jit(solution)/shard_map/ppermute | solution.py:46
  281.5 513.8 %reduce-scatter.7.cloned.1.call-start = ((), (), s32[]{:S(2)}) async-start(), calls=%async_computation.5 | async-start | bytes 3932160 | tf_op jit(solution)/shard_map/reduce_scatter | solution.py:503
  426.7 371.7 %reduce-scatter.9.cloned.1.call-start = ((), (), s32[]{:S(2)}) async-start(), calls=%async_computation.6 | async-start | bytes 3932160 | tf_op jit(solution)/shard_map/reduce_scatter | solution.py:503
  482.0 318.2 %reduce-scatter.11.cloned.1.call-start = ((), (), s32[]{:S(2)}) async-start(), calls=%async_computation.7 | async-start | bytes 3932160 | tf_op jit(solution)/shard_map/reduce_scatter | solution.py:503
  556.8 245.3 %reduce-scatter.5.cloned.1.call-start = ((), (), s32[]{:S(2)}) async-start(), calls=%async_computation.4 | async-start | bytes 3932160 | tf_op jit(solution)/shard_map/reduce_scatter | solution.py:503
  565.6 89.7 %collective-permute-start.33 = (bf16[2,256,1024]{2,1,0:T(8,128)(2,1)S(1)}, bf16[2,256,1024]{2,1,0:T(8,128)(2,1)S(1)}, u32[]{:S(2)}, u32[]{:S(2)}) collective-permute-start(bf16[2,256,1024]{2,1,0:T(8,128)(2,1)S(1)} %fusion.3), channel_id=1, source_target_pairs={{0,2},{2,0},{1,3},{3,1},{4,6},{6,4},{5,7},{7,5},{8,10},{10,8},{9,1... | collective-permute-start | bytes 3145736 | tf_op jit(solution)/shard_map/ppermute | solution.py:46
  569.0 62.9 %collective-permute-start.43 = (bf16[2,256,1024]{2,1,0:T(8,128)(2,1)S(1)}, bf16[2,256,1024]{2,1,0:T(8,128)(2,1)S(1)}, u32[]{:S(2)}, u32[]{:S(2)}) collective-permute-start(bf16[2,256,1024]{2,1,0:T(8,128)(2,1)S(1)} %fusion.1), channel_id=1, source_target_pairs={{0,2},{2,0},{1,3},{3,1},{4,6},{6,4},{5,7},{7,5},{8,10},{10,8},{9,1... | collective-permute-start | bytes 3145736 | tf_op jit(solution)/shard_map/ppermute | solution.py:46
  573.6 80.0 %collective-permute-start.36 = (bf16[2,256,1024]{2,1,0:T(8,128)(2,1)S(1)}, bf16[2,256,1024]{2,1,0:T(8,128)(2,1)S(1)}, u32[]{:S(2)}, u32[]{:S(2)}) collective-permute-start(bf16[2,256,1024]{2,1,0:T(8,128)(2,1)S(1)} %fusion.2), channel_id=1, source_target_pairs={{0,2},{2,0},{1,3},{3,1},{4,6},{6,4},{5,7},{7,5},{8,10},{10,8},{9,1... | collective-permute-start | bytes 3145736 | tf_op jit(solution)/shard_map/ppermute | solution.py:46
  587.4 82.5 %collective-permute-start.31 = (bf16[256,1024]{1,0:T(8,128)(2,1)S(1)}, bf16[256,1024]{1,0:T(8,128)(2,1)S(1)}, u32[]{:S(2)}, u32[]{:S(2)}) collective-permute-start(bf16[256,1024]{1,0:T(8,128)(2,1)S(1)} %fusion.21), channel_id=1, source_target_pairs={{0,4},{4,0},{1,5},{5,1},{2,6},{6,2},{3,7},{7,3},{8,12},{12,8},{9,1... | collective-permute-start | bytes 1572872 | tf_op jit(solution)/shard_map/ppermute | solution.py:46
  758.3 32.3 %collective-permute-start.40 = (bf16[512,1024]{1,0:T(8,128)(2,1)}, bf16[512,1024]{1,0:T(8,128)(2,1)}, u32[]{:S(2)}, u32[]{:S(2)}) collective-permute-start(bf16[512,1024]{1,0:T(8,128)(2,1)} %get-tuple-element.55), channel_id=1, source_target_pairs={{0,1},{1,0},{2,3},{3,2},{4,5},{5,4},{6,7},{7,6},{8,9},{9,8},{10,11... | collective-permute-start | bytes 3145736 | tf_op jit(solution)/shard_map/ppermute | solution.py:46
  789.4 44.3 %collective-permute-start.48 = (bf16[256,1024]{1,0:T(8,128)(2,1)}, bf16[256,1024]{1,0:T(8,128)(2,1)}, u32[]{:S(2)}, u32[]{:S(2)}) collective-permute-start(bf16[256,1024]{1,0:T(8,128)(2,1)} %fusion.19), channel_id=1, source_target_pairs={{0,2},{2,0},{1,3},{3,1},{4,6},{6,4},{5,7},{7,5},{8,10},{10,8},{9,1... | collective-permute-start | bytes 1572872 | tf_op jit(solution)/shard_map/ppermute | solution.py:46
  794.5 39.2 %collective-permute-start.41 = (bf16[256,1024]{1,0:T(8,128)(2,1)}, bf16[256,1024]{1,0:T(8,128)(2,1)}, u32[]{:S(2)}, u32[]{:S(2)}) collective-permute-start(bf16[256,1024]{1,0:T(8,128)(2,1)} %fusion.18), channel_id=1, source_target_pairs={{0,2},{2,0},{1,3},{3,1},{4,6},{6,4},{5,7},{7,5},{8,10},{10,8},{9,1... | collective-permute-start | bytes 1572872 | tf_op jit(solution)/shard_map/ppermute | solution.py:46
  (118 other events, 1390.6 us)
Sparse Core Ops, SparseCore 0:
  66.3 68.0 all-gather.14
  135.9 62.6 all-gather.12
  200.2 62.1 all-gather.10
  281.7 64.5 all-gather.8
  426.8 61.2 reduce-scatter.6
  490.2 60.2 reduce-scatter.8
  556.9 61.1 reduce-scatter.10
  705.9 60.9 reduce-scatter.4

commit v3 on v2

v3 whole, which is shorter than its diff:
```python
import functools

import jax
import jax.numpy as jnp
from jax import lax
from jax.experimental import pallas as pl
from jax.experimental.pallas import tpu as pltpu
from jax.sharding import Mesh
from jax.sharding import PartitionSpec as P

HD = 64
E = 32
CHUNKS = (3, 2, 2, 1)

EPSILON = 1e-06
BF = jnp.bfloat16
FP = jnp.float32


def dot_nn(left, right):
    return lax.dot_general(left, right, (((1,), (0,)), ((), ())), preferred_element_type=FP)


def dot_tn(left, right):
    return lax.dot_general(left, right, (((0,), (0,)), ((), ())), preferred_element_type=FP)


def dot_nt(left, right):
    return lax.dot_general(left, right, (((1,), (1,)), ((), ())), preferred_element_type=FP)


def row_norm(in_rows, gain_vec):
    row_scale = lax.rsqrt(jnp.mean(in_rows * in_rows, axis=-1, keepdims=True) + EPSILON)
    return (in_rows * row_scale * gain_vec, row_scale)


def norm_back(in_rows, row_scale, gain_vec, grad_in):
    weighted = grad_in * gain_vec
    inner = jnp.mean(weighted * in_rows, axis=-1, keepdims=True)
    returned = row_scale * weighted - in_rows * row_scale * row_scale * row_scale * inner
    gain_part = jnp.sum(grad_in * in_rows * row_scale, axis=0)
    return (returned, gain_part)


def swap(value, axis):
    return lax.ppermute(value, axis, [(0, 1), (1, 0)])


def after(value, *earlier):
    return lax.optimization_barrier((value, *earlier))[0]


def gather_rows(rows):
    across = swap(rows, "x")
    return [rows, across, swap(rows, "c"), swap(across, "c")]


def gather_pair(rows):
    near = swap(rows, "y")
    blocks = jnp.stack([rows, near, swap(rows, "x"), swap(near, "x")])
    return blocks, swap(blocks, "c")


def scatter_rows(kept, sent):
    got = swap(sent, "c").astype(FP)
    across = swap((kept[1] + got[1]).astype(BF), "x").astype(FP)
    return kept[0] + got[0] + across


def scatter_pair(kept, sent):
    got = swap(sent, "c").astype(FP)
    across = swap((kept[2:] + got[2:]).astype(BF), "x").astype(FP)
    near = swap((kept[1] + got[1] + across[1]).astype(BF), "y").astype(FP)
    return kept[0] + got[0] + across[0] + near


def turns(depth):
    up = [(i, (i + 1) % depth) for i in range(depth)]
    down = [(i, (i - 1) % depth) for i in range(depth)]
    return up, down


def gather_dp(shard, depth):
    turn_up, turn_down = turns(depth)
    place, side = lax.axis_index("z"), lax.axis_index("y")
    line = [(shard, place)]
    piece = shard
    for k in range(1, depth // 2 + 1):
        piece = lax.ppermute(piece, "z", turn_up)
        line.append((piece, lax.rem(place + depth - k, depth)))
    piece = shard
    for k in range(1, (depth - 1) // 2 + 1):
        piece = lax.ppermute(piece, "z", turn_down)
        line.append((piece, lax.rem(place + k, depth)))
    pieces = [p for p, _ in line] + [swap(p, "y") for p, _ in line]
    index = [2 * z + side for _, z in line] + [2 * z + 1 - side for _, z in line]
    return pieces, jnp.stack(index).astype(jnp.int32)


def scatter_dp(kept, sent, depth):
    column = kept + swap(sent, "y").astype(FP)
    turn_up, turn_down = turns(depth)
    total = column[0]
    for turn, sign, steps in ((turn_up, 1, depth // 2), (turn_down, -1, (depth - 1) // 2)):
        carried = None
        for distance in range(steps, 0, -1):
            block = column[(sign * distance) % depth]
            carried = block if carried is None else block + carried
            carried = lax.ppermute(carried.astype(BF), "z", turn).astype(FP)
        if carried is not None:
            total = total + carried
    return total


def sum_all(value, depth):
    for axis in ("c", "x", "y"):
        value = value + swap(value, axis)
    reach = 1
    while reach < depth:
        pairs = [(i, i ^ reach) for i in range(depth)]
        value = value + lax.ppermute(value, "z", pairs)
        reach *= 2
    return value


SMEM = pl.BlockSpec(memory_space=pltpu.SMEM)
VMEM = pl.BlockSpec(memory_space=pltpu.VMEM)


def pack_kernel(side_ref, gate_up_ref, down_ref, *rest):
    *outs, rows_scr = rest
    blk = down_ref.shape[2]
    offset = 0
    for mine_ref, theirs_ref in zip(outs[::2], outs[1::2]):
        pairs = mine_ref.shape[0]
        hidden_local = mine_ref.shape[2] // 6
        for out_ref, half in ((theirs_ref, 1 - side_ref[0]), (mine_ref, side_ref[0])):
            for p in range(pairs):
                for i in range(2):
                    expert = half * (E // 2) + 2 * (offset + p) + i
                    rows_scr[...] = gate_up_ref[expert].astype(FP)
                    for part in range(2):
                        cols = slice((2 * part + i) * hidden_local, (2 * part + i + 1) * hidden_local)
                        out_ref[p, :, cols] = rows_scr[pl.ds(part, blk, stride=2), :].astype(BF)
                    cols = slice((4 + i) * hidden_local, (5 + i) * hidden_local)
                    out_ref[p, :, cols] = down_ref[expert].astype(FP).T.astype(BF)
        offset += pairs


def pack_experts(side, w_gate_up, w_down):
    experts, blk, _, hidden_local = w_gate_up.shape
    shapes = [jax.ShapeDtypeStruct((pairs, blk, 6 * hidden_local), BF) for pairs in CHUNKS]
    outs = pl.pallas_call(
        pack_kernel,
        in_specs=[SMEM, VMEM, VMEM],
        out_specs=[VMEM] * (2 * len(CHUNKS)),
        out_shape=[shape for shape in shapes for _ in range(2)],
        scratch_shapes=[pltpu.VMEM((2 * blk, hidden_local), FP)],
        compiler_params=pltpu.CompilerParams(vmem_limit_bytes=32 << 20),
        cost_estimate=pl.CostEstimate(flops=1 << 20, bytes_accessed=8 << 20, transcendentals=0),
    )(side, w_gate_up.reshape(experts, 2 * blk, hidden_local), w_down)
    return list(zip(outs[::2], outs[1::2]))


def unpack_kernel(side_ref, *refs):
    *ins, gate_up_ref, down_ref = refs
    blk = down_ref.shape[2]
    offset = 0
    for kept_ref, got_ref in zip(ins[::2], ins[1::2]):
        pairs = got_ref.shape[0]
        hidden_local = got_ref.shape[2] // 6
        for mine, half in ((True, side_ref[0]), (False, 1 - side_ref[0])):
            for p in range(pairs):
                packed = (kept_ref[0, p] if mine else got_ref[p]).astype(FP)
                for i in range(2):
                    expert = half * (E // 2) + 2 * (offset + p) + i
                    for part in range(2):
                        cols = slice((2 * part + i) * hidden_local, (2 * part + i + 1) * hidden_local)
                        gate_up_ref[expert, pl.ds(part, blk, stride=2), :] = packed[:, cols]
                    down_ref[expert] = packed[:, (4 + i) * hidden_local : (5 + i) * hidden_local].T
        offset += pairs


def unpack_experts(side, shards):
    blk, width = shards[0][1].shape[1:]
    hidden_local = width // 6
    operands = [array for shard in shards for array in shard]
    gate_up, down = pl.pallas_call(
        unpack_kernel,
        in_specs=[SMEM] + [VMEM] * len(operands),
        out_specs=[VMEM, VMEM],
        out_shape=[
            jax.ShapeDtypeStruct((E, 2 * blk, hidden_local), FP),
            jax.ShapeDtypeStruct((E, hidden_local, blk), FP),
        ],
        compiler_params=pltpu.CompilerParams(vmem_limit_bytes=32 << 20),
        cost_estimate=pl.CostEstimate(flops=1 << 20, bytes_accessed=12 << 20, transcendentals=0),
    )(side, *operands)
    return gate_up.reshape(E, blk, 2, hidden_local), down


def pack_attn_kernel(query_ref, key_ref, value_ref, out_ref, packed_ref):
    start = 0
    for ref in (query_ref, key_ref, value_ref):
        packed_ref[:, start : start + ref.shape[1]] = ref[...]
        start += ref.shape[1]
    packed_ref[:, start:] = out_ref[...].astype(FP).T.astype(BF)


def pack_attn(w_query, w_key, w_value, w_out):
    width = w_query.shape[1] + w_key.shape[1] + w_value.shape[1] + w_out.shape[0]
    return pl.pallas_call(
        pack_attn_kernel,
        in_specs=[VMEM] * 4,
        out_specs=VMEM,
        out_shape=jax.ShapeDtypeStruct((w_query.shape[0], width), BF),
        cost_estimate=pl.CostEstimate(flops=1 << 20, bytes_accessed=1 << 20, transcendentals=0),
    )(w_query, w_key, w_value, w_out)


def moe_kernel(first, last, start, column, side_ref, xa_ref, xb_ref, ga_ref, gb_ref, gate_ref, w_ref, *rest):
    rest = list(rest)
    sums_in = [] if first else [rest.pop(0), rest.pop(0)]
    earlier_ref = None if start else rest.pop(0)
    acc = rest.pop()
    grads_ref = rest.pop()
    sums_out = rest
    step = pl.program_id(0)
    blocks, pairs, blk, width = w_ref.shape
    model_width = blocks * blk
    half = width // 3
    hidden_local = half // 2

    def spot(block):
        place = (block // 2) * 2 + (side_ref[0] + block % 2) % 2
        return pl.ds(pl.multiple_of(place * blk, blk), blk)

    @pl.when(step == 0)
    def _():
        if start:
            acc[...] = jnp.zeros_like(acc)
        else:
            for p in range(pairs):
                for block in range(blocks):
                    acc[p, spot(block), :] = earlier_ref[block, p].astype(FP)

    x = jnp.concatenate([xa_ref[...], xb_ref[...]], axis=0)
    g = jnp.concatenate([ga_ref[...], gb_ref[...]], axis=0)
    totals = [None, None]
    for p in range(pairs):
        weights = w_ref[:, p].reshape(model_width, width)
        pre = dot_nn(x, weights[:, : 2 * half])
        out_back = dot_nn(g, weights[:, 2 * half :])
        gate = pre[:, :half]
        up = pre[:, half:]
        sig = 0.5 + 0.5 * jnp.tanh(0.5 * gate)
        share = jnp.concatenate(
            [
                jnp.broadcast_to(gate_ref[:, i : i + 1], (x.shape[0], hidden_local))
                for i in (column + 2 * p, column + 2 * p + 1)
            ],
            axis=1,
        )
        silu = gate * sig
        hidden = (share * (silu * up)).astype(BF)
        hidden_grad = share * out_back
        gate_grad = (hidden_grad * up * (sig + silu * (1.0 - sig))).astype(BF)
        up_grad = (hidden_grad * silu).astype(BF)
        pair_grad = jnp.concatenate([gate_grad, up_grad], axis=1)
        terms = (
            dot_nt(hidden, weights[:, 2 * half :]),
            dot_nt(pair_grad, weights[:, : 2 * half]),
        )
        totals = [t if s is None else s + t for s, t in zip(totals, terms)]
        acc[p, :, : 2 * half] += dot_tn(x, pair_grad)
        acc[p, :, 2 * half :] += dot_tn(g, hidden)
    if not first:
        totals = [s[...] + t for s, t in zip(sums_in, totals)]
    if last:
        rows = xa_ref.shape[0]
        for kept_ref, sent_ref, total in zip(sums_out[::2], sums_out[1::2], totals):
            kept_ref[...] = total[:rows]
            sent_ref[...] = total[rows:].astype(BF)
    else:
        for out_ref, total in zip(sums_out, totals):
            out_ref[...] = total

    @pl.when(step == pl.num_programs(0) - 1)
    def _():
        for p in range(pairs):
            for block in range(blocks):
                grads_ref[block, p] = acc[p, spot(block), :].astype(BF)


def moe_chunk(side, x, g, gates, weights, sums, earlier, micro, column, last):
    count, rows, model_width = x[0].shape
    blocks, pairs, blk, width = weights.shape
    once = pl.Buffered(1)
    row = pl.BlockSpec((None, 2 * rows, model_width), lambda i: (i, 0, 0))
    half = pl.BlockSpec((None, rows, model_width), lambda i: (i, 0, 0))
    g_spec = pl.BlockSpec((None, None, rows, model_width), lambda i: (i, micro, 0, 0))
    gate_spec = pl.BlockSpec((None, None, 2 * rows, gates.shape[-1]), lambda i: (micro, i, 0, 0))
    whole = pl.BlockSpec(weights.shape, lambda i: (0, 0, 0, 0), pipeline_mode=once)
    first, start = sums is None, earlier is None
    operands = [side, *x, *g, gates, weights] + ([] if first else list(sums))
    operands += [] if start else [earlier]
    if last:
        out_specs = [half] * 4
        outs = [jax.ShapeDtypeStruct((count, rows, model_width), t) for t in (FP, BF, FP, BF)]
    else:
        out_specs = [row] * 2
        outs = [jax.ShapeDtypeStruct((count, 2 * rows, model_width), FP)] * 2
    *sums, grads = pl.pallas_call(
        functools.partial(moe_kernel, first, last, start, column),
        grid=(count,),
        in_specs=[SMEM, half, half, g_spec, g_spec, gate_spec, whole]
        + ([] if first else [row, row])
        + ([] if start else [whole]),
        out_specs=out_specs + [whole],
        scratch_shapes=[pltpu.VMEM((pairs, model_width, width), FP)],
        out_shape=outs + [jax.ShapeDtypeStruct(weights.shape, BF)],
        input_output_aliases={} if first or last else {7: 0, 8: 1},
        compiler_params=pltpu.CompilerParams(vmem_limit_bytes=60 << 20),
        cost_estimate=pl.CostEstimate(
            flops=12 * count * rows * model_width * pairs * width,
            bytes_accessed=48 << 20,
            transcendentals=2 * count * rows * pairs * width // 3,
        ),
    )(*operands)
    return sums, grads


def place_rows(spots_ref, pieces, whole_ref):
    rows = pieces[0].shape[0]
    for i, piece in enumerate(pieces):
        whole_ref[pl.ds(pl.multiple_of(spots_ref[i] * rows, rows), rows), :] = piece[...]


def product_rows(spots_ref, left_ref, right, kept_ref, sent_ref):
    rows = kept_ref.shape[1]
    for i in range(4):
        here = pl.ds(pl.multiple_of(spots_ref[i] * rows, rows), rows)
        value = dot_nt(left_ref[here, :], right)
        if i < 2:
            kept_ref[i] = value
        else:
            sent_ref[i - 2] = value.astype(BF)


def attn_forward_kernel(widths, n_weights, spots_ref, weight_spots_ref, *rest):
    q_width, kv_width = widths
    x_pieces, rest = rest[:4], rest[4:]
    w_pieces, rest = rest[:n_weights], rest[n_weights:]
    if n_weights > 1:
        qkv_ref, heads_ref, kept_ref, sent_ref, w_ref, x_scr = rest
        place_rows(weight_spots_ref, w_pieces, w_ref)
    else:
        qkv_ref, heads_ref, kept_ref, sent_ref, x_scr = rest
        w_ref = w_pieces[0]
    place_rows(spots_ref, x_pieces, x_scr)
    rows = x_scr.shape[0]
    proj_width = q_width + 2 * kv_width
    ratio = q_width // kv_width
    tile = min(256, rows)
    qkv_ref[...] = dot_nn(x_scr[...], w_ref[:, :proj_width]).astype(BF)
    for kv in range(kv_width // HD):
        keys = qkv_ref[:, q_width + kv * HD : q_width + (kv + 1) * HD]
        values = qkv_ref[:, q_width + kv_width + kv * HD : q_width + kv_width + (kv + 1) * HD]
        cols = [slice((kv * ratio + r) * HD, (kv * ratio + r + 1) * HD) for r in range(ratio)]
        for start in range(0, rows, tile):
            stop = start + tile
            query = jnp.concatenate([qkv_ref[start:stop, c] for c in cols], axis=0) * BF(HD**-0.5)
            near = dot_nt(query, keys[start:stop])
            row_pos = lax.broadcasted_iota(jnp.int32, near.shape, 0) & (tile - 1)
            col_pos = lax.broadcasted_iota(jnp.int32, near.shape, 1)
            scores = jnp.where(col_pos <= row_pos, near, -1e30)
            if start:
                scores = jnp.concatenate([dot_nt(query, keys[:start]), scores], axis=1)
            exponent = jnp.exp(scores - jnp.max(scores, axis=-1, keepdims=True))
            total = jnp.sum(exponent, axis=-1, keepdims=True)
            probs = (exponent * (1.0 / total)).astype(BF)
            out = dot_nn(probs, values[:stop]).astype(BF)
            for r, c in enumerate(cols):
                heads_ref[start:stop, c] = out[r * tile : (r + 1) * tile]
    product_rows(spots_ref, heads_ref, w_ref[:, proj_width:], kept_ref, sent_ref)


def attn_backward_kernel(widths, first, spots_ref, block_spots_ref, *rest):
    q_width, kv_width = widths
    proj_width = q_width + 2 * kv_width
    dy_pieces, x_pieces, rest = rest[:4], rest[4:8], list(rest[8:])
    qkv_ref, heads_ref, w_ref = rest[:3]
    rest = rest[3:]
    if first:
        grads_ref, kept_ref, sent_ref = rest[:3]
        rest = rest[3:]
    else:
        earlier_ref, grads_kept_ref, grads_sent_ref, kept_ref, sent_ref = rest[:5]
        grads_ref = rest[5]
        rest = rest[6:]
    dy_scr, x_scr, head_grad_ref, proj_grad_ref, key_acc, value_acc = rest
    place_rows(spots_ref, dy_pieces, dy_scr)
    place_rows(spots_ref, x_pieces, x_scr)
    rows = x_scr.shape[0]
    ratio = q_width // kv_width
    tile = min(256, rows)
    head_grad_ref[...] = dot_nn(dy_scr[...], w_ref[:, proj_width:]).astype(BF)
    for kv in range(kv_width // HD):
        key_cols = slice(q_width + kv * HD, q_width + (kv + 1) * HD)
        value_cols = slice(q_width + kv_width + kv * HD, q_width + kv_width + (kv + 1) * HD)
        cols = [slice((kv * ratio + r) * HD, (kv * ratio + r + 1) * HD) for r in range(ratio)]
        keys = qkv_ref[:, key_cols]
        values = qkv_ref[:, value_cols]
        key_acc[...] = jnp.zeros_like(key_acc)
        value_acc[...] = jnp.zeros_like(value_acc)
        for start in range(0, rows, tile):
            stop = start + tile
            query = jnp.concatenate([qkv_ref[start:stop, c] for c in cols], axis=0) * BF(HD**-0.5)
            out_grad = jnp.concatenate([head_grad_ref[start:stop, c] for c in cols], axis=0)
            near = dot_nt(keys[start:stop], query)
            key_pos = lax.broadcasted_iota(jnp.int32, near.shape, 0)
            row_pos = lax.broadcasted_iota(jnp.int32, near.shape, 1) & (tile - 1)
            scores = jnp.where(key_pos <= row_pos, near, -1e30)
            if start:
                scores = jnp.concatenate([dot_nt(keys[:start], query), scores], axis=0)
            exponent = jnp.exp(scores - jnp.max(scores, axis=0, keepdims=True))
            probs = exponent * (1.0 / jnp.sum(exponent, axis=0, keepdims=True))
            prob_grad = dot_nt(values[:stop], out_grad)
            inner = jnp.sum(probs * prob_grad, axis=0, keepdims=True)
            score_grad = (probs * (prob_grad - inner)).astype(BF)
            value_acc[:stop] += dot_nn(probs.astype(BF), out_grad)
            key_acc[:stop] += dot_nn(score_grad, query)
            query_grad = (dot_tn(score_grad, keys[:stop]) * (HD**-0.5)).astype(BF)
            for r, c in enumerate(cols):
                proj_grad_ref[start:stop, c] = query_grad[r * tile : (r + 1) * tile]
        proj_grad_ref[:, key_cols] = key_acc[...].astype(BF)
        proj_grad_ref[:, value_cols] = value_acc[...].astype(BF)
    product_rows(spots_ref, proj_grad_ref, w_ref[:, :proj_width], kept_ref, sent_ref)
    proj_part = dot_tn(x_scr[...], proj_grad_ref[...])
    out_part = dot_tn(dy_scr[...], heads_ref[...])
    if first:
        grads_ref[:, :proj_width] = proj_part
        grads_ref[:, proj_width:] = out_part
    else:
        grads_ref[:, :proj_width] = earlier_ref[:, :proj_width] + proj_part
        grads_ref[:, proj_width:] = earlier_ref[:, proj_width:] + out_part
        depth, blk, _ = grads_kept_ref.shape
        for r in range(depth):
            here = pl.ds(pl.multiple_of(block_spots_ref[r] * blk, blk), blk)
            grads_kept_ref[r] = grads_ref[here, :]
            here = pl.ds(pl.multiple_of(block_spots_ref[depth + r] * blk, blk), blk)
            grads_sent_ref[r] = grads_ref[here, :].astype(BF)


def attn_forward(spots, weight_spots, pieces, weights, widths):
    rows, model_width = pieces[0].shape
    width = weights[0].shape[1]
    whole = len(weights) == 1
    outs = [
        jax.ShapeDtypeStruct((4 * rows, widths[0] + 2 * widths[1]), BF),
        jax.ShapeDtypeStruct((4 * rows, widths[0]), BF),
        jax.ShapeDtypeStruct((2, rows, model_width), FP),
        jax.ShapeDtypeStruct((2, rows, model_width), BF),
    ] + ([] if whole else [jax.ShapeDtypeStruct((model_width, width), BF)])
    results = pl.pallas_call(
        functools.partial(attn_forward_kernel, widths, len(weights)),
        in_specs=[SMEM] * 2 + [VMEM] * (4 + len(weights)),
        out_specs=[VMEM] * len(outs),
        out_shape=outs,
        scratch_shapes=[pltpu.VMEM((4 * rows, model_width), BF)],
        compiler_params=pltpu.CompilerParams(vmem_limit_bytes=56 << 20),
        cost_estimate=pl.CostEstimate(
            flops=14 << 30, bytes_accessed=10 << 20, transcendentals=3 << 20
        ),
    )(spots, weight_spots, *pieces, *weights)
    return results if not whole else [*results, weights[0]]


def attn_backward(spots, block_spots, dy, x, qkv, heads, weights, earlier, widths):
    rows, model_width = x[0].shape
    width = weights.shape[1]
    first = earlier is None
    operands = [*dy, *x, qkv, heads, weights] + ([] if first else [earlier])
    depth = block_spots.shape[0] // 2
    whole = (model_width, width)
    blocks = (depth, model_width // depth // 2, width)
    scratch = [
        pltpu.VMEM((4 * rows, model_width), BF),
        pltpu.VMEM((4 * rows, model_width), BF),
        pltpu.VMEM(heads.shape, BF),
        pltpu.VMEM(qkv.shape, BF),
        pltpu.VMEM((4 * rows, HD), FP),
        pltpu.VMEM((4 * rows, HD), FP),
    ]
    if first:
        outs = [jax.ShapeDtypeStruct(whole, FP)]
    else:
        outs = [jax.ShapeDtypeStruct(blocks, FP), jax.ShapeDtypeStruct(blocks, BF)]
        scratch = [pltpu.VMEM(whole, FP)] + scratch
    outs += [jax.ShapeDtypeStruct((2, rows, model_width), t) for t in (FP, BF)]
    return pl.pallas_call(
        functools.partial(attn_backward_kernel, widths, first),
        in_specs=[SMEM] * 2 + [VMEM] * len(operands),
        out_specs=[VMEM] * len(outs),
        out_shape=outs,
        scratch_shapes=scratch,
        compiler_params=pltpu.CompilerParams(vmem_limit_bytes=58 << 20),
        cost_estimate=pl.CostEstimate(
            flops=30 << 30, bytes_accessed=16 << 20, transcendentals=3 << 20
        ),
    )(spots, block_spots, *operands)


def on_device(
    block_input,
    cotangent,
    routes,
    gate_weights,
    w_query,
    w_key,
    w_value,
    w_out,
    w_gate_up,
    w_down,
    norm_attn,
    norm_moe,
):
    depth = lax.axis_size("z")
    micro_count, rows_local, model_width = block_input.shape
    q_width, kv_width = w_query.shape[1], w_key.shape[1]
    widths = (q_width, kv_width)
    proj_width = q_width + 2 * kv_width
    side, chip, core = lax.axis_index("y"), lax.axis_index("x"), lax.axis_index("c")
    side_at = side.astype(jnp.int32).reshape(1)
    spots = jnp.stack([2 * x + c for c in (core, 1 - core) for x in (chip, 1 - chip)])
    spots = spots.astype(jnp.int32)
    place = lax.axis_index("z")
    block_spots = jnp.stack(
        [2 * lax.rem(place + r, depth) + s for s in (side, 1 - side) for r in range(depth)]
    ).astype(jnp.int32)

    in_rows = block_input.astype(FP)
    normed_attn, scale_attn = row_norm(in_rows, norm_attn)
    normed_attn = normed_attn.astype(BF)
    attn_in = [gather_rows(normed_attn[m]) for m in range(micro_count)]
    attn_pieces, weight_spots = gather_dp(pack_attn(w_query, w_key, w_value, w_out), depth)

    packed = pack_experts(side_at, w_gate_up, w_down)
    chunk_weights = []
    for mine, theirs in packed:
        got = swap(theirs, "y")
        if chunk_weights:
            got = after(got, chunk_weights[-1][:1, :1, :8, :128])
        first = side == 0
        shard = jnp.stack([jnp.where(first, mine, got), jnp.where(first, got, mine)])
        whole = lax.all_gather(shard, "z", axis=0)
        chunk_weights.append(whole.reshape(-1, *whole.shape[2:]))

    expert_ids = jnp.arange(E, dtype=jnp.int32)[:, None, None, None]
    gates = jnp.sum(jnp.where(routes == expert_ids, gate_weights, 0.0), axis=3)
    gates = gates.reshape(2, E // 2, micro_count, 2, 2, rows_local)
    gates = jnp.where(chip == 0, gates, gates[:, :, :, ::-1])
    gates = jnp.where(core == 0, gates, gates[:, :, :, :, ::-1])
    mine = lax.dynamic_index_in_dim(gates, side, 0, False)
    theirs = lax.dynamic_index_in_dim(gates, 1 - side, 0, False)
    gates = jnp.stack([mine, swap(theirs.reshape(E // 2, -1), "y").reshape(mine.shape)])
    gates = gates.transpose(2, 3, 0, 4, 5, 1).reshape(micro_count, 4, 2 * rows_local, E // 2)

    moe_grad = gather_pair(after(cotangent, attn_in[-1][1]))
    saved, middle, scale_moe, moe_in = [], [], [], []
    weights = attn_pieces
    for m in range(micro_count):
        qkv, heads, kept, sent, whole = attn_forward(
            spots, weight_spots, attn_in[m], weights, widths
        )
        weights = [whole]
        saved.append((qkv, heads))
        middle.append(in_rows[m] + scatter_rows(kept, sent))
        normed_moe, scale = row_norm(middle[m], norm_moe)
        scale_moe.append(scale)
        moe_in.append(gather_pair(normed_moe.astype(BF)))

    sums = [None] * micro_count
    shards = []
    column = 0
    for chunk, pairs in enumerate(CHUNKS):
        grads = None
        for m in range(micro_count):
            sums[m], grads = moe_chunk(
                side_at,
                moe_in[m],
                moe_grad,
                gates,
                chunk_weights[chunk],
                sums[m],
                grads,
                m,
                column,
                chunk == len(CHUNKS) - 1,
            )
        column += 2 * pairs
        grads = grads.reshape(depth, 2, *grads.shape[1:])
        grads = lax.psum_scatter(grads, "z", scatter_dimension=0, tiled=False)
        shards.append((grads, swap(grads[1], "y")))
    shard_pair, shard_down = unpack_experts(side_at, shards)

    out_grad = cotangent.astype(FP)
    outputs, input_grads = [], []
    gains = jnp.zeros((2, model_width), FP)
    middle_grad, branch_grad = [], []
    for m in range(micro_count):
        moe_in_grad = scatter_pair(*sums[m][2:])
        middle_back, gain_moe = norm_back(middle[m], scale_moe[m], norm_moe, moe_in_grad)
        middle_grad.append(out_grad[m] + middle_back)
        branch_grad.append(gather_rows(middle_grad[m].astype(BF)))
        gains = gains.at[1].add(gain_moe)
    results = None
    for m in range(micro_count):
        results = attn_backward(
            spots,
            block_spots,
            branch_grad[m],
            attn_in[m],
            *saved[m],
            weights[0],
            None if results is None else results[0],
            widths,
        )
        attn_in_grad = scatter_rows(*results[-2:])
        in_back, gain_attn = norm_back(in_rows[m], scale_attn[m], norm_attn, attn_in_grad)
        input_grads.append(middle_grad[m] + in_back)
        gains = gains.at[0].add(gain_attn)
    for m in range(micro_count):
        kept, sent = sums[m][:2]
        sent = after(sent, branch_grad[-1][1])
        outputs.append((middle[m] + scatter_pair(kept, sent)).astype(BF))
    attn_shard = scatter_dp(results[0], results[1], depth)
    gains = sum_all(gains.reshape(16, -1), depth).reshape(2, model_width)
    return (
        jnp.stack(outputs),
        jnp.stack(input_grads),
        attn_shard[:, :q_width],
        attn_shard[:, q_width : q_width + kv_width],
        attn_shard[:, q_width + kv_width : proj_width],
        attn_shard[:, proj_width:].T,
        shard_pair,
        shard_down,
        gains[0],
        gains[1],
    )


def solution(mesh):
    dp, tensor = mesh.shape["dp"], mesh.shape["tensor"]
    fine = Mesh(mesh.devices.reshape(dp // 2, 2, tensor // 2, 2), ("z", "y", "x", "c"))
    dp_axes, tensor_axes = ("z", "y"), ("x", "c")
    rows = P(None, dp_axes + tensor_axes, None)
    return jax.shard_map(
        on_device,
        mesh=fine,
        in_specs=(
            rows,
            rows,
            P(None, dp_axes, None),
            P(None, dp_axes, None),
            P(dp_axes, tensor_axes),
            P(dp_axes, tensor_axes),
            P(dp_axes, tensor_axes),
            P(tensor_axes, dp_axes),
            P(None, dp_axes, None, tensor_axes),
            P(None, tensor_axes, dp_axes),
            P(),
            P(),
        ),
        out_specs=(
            rows,
            rows,
            P(dp_axes, tensor_axes),
            P(dp_axes, tensor_axes),
            P(dp_axes, tensor_axes),
            P(tensor_axes, dp_axes),
            P(None, dp_axes, None, tensor_axes),
            P(None, tensor_axes, dp_axes),
            P(),
            P(),
        ),
        check_vma=False,
    )
```

time: 891 us -> 880 us (0.988)
  local copies, waits for them, and re-layouts: 108 us -> 29.7 us
  waiting for transfers between devices: 308 us -> 360 us
  Pallas kernels: 287 us -> 325 us
  other arithmetic: 107 us -> 76.4 us
  starting transfers between devices: 58.4 us -> 69.5 us
    pallas_call x8 -> x15, Pallas kernels: 287 us -> 325 us  [the longest x8 253 us: moe_chunk(): pl.pallas_call(functools.partial(moe_kernel, first, last, start, column),...]
    another operation x44 -> x14, other arithmetic: 47.8 us -> 14.6 us  [the longest x4 6.07 us: gather_pair(): blocks = jnp.stack([rows, near, swap(rows, 'x'), swap(near, 'x')])]
    convert_element_type x2 -> x25, other arithmetic: 5.18 us -> 35.3 us  [the longest x4 9.37 us: scatter_pair(): got = swap(sent, 'c').astype(FP)]
    ppermute x54 -> x61, waiting for transfers between devices: 291 us -> 320 us  [swap(): return lax.ppermute(value, axis, [(0, 1), (1, 0)])]
    slice x10 -> x0, local copies, waits for them, and re-layouts: 27.3 us -> none  [the longest x2 6.83 us: on_device(): moe_in_grad = scatter_pair(back_kept[m], back_sent[m])]
    reshape x5 -> x4, local copies, waits for them, and re-layouts: 23.7 us -> 0.45 us  [the longest x2 0.34 us: on_device(): gates = gates.reshape(2, E // 2, micro_count, 2, 2, rows_local)]
    add x14 -> x2, other arithmetic: 21.9 us -> 0.01 us  [the longest x1 0.01 us: on_device(): gains = gains.at[0].add(gain_attn)]
    concatenate x4 -> x0, other arithmetic: 17.6 us -> none  [the longest x1 7.88 us: on_device(): jnp.concatenate([gather_pair(cotangent[m]) for m in range(micro_count)])]
  transfers between devices with their start and end apart: 70 -> 77, of which waited for: 30 -> 39; matrix products, arithmetic and copies ran while one was open for 21% -> 10% of each run, Pallas kernels for 32% -> 20%
where the time goes in v3:
time: 880 us; the launch traced here: 876 us
  waiting for transfers between devices  360 us (41%)
  Pallas kernels  325 us (37%)
  other arithmetic  76.4 us (9%)
  starting transfers between devices  69.5 us (8%)
  local copies, waits for them, and re-layouts  29.7 us (3%)
  between operations  15.6 us (2%)
    ppermute x61, waiting for transfers between devices, swap(): return lax.ppermute(value, axis, [(0, 1), (1, 0)])  320 us
    pallas_call x8, Pallas kernels, moe_chunk(): pl.pallas_call(functools.partial(moe_kernel, first, last, start, column),...  253 us
    ppermute x61, starting transfers between devices, swap(): return lax.ppermute(value, axis, [(0, 1), (1, 0)])  44.5 us
    pallas_call x2, Pallas kernels, attn_backward(): pl.pallas_call(functools.partial(attn_backward_kernel, widths, first), in...  42.5 us
    pallas_call x2, Pallas kernels, attn_forward(): pl.pallas_call(functools.partial(attn_forward_kernel, widths, len(weights...  23.4 us
  transfers between devices with their start and end apart: 77, of which 39 were waited for; matrix products, arithmetic and copies ran while one was open for 10% of the time, Pallas kernels for 20%

profile of v3, /device:TPU:0, one launch (start us, length us, event | category | flops | bytes accessed | tf_op | source)
XLA Modules:
  0.0 875.9 jit_solution(13769988222079397929)
XLA Ops:
  14.1 13.4 %collective-permute-done.25 = bf16[3,128,768]{2,1,0:T(8,128)(2,1)} collective-permute-done((bf16[3,128,768]{2,1,0:T(8,128)(2,1)S(1)}, bf16[3,128,768]{2,1,0:T(8,128)(2,1)}, u32[]{:S(2)}, u32[]{:S(2)}) %collective-permute-start.25) | collective-permute-done | bytes 589856 | tf_op jit(solution)/shard_map/ppermute | solution.py:46
  84.2 11.9 %shard_map.196 = (bf16[1024,512]{1,0:T(8,128)(2,1)}, bf16[1024,256]{1,0:T(8,128)(2,1)}, f32[2,256,1024]{2,1,0:T(8,128)}, bf16[2,256,1024]{2,1,0:T(8,128)(2,1)}, bf16[1024,768]{1,0:T(8,128)(2,1)}) custom-call(s32[4]{0:T(128)} %pad_add_fusion.spots_ref, s32[8]{0:T(128)} %stack.179.weight_spots_ref, bf16[256,1024]{1,0:T(8,128)(2,1)} %get-tuple-element.256.rest_0_.rest_4_, ...), custom_call_target="tpu_custom_call" | custom-call | flops 15032385536 | bytes 10485760 | tf_op jit(solution)/shard_map/pallas_call | solution.py:465
  97.1 11.6 %shard_map.202 = (bf16[1024,512]{1,0:T(8,128)(2,1)}, bf16[1024,256]{1,0:T(8,128)(2,1)}, f32[2,256,1024]{2,1,0:T(8,128)}, bf16[2,256,1024]{2,1,0:T(8,128)(2,1)}) custom-call(s32[4]{0:T(128)} %pad_add_fusion.spots_ref, s32[8]{0:T(128)} %stack.179.weight_spots_ref, bf16[256,1024]{1,0:T(8,128)(2,1)} %copy-done.37, ...), custom_call_target="tpu_custom_call" | custom-call | flops 15032385536 | bytes 10485760 | tf_op jit(solution)/shard_map/pallas_call | solution.py:465
  109.5 10.8 %collective-permute-done.23 = bf16[2,128,768]{2,1,0:T(8,128)(2,1)S(1)} collective-permute-done((bf16[2,128,768]{2,1,0:T(8,128)(2,1)S(1)}, bf16[2,128,768]{2,1,0:T(8,128)(2,1)S(1)}, u32[]{:S(2)}, u32[]{:S(2)}) %collective-permute-start.23) | collective-permute-done | bytes 393248 | tf_op jit(solution)/shard_map/ppermute | solution.py:46
  131.4 15.3 %collective-permute-done.18 = bf16[2,256,1024]{2,1,0:T(8,128)(2,1)} collective-permute-done((bf16[2,256,1024]{2,1,0:T(8,128)(2,1)}, bf16[2,256,1024]{2,1,0:T(8,128)(2,1)}, u32[]{:S(2)}, u32[]{:S(2)}) %collective-permute-start.18) | collective-permute-done | bytes 1048608 | tf_op jit(solution)/shard_map/ppermute | solution.py:46
  146.7 22.5 %collective-permute-done.19 = bf16[2,256,1024]{2,1,0:T(8,128)(2,1)} collective-permute-done((bf16[2,256,1024]{2,1,0:T(8,128)(2,1)}, bf16[2,256,1024]{2,1,0:T(8,128)(2,1)}, u32[]{:S(2)}, u32[]{:S(2)}) %collective-permute-start.19) | collective-permute-done | bytes 1048608 | tf_op jit(solution)/shard_map/ppermute | solution.py:46
  193.8 10.4 %collective-permute-done.12 = bf16[256,1024]{1,0:T(8,128)(2,1)S(1)} collective-permute-done((bf16[256,1024]{1,0:T(8,128)(2,1)S(1)}, bf16[256,1024]{1,0:T(8,128)(2,1)S(1)}, u32[]{:S(2)}, u32[]{:S(2)}) %collective-permute-start.12) | collective-permute-done | bytes 524320 | tf_op jit(solution)/shard_map/ppermute | solution.py:46
  231.0 41.0 %shard_map.198 = (f32[4,512,1024]{2,1,0:T(8,128)}, f32[4,512,1024]{2,1,0:T(8,128)}, bf16[8,3,128,768]{3,2,1,0:T(8,128)(2,1)}) custom-call(s32[1]{0:T(128)} %bitcast.16.side_ref, bf16[4,256,1024]{2,1,0:T(8,128)(2,1)} %pad_maximum_fusion.1.xa_ref, bf16[4,256,1024]{2,1,0:T(8,128)(2,1)} %collective-permute-done.15.xb_ref, ...), custom_call_target="tpu_custom_call" | custom-call | flops 28991029248 | bytes 50331648 | tf_op jit(solution)/shard_map/pallas_call | solution.py:313
  272.0 32.0 %shard_map.199 = (f32[4,512,1024]{2,1,0:T(8,128)}, f32[4,512,1024]{2,1,0:T(8,128)}, bf16[8,2,128,768]{3,2,1,0:T(8,128)(2,1)}) custom-call(s32[1]{0:T(128)} %bitcast.16.side_ref, bf16[4,256,1024]{2,1,0:T(8,128)(2,1)} %pad_maximum_fusion.1.xa_ref, bf16[4,256,1024]{2,1,0:T(8,128)(2,1)} %collective-permute-done.15.xb_ref, ...), custom_call_target="tpu_custom_call", output_to_operand_aliasing={{0}: (7, {}), {1}: (8, {})} | custom-call | flops 19327352832 | bytes 50331648 | tf_op jit(solution)/shard_map/pallas_call | solution.py:313
  304.0 31.8 %shard_map.200 = (f32[4,512,1024]{2,1,0:T(8,128)}, f32[4,512,1024]{2,1,0:T(8,128)}, bf16[8,2,128,768]{3,2,1,0:T(8,128)(2,1)}) custom-call(s32[1]{0:T(128)} %bitcast.16.side_ref, bf16[4,256,1024]{2,1,0:T(8,128)(2,1)} %pad_maximum_fusion.1.xa_ref, bf16[4,256,1024]{2,1,0:T(8,128)(2,1)} %collective-permute-done.15.xb_ref, ...), custom_call_target="tpu_custom_call", output_to_operand_aliasing={{0}: (7, {}), {1}: (8, {})} | custom-call | flops 19327352832 | bytes 50331648 | tf_op jit(solution)/shard_map/pallas_call | solution.py:313
  335.9 20.4 %shard_map.201 = (f32[4,256,1024]{2,1,0:T(8,128)}, bf16[4,256,1024]{2,1,0:T(8,128)(2,1)}, f32[4,256,1024]{2,1,0:T(8,128)}, bf16[4,256,1024]{2,1,0:T(8,128)(2,1)}, bf16[8,1,128,768]{3,2,1,0:T(8,128)(2,1)}) custom-call(s32[1]{0:T(128)} %bitcast.16.side_ref, bf16[4,256,1024]{2,1,0:T(8,128)(2,1)} %pad_maximum_fusion.1.xa_ref, ...), custom_call_target="tpu_custom_call" | custom-call | flops 9663676416 | bytes 50331648 | tf_op jit(solution)/shard_map/pallas_call | solution.py:313
  363.3 23.7 %collective-permute-done.45 = bf16[2,256,1024]{2,1,0:T(8,128)(2,1)S(1)} collective-permute-done((bf16[2,256,1024]{2,1,0:T(8,128)(2,1)S(1)}, bf16[2,256,1024]{2,1,0:T(8,128)(2,1)S(1)}, u32[]{:S(2)}, u32[]{:S(2)}) %collective-permute-start.45) | collective-permute-done | bytes 1048608 | tf_op jit(solution)/shard_map/ppermute | solution.py:46
  389.3 11.5 %collective-permute-done.46 = bf16[256,1024]{1,0:T(8,128)(2,1)S(1)} collective-permute-done((bf16[256,1024]{1,0:T(8,128)(2,1)S(1)}, bf16[256,1024]{1,0:T(8,128)(2,1)S(1)}, u32[]{:S(2)}, u32[]{:S(2)}) %collective-permute-start.46) | collective-permute-done | bytes 524320 | tf_op jit(solution)/shard_map/ppermute | solution.py:46
  434.7 42.3 %shard_map.203 = (f32[4,512,1024]{2,1,0:T(8,128)}, f32[4,512,1024]{2,1,0:T(8,128)}, bf16[8,3,128,768]{3,2,1,0:T(8,128)(2,1)}) custom-call(s32[1]{0:T(128)} %bitcast.16.side_ref, bf16[4,256,1024]{2,1,0:T(8,128)(2,1)} %copy-done.35, bf16[4,256,1024]{2,1,0:T(8,128)(2,1)} %copy-done.48, bf16[4,2,256,1024]{3,2,1,0:T(8,128)(2,1)} %pad_maximum_fusion.ga_ref, ...), custom_call_target="tpu_custom_call" | custom-call | flops 28991029248 | bytes 50331648 | tf_op jit(solution)/shard_map/pallas_call | solution.py:313
  477.0 32.7 %shard_map.204 = (f32[4,512,1024]{2,1,0:T(8,128)}, f32[4,512,1024]{2,1,0:T(8,128)}, bf16[8,2,128,768]{3,2,1,0:T(8,128)(2,1)}) custom-call(s32[1]{0:T(128)} %bitcast.16.side_ref, bf16[4,256,1024]{2,1,0:T(8,128)(2,1)} %copy-done.35, bf16[4,256,1024]{2,1,0:T(8,128)(2,1)} %copy-done.48, ...), custom_call_target="tpu_custom_call", output_to_operand_aliasing={{0}: (7, {}), {1}: (8, {})} | custom-call | flops 19327352832 | bytes 50331648 | tf_op jit(solution)/shard_map/pallas_call | solution.py:313
  509.8 32.6 %shard_map.205 = (f32[4,512,1024]{2,1,0:T(8,128)}, f32[4,512,1024]{2,1,0:T(8,128)}, bf16[8,2,128,768]{3,2,1,0:T(8,128)(2,1)}) custom-call(s32[1]{0:T(128)} %bitcast.16.side_ref, bf16[4,256,1024]{2,1,0:T(8,128)(2,1)} %copy-done.35, bf16[4,256,1024]{2,1,0:T(8,128)(2,1)} %copy-done.48, ...), custom_call_target="tpu_custom_call", output_to_operand_aliasing={{0}: (7, {}), {1}: (8, {})} | custom-call | flops 19327352832 | bytes 50331648 | tf_op jit(solution)/shard_map/pallas_call | solution.py:313
  542.4 20.2 %shard_map.206 = (f32[4,256,1024]{2,1,0:T(8,128)}, bf16[4,256,1024]{2,1,0:T(8,128)(2,1)}, f32[4,256,1024]{2,1,0:T(8,128)}, bf16[4,256,1024]{2,1,0:T(8,128)(2,1)}, bf16[8,1,128,768]{3,2,1,0:T(8,128)(2,1)}) custom-call(s32[1]{0:T(128)} %bitcast.16.side_ref, bf16[4,256,1024]{2,1,0:T(8,128)(2,1)} %copy-done.35, bf16[4,256,1024]{2,1,0:T(8,128)(2,1)} %copy-done.48, ...), custom_call_target="tpu_custom_call" | custom-call | flops 9663676416 | bytes 50331648 | tf_op jit(solution)/shard_map/pallas_call | solution.py:313
  571.9 23.6 %collective-permute-done.35 = bf16[2,256,1024]{2,1,0:T(8,128)(2,1)S(1)} collective-permute-done((bf16[2,256,1024]{2,1,0:T(8,128)(2,1)S(1)}, bf16[2,256,1024]{2,1,0:T(8,128)(2,1)S(1)}, u32[]{:S(2)}, u32[]{:S(2)}) %collective-permute-start.35) | collective-permute-done | bytes 1048608 | tf_op jit(solution)/shard_map/ppermute | solution.py:46
  598.1 11.4 %collective-permute-done.36 = bf16[256,1024]{1,0:T(8,128)(2,1)S(1)} collective-permute-done((bf16[256,1024]{1,0:T(8,128)(2,1)S(1)}, bf16[256,1024]{1,0:T(8,128)(2,1)S(1)}, u32[]{:S(2)}, u32[]{:S(2)}) %collective-permute-start.36) | collective-permute-done | bytes 524320 | tf_op jit(solution)/shard_map/ppermute | solution.py:46
  614.2 12.9 %collective-permute-done.47.rest_1_ = bf16[256,1024]{1,0:T(8,128)(2,1)} collective-permute-done((bf16[256,1024]{1,0:T(8,128)(2,1)S(1)}, bf16[256,1024]{1,0:T(8,128)(2,1)}, u32[]{:S(2)}, u32[]{:S(2)}) %collective-permute-start.47) | collective-permute-done | bytes 524320 | tf_op jit(solution)/shard_map/ppermute | solution.py:46
  635.8 20.4 %shard_map.207 = (f32[1024,768]{1,0:T(8,128)}, f32[2,256,1024]{2,1,0:T(8,128)}, bf16[2,256,1024]{2,1,0:T(8,128)(2,1)}) custom-call(s32[4]{0:T(128)} %pad_add_fusion.spots_ref, s32[8]{0:T(128)} %stack.216.block_spots_ref, bf16[256,1024]{1,0:T(8,128)(2,1)} %copy-done.39, bf16[256,1024]{1,0:T(8,128)(2,1)} %collective-permute-done.47.rest_1_, ...), custom_call_target="tpu_custom_call" | custom-call | flops 32212254720 | bytes 16777216 | tf_op jit(solution)/shard_map/pallas_call | solution.py:501
  657.1 22.1 %shard_map.208 = (f32[4,128,768]{2,1,0:T(8,128)}, bf16[4,128,768]{2,1,0:T(8,128)(2,1)}, f32[2,256,1024]{2,1,0:T(8,128)}, bf16[2,256,1024]{2,1,0:T(8,128)(2,1)}) custom-call(s32[4]{0:T(128)} %pad_add_fusion.spots_ref, s32[8]{0:T(128)} %stack.216.block_spots_ref, bf16[256,1024]{1,0:T(8,128)(2,1)} %copy-done.38, bf16[256,1024]{1,0:T(8,128)(2,1)} %copy-done.52, ...), custom_call_target="tpu_custom_call" | custom-call | flops 32212254720 | bytes 16777216 | tf_op jit(solution)/shard_map/pallas_call | solution.py:501
  680.4 18.9 %collective-permute-done.56 = bf16[4,128,768]{2,1,0:T(8,128)(2,1)S(1)} collective-permute-done((bf16[4,128,768]{2,1,0:T(8,128)(2,1)}, bf16[4,128,768]{2,1,0:T(8,128)(2,1)S(1)}, u32[]{:S(2)}, u32[]{:S(2)}) %collective-permute-start.56) | collective-permute-done | bytes 786464 | tf_op jit(solution)/shard_map/ppermute | solution.py:46
  773.8 33.5 %collective-permute-done.65 = f32[16,128]{1,0:T(8,128)S(1)} collective-permute-done((f32[16,128]{1,0:T(8,128)S(1)}, f32[16,128]{1,0:T(8,128)S(1)}, u32[]{:S(2)}, u32[]{:S(2)}) %collective-permute-start.65) | collective-permute-done | bytes 8224 | tf_op jit(solution)/shard_map/ppermute | solution.py:46
  (371 shorter events, 333.6 us)
Async XLA Ops:
  7.2 223.8 %all-gather.15.cloned.1.call-start = ((), (), s32[]{:S(2)}) async-start(), calls=%async_computation.11 | async-start | bytes 5898240 | tf_op jit(solution)/shard_map/all_gather | solution.py:556
  29.8 242.2 %all-gather.13.cloned.1.call-start = ((), (), s32[]{:S(2)}) async-start(), calls=%async_computation.10 | async-start | bytes 3932160 | tf_op jit(solution)/shard_map/all_gather | solution.py:556
  37.6 34.2 %collective-permute-start.16 = (bf16[256,1024]{1,0:T(8,128)(2,1)S(1)}, bf16[256,1024]{1,0:T(8,128)(2,1)}, u32[]{:S(2)}, u32[]{:S(2)}) collective-permute-start(bf16[256,1024]{1,0:T(8,128)(2,1)S(1)} %get-tuple-element.257.rest_0_.rest_4_), channel_id=1, source_target_pairs={{0,2},{2,0},{1,3},{3,1},{4,6},{6,4},{5,7},{7,5},{8,10},{10,8},{9,1... | collective-permute-start | bytes 1572872 | tf_op jit(solution)/shard_map/ppermute | solution.py:46
  45.8 34.0 %collective-permute-start.1 = (bf16[256,1024]{1,0:T(8,128)(2,1)}, bf16[256,1024]{1,0:T(8,128)(2,1)}, u32[]{:S(2)}, u32[]{:S(2)}) collective-permute-start(bf16[256,1024]{1,0:T(8,128)(2,1)} %get-tuple-element.256.rest_0_.rest_4_), channel_id=1, source_target_pairs={{0,1},{1,0},{2,3},{3,2},{4,5},{5,4},{6,7},{7,6},{8,9},{9,8},{10,11... | collective-permute-start | bytes 1572872 | tf_op jit(solution)/shard_map/ppermute | solution.py:46
  74.7 229.3 %all-gather.11.cloned.1.call-start = ((), (), s32[]{:S(2)}) async-start(), calls=%async_computation.9 | async-start | bytes 3932160 | tf_op jit(solution)/shard_map/all_gather | solution.py:556
  79.5 42.3 %collective-permute-start.17 = (bf16[2,256,1024]{2,1,0:T(8,128)(2,1)}, bf16[2,256,1024]{2,1,0:T(8,128)(2,1)}, u32[]{:S(2)}, u32[]{:S(2)}) collective-permute-start(bf16[2,256,1024]{2,1,0:T(8,128)(2,1)} %param.21), channel_id=1, source_target_pairs={{0,4},{4,0},{1,5},{5,1},{2,6},{6,2},{3,7},{7,3},{8,12},{12,8},{9,1... | collective-permute-start | bytes 3145736 | tf_op jit(solution)/shard_map/ppermute | solution.py:46
  121.8 47.3 %collective-permute-start.19 = (bf16[2,256,1024]{2,1,0:T(8,128)(2,1)}, bf16[2,256,1024]{2,1,0:T(8,128)(2,1)}, u32[]{:S(2)}, u32[]{:S(2)}) collective-permute-start(bf16[2,256,1024]{2,1,0:T(8,128)(2,1)} %collective-permute-done.17), channel_id=1, source_target_pairs={{0,2},{2,0},{1,3},{3,1},{4,6},{6,4},{5,7},{7,5},{8,10},{10,8},{9,1... | collective-permute-start | bytes 3145736 | tf_op jit(solution)/shard_map/ppermute | solution.py:46
  125.6 54.7 %collective-permute-start.29 = (bf16[256,1024]{1,0:T(8,128)(2,1)}, bf16[256,1024]{1,0:T(8,128)(2,1)S(1)}, u32[]{:S(2)}, u32[]{:S(2)}) collective-permute-start(bf16[256,1024]{1,0:T(8,128)(2,1)} %fusion.37), channel_id=1, source_target_pairs={{0,2},{2,0},{1,3},{3,1},{4,6},{6,4},{5,7},{7,5},{8,10},{10,8},{9,1... | collective-permute-start | bytes 1572872 | tf_op jit(solution)/shard_map/ppermute | solution.py:46
  129.6 60.3 %collective-permute-start.11 = (bf16[256,1024]{1,0:T(8,128)(2,1)}, bf16[256,1024]{1,0:T(8,128)(2,1)}, u32[]{:S(2)}, u32[]{:S(2)}) collective-permute-start(bf16[256,1024]{1,0:T(8,128)(2,1)} %fusion.36), channel_id=1, source_target_pairs={{0,2},{2,0},{1,3},{3,1},{4,6},{6,4},{5,7},{7,5},{8,10},{10,8},{9,1... | collective-permute-start | bytes 1572872 | tf_op jit(solution)/shard_map/ppermute | solution.py:46
  131.1 204.8 %all-gather.9.cloned.1.call-start = ((), (), s32[]{:S(2)}) async-start(), calls=%async_computation.8 | async-start | bytes 1966080 | tf_op jit(solution)/shard_map/all_gather | solution.py:556
  173.2 57.7 %collective-permute-start.20 = (bf16[4,2,256,1024]{3,2,1,0:T(8,128)(2,1)}, bf16[4,2,256,1024]{3,2,1,0:T(8,128)(2,1)}, u32[]{:S(2)}, u32[]{:S(2)}) collective-permute-start(bf16[4,2,256,1024]{3,2,1,0:T(8,128)(2,1)} %pad_maximum_fusion.ga_ref), channel_id=1, source_target_pairs={{0,1},{1,0},{2,3},{3,2},{4,5},{5,4},{6,7},{7,6},{8,9},{9,8},{10,11... | collective-permute-start | bytes 12582920 | tf_op jit(solution)/shard_map/ppermute | solution.py:46
  230.5 477.8 %reduce-scatter.11.cloned.1.call-start = ((), (), s32[]{:S(2)}) async-start(), calls=%async_computation.7 | async-start | bytes 1966080 | tf_op jit(solution)/shard_map/reduce_scatter | solution.py:603
  562.5 182.2 %reduce-scatter.9.cloned.1.call-start = ((), (), s32[]{:S(2)}) async-start(), calls=%async_computation.6 | async-start | bytes 3932160 | tf_op jit(solution)/shard_map/reduce_scatter | solution.py:603
  563.1 208.9 %reduce-scatter.7.cloned.1.call-start = ((), (), s32[]{:S(2)}) async-start(), calls=%async_computation.5 | async-start | bytes 3932160 | tf_op jit(solution)/shard_map/reduce_scatter | solution.py:603
  563.9 270.3 %reduce-scatter.5.cloned.1.call-start = ((), (), s32[]{:S(2)}) async-start(), calls=%async_computation.4 | async-start | bytes 5898240 | tf_op jit(solution)/shard_map/reduce_scatter | solution.py:603
  679.7 66.1 %collective-permute-start.38 = (bf16[4,256,1024]{2,1,0:T(8,128)(2,1)}, bf16[4,256,1024]{2,1,0:T(8,128)(2,1)}, u32[]{:S(2)}, u32[]{:S(2)}) collective-permute-start(bf16[4,256,1024]{2,1,0:T(8,128)(2,1)} %get-tuple-element.149), channel_id=1, source_target_pairs={{0,1},{1,0},{2,3},{3,2},{4,5},{5,4},{6,7},{7,6},{8,9},{9,8},{10,11... | collective-permute-start | bytes 6291464 | tf_op jit(solution)/shard_map/ppermute | solution.py:46
  679.9 39.7 %collective-permute-start.54 = (bf16[2,256,1024]{2,1,0:T(8,128)(2,1)}, bf16[2,256,1024]{2,1,0:T(8,128)(2,1)}, u32[]{:S(2)}, u32[]{:S(2)}) collective-permute-start(bf16[2,256,1024]{2,1,0:T(8,128)(2,1)} %get-tuple-element.163), channel_id=1, source_target_pairs={{0,1},{1,0},{2,3},{3,2},{4,5},{5,4},{6,7},{7,6},{8,9},{9,8},{10,11... | collective-permute-start | bytes 3145736 | tf_op jit(solution)/shard_map/ppermute | solution.py:46
  680.3 50.1 %collective-permute-start.50 = (bf16[2,256,1024]{2,1,0:T(8,128)(2,1)}, bf16[2,256,1024]{2,1,0:T(8,128)(2,1)}, u32[]{:S(2)}, u32[]{:S(2)}) collective-permute-start(bf16[2,256,1024]{2,1,0:T(8,128)(2,1)} %get-tuple-element.158), channel_id=1, source_target_pairs={{0,1},{1,0},{2,3},{3,2},{4,5},{5,4},{6,7},{7,6},{8,9},{9,8},{10,11... | collective-permute-start | bytes 3145736 | tf_op jit(solution)/shard_map/ppermute | solution.py:46
  709.9 150.1 %collective-permute-start.63 = (bf16[1,128,768]{2,1,0:T(8,128)(2,1)}, bf16[1,128,768]{2,1,0:T(8,128)(2,1)S(1)}, u32[]{:S(2)}, u32[]{:S(2)}) collective-permute-start(bf16[1,128,768]{2,1,0:T(8,128)(2,1)} %slice_bitcast_fusion.11), channel_id=1, source_target_pairs={{0,4},{4,0},{1,5},{5,1},{2,6},{6,2},{3,7},{7,3},{8,12},{12,8},{9,1... | collective-permute-start | bytes 589832 | tf_op jit(solution)/shard_map/ppermute | solution.py:46
  745.8 114.3 %collective-permute-start.62 = (bf16[2,128,768]{2,1,0:T(8,128)(2,1)S(1)}, bf16[2,128,768]{2,1,0:T(8,128)(2,1)S(1)}, u32[]{:S(2)}, u32[]{:S(2)}) collective-permute-start(bf16[2,128,768]{2,1,0:T(8,128)(2,1)S(1)} %slice_bitcast_fusion.7), channel_id=1, source_target_pairs={{0,4},{4,0},{1,5},{5,1},{2,6},{6,2},{3,7},{7,3},{8,12},{12,8},{9,1... | collective-permute-start | bytes 1179656 | tf_op jit(solution)/shard_map/ppermute | solution.py:46
  752.1 71.1 %collective-permute-start.39 = (bf16[2,256,1024]{2,1,0:T(8,128)(2,1)}, bf16[2,256,1024]{2,1,0:T(8,128)(2,1)}, u32[]{:S(2)}, u32[]{:S(2)}) collective-permute-start(bf16[2,256,1024]{2,1,0:T(8,128)(2,1)} %fusion.2), channel_id=1, source_target_pairs={{0,2},{2,0},{1,3},{3,1},{4,6},{6,4},{5,7},{7,5},{8,10},{10,8},{9,1... | collective-permute-start | bytes 3145736 | tf_op jit(solution)/shard_map/ppermute | solution.py:46
  770.0 59.3 %collective-permute-start.42 = (bf16[2,256,1024]{2,1,0:T(8,128)(2,1)}, bf16[2,256,1024]{2,1,0:T(8,128)(2,1)}, u32[]{:S(2)}, u32[]{:S(2)}) collective-permute-start(bf16[2,256,1024]{2,1,0:T(8,128)(2,1)} %fusion.1), channel_id=1, source_target_pairs={{0,2},{2,0},{1,3},{3,1},{4,6},{6,4},{5,7},{7,5},{8,10},{10,8},{9,1... | collective-permute-start | bytes 3145736 | tf_op jit(solution)/shard_map/ppermute | solution.py:46
  770.0 37.3 %collective-permute-start.65 = (f32[16,128]{1,0:T(8,128)S(1)}, f32[16,128]{1,0:T(8,128)S(1)}, u32[]{:S(2)}, u32[]{:S(2)}) collective-permute-start(f32[16,128]{1,0:T(8,128)S(1)} %add.433), channel_id=1, source_target_pairs={{0,2},{2,0},{1,3},{3,1},{4,6},{6,4},{5,7},{7,5},{8,10},{10,8},{9,1... | collective-permute-start | bytes 24584 | tf_op jit(solution)/shard_map/ppermute | solution.py:46
  822.6 37.5 %collective-permute-start.61 = (bf16[2,128,768]{2,1,0:T(8,128)(2,1)}, bf16[2,128,768]{2,1,0:T(8,128)(2,1)S(1)}, u32[]{:S(2)}, u32[]{:S(2)}) collective-permute-start(bf16[2,128,768]{2,1,0:T(8,128)(2,1)} %slice_bitcast_fusion.8), channel_id=1, source_target_pairs={{0,4},{4,0},{1,5},{5,1},{2,6},{6,2},{3,7},{7,3},{8,12},{12,8},{9,1... | collective-permute-start | bytes 1179656 | tf_op jit(solution)/shard_map/ppermute | solution.py:46
  (113 other events, 1796.4 us)
Sparse Core Ops, SparseCore 0:
  29.9 101.8 all-gather.14
  133.4 61.7 all-gather.12
  196.8 62.1 all-gather.10
  260.4 35.7 all-gather.8
  562.7 40.1 reduce-scatter.10
  605.0 59.2 reduce-scatter.8
  666.6 64.4 reduce-scatter.6
  733.4 86.7 reduce-scatter.4

commit v4 on v3

--- a/solution.py
+++ b/solution.py
@@ -10,7 +10,7 @@
 
 HD = 64
 E = 32
-CHUNKS = (3, 2, 2, 1)
+CHUNKS = (4, 4)
 
 EPSILON = 1e-06
 BF = jnp.bfloat16
@@ -50,65 +50,45 @@
     return lax.optimization_barrier((value, *earlier))[0]
 
 
-def gather_rows(rows):
-    across = swap(rows, "x")
-    return [rows, across, swap(rows, "c"), swap(across, "c")]
-
-
-def gather_pair(rows):
-    near = swap(rows, "y")
-    blocks = jnp.stack([rows, near, swap(rows, "x"), swap(near, "x")])
-    return blocks, swap(blocks, "c")
-
-
-def scatter_rows(kept, sent):
-    got = swap(sent, "c").astype(FP)
-    across = swap((kept[1] + got[1]).astype(BF), "x").astype(FP)
-    return kept[0] + got[0] + across
+def together(*values):
+    return lax.optimization_barrier(values)
+
+
+def cross(value):
+    return lax.ppermute(value, ("y", "x"), [(i, 3 - i) for i in range(4)])
+
+
+def plus(left, right):
+    return left + right.astype(FP)
 
 
 def scatter_pair(kept, sent):
-    got = swap(sent, "c").astype(FP)
-    across = swap((kept[2:] + got[2:]).astype(BF), "x").astype(FP)
-    near = swap((kept[1] + got[1] + across[1]).astype(BF), "y").astype(FP)
-    return kept[0] + got[0] + across[0] + near
-
-
-def turns(depth):
-    up = [(i, (i + 1) % depth) for i in range(depth)]
-    down = [(i, (i - 1) % depth) for i in range(depth)]
-    return up, down
-
-
-def gather_dp(shard, depth):
-    turn_up, turn_down = turns(depth)
-    place, side = lax.axis_index("z"), lax.axis_index("y")
-    line = [(shard, place)]
-    piece = shard
-    for k in range(1, depth // 2 + 1):
-        piece = lax.ppermute(piece, "z", turn_up)
-        line.append((piece, lax.rem(place + depth - k, depth)))
-    piece = shard
-    for k in range(1, (depth - 1) // 2 + 1):
-        piece = lax.ppermute(piece, "z", turn_down)
-        line.append((piece, lax.rem(place + k, depth)))
-    pieces = [p for p, _ in line] + [swap(p, "y") for p, _ in line]
-    index = [2 * z + side for _, z in line] + [2 * z + 1 - side for _, z in line]
-    return pieces, jnp.stack(index).astype(jnp.int32)
+    got = swap(sent, "c")
+    sent = [plus(kept[i], got[i]).astype(BF) for i in (1, 2, 3)]
+    return plus(kept[0], got[0]), sent, [swap(sent[0], "y"), swap(sent[1], "x"), cross(sent[2])]
+
+
+def sum_of(total, parts):
+    for part in parts:
+        total = plus(total, part)
+    return total
+
+
+def along_z(shard, depth):
+    place = lax.axis_index("z")
+    turns_taken = [k for k in range(-((depth - 1) // 2), depth // 2 + 1) if k]
+    pieces = [shard]
+    for k in turns_taken:
+        pieces.append(lax.ppermute(shard, "z", [(i, (i + k) % depth) for i in range(depth)]))
+    return pieces, [lax.rem(place + depth - k, depth) for k in [0, *turns_taken]]
 
 
 def scatter_dp(kept, sent, depth):
     column = kept + swap(sent, "y").astype(FP)
-    turn_up, turn_down = turns(depth)
     total = column[0]
-    for turn, sign, steps in ((turn_up, 1, depth // 2), (turn_down, -1, (depth - 1) // 2)):
-        carried = None
-        for distance in range(steps, 0, -1):
-            block = column[(sign * distance) % depth]
-            carried = block if carried is None else block + carried
-            carried = lax.ppermute(carried.astype(BF), "z", turn).astype(FP)
-        if carried is not None:
-            total = total + carried
+    for r in range(1, depth):
+        turn = [(i, (i + r) % depth) for i in range(depth)]
+        total = plus(total, lax.ppermute(column[r].astype(BF), "z", turn))
     return total
 
 
@@ -123,6 +103,11 @@
     return value
 
 
+def cost(flops):
+    return pl.CostEstimate(flops=flops, bytes_accessed=1 << 20, transcendentals=0)
+
+
+SMALL = cost(1 << 30)
 SMEM = pl.BlockSpec(memory_space=pltpu.SMEM)
 VMEM = pl.BlockSpec(memory_space=pltpu.VMEM)
 
@@ -157,7 +142,7 @@
         out_shape=[shape for shape in shapes for _ in range(2)],
         scratch_shapes=[pltpu.VMEM((2 * blk, hidden_local), FP)],
         compiler_params=pltpu.CompilerParams(vmem_limit_bytes=32 << 20),
-        cost_estimate=pl.CostEstimate(flops=1 << 20, bytes_accessed=8 << 20, transcendentals=0),
+        cost_estimate=SMALL,
     )(side, w_gate_up.reshape(experts, 2 * blk, hidden_local), w_down)
     return list(zip(outs[::2], outs[1::2]))
 
@@ -194,7 +179,7 @@
             jax.ShapeDtypeStruct((E, hidden_local, blk), FP),
         ],
         compiler_params=pltpu.CompilerParams(vmem_limit_bytes=32 << 20),
-        cost_estimate=pl.CostEstimate(flops=1 << 20, bytes_accessed=12 << 20, transcendentals=0),
+        cost_estimate=SMALL,
     )(side, *operands)
     return gate_up.reshape(E, blk, 2, hidden_local), down
 
@@ -214,7 +199,7 @@
         in_specs=[VMEM] * 4,
         out_specs=VMEM,
         out_shape=jax.ShapeDtypeStruct((w_query.shape[0], width), BF),
-        cost_estimate=pl.CostEstimate(flops=1 << 20, bytes_accessed=1 << 20, transcendentals=0),
+        cost_estimate=SMALL,
     )(w_query, w_key, w_value, w_out)
 
 
@@ -246,6 +231,7 @@
 
     x = jnp.concatenate([xa_ref[...], xb_ref[...]], axis=0)
     g = jnp.concatenate([ga_ref[...], gb_ref[...]], axis=0)
+    gates = gate_ref[...].reshape(x.shape[0], gate_ref.shape[-1])
     totals = [None, None]
     for p in range(pairs):
         weights = w_ref[:, p].reshape(model_width, width)
@@ -256,7 +242,7 @@
         sig = 0.5 + 0.5 * jnp.tanh(0.5 * gate)
         share = jnp.concatenate(
             [
-                jnp.broadcast_to(gate_ref[:, i : i + 1], (x.shape[0], hidden_local))
+                jnp.broadcast_to(gates[:, i : i + 1], (x.shape[0], hidden_local))
                 for i in (column + 2 * p, column + 2 * p + 1)
             ],
             axis=1,
@@ -275,7 +261,7 @@
         acc[p, :, : 2 * half] += dot_tn(x, pair_grad)
         acc[p, :, 2 * half :] += dot_tn(g, hidden)
     if not first:
-        totals = [s[...] + t for s, t in zip(sums_in, totals)]
+        totals = [s[...].reshape(t.shape) + t for s, t in zip(sums_in, totals)]
     if last:
         rows = xa_ref.shape[0]
         for kept_ref, sent_ref, total in zip(sums_out[::2], sums_out[1::2], totals):
@@ -283,7 +269,7 @@
             sent_ref[...] = total[rows:].astype(BF)
     else:
         for out_ref, total in zip(sums_out, totals):
-            out_ref[...] = total
+            out_ref[...] = total.reshape(out_ref.shape)
 
     @pl.when(step == pl.num_programs(0) - 1)
     def _():
@@ -292,28 +278,33 @@
                 grads_ref[block, p] = acc[p, spot(block), :].astype(BF)
 
 
-def moe_chunk(side, x, g, gates, weights, sums, earlier, micro, column, last):
-    count, rows, model_width = x[0].shape
+def moe_chunk(side, rows_in, gates, weights, sums, earlier, micro, column, last):
+    count, rows, model_width = rows_in[0].shape
+    count //= 2
     blocks, pairs, blk, width = weights.shape
     once = pl.Buffered(1)
-    row = pl.BlockSpec((None, 2 * rows, model_width), lambda i: (i, 0, 0))
-    half = pl.BlockSpec((None, rows, model_width), lambda i: (i, 0, 0))
-    g_spec = pl.BlockSpec((None, None, rows, model_width), lambda i: (i, micro, 0, 0))
-    gate_spec = pl.BlockSpec((None, None, 2 * rows, gates.shape[-1]), lambda i: (micro, i, 0, 0))
+    tile = min(128, rows)
+    parts = rows // tile
+    row = pl.BlockSpec((None, 2, tile, model_width), lambda i: (i // parts, 0, i % parts, 0))
+    half = pl.BlockSpec((None, tile, model_width), lambda i: (i // parts, i % parts, 0))
+    g_half = pl.BlockSpec((None, tile, model_width), lambda i: (count + i // parts, i % parts, 0))
+    gate_spec = pl.BlockSpec(
+        (None, None, 2, tile, gates.shape[-1]), lambda i: (micro, i // parts, 0, i % parts, 0)
+    )
     whole = pl.BlockSpec(weights.shape, lambda i: (0, 0, 0, 0), pipeline_mode=once)
     first, start = sums is None, earlier is None
-    operands = [side, *x, *g, gates, weights] + ([] if first else list(sums))
+    operands = [side, *rows_in, *rows_in, gates, weights] + ([] if first else list(sums))
     operands += [] if start else [earlier]
     if last:
         out_specs = [half] * 4
         outs = [jax.ShapeDtypeStruct((count, rows, model_width), t) for t in (FP, BF, FP, BF)]
     else:
         out_specs = [row] * 2
-        outs = [jax.ShapeDtypeStruct((count, 2 * rows, model_width), FP)] * 2
+        outs = [jax.ShapeDtypeStruct((count, 2, rows, model_width), FP)] * 2
     *sums, grads = pl.pallas_call(
         functools.partial(moe_kernel, first, last, start, column),
-        grid=(count,),
-        in_specs=[SMEM, half, half, g_spec, g_spec, gate_spec, whole]
+        grid=(count * parts,),
+        in_specs=[SMEM, half, half, g_half, g_half, gate_spec, whole]
         + ([] if first else [row, row])
         + ([] if start else [whole]),
         out_specs=out_specs + [whole],
@@ -321,11 +312,7 @@
         out_shape=outs + [jax.ShapeDtypeStruct(weights.shape, BF)],
         input_output_aliases={} if first or last else {7: 0, 8: 1},
         compiler_params=pltpu.CompilerParams(vmem_limit_bytes=60 << 20),
-        cost_estimate=pl.CostEstimate(
-            flops=12 * count * rows * model_width * pairs * width,
-            bytes_accessed=48 << 20,
-            transcendentals=2 * count * rows * pairs * width // 3,
-        ),
+        cost_estimate=cost(6 << 30),
     )(*operands)
     return sums, grads
 
@@ -469,9 +456,7 @@
         out_shape=outs,
         scratch_shapes=[pltpu.VMEM((4 * rows, model_width), BF)],
         compiler_params=pltpu.CompilerParams(vmem_limit_bytes=56 << 20),
-        cost_estimate=pl.CostEstimate(
-            flops=14 << 30, bytes_accessed=10 << 20, transcendentals=3 << 20
-        ),
+        cost_estimate=cost(14 << 30),
     )(spots, weight_spots, *pieces, *weights)
     return results if not whole else [*results, weights[0]]
 
@@ -505,9 +490,7 @@
         out_shape=outs,
         scratch_shapes=scratch,
         compiler_params=pltpu.CompilerParams(vmem_limit_bytes=58 << 20),
-        cost_estimate=pl.CostEstimate(
-            flops=30 << 30, bytes_accessed=16 << 20, transcendentals=3 << 20
-        ),
+        cost_estimate=cost(24 << 30),
     )(spots, block_spots, *operands)
 
 
@@ -539,85 +522,166 @@
         [2 * lax.rem(place + r, depth) + s for s in (side, 1 - side) for r in range(depth)]
     ).astype(jnp.int32)
 
+    packed_attn = pack_attn(w_query, w_key, w_value, w_out)
+    packed = pack_experts(after(side_at, packed_attn), w_gate_up, w_down)
     in_rows = block_input.astype(FP)
     normed_attn, scale_attn = row_norm(in_rows, norm_attn)
-    normed_attn = normed_attn.astype(BF)
-    attn_in = [gather_rows(normed_attn[m]) for m in range(micro_count)]
-    attn_pieces, weight_spots = gather_dp(pack_attn(w_query, w_key, w_value, w_out), depth)
-
-    packed = pack_experts(side_at, w_gate_up, w_down)
-    chunk_weights = []
-    for mine, theirs in packed:
-        got = swap(theirs, "y")
-        if chunk_weights:
-            got = after(got, chunk_weights[-1][:1, :1, :8, :128])
+    normed = [normed_attn[m].astype(BF) for m in range(micro_count)]
+    cots = [cotangent[m] for m in range(micro_count)]
+
+    def shard_of(chunk, got):
+        mine = packed[chunk][0]
         first = side == 0
-        shard = jnp.stack([jnp.where(first, mine, got), jnp.where(first, got, mine)])
+        return jnp.stack([jnp.where(first, mine, got), jnp.where(first, got, mine)])
+
+    def whole_of(shard):
         whole = lax.all_gather(shard, "z", axis=0)
-        chunk_weights.append(whole.reshape(-1, *whole.shape[2:]))
-
+        return whole.reshape(-1, *whole.shape[2:])
+
+    column, places = along_z(packed_attn, depth)
+    weight_spots = jnp.stack([2 * z + s for s in (side, 1 - side) for z in places])
+    weight_spots = weight_spots.astype(jnp.int32)
+    across = swap(normed[0], "x")
+    got = swap(packed[0][1], "y")
+    own_across = swap(packed_attn, "y")
+    *column, across, next_normed = together(*column, across, normed[1])
+
+    weights = column + [own_across] + [swap(piece, "y") for piece in column[1:]]
+    near_rows, far_rows = swap(normed[0], "c"), swap(across, "c")
+    next_across = swap(next_normed, "x")
+    *weights, near_rows, far_rows, got, cot, next_across = together(
+        *weights, near_rows, far_rows, got, cots[0], next_across
+    )
+    attn_in = [[normed[0], across, near_rows, far_rows]]
+    shards = [shard_of(0, got)]
+    chunk_weights = [whole_of(shards[0])]
+
+    cot_near, cot_across = swap(cot, "y"), swap(cot, "x")
+    turn = after(spots, shards[0])
+    qkv, heads, kept, sent, whole = attn_forward(turn, weight_spots, attn_in[0], weights, widths)
+    weights = [whole]
+    saved = [(qkv, heads)]
+    sent, cot_near, cot_across, across = together(sent, cot_near, cot_across, next_across)
+
+    got = swap(sent, "c")
+    near_rows, far_rows = swap(normed[1], "c"), swap(across, "c")
+    along = plus(kept[1], got[1]).astype(BF)
+    own = plus(kept[0], got[0])
+    along, near_rows, far_rows, theirs, turn = together(
+        along, near_rows, far_rows, packed[1][1], spots
+    )
+    attn_in.append([normed[1], across, near_rows, far_rows])
+
+    came = swap(along, "x")
+    theirs = swap(theirs, "y")
+    qkv, heads, kept, sent, _ = attn_forward(turn, weight_spots, attn_in[1], weights, widths)
+    saved.append((qkv, heads))
+    sent, came = together(sent, came)
+
+    def moe_rows(middle):
+        normed, scale = row_norm(middle, norm_moe)
+        return normed.astype(BF), scale
+
+    got = swap(sent, "c")
+    middle = [in_rows[0] + plus(own, came)]
+    low, scale = moe_rows(middle[0])
+    normed, scale_moe = [low], [scale]
+    along = plus(kept[1], got[1]).astype(BF)
+    own = plus(kept[0], got[0])
+    along, low, cot = together(along, low, cots[0])
+
+    came = swap(along, "x")
+    near, across = swap(low, "y"), swap(low, "x")
     expert_ids = jnp.arange(E, dtype=jnp.int32)[:, None, None, None]
     gates = jnp.sum(jnp.where(routes == expert_ids, gate_weights, 0.0), axis=3)
     gates = gates.reshape(2, E // 2, micro_count, 2, 2, rows_local)
     gates = jnp.where(chip == 0, gates, gates[:, :, :, ::-1])
     gates = jnp.where(core == 0, gates, gates[:, :, :, :, ::-1])
     mine = lax.dynamic_index_in_dim(gates, side, 0, False)
-    theirs = lax.dynamic_index_in_dim(gates, 1 - side, 0, False)
-    gates = jnp.stack([mine, swap(theirs.reshape(E // 2, -1), "y").reshape(mine.shape)])
-    gates = gates.transpose(2, 3, 0, 4, 5, 1).reshape(micro_count, 4, 2 * rows_local, E // 2)
-
-    moe_grad = gather_pair(after(cotangent, attn_in[-1][1]))
-    saved, middle, scale_moe, moe_in = [], [], [], []
-    weights = attn_pieces
-    for m in range(micro_count):
-        qkv, heads, kept, sent, whole = attn_forward(
-            spots, weight_spots, attn_in[m], weights, widths
-        )
-        weights = [whole]
-        saved.append((qkv, heads))
-        middle.append(in_rows[m] + scatter_rows(kept, sent))
-        normed_moe, scale = row_norm(middle[m], norm_moe)
-        scale_moe.append(scale)
-        moe_in.append(gather_pair(normed_moe.astype(BF)))
+    other = lax.dynamic_index_in_dim(gates, 1 - side, 0, False)
+    gates = jnp.stack([mine, swap(other.reshape(E // 2, -1), "y").reshape(mine.shape)])
+    gates = gates.transpose(2, 3, 0, 4, 5, 1).reshape(micro_count, 4, 2, rows_local, E // 2)
+    came, near, across, gates, theirs, low, cot = together(
+        came, near, across, gates, theirs, low, cot
+    )
+
+    diagonal, cot_diagonal = cross(low), cross(cot)
+    shards.append(shard_of(1, theirs))
+    chunk_weights.append(whole_of(shards[1]))
+    middle.append(in_rows[1] + plus(own, came))
+    low, scale = moe_rows(middle[1])
+    normed.append(low)
+    scale_moe.append(scale)
+    diagonal, cot_diagonal, low, cot = together(diagonal, cot_diagonal, low, cots[1])
+    blocks = jnp.stack(
+        [normed[0], near, across, diagonal, cots[0], cot_near, cot_across, cot_diagonal]
+    )
+    experts_in = [(blocks, swap(blocks, "c"))]
+    neighbours = [f(v) for v in (low, cot) for f in (lambda r: swap(r, "y"), lambda r: swap(r, "x"), cross)]
 
     sums = [None] * micro_count
-    shards = []
-    column = 0
+    turn = after(side_at, shards[1])
+    all_grads = []
+    back = []
+    first_expert = 0
     for chunk, pairs in enumerate(CHUNKS):
+        last = chunk == len(CHUNKS) - 1
         grads = None
         for m in range(micro_count):
             sums[m], grads = moe_chunk(
-                side_at,
-                moe_in[m],
-                moe_grad,
+                turn,
+                experts_in[m],
                 gates,
                 chunk_weights[chunk],
                 sums[m],
                 grads,
                 m,
-                column,
-                chunk == len(CHUNKS) - 1,
+                first_expert,
+                last,
             )
-        column += 2 * pairs
-        grads = grads.reshape(depth, 2, *grads.shape[1:])
-        grads = lax.psum_scatter(grads, "z", scatter_dimension=0, tiled=False)
-        shards.append((grads, swap(grads[1], "y")))
-    shard_pair, shard_down = unpack_experts(side_at, shards)
+            waited = [grads]
+            if m == 0 and chunk == 0:
+                *neighbours, _ = together(*neighbours, grads)
+                blocks = jnp.stack([low, *neighbours[:3], cot, *neighbours[3:]])
+                experts_in.append((blocks, swap(blocks, "c")))
+            if m == 0 and last:
+                back.append(scatter_pair(*sums[m][2:]))
+                waited += back[0][1]
+            turn = after(side_at, *waited)
+        first_expert += 2 * pairs
+        all_grads.append(grads.reshape(depth, 2, *grads.shape[1:]))
+
+    def reduce_grads(grads):
+        return lax.psum_scatter(grads, "z", scatter_dimension=0, tiled=False)
+
+    grad_shards = [reduce_grads(all_grads[0])]
 
     out_grad = cotangent.astype(FP)
-    outputs, input_grads = [], []
-    gains = jnp.zeros((2, model_width), FP)
-    middle_grad, branch_grad = [], []
+    input_grads = []
+    gains = [0.0, 0.0]
+    middle_grad, branch_grad, outputs = [], [], []
+    results = None
+    turn = spots
+    ends = grads
     for m in range(micro_count):
-        moe_in_grad = scatter_pair(*sums[m][2:])
+        if m:
+            kept, sent = sums[m][2:]
+            back.append(scatter_pair(kept, after(sent, middle_low)))
+            ends = results[0]
+        own, _, came = back[m]
+        *came, _ = together(*came, ends)
+        moe_in_grad = sum_of(own, came)
         middle_back, gain_moe = norm_back(middle[m], scale_moe[m], norm_moe, moe_in_grad)
         middle_grad.append(out_grad[m] + middle_back)
-        branch_grad.append(gather_rows(middle_grad[m].astype(BF)))
-        gains = gains.at[1].add(gain_moe)
-    results = None
-    for m in range(micro_count):
+        middle_low = middle_grad[m].astype(BF)
+        if m == 0:
+            grads, _ = together(all_grads[1], grad_shards[0])
+            grad_shards.append(reduce_grads(grads))
+        across = swap(middle_low, "x")
+        branch_grad.append([middle_low, across, swap(middle_low, "c"), swap(across, "c")])
+        gains[1] = gains[1] + gain_moe
         results = attn_backward(
-            spots,
+            turn,
             block_spots,
             branch_grad[m],
             attn_in[m],
@@ -626,16 +690,21 @@
             None if results is None else results[0],
             widths,
         )
-        attn_in_grad = scatter_rows(*results[-2:])
+        kept, sent = results[-2:]
+        got = swap(sent, "c")
+        along = plus(kept[1], got[1]).astype(BF)
+        attn_in_grad = sum_of(plus(kept[0], got[0]), [swap(along, "x")])
+        turn = after(spots, along)
         in_back, gain_attn = norm_back(in_rows[m], scale_attn[m], norm_attn, attn_in_grad)
         input_grads.append(middle_grad[m] + in_back)
-        gains = gains.at[0].add(gain_attn)
+        gains[0] = gains[0] + gain_attn
     for m in range(micro_count):
         kept, sent = sums[m][:2]
-        sent = after(sent, branch_grad[-1][1])
-        outputs.append((middle[m] + scatter_pair(kept, sent)).astype(BF))
+        own, _, came = scatter_pair(kept, after(sent, along if m else branch_grad[-1][1]))
+        outputs.append((middle[m] + sum_of(own, came)).astype(BF))
+    shard_pair, shard_down = unpack_experts(side_at, [(g, swap(g[1], "y")) for g in grad_shards])
     attn_shard = scatter_dp(results[0], results[1], depth)
-    gains = sum_all(gains.reshape(16, -1), depth).reshape(2, model_width)
+    gains = sum_all(jnp.concatenate(gains).reshape(16, -1), depth).reshape(2, model_width)
     return (
         jnp.stack(outputs),
         jnp.stack(input_grads),

time: 880 us -> 696 us (0.79)
  waiting for transfers between devices: 360 us -> 207 us
  Pallas kernels: 325 us -> 297 us
  other arithmetic: 76.4 us -> 57.5 us
  local copies, waits for them, and re-layouts: 29.7 us -> 41.4 us
    ppermute x61 -> x55, waiting for transfers between devices: 320 us -> 157 us  [swap(): return lax.ppermute(value, axis, [(0, 1), (1, 0)])]
    pallas_call x8 -> x4, Pallas kernels: 253 us -> 224 us  [moe_chunk(): pl.pallas_call(functools.partial(moe_kernel, first, last, start, column),...]
    ppermute x6 -> x14, waiting for transfers between devices: 31.8 us -> 48.8 us  [the longest x3 21.4 us: scatter_dp(): total = plus(total, lax.ppermute(column[r].astype(BF), 'z', turn))]
    convert_element_type x28 -> x11, other arithmetic: 38 us -> 23.2 us  [the longest x4 14.9 us: scatter_pair(): sent = [plus(kept[i], got[i]).astype(BF) for i in (1, 2, 3)]]
    unnamed x121 -> x108, local copies, waits for them, and re-layouts: 16.6 us -> 26.8 us
    ppermute x2, starting transfers between devices: 0.01 us -> 8.85 us  [sum_all(): value = value + lax.ppermute(value, 'z', pairs)]
    ppermute x6 -> x14, starting transfers between devices: 23.7 us -> 19.2 us  [the longest x8 9.84 us: cross(): return lax.ppermute(value, ('y', 'x'), [(i, 3 - i) for i in range(4)])]
    ppermute x61 -> x55, starting transfers between devices: 44.5 us -> 44.7 us  [swap(): return lax.ppermute(value, axis, [(0, 1), (1, 0)])]
  transfers between devices with their start and end apart: 77 -> 75, of which waited for: 39 -> 28; matrix products, arithmetic and copies ran while one was open for 10% -> 13% of each run, Pallas kernels for 20% -> 43%
where the time goes in v4:
time: 696 us; the launch traced here: 692 us
  Pallas kernels  297 us (43%)
  waiting for transfers between devices  207 us (30%)
  starting transfers between devices  73.4 us (11%)
  other arithmetic  57.5 us (8%)
  local copies, waits for them, and re-layouts  41.4 us (6%)
  between operations  14.8 us (2%)
    pallas_call x4, Pallas kernels, moe_chunk(): pl.pallas_call(functools.partial(moe_kernel, first, last, start, column),...  224 us
    ppermute x55, waiting for transfers between devices, swap(): return lax.ppermute(value, axis, [(0, 1), (1, 0)])  157 us
    ppermute x55, starting transfers between devices, swap(): return lax.ppermute(value, axis, [(0, 1), (1, 0)])  44.7 us
    pallas_call x2, Pallas kernels, attn_backward(): pl.pallas_call(functools.partial(attn_backward_kernel, widths, first), in...  42.9 us
    unnamed x108, local copies, waits for them, and re-layouts  26.8 us
    pallas_call x2, Pallas kernels, attn_forward(): pl.pallas_call(functools.partial(attn_forward_kernel, widths, len(weights...  23.5 us
    ppermute x3, waiting for transfers between devices, scatter_dp(): total = plus(total, lax.ppermute(column[r].astype(BF), 'z', turn))  21.4 us
    ppermute x8, waiting for transfers between devices, cross(): return lax.ppermute(value, ('y', 'x'), [(i, 3 - i) for i in range(4)])  17.2 us
  transfers between devices with their start and end apart: 75, of which 28 were waited for; matrix products, arithmetic and copies ran while one was open for 13% of the time, Pallas kernels for 43%

profile of v4, /device:TPU:0, one launch (start us, length us, event | category | flops | bytes accessed | tf_op | source)
XLA Modules:
  0.0 691.6 jit_solution(9469815374163751712)
XLA Ops:
  31.0 6.2 collective-permute-done.2.rest_7_
  37.9 9.4 %collective-permute-done.4.rest_8_ = bf16[128,768]{1,0:T(8,128)(2,1)S(1)} collective-permute-done((bf16[128,768]{1,0:T(8,128)(2,1)S(1)}, bf16[128,768]{1,0:T(8,128)(2,1)S(1)}, u32[]{:S(2)}, u32[]{:S(2)}) %collective-permute-start.4) | collective-permute-done | bytes 196640 | tf_op jit(solution)/shard_map/ppermute | solution.py:46
  66.4 12.1 %shard_map.197 = (bf16[1024,512]{1,0:T(8,128)(2,1)}, bf16[1024,256]{1,0:T(8,128)(2,1)}, f32[2,256,1024]{2,1,0:T(8,128)}, bf16[2,256,1024]{2,1,0:T(8,128)(2,1)}, bf16[1024,768]{1,0:T(8,128)(2,1)}) custom-call(s32[4]{0:T(128)} %pad_add_fusion.spots_ref, s32[8]{0:T(128)} %stack.168.weight_spots_ref, bf16[256,1024]{1,0:T(8,128)(2,1)} %get-tuple-element.315.rest_0_.rest_4_, ...), custom_call_target="tpu_custom_call" | custom-call | flops 15032385536 | bytes 1048576 | tf_op jit(solution)/shard_map/pallas_call | solution.py:452
  85.2 11.5 %shard_map.198 = (bf16[1024,512]{1,0:T(8,128)(2,1)}, bf16[1024,256]{1,0:T(8,128)(2,1)}, f32[2,256,1024]{2,1,0:T(8,128)}, bf16[2,256,1024]{2,1,0:T(8,128)(2,1)}) custom-call(s32[4]{0:T(128)} %pad_add_fusion.spots_ref, s32[8]{0:T(128)} %stack.168.weight_spots_ref, bf16[256,1024]{1,0:T(8,128)(2,1)} %get-tuple-element.123.rest_0_.rest_4_, ...), custom_call_target="tpu_custom_call" | custom-call | flops 15032385536 | bytes 1048576 | tf_op jit(solution)/shard_map/pallas_call | solution.py:452
  110.6 22.1 %collective-permute-done.22 = f32[16,2048]{1,0:T(8,128)S(1)} collective-permute-done((f32[16,2048]{1,0:T(8,128)S(1)}, f32[16,2048]{1,0:T(8,128)S(1)}, u32[]{:S(2)}, u32[]{:S(2)}) %collective-permute-start.22) | collective-permute-done | bytes 131104 | tf_op jit(solution)/shard_map/ppermute | solution.py:46
  150.9 9.1 %collective-permute-done.25 = bf16[256,1024]{1,0:T(8,128)(2,1)S(1)} collective-permute-done((bf16[256,1024]{1,0:T(8,128)(2,1)}, bf16[256,1024]{1,0:T(8,128)(2,1)S(1)}, u32[]{:S(2)}, u32[]{:S(2)}) %collective-permute-start.25) | collective-permute-done | bytes 524320 | tf_op jit(solution)/shard_map/ppermute | solution.py:58
  175.2 9.1 %collective-permute-done.27 = bf16[256,1024]{1,0:T(8,128)(2,1)S(1)} collective-permute-done((bf16[256,1024]{1,0:T(8,128)(2,1)}, bf16[256,1024]{1,0:T(8,128)(2,1)S(1)}, u32[]{:S(2)}, u32[]{:S(2)}) %collective-permute-start.27) | collective-permute-done | bytes 524320 | tf_op jit(solution)/shard_map/ppermute | solution.py:46
  186.5 54.9 %shard_map.199 = (f32[4,2,256,1024]{3,2,1,0:T(8,128)}, f32[4,2,256,1024]{3,2,1,0:T(8,128)}, bf16[8,4,128,768]{3,2,1,0:T(8,128)(2,1)}) custom-call(s32[1]{0:T(128)} %bitcast.5.side_ref, bf16[8,256,1024]{2,1,0:T(8,128)(2,1)} %bitcast_dynamic-update-slice_fusion.8.xa_ref.ga_ref, bf16[8,256,1024]{2,1,0:T(8,128)(2,1)} %collective-permute-done.26.xb_ref.gb_ref, ...), custom_call_target="tpu_custom_call" | custom-call | flops 6442450944 | bytes 1048576 | tf_op jit(solution)/shard_map/pallas_call | solution.py:304
  252.5 7.5 %collective-permute-done.33.xb_ref.gb_ref = bf16[8,256,1024]{2,1,0:T(8,128)(2,1)} collective-permute-done((bf16[8,256,1024]{2,1,0:T(8,128)(2,1)}, bf16[8,256,1024]{2,1,0:T(8,128)(2,1)}, u32[]{:S(2)}, u32[]{:S(2)}) %collective-permute-start.33) | collective-permute-done | bytes 4194336 | tf_op jit(solution)/shard_map/ppermute | solution.py:46
  260.0 56.8 %shard_map.200 = (f32[4,2,256,1024]{3,2,1,0:T(8,128)}, f32[4,2,256,1024]{3,2,1,0:T(8,128)}, bf16[8,4,128,768]{3,2,1,0:T(8,128)(2,1)}) custom-call(s32[1]{0:T(128)} %bitcast.5.side_ref, bf16[8,256,1024]{2,1,0:T(8,128)(2,1)} %bitcast_dynamic-update-slice_fusion.xa_ref.ga_ref, bf16[8,256,1024]{2,1,0:T(8,128)(2,1)} %collective-permute-done.33.xb_ref.gb_ref, ...), custom_call_target="tpu_custom_call" | custom-call | flops 6442450944 | bytes 1048576 | tf_op jit(solution)/shard_map/pallas_call | solution.py:304
  316.9 55.3 %shard_map.201 = (f32[4,256,1024]{2,1,0:T(8,128)}, bf16[4,256,1024]{2,1,0:T(8,128)(2,1)}, f32[4,256,1024]{2,1,0:T(8,128)}, bf16[4,256,1024]{2,1,0:T(8,128)(2,1)}, bf16[8,4,128,768]{3,2,1,0:T(8,128)(2,1)}) custom-call(s32[1]{0:T(128)} %bitcast.5.side_ref, bf16[8,256,1024]{2,1,0:T(8,128)(2,1)} %bitcast_dynamic-update-slice_fusion.8.xa_ref.ga_ref, ...), custom_call_target="tpu_custom_call" | custom-call | flops 6442450944 | bytes 1048576 | tf_op jit(solution)/shard_map/pallas_call | solution.py:304
  384.3 57.5 %shard_map.202 = (f32[4,256,1024]{2,1,0:T(8,128)}, bf16[4,256,1024]{2,1,0:T(8,128)(2,1)}, f32[4,256,1024]{2,1,0:T(8,128)}, bf16[4,256,1024]{2,1,0:T(8,128)(2,1)}, bf16[8,4,128,768]{3,2,1,0:T(8,128)(2,1)}) custom-call(s32[1]{0:T(128)} %bitcast.5.side_ref, bf16[8,256,1024]{2,1,0:T(8,128)(2,1)} %bitcast_dynamic-update-slice_fusion.xa_ref.ga_ref, ...), custom_call_target="tpu_custom_call" | custom-call | flops 6442450944 | bytes 1048576 | tf_op jit(solution)/shard_map/pallas_call | solution.py:304
  446.7 13.2 %collective-permute-done.42.rest_1_ = bf16[256,1024]{1,0:T(8,128)(2,1)} collective-permute-done((bf16[256,1024]{1,0:T(8,128)(2,1)S(1)}, bf16[256,1024]{1,0:T(8,128)(2,1)}, u32[]{:S(2)}, u32[]{:S(2)}) %collective-permute-start.42) | collective-permute-done | bytes 524320 | tf_op jit(solution)/shard_map/ppermute | solution.py:46
  467.8 20.9 %shard_map.203 = (f32[1024,768]{1,0:T(8,128)}, f32[2,256,1024]{2,1,0:T(8,128)}, bf16[2,256,1024]{2,1,0:T(8,128)(2,1)}) custom-call(s32[4]{0:T(128)} %pad_add_fusion.spots_ref, s32[8]{0:T(128)} %stack.194.block_spots_ref, bf16[256,1024]{1,0:T(8,128)(2,1)} %copy-done.27, bf16[256,1024]{1,0:T(8,128)(2,1)} %collective-permute-done.42.rest_1_, ...), custom_call_target="tpu_custom_call" | custom-call | flops 25769803776 | bytes 1048576 | tf_op jit(solution)/shard_map/pallas_call | solution.py:486
  495.5 12.3 %collective-permute-done.45.rest_1_ = bf16[256,1024]{1,0:T(8,128)(2,1)S(1)} collective-permute-done((bf16[256,1024]{1,0:T(8,128)(2,1)S(1)}, bf16[256,1024]{1,0:T(8,128)(2,1)S(1)}, u32[]{:S(2)}, u32[]{:S(2)}) %collective-permute-start.45) | collective-permute-done | bytes 524320 | tf_op jit(solution)/shard_map/ppermute | solution.py:46
  510.8 22.0 %shard_map.204 = (f32[4,128,768]{2,1,0:T(8,128)}, bf16[4,128,768]{2,1,0:T(8,128)(2,1)}, f32[2,256,1024]{2,1,0:T(8,128)}, bf16[2,256,1024]{2,1,0:T(8,128)(2,1)}) custom-call(s32[4]{0:T(128)} %pad_add_fusion.spots_ref, s32[8]{0:T(128)} %stack.194.block_spots_ref, bf16[256,1024]{1,0:T(8,128)(2,1)} %copy-done.28, bf16[256,1024]{1,0:T(8,128)(2,1)} %copy-done.39, ...), custom_call_target="tpu_custom_call" | custom-call | flops 25769803776 | bytes 1048576 | tf_op jit(solution)/shard_map/pallas_call | solution.py:486
  535.9 17.2 %collective-permute-done.60 = bf16[4,128,768]{2,1,0:T(8,128)(2,1)S(1)} collective-permute-done((bf16[4,128,768]{2,1,0:T(8,128)(2,1)}, bf16[4,128,768]{2,1,0:T(8,128)(2,1)S(1)}, u32[]{:S(2)}, u32[]{:S(2)}) %collective-permute-start.60) | collective-permute-done | bytes 786464 | tf_op jit(solution)/shard_map/ppermute | solution.py:46
  559.9 9.0 %collective-permute-done.61 = bf16[128,768]{1,0:T(8,128)(2,1)S(1)} collective-permute-done((bf16[128,768]{1,0:T(8,128)(2,1)S(1)}, bf16[128,768]{1,0:T(8,128)(2,1)S(1)}, u32[]{:S(2)}, u32[]{:S(2)}) %collective-permute-start.61) | collective-permute-done | bytes 196640 | tf_op jit(solution)/shard_map/ppermute | solution.py:91
  569.9 12.2 %collective-permute-done.62 = bf16[128,768]{1,0:T(8,128)(2,1)S(1)} collective-permute-done((bf16[128,768]{1,0:T(8,128)(2,1)S(1)}, bf16[128,768]{1,0:T(8,128)(2,1)S(1)}, u32[]{:S(2)}, u32[]{:S(2)}) %collective-permute-start.62) | collective-permute-done | bytes 196640 | tf_op jit(solution)/shard_map/ppermute | solution.py:91
  597.7 9.0 %collective-permute-done.68 = f32[16,128]{1,0:T(8,128)S(1)} collective-permute-done((f32[16,128]{1,0:T(8,128)S(1)}, f32[16,128]{1,0:T(8,128)S(1)}, u32[]{:S(2)}, u32[]{:S(2)}) %collective-permute-start.68) | collective-permute-done | bytes 8224 | tf_op jit(solution)/shard_map/ppermute | solution.py:46
  606.7 7.3 %collective-permute-start.69 = (f32[16,128]{1,0:T(8,128)S(1)}, f32[16,128]{1,0:T(8,128)S(1)}, u32[]{:S(2)}, u32[]{:S(2)}) collective-permute-start(f32[16,128]{1,0:T(8,128)S(1)} %add.434), channel_id=1, source_target_pairs={{0,8},{8,0},{16,24},{24,16},{1,9},{9,1},{17,25},{25,17},{2,10},{10... | collective-permute-start | bytes 24584 | tf_op jit(solution)/shard_map/ppermute | solution.py:101
  634.8 16.4 %collective-permute-done.55 = bf16[256,1024]{1,0:T(8,128)(2,1)} collective-permute-done((bf16[256,1024]{1,0:T(8,128)(2,1)}, bf16[256,1024]{1,0:T(8,128)(2,1)}, u32[]{:S(2)}, u32[]{:S(2)}) %collective-permute-start.55) | collective-permute-done | bytes 524320 | tf_op jit(solution)/shard_map/ppermute | solution.py:46
  654.6 13.3 %collective-permute-done.64.refs_1_ = bf16[4,128,768]{2,1,0:T(8,128)(2,1)S(1)} collective-permute-done((bf16[4,128,768]{2,1,0:T(8,128)(2,1)}, bf16[4,128,768]{2,1,0:T(8,128)(2,1)S(1)}, u32[]{:S(2)}, u32[]{:S(2)}) %collective-permute-start.64) | collective-permute-done | bytes 786464 | tf_op jit(solution)/shard_map/ppermute | solution.py:46
  667.9 13.7 %collective-permute-done.65.refs_3_ = bf16[4,128,768]{2,1,0:T(8,128)(2,1)S(1)} collective-permute-done((bf16[4,128,768]{2,1,0:T(8,128)(2,1)S(1)}, bf16[4,128,768]{2,1,0:T(8,128)(2,1)S(1)}, u32[]{:S(2)}, u32[]{:S(2)}) %collective-permute-start.65) | collective-permute-done | bytes 786464 | tf_op jit(solution)/shard_map/ppermute | solution.py:46
  (321 shorter events, 198.9 us)
Async XLA Ops:
  7.2 179.3 %all-gather.5.cloned.1.call-start = ((), (), s32[]{:S(2)}) async-start(), calls=%async_computation.4 | async-start | bytes 7864320 | tf_op jit(solution)/shard_map/all_gather | solution.py:538
  19.6 30.5 %collective-permute-start.8 = (bf16[256,1024]{1,0:T(8,128)(2,1)}, bf16[256,1024]{1,0:T(8,128)(2,1)}, u32[]{:S(2)}, u32[]{:S(2)}) collective-permute-start(bf16[256,1024]{1,0:T(8,128)(2,1)} %get-tuple-element.315.rest_0_.rest_4_), channel_id=1, source_target_pairs={{0,1},{1,0},{2,3},{3,2},{4,5},{5,4},{6,7},{7,6},{8,9},{9,8},{10,11... | collective-permute-start | bytes 1572872 | tf_op jit(solution)/shard_map/ppermute | solution.py:46
  22.9 39.6 %collective-permute-start.10 = (bf16[4,128,768]{2,1,0:T(8,128)(2,1)}, bf16[4,128,768]{2,1,0:T(8,128)(2,1)S(1)}, u32[]{:S(2)}, u32[]{:S(2)}) collective-permute-start(bf16[4,128,768]{2,1,0:T(8,128)(2,1)} %get-tuple-element.122), channel_id=1, source_target_pairs={{0,4},{4,0},{1,5},{5,1},{2,6},{6,2},{3,7},{7,3},{8,12},{12,8},{9,1... | collective-permute-start | bytes 2359304 | tf_op jit(solution)/shard_map/ppermute | solution.py:46
  66.2 250.7 %all-gather.7.cloned.1.call-start = ((), (), s32[]{:S(2)}) async-start(), calls=%async_computation.5 | async-start | bytes 7864320 | tf_op jit(solution)/shard_map/all_gather | solution.py:538
  99.4 35.5 %collective-permute-start.23 = (bf16[4,128,768]{2,1,0:T(8,128)(2,1)S(1)}, bf16[4,128,768]{2,1,0:T(8,128)(2,1)}, u32[]{:S(2)}, u32[]{:S(2)}) collective-permute-start(bf16[4,128,768]{2,1,0:T(8,128)(2,1)S(1)} %get-tuple-element.155), channel_id=1, source_target_pairs={{0,4},{4,0},{1,5},{5,1},{2,6},{6,2},{3,7},{7,3},{8,12},{12,8},{9,1... | collective-permute-start | bytes 2359304 | tf_op jit(solution)/shard_map/ppermute | solution.py:46
  106.2 28.7 %collective-permute-start.20 = (bf16[256,1024]{1,0:T(8,128)(2,1)}, bf16[256,1024]{1,0:T(8,128)(2,1)}, u32[]{:S(2)}, u32[]{:S(2)}) collective-permute-start(bf16[256,1024]{1,0:T(8,128)(2,1)} %get-tuple-element.161), channel_id=1, source_target_pairs={{0,4},{4,0},{1,5},{5,1},{2,6},{6,2},{3,7},{7,3},{8,12},{12,8},{9,1... | collective-permute-start | bytes 1572872 | tf_op jit(solution)/shard_map/ppermute | solution.py:46
  169.0 291.5 %reduce-scatter.3.cloned.1.call-start = ((), (), s32[]{:S(2)}) async-start(), calls=%async_computation.2 | async-start | bytes 7864320 | tf_op jit(solution)/shard_map/reduce_scatter | solution.py:655
  169.9 71.6 %collective-permute-start.28 = (bf16[256,1024]{1,0:T(8,128)(2,1)}, bf16[256,1024]{1,0:T(8,128)(2,1)}, u32[]{:S(2)}, u32[]{:S(2)}) collective-permute-start(bf16[256,1024]{1,0:T(8,128)(2,1)} %multiply_convert_fusion.1), channel_id=1, source_target_pairs={{0,2},{2,0},{1,3},{3,1},{4,6},{6,4},{5,7},{7,5},{8,10},{10,8},{9,1... | collective-permute-start | bytes 1572872 | tf_op jit(solution)/shard_map/ppermute | solution.py:46
  171.3 70.1 %collective-permute-start.29 = (bf16[256,1024]{1,0:T(8,128)(2,1)}, bf16[256,1024]{1,0:T(8,128)(2,1)}, u32[]{:S(2)}, u32[]{:S(2)}) collective-permute-start(bf16[256,1024]{1,0:T(8,128)(2,1)} %multiply_convert_fusion.1), channel_id=1, source_target_pairs={{0,6},{2,4},{4,2},{6,0},{1,7},{3,5},{5,3},{7,1},{8,14},{10,12},{12... | collective-permute-start | bytes 1572872 | tf_op jit(solution)/shard_map/ppermute | solution.py:58
  172.8 68.6 %collective-permute-start.30 = (bf16[256,1024]{1,0:T(8,128)(2,1)S(1)}, bf16[256,1024]{1,0:T(8,128)(2,1)}, u32[]{:S(2)}, u32[]{:S(2)}) collective-permute-start(bf16[256,1024]{1,0:T(8,128)(2,1)S(1)} %copy-done.26), channel_id=1, source_target_pairs={{0,4},{4,0},{1,5},{5,1},{2,6},{6,2},{3,7},{7,3},{8,12},{12,8},{9,1... | collective-permute-start | bytes 1572872 | tf_op jit(solution)/shard_map/ppermute | solution.py:46
  184.3 57.2 %collective-permute-start.31 = (bf16[256,1024]{1,0:T(8,128)(2,1)S(1)}, bf16[256,1024]{1,0:T(8,128)(2,1)}, u32[]{:S(2)}, u32[]{:S(2)}) collective-permute-start(bf16[256,1024]{1,0:T(8,128)(2,1)S(1)} %copy-done.26), channel_id=1, source_target_pairs={{0,2},{2,0},{1,3},{3,1},{4,6},{6,4},{5,7},{7,5},{8,10},{10,8},{9,1... | collective-permute-start | bytes 1572872 | tf_op jit(solution)/shard_map/ppermute | solution.py:46
  185.8 55.7 %collective-permute-start.32 = (bf16[256,1024]{1,0:T(8,128)(2,1)S(1)}, bf16[256,1024]{1,0:T(8,128)(2,1)}, u32[]{:S(2)}, u32[]{:S(2)}) collective-permute-start(bf16[256,1024]{1,0:T(8,128)(2,1)S(1)} %copy-done.26), channel_id=1, source_target_pairs={{0,6},{2,4},{4,2},{6,0},{1,7},{3,5},{5,3},{7,1},{8,14},{10,12},{12... | collective-permute-start | bytes 1572872 | tf_op jit(solution)/shard_map/ppermute | solution.py:58
  316.8 312.4 %reduce-scatter.5.cloned.1.call-start = ((), (), s32[]{:S(2)}) async-start(), calls=%async_computation.3 | async-start | bytes 7864320 | tf_op jit(solution)/shard_map/reduce_scatter | solution.py:655
  380.8 61.0 %collective-permute-start.35 = (bf16[256,1024]{1,0:T(8,128)(2,1)}, bf16[256,1024]{1,0:T(8,128)(2,1)S(1)}, u32[]{:S(2)}, u32[]{:S(2)}) collective-permute-start(bf16[256,1024]{1,0:T(8,128)(2,1)} %get-tuple-element.305), channel_id=1, source_target_pairs={{0,4},{4,0},{1,5},{5,1},{2,6},{6,2},{3,7},{7,3},{8,12},{12,8},{9,1... | collective-permute-start | bytes 1572872 | tf_op jit(solution)/shard_map/ppermute | solution.py:46
  382.2 59.6 %collective-permute-start.36 = (bf16[256,1024]{1,0:T(8,128)(2,1)}, bf16[256,1024]{1,0:T(8,128)(2,1)S(1)}, u32[]{:S(2)}, u32[]{:S(2)}) collective-permute-start(bf16[256,1024]{1,0:T(8,128)(2,1)} %get-tuple-element.304), channel_id=1, source_target_pairs={{0,2},{2,0},{1,3},{3,1},{4,6},{6,4},{5,7},{7,5},{8,10},{10,8},{9,1... | collective-permute-start | bytes 1572872 | tf_op jit(solution)/shard_map/ppermute | solution.py:46
  383.4 58.5 %collective-permute-start.37 = (bf16[256,1024]{1,0:T(8,128)(2,1)}, bf16[256,1024]{1,0:T(8,128)(2,1)}, u32[]{:S(2)}, u32[]{:S(2)}) collective-permute-start(bf16[256,1024]{1,0:T(8,128)(2,1)} %get-tuple-element.303), channel_id=1, source_target_pairs={{0,6},{2,4},{4,2},{6,0},{1,7},{3,5},{5,3},{7,1},{8,14},{10,12},{12... | collective-permute-start | bytes 1572872 | tf_op jit(solution)/shard_map/ppermute | solution.py:58
  534.5 48.6 %collective-permute-start.58 = (bf16[256,1024]{1,0:T(8,128)(2,1)}, bf16[256,1024]{1,0:T(8,128)(2,1)S(1)}, u32[]{:S(2)}, u32[]{:S(2)}) collective-permute-start(bf16[256,1024]{1,0:T(8,128)(2,1)} %fusion.27), channel_id=1, source_target_pairs={{0,2},{2,0},{1,3},{3,1},{4,6},{6,4},{5,7},{7,5},{8,10},{10,8},{9,1... | collective-permute-start | bytes 1572872 | tf_op jit(solution)/shard_map/ppermute | solution.py:46
  535.8 52.8 %collective-permute-start.46 = (bf16[4,256,1024]{2,1,0:T(8,128)(2,1)}, bf16[4,256,1024]{2,1,0:T(8,128)(2,1)}, u32[]{:S(2)}, u32[]{:S(2)}) collective-permute-start(bf16[4,256,1024]{2,1,0:T(8,128)(2,1)} %get-tuple-element.204), channel_id=1, source_target_pairs={{0,1},{1,0},{2,3},{3,2},{4,5},{5,4},{6,7},{7,6},{8,9},{9,8},{10,11... | collective-permute-start | bytes 6291464 | tf_op jit(solution)/shard_map/ppermute | solution.py:46
  583.1 38.7 %collective-permute-start.54 = (bf16[4,256,1024]{2,1,0:T(8,128)(2,1)}, bf16[4,256,1024]{2,1,0:T(8,128)(2,1)}, u32[]{:S(2)}, u32[]{:S(2)}) collective-permute-start(bf16[4,256,1024]{2,1,0:T(8,128)(2,1)} %get-tuple-element.214), channel_id=1, source_target_pairs={{0,1},{1,0},{2,3},{3,2},{4,5},{5,4},{6,7},{7,6},{8,9},{9,8},{10,11... | collective-permute-start | bytes 6291464 | tf_op jit(solution)/shard_map/ppermute | solution.py:46
  592.6 35.1 %collective-permute-start.47 = (bf16[256,1024]{1,0:T(8,128)(2,1)S(1)}, bf16[256,1024]{1,0:T(8,128)(2,1)}, u32[]{:S(2)}, u32[]{:S(2)}) collective-permute-start(bf16[256,1024]{1,0:T(8,128)(2,1)S(1)} %get-tuple-element.294), channel_id=1, source_target_pairs={{0,4},{4,0},{1,5},{5,1},{2,6},{6,2},{3,7},{7,3},{8,12},{12,8},{9,1... | collective-permute-start | bytes 1572872 | tf_op jit(solution)/shard_map/ppermute | solution.py:46
  594.2 36.3 %collective-permute-start.48 = (bf16[256,1024]{1,0:T(8,128)(2,1)}, bf16[256,1024]{1,0:T(8,128)(2,1)}, u32[]{:S(2)}, u32[]{:S(2)}) collective-permute-start(bf16[256,1024]{1,0:T(8,128)(2,1)} %get-tuple-element.296), channel_id=1, source_target_pairs={{0,2},{2,0},{1,3},{3,1},{4,6},{6,4},{5,7},{7,5},{8,10},{10,8},{9,1... | collective-permute-start | bytes 1572872 | tf_op jit(solution)/shard_map/ppermute | solution.py:46
  594.8 37.1 %collective-permute-start.49 = (bf16[256,1024]{1,0:T(8,128)(2,1)}, bf16[256,1024]{1,0:T(8,128)(2,1)}, u32[]{:S(2)}, u32[]{:S(2)}) collective-permute-start(bf16[256,1024]{1,0:T(8,128)(2,1)} %get-tuple-element.295), channel_id=1, source_target_pairs={{0,6},{2,4},{4,2},{6,0},{1,7},{3,5},{5,3},{7,1},{8,14},{10,12},{12... | collective-permute-start | bytes 1572872 | tf_op jit(solution)/shard_map/ppermute | solution.py:58
  630.4 37.5 %collective-permute-start.64 = (bf16[4,128,768]{2,1,0:T(8,128)(2,1)}, bf16[4,128,768]{2,1,0:T(8,128)(2,1)S(1)}, u32[]{:S(2)}, u32[]{:S(2)}) collective-permute-start(bf16[4,128,768]{2,1,0:T(8,128)(2,1)} %slice_bitcast_fusion.5), channel_id=1, source_target_pairs={{0,4},{4,0},{1,5},{5,1},{2,6},{6,2},{3,7},{7,3},{8,12},{12,8},{9,1... | collective-permute-start | bytes 2359304 | tf_op jit(solution)/shard_map/ppermute | solution.py:46
  632.0 49.7 %collective-permute-start.65 = (bf16[4,128,768]{2,1,0:T(8,128)(2,1)S(1)}, bf16[4,128,768]{2,1,0:T(8,128)(2,1)S(1)}, u32[]{:S(2)}, u32[]{:S(2)}) collective-permute-start(bf16[4,128,768]{2,1,0:T(8,128)(2,1)S(1)} %slice_bitcast_fusion.4), channel_id=1, source_target_pairs={{0,4},{4,0},{1,5},{5,1},{2,6},{6,2},{3,7},{7,3},{8,12},{12,8},{9,1... | collective-permute-start | bytes 2359304 | tf_op jit(solution)/shard_map/ppermute | solution.py:46
  (98 other events, 1741.8 us)
Sparse Core Ops, SparseCore 0:
  66.3 115.8 all-gather.4
  184.3 113.5 all-gather.6
  316.9 111.9 reduce-scatter.2
  460.7 124.7 reduce-scatter.4

commit v5 on v4

--- a/solution.py
+++ b/solution.py
@@ -37,9 +37,7 @@
 def norm_back(in_rows, row_scale, gain_vec, grad_in):
     weighted = grad_in * gain_vec
     inner = jnp.mean(weighted * in_rows, axis=-1, keepdims=True)
-    returned = row_scale * weighted - in_rows * row_scale * row_scale * row_scale * inner
-    gain_part = jnp.sum(grad_in * in_rows * row_scale, axis=0)
-    return (returned, gain_part)
+    return row_scale * weighted - in_rows * row_scale * row_scale * row_scale * inner
 
 
 def swap(value, axis):
@@ -58,14 +56,18 @@
     return lax.ppermute(value, ("y", "x"), [(i, 3 - i) for i in range(4)])
 
 
+def to_neighbours(rows):
+    return [swap(rows[0], "y"), swap(rows[1], "x"), cross(rows[2])]
+
+
 def plus(left, right):
     return left + right.astype(FP)
 
 
-def scatter_pair(kept, sent):
+def half_sums(kept, sent):
     got = swap(sent, "c")
-    sent = [plus(kept[i], got[i]).astype(BF) for i in (1, 2, 3)]
-    return plus(kept[0], got[0]), sent, [swap(sent[0], "y"), swap(sent[1], "x"), cross(sent[2])]
+    low = [plus(kept[i], got[i]).astype(BF) for i in range(1, kept.shape[0])]
+    return plus(kept[0], got[0]), low
 
 
 def sum_of(total, parts):
@@ -83,18 +85,14 @@
     return pieces, [lax.rem(place + depth - k, depth) for k in [0, *turns_taken]]
 
 
-def scatter_dp(kept, sent, depth):
-    column = kept + swap(sent, "y").astype(FP)
-    total = column[0]
-    for r in range(1, depth):
-        turn = [(i, (i + r) % depth) for i in range(depth)]
-        total = plus(total, lax.ppermute(column[r].astype(BF), "z", turn))
-    return total
-
-
-def sum_all(value, depth):
-    for axis in ("c", "x", "y"):
-        value = value + swap(value, axis)
+def along_z_sent(column, depth):
+    return [
+        lax.ppermute(column[r].astype(BF), "z", [(i, (i + r) % depth) for i in range(depth)])
+        for r in range(1, depth)
+    ]
+
+
+def sum_over_z(value, depth):
     reach = 1
     while reach < depth:
         pairs = [(i, i ^ reach) for i in range(depth)]
@@ -110,6 +108,27 @@
 SMALL = cost(1 << 30)
 SMEM = pl.BlockSpec(memory_space=pltpu.SMEM)
 VMEM = pl.BlockSpec(memory_space=pltpu.VMEM)
+
+
+def stack_kernel(*refs):
+    *ins, out_ref, sems = refs
+    copies = [pltpu.make_async_copy(ref, out_ref.at[i], sems.at[i]) for i, ref in enumerate(ins)]
+    for copy in copies:
+        copy.start()
+    for copy in copies:
+        copy.wait()
+
+
+def stacked(arrays):
+    return pl.pallas_call(
+        stack_kernel,
+        in_specs=[pl.BlockSpec(memory_space=pl.ANY)] * len(arrays),
+        out_specs=VMEM,
+        out_shape=jax.ShapeDtypeStruct((len(arrays), *arrays[0].shape), arrays[0].dtype),
+        scratch_shapes=[pltpu.SemaphoreType.DMA((len(arrays),))],
+        compiler_params=pltpu.CompilerParams(vmem_limit_bytes=32 << 20),
+        cost_estimate=cost(1 << 30),
+    )(*arrays)
 
 
 def pack_kernel(side_ref, gate_up_ref, down_ref, *rest):
@@ -287,7 +306,8 @@
     parts = rows // tile
     row = pl.BlockSpec((None, 2, tile, model_width), lambda i: (i // parts, 0, i % parts, 0))
     half = pl.BlockSpec((None, tile, model_width), lambda i: (i // parts, i % parts, 0))
-    g_half = pl.BlockSpec((None, tile, model_width), lambda i: (count + i // parts, i % parts, 0))
+    x_half = pl.BlockSpec((None, tile, model_width), lambda i: (2 * (i // parts), i % parts, 0))
+    g_half = pl.BlockSpec((None, tile, model_width), lambda i: (2 * (i // parts) + 1, i % parts, 0))
     gate_spec = pl.BlockSpec(
         (None, None, 2, tile, gates.shape[-1]), lambda i: (micro, i // parts, 0, i % parts, 0)
     )
@@ -304,7 +324,7 @@
     *sums, grads = pl.pallas_call(
         functools.partial(moe_kernel, first, last, start, column),
         grid=(count * parts,),
-        in_specs=[SMEM, half, half, g_half, g_half, gate_spec, whole]
+        in_specs=[SMEM, x_half, x_half, g_half, g_half, gate_spec, whole]
         + ([] if first else [row, row])
         + ([] if start else [whole]),
         out_specs=out_specs + [whole],
@@ -323,8 +343,9 @@
         whole_ref[pl.ds(pl.multiple_of(spots_ref[i] * rows, rows), rows), :] = piece[...]
 
 
-def product_rows(spots_ref, left_ref, right, kept_ref, sent_ref):
+def product_rows(spots_ref, left_ref, right, kept_ref, sent_ref, x_ref=None, gain_ref=None):
     rows = kept_ref.shape[1]
+    gain = 0.0
     for i in range(4):
         here = pl.ds(pl.multiple_of(spots_ref[i] * rows, rows), rows)
         value = dot_nt(left_ref[here, :], right)
@@ -332,6 +353,10 @@
             kept_ref[i] = value
         else:
             sent_ref[i - 2] = value.astype(BF)
+        if x_ref is not None:
+            gain += jnp.sum(value * x_ref[here, :].astype(FP), axis=0, keepdims=True)
+    if x_ref is not None:
+        gain_ref[...] = gain
 
 
 def attn_forward_kernel(widths, n_weights, spots_ref, weight_spots_ref, *rest):
@@ -379,12 +404,12 @@
     qkv_ref, heads_ref, w_ref = rest[:3]
     rest = rest[3:]
     if first:
-        grads_ref, kept_ref, sent_ref = rest[:3]
-        rest = rest[3:]
+        grads_ref, kept_ref, sent_ref, gain_ref = rest[:4]
+        rest = rest[4:]
     else:
-        earlier_ref, grads_kept_ref, grads_sent_ref, kept_ref, sent_ref = rest[:5]
-        grads_ref = rest[5]
-        rest = rest[6:]
+        earlier_ref, grads_kept_ref, grads_sent_ref, kept_ref, sent_ref, gain_ref = rest[:6]
+        grads_ref = rest[6]
+        rest = rest[7:]
     dy_scr, x_scr, head_grad_ref, proj_grad_ref, key_acc, value_acc = rest
     place_rows(spots_ref, dy_pieces, dy_scr)
     place_rows(spots_ref, x_pieces, x_scr)
@@ -422,7 +447,7 @@
                 proj_grad_ref[start:stop, c] = query_grad[r * tile : (r + 1) * tile]
         proj_grad_ref[:, key_cols] = key_acc[...].astype(BF)
         proj_grad_ref[:, value_cols] = value_acc[...].astype(BF)
-    product_rows(spots_ref, proj_grad_ref, w_ref[:, :proj_width], kept_ref, sent_ref)
+    product_rows(spots_ref, proj_grad_ref, w_ref[:, :proj_width], kept_ref, sent_ref, x_scr, gain_ref)
     proj_part = dot_tn(x_scr[...], proj_grad_ref[...])
     out_part = dot_tn(dy_scr[...], heads_ref[...])
     if first:
@@ -483,6 +508,7 @@
         outs = [jax.ShapeDtypeStruct(blocks, FP), jax.ShapeDtypeStruct(blocks, BF)]
         scratch = [pltpu.VMEM(whole, FP)] + scratch
     outs += [jax.ShapeDtypeStruct((2, rows, model_width), t) for t in (FP, BF)]
+    outs += [jax.ShapeDtypeStruct((1, model_width), FP)]
     return pl.pallas_call(
         functools.partial(attn_backward_kernel, widths, first),
         in_specs=[SMEM] * 2 + [VMEM] * len(operands),
@@ -490,7 +516,7 @@
         out_shape=outs,
         scratch_shapes=scratch,
         compiler_params=pltpu.CompilerParams(vmem_limit_bytes=58 << 20),
-        cost_estimate=cost(24 << 30),
+        cost_estimate=cost(4 << 30),
     )(spots, block_spots, *operands)
 
 
@@ -522,9 +548,9 @@
         [2 * lax.rem(place + r, depth) + s for s in (side, 1 - side) for r in range(depth)]
     ).astype(jnp.int32)
 
-    packed_attn = pack_attn(w_query, w_key, w_value, w_out)
-    packed = pack_experts(after(side_at, packed_attn), w_gate_up, w_down)
-    in_rows = block_input.astype(FP)
+    packed = pack_experts(side_at, w_gate_up, w_down)
+    packed_attn = pack_attn(after(w_query, packed[0][1]), w_key, w_value, w_out)
+    in_rows = after(block_input, packed_attn).astype(FP)
     normed_attn, scale_attn = row_norm(in_rows, norm_attn)
     normed = [normed_attn[m].astype(BF) for m in range(micro_count)]
     cots = [cotangent[m] for m in range(micro_count)]
@@ -544,39 +570,44 @@
     across = swap(normed[0], "x")
     got = swap(packed[0][1], "y")
     own_across = swap(packed_attn, "y")
-    *column, across, next_normed = together(*column, across, normed[1])
+    *column, across, got = together(*column, across, got)
+    shards = [shard_of(0, got)]
+    chunk_weights = [whole_of(shards[0])]
+    *column, across, next_normed, cot, _ = together(
+        *column, across, normed[1], cots[0], shards[0]
+    )
 
     weights = column + [own_across] + [swap(piece, "y") for piece in column[1:]]
     near_rows, far_rows = swap(normed[0], "c"), swap(across, "c")
-    next_across = swap(next_normed, "x")
-    *weights, near_rows, far_rows, got, cot, next_across = together(
-        *weights, near_rows, far_rows, got, cots[0], next_across
+    next_across, cot_across = swap(next_normed, "x"), swap(cot, "x")
+    *weights, near_rows, far_rows, cot, next_across = together(
+        *weights, near_rows, far_rows, cots[0], next_across
     )
     attn_in = [[normed[0], across, near_rows, far_rows]]
-    shards = [shard_of(0, got)]
-    chunk_weights = [whole_of(shards[0])]
-
-    cot_near, cot_across = swap(cot, "y"), swap(cot, "x")
+
+    cot_diagonal = cross(cot)
     turn = after(spots, shards[0])
     qkv, heads, kept, sent, whole = attn_forward(turn, weight_spots, attn_in[0], weights, widths)
     weights = [whole]
     saved = [(qkv, heads)]
-    sent, cot_near, cot_across, across = together(sent, cot_near, cot_across, next_across)
+    sent, cot_diagonal, cot_across, across = together(
+        sent, cot_diagonal, cot_across, next_across
+    )
 
     got = swap(sent, "c")
     near_rows, far_rows = swap(normed[1], "c"), swap(across, "c")
     along = plus(kept[1], got[1]).astype(BF)
     own = plus(kept[0], got[0])
-    along, near_rows, far_rows, theirs, turn = together(
-        along, near_rows, far_rows, packed[1][1], spots
+    along, near_rows, far_rows, cot, theirs, turn = together(
+        along, near_rows, far_rows, cots[0], packed[1][1], spots
     )
     attn_in.append([normed[1], across, near_rows, far_rows])
 
-    came = swap(along, "x")
+    came, cot_near = swap(along, "x"), swap(cot, "y")
     theirs = swap(theirs, "y")
     qkv, heads, kept, sent, _ = attn_forward(turn, weight_spots, attn_in[1], weights, widths)
     saved.append((qkv, heads))
-    sent, came = together(sent, came)
+    sent, came, cot_near = together(sent, came, cot_near)
 
     def moe_rows(middle):
         normed, scale = row_norm(middle, norm_moe)
@@ -588,7 +619,7 @@
     normed, scale_moe = [low], [scale]
     along = plus(kept[1], got[1]).astype(BF)
     own = plus(kept[0], got[0])
-    along, low, cot = together(along, low, cots[0])
+    along, low = together(along, low)
 
     came = swap(along, "x")
     near, across = swap(low, "y"), swap(low, "x")
@@ -601,28 +632,26 @@
     other = lax.dynamic_index_in_dim(gates, 1 - side, 0, False)
     gates = jnp.stack([mine, swap(other.reshape(E // 2, -1), "y").reshape(mine.shape)])
     gates = gates.transpose(2, 3, 0, 4, 5, 1).reshape(micro_count, 4, 2, rows_local, E // 2)
-    came, near, across, gates, theirs, low, cot = together(
-        came, near, across, gates, theirs, low, cot
-    )
-
-    diagonal, cot_diagonal = cross(low), cross(cot)
+    came, near, across, gates, theirs, low = together(came, near, across, gates, theirs, low)
+
+    diagonal = cross(low)
     shards.append(shard_of(1, theirs))
     chunk_weights.append(whole_of(shards[1]))
     middle.append(in_rows[1] + plus(own, came))
     low, scale = moe_rows(middle[1])
     normed.append(low)
     scale_moe.append(scale)
-    diagonal, cot_diagonal, low, cot = together(diagonal, cot_diagonal, low, cots[1])
-    blocks = jnp.stack(
-        [normed[0], near, across, diagonal, cots[0], cot_near, cot_across, cot_diagonal]
+    pair = stacked([low, cots[1]])
+    diagonal, pair, _ = together(diagonal, pair, shards[1])
+    blocks = stacked(
+        [normed[0], cots[0], near, cot_near, across, cot_across, diagonal, cot_diagonal]
     )
     experts_in = [(blocks, swap(blocks, "c"))]
-    neighbours = [f(v) for v in (low, cot) for f in (lambda r: swap(r, "y"), lambda r: swap(r, "x"), cross)]
+    neighbours = to_neighbours([pair] * 3)
 
     sums = [None] * micro_count
     turn = after(side_at, shards[1])
     all_grads = []
-    back = []
     first_expert = 0
     for chunk, pairs in enumerate(CHUNKS):
         last = chunk == len(CHUNKS) - 1
@@ -642,12 +671,17 @@
             waited = [grads]
             if m == 0 and chunk == 0:
                 *neighbours, _ = together(*neighbours, grads)
-                blocks = jnp.stack([low, *neighbours[:3], cot, *neighbours[3:]])
+                blocks = stacked([pair, *neighbours])
+                blocks = blocks.reshape(-1, *blocks.shape[2:])
                 experts_in.append((blocks, swap(blocks, "c")))
             if m == 0 and last:
-                back.append(scatter_pair(*sums[m][2:]))
-                waited += back[0][1]
-            turn = after(side_at, *waited)
+                mixed_own, mixed_along = half_sums(*sums[0][:2])
+                own, along = half_sums(*sums[0][2:])
+                along = [jnp.stack(both) for both in zip(along, mixed_along)]
+                *along, turn, _ = together(*along, side_at, *waited)
+                came = to_neighbours(along)
+            else:
+                turn = after(side_at, *waited)
         first_expert += 2 * pairs
         all_grads.append(grads.reshape(depth, 2, *grads.shape[1:]))
 
@@ -656,55 +690,81 @@
 
     grad_shards = [reduce_grads(all_grads[0])]
 
-    out_grad = cotangent.astype(FP)
-    input_grads = []
-    gains = [0.0, 0.0]
-    middle_grad, branch_grad, outputs = [], [], []
-    results = None
-    turn = spots
-    ends = grads
-    for m in range(micro_count):
-        if m:
-            kept, sent = sums[m][2:]
-            back.append(scatter_pair(kept, after(sent, middle_low)))
-            ends = results[0]
-        own, _, came = back[m]
-        *came, _ = together(*came, ends)
+    def middle_back(m, own, came):
         moe_in_grad = sum_of(own, came)
-        middle_back, gain_moe = norm_back(middle[m], scale_moe[m], norm_moe, moe_in_grad)
-        middle_grad.append(out_grad[m] + middle_back)
-        middle_low = middle_grad[m].astype(BF)
-        if m == 0:
-            grads, _ = together(all_grads[1], grad_shards[0])
-            grad_shards.append(reduce_grads(grads))
-        across = swap(middle_low, "x")
-        branch_grad.append([middle_low, across, swap(middle_low, "c"), swap(across, "c")])
-        gains[1] = gains[1] + gain_moe
-        results = attn_backward(
-            turn,
-            block_spots,
-            branch_grad[m],
-            attn_in[m],
-            *saved[m],
-            weights[0],
-            None if results is None else results[0],
-            widths,
+        back = norm_back(middle[m], scale_moe[m], norm_moe, moe_in_grad)
+        gain = jnp.sum(moe_in_grad * middle[m] * scale_moe[m], axis=0)
+        grad = cots[m].astype(FP) + back
+        return grad, grad.astype(BF), gain
+
+    def input_back(m, middle_grad, own, came):
+        return middle_grad + norm_back(in_rows[m], scale_attn[m], norm_attn, plus(own, came))
+
+    def backward(m, turn, rows, earlier):
+        return attn_backward(
+            turn, block_spots, rows, attn_in[m], *saved[m], weights[0], earlier, widths
         )
-        kept, sent = results[-2:]
-        got = swap(sent, "c")
-        along = plus(kept[1], got[1]).astype(BF)
-        attn_in_grad = sum_of(plus(kept[0], got[0]), [swap(along, "x")])
-        turn = after(spots, along)
-        in_back, gain_attn = norm_back(in_rows[m], scale_attn[m], norm_attn, attn_in_grad)
-        input_grads.append(middle_grad[m] + in_back)
-        gains[0] = gains[0] + gain_attn
-    for m in range(micro_count):
-        kept, sent = sums[m][:2]
-        own, _, came = scatter_pair(kept, after(sent, along if m else branch_grad[-1][1]))
-        outputs.append((middle[m] + sum_of(own, came)).astype(BF))
-    shard_pair, shard_down = unpack_experts(side_at, [(g, swap(g[1], "y")) for g in grad_shards])
-    attn_shard = scatter_dp(results[0], results[1], depth)
-    gains = sum_all(jnp.concatenate(gains).reshape(16, -1), depth).reshape(2, model_width)
+
+    *came, grads, kept, sent, last_mixed_kept, last_mixed_sent, first_shard = together(
+        *came, all_grads[1], sums[1][2], sums[1][3], *sums[1][:2], grad_shards[0]
+    )
+    grad_shards = [first_shard, reduce_grads(grads)]
+    outputs = [(middle[0] + sum_of(mixed_own, [c[1] for c in came])).astype(BF)]
+    middle_grad, low, gain_moe = middle_back(0, own, [c[0] for c in came])
+    shard_got = [swap(first_shard[1], "y")]
+    across, near_rows = swap(low, "x"), swap(low, "c")
+    own, along = half_sums(kept, after(sent, low))
+    across, near_rows, *along = together(across, near_rows, *along)
+    far_rows = swap(across, "c")
+    came = to_neighbours(along)
+    results = backward(0, spots, [low, across, near_rows, far_rows], None)
+    *came, earlier, kept, sent, gain_attn = together(*came, *results)
+
+    middle_grads = [middle_grad]
+    middle_grad, low, gain = middle_back(1, own, came)
+    middle_grads.append(middle_grad)
+    gain_moe = gain_moe + gain
+    across, near_rows = swap(low, "x"), swap(low, "c")
+    input_own, input_along = half_sums(kept, sent)
+    mixed_own, mixed_along = half_sums(last_mixed_kept, after(last_mixed_sent, low))
+    across, near_rows, *mixed_along, input_along, shard_got[0], outputs[0] = together(
+        across, near_rows, *mixed_along, *input_along, shard_got[0], outputs[0]
+    )
+    far_rows = swap(across, "c")
+    input_came = swap(input_along, "x")
+    mixed_came = [swap(mixed_along[0], "y"), swap(mixed_along[1], "x")]
+    results = backward(1, spots, [low, across, near_rows, far_rows], earlier)
+    input_came, *mixed_came, grads_kept, grads_sent, kept, sent, gain = together(
+        input_came, *mixed_came, *results
+    )
+
+    gains = jnp.concatenate([(gain_attn + gain)[0] / norm_attn, gain_moe]).reshape(16, -1)
+    own, along = half_sums(kept, sent)
+    first_input = input_back(0, middle_grads[0], input_own, input_came)
+    for axis in ("c", "x", "y"):
+        gains = gains + swap(gains, axis)
+    along, gains, first_input, grads_sent, diagonal = together(
+        along[0], gains, first_input, grads_sent, mixed_along[2]
+    )
+    input_came, grads_got = swap(along, "x"), swap(grads_sent, "y")
+    gains = sum_over_z(gains, depth).reshape(2, model_width)
+    input_came, grads_got, gains, last_shard, diagonal = together(
+        input_came, grads_got, gains, grad_shards[1], diagonal
+    )
+    shard_got.append(swap(last_shard[1], "y"))
+    diagonal = cross(diagonal)
+    column = grads_kept + grads_got.astype(FP)
+    pieces = along_z_sent(column, depth)
+    last_input = input_back(1, middle_grads[1], own, input_came)
+    shard_got[1], diagonal, last_input, *pieces = together(
+        shard_got[1], diagonal, last_input, *pieces
+    )
+    shard_pair, shard_down = unpack_experts(
+        side_at, list(zip([grad_shards[0], last_shard], shard_got))
+    )
+    attn_shard = sum_of(column[0], pieces)
+    outputs.append((middle[1] + sum_of(mixed_own, [*mixed_came, diagonal])).astype(BF))
+    input_grads = [first_input, last_input]
     return (
         jnp.stack(outputs),
         jnp.stack(input_grads),

time: 696 us -> 599 us (0.86)
  waiting for transfers between devices: 207 us -> 129 us
  local copies, waits for them, and re-layouts: 41.4 us -> 30.7 us
  other arithmetic: 57.5 us -> 49.9 us
    ppermute x55 -> x51, waiting for transfers between devices: 157 us -> 93.7 us  [swap(): return lax.ppermute(value, axis, [(0, 1), (1, 0)])]
    ppermute x5, waiting for transfers between devices: 22.9 us -> 12 us  [the longest x3 8.71 us: along_z_sent(): lax.ppermute(column[r].astype(BF), 'z', [(i, (i + r) % depth) for i in ra...]
    unnamed x108 -> x133, local copies, waits for them, and re-layouts: 26.8 us -> 16.1 us
    convert_element_type x8 -> x9, other arithmetic: 20.7 us -> 11.8 us  [the longest x6 7.46 us: half_sums(): low = [plus(kept[i], got[i]).astype(BF) for i in range(1, kept.shape[0])]]
    ppermute x55 -> x51, starting transfers between devices: 44.7 us -> 36.1 us  [swap(): return lax.ppermute(value, axis, [(0, 1), (1, 0)])]
    ppermute x8 -> x6, waiting for transfers between devices: 17.2 us -> 11.9 us  [cross(): return lax.ppermute(value, ('y', 'x'), [(i, 3 - i) for i in range(4)])]
  transfers between devices with their start and end apart: 75 -> 69, of which waited for: 28 -> 26; matrix products, arithmetic and copies ran while one was open for 13% -> 10% of each run, Pallas kernels for 43% -> 50%
where the time goes in v5:
time: 599 us; the launch traced here: 594 us
  Pallas kernels  303 us (51%)
  waiting for transfers between devices  129 us (22%)
  starting transfers between devices  66.8 us (11%)
  other arithmetic  49.9 us (8%)
  local copies, waits for them, and re-layouts  30.7 us (5%)
  between operations  15 us (3%)
    pallas_call x4, Pallas kernels, moe_chunk(): pl.pallas_call(functools.partial(moe_kernel, first, last, start, column),...  225 us
    ppermute x51, waiting for transfers between devices, swap(): return lax.ppermute(value, axis, [(0, 1), (1, 0)])  93.7 us
    pallas_call x2, Pallas kernels, attn_backward(): pl.pallas_call(functools.partial(attn_backward_kernel, widths, first), in...  42.5 us
    ppermute x51, starting transfers between devices, swap(): return lax.ppermute(value, axis, [(0, 1), (1, 0)])  36.1 us
    pallas_call x2, Pallas kernels, attn_forward(): pl.pallas_call(functools.partial(attn_forward_kernel, widths, len(weights...  23.4 us
    unnamed x133, local copies, waits for them, and re-layouts  16.1 us
  transfers between devices with their start and end apart: 69, of which 26 were waited for; matrix products, arithmetic and copies ran while one was open for 10% of the time, Pallas kernels for 50%

profile of v5, /device:TPU:0, one launch (start us, length us, event | category | flops | bytes accessed | tf_op | source)
XLA Modules:
  0.0 593.6 jit_solution(10028760918231589554)
XLA Ops:
  26.0 10.5 %collective-permute-done.2.rest_7_ = bf16[128,768]{1,0:T(8,128)(2,1)} collective-permute-done((bf16[128,768]{1,0:T(8,128)(2,1)}, bf16[128,768]{1,0:T(8,128)(2,1)}, u32[]{:S(2)}, u32[]{:S(2)}) %collective-permute-start.2) | collective-permute-done | bytes 196640 | tf_op jit(solution)/shard_map/ppermute | solution.py:84
  42.3 5.9 collective-permute-done.5.rest_8_
  56.6 3.6 collective-permute-done.8.rest_11_
  62.4 11.9 %shard_map.197 = (bf16[1024,512]{1,0:T(8,128)(2,1)}, bf16[1024,256]{1,0:T(8,128)(2,1)}, f32[2,256,1024]{2,1,0:T(8,128)}, bf16[2,256,1024]{2,1,0:T(8,128)(2,1)}, bf16[1024,768]{1,0:T(8,128)(2,1)}) custom-call(s32[4]{0:T(128)} %pad_add_fusion.spots_ref, s32[8]{0:T(128)} %stack.132.weight_spots_ref, bf16[256,1024]{1,0:T(8,128)(2,1)} %get-tuple-element.408.rest_0_.rest_4_, ...), custom_call_target="tpu_custom_call" | custom-call | flops 15032385536 | bytes 1048576 | tf_op jit(solution)/shard_map/pallas_call | solution.py:477
  84.4 11.5 %shard_map.198 = (bf16[1024,512]{1,0:T(8,128)(2,1)}, bf16[1024,256]{1,0:T(8,128)(2,1)}, f32[2,256,1024]{2,1,0:T(8,128)}, bf16[2,256,1024]{2,1,0:T(8,128)(2,1)}) custom-call(s32[4]{0:T(128)} %pad_add_fusion.spots_ref, s32[8]{0:T(128)} %stack.132.weight_spots_ref, bf16[256,1024]{1,0:T(8,128)(2,1)} %get-tuple-element.182.rest_0_.rest_4_, ...), custom_call_target="tpu_custom_call" | custom-call | flops 15032385536 | bytes 1048576 | tf_op jit(solution)/shard_map/pallas_call | solution.py:477
  111.8 20.9 %collective-permute-done.23 = f32[16,2048]{1,0:T(8,128)} collective-permute-done((f32[16,2048]{1,0:T(8,128)}, f32[16,2048]{1,0:T(8,128)}, u32[]{:S(2)}, u32[]{:S(2)}) %collective-permute-start.23) | collective-permute-done | bytes 131104 | tf_op jit(solution)/shard_map/ppermute | solution.py:44
  145.8 7.3 %collective-permute-done.25.refs_6_ = bf16[256,1024]{1,0:T(8,128)(2,1)} collective-permute-done((bf16[256,1024]{1,0:T(8,128)(2,1)S(1)}, bf16[256,1024]{1,0:T(8,128)(2,1)}, u32[]{:S(2)}, u32[]{:S(2)}) %collective-permute-start.25) | collective-permute-done | bytes 524320 | tf_op jit(solution)/shard_map/ppermute | solution.py:56
  163.6 3.6 collective-permute-done.26.xb_ref.gb_ref
  167.2 55.5 %shard_map.201 = (f32[4,2,256,1024]{3,2,1,0:T(8,128)}, f32[4,2,256,1024]{3,2,1,0:T(8,128)}, bf16[8,4,128,768]{3,2,1,0:T(8,128)(2,1)}) custom-call(s32[1]{0:T(128)} %bitcast.1.side_ref, bf16[8,256,1024]{2,1,0:T(8,128)(2,1)} %shard_map.200.xa_ref.ga_ref, bf16[8,256,1024]{2,1,0:T(8,128)(2,1)} %collective-permute-done.26.xb_ref.gb_ref, ...), custom_call_target="tpu_custom_call" | custom-call | flops 6442450944 | bytes 1048576 | tf_op jit(solution)/shard_map/pallas_call | solution.py:324
  226.1 7.3 %collective-permute-done.30.xb_ref.gb_ref = bf16[8,256,1024]{2,1,0:T(8,128)(2,1)} collective-permute-done((bf16[8,256,1024]{2,1,0:T(8,128)(2,1)S(1)}, bf16[8,256,1024]{2,1,0:T(8,128)(2,1)}, u32[]{:S(2)}, u32[]{:S(2)}) %collective-permute-start.30) | collective-permute-done | bytes 4194336 | tf_op jit(solution)/shard_map/ppermute | solution.py:44
  233.3 57.0 %shard_map.203 = (f32[4,2,256,1024]{3,2,1,0:T(8,128)}, f32[4,2,256,1024]{3,2,1,0:T(8,128)}, bf16[8,4,128,768]{3,2,1,0:T(8,128)(2,1)}) custom-call(s32[1]{0:T(128)} %bitcast.1.side_ref, bf16[8,256,1024]{2,1,0:T(8,128)(2,1)} %bitcast.183, bf16[8,256,1024]{2,1,0:T(8,128)(2,1)} %collective-permute-done.30.xb_ref.gb_ref, bf16[8,256,1024]{2,1,0:T(8,128)(2,1)} %bitcast.184, ...), custom_call_target="tpu_custom_call" | custom-call | flops 6442450944 | bytes 1048576 | tf_op jit(solution)/shard_map/pallas_call | solution.py:324
  290.4 55.4 %shard_map.204 = (f32[4,256,1024]{2,1,0:T(8,128)}, bf16[4,256,1024]{2,1,0:T(8,128)(2,1)}, f32[4,256,1024]{2,1,0:T(8,128)}, bf16[4,256,1024]{2,1,0:T(8,128)(2,1)}, bf16[8,4,128,768]{3,2,1,0:T(8,128)(2,1)}) custom-call(s32[1]{0:T(128)} %bitcast.1.side_ref, bf16[8,256,1024]{2,1,0:T(8,128)(2,1)} %shard_map.200.xa_ref.ga_ref, ...), custom_call_target="tpu_custom_call" | custom-call | flops 6442450944 | bytes 1048576 | tf_op jit(solution)/shard_map/pallas_call | solution.py:324
  346.4 3.9 collective-permute-done.31
  358.8 57.6 %shard_map.205 = (f32[4,256,1024]{2,1,0:T(8,128)}, bf16[4,256,1024]{2,1,0:T(8,128)(2,1)}, f32[4,256,1024]{2,1,0:T(8,128)}, bf16[4,256,1024]{2,1,0:T(8,128)(2,1)}, bf16[8,4,128,768]{3,2,1,0:T(8,128)(2,1)}) custom-call(s32[1]{0:T(128)} %bitcast.1.side_ref, bf16[8,256,1024]{2,1,0:T(8,128)(2,1)} %bitcast.185, ...), custom_call_target="tpu_custom_call" | custom-call | flops 6442450944 | bytes 1048576 | tf_op jit(solution)/shard_map/pallas_call | solution.py:324
  417.7 4.7 fusion.10
  424.5 3.5 collective-permute-done.36
  429.3 9.0 %collective-permute-done.37.rest_1_ = bf16[256,1024]{1,0:T(8,128)(2,1)} collective-permute-done((bf16[256,1024]{1,0:T(8,128)(2,1)S(1)}, bf16[256,1024]{1,0:T(8,128)(2,1)}, u32[]{:S(2)}, u32[]{:S(2)}) %collective-permute-start.37) | collective-permute-done | bytes 524320 | tf_op jit(solution)/shard_map/ppermute | solution.py:44
  442.4 20.4 %shard_map.206 = (f32[1024,768]{1,0:T(8,128)}, f32[2,256,1024]{2,1,0:T(8,128)}, bf16[2,256,1024]{2,1,0:T(8,128)(2,1)}, f32[1,1024]{1,0:T(1,128)}) custom-call(s32[4]{0:T(128)} %pad_add_fusion.spots_ref, s32[8]{0:T(128)} %stack.144.block_spots_ref, bf16[256,1024]{1,0:T(8,128)(2,1)} %copy-done.48, bf16[256,1024]{1,0:T(8,128)(2,1)} %collective-permute-done.37.rest_1_, ...), custom_call_target="tpu_custom_call" | custom-call | flops 4294967296 | bytes 1048576 | tf_op jit(solution)/shard_map/pallas_call | solution.py:512
  477.4 11.7 %collective-permute-done.47.refs_1_ = bf16[4,128,768]{2,1,0:T(8,128)(2,1)S(1)} collective-permute-done((bf16[4,128,768]{2,1,0:T(8,128)(2,1)S(1)}, bf16[4,128,768]{2,1,0:T(8,128)(2,1)S(1)}, u32[]{:S(2)}, u32[]{:S(2)}) %collective-permute-start.47) | collective-permute-done | bytes 786464 | tf_op jit(solution)/shard_map/ppermute | solution.py:44
  493.4 22.1 %shard_map.207 = (f32[4,128,768]{2,1,0:T(8,128)}, bf16[4,128,768]{2,1,0:T(8,128)(2,1)}, f32[2,256,1024]{2,1,0:T(8,128)}, bf16[2,256,1024]{2,1,0:T(8,128)(2,1)}, f32[1,1024]{1,0:T(1,128)}) custom-call(s32[4]{0:T(128)} %pad_add_fusion.spots_ref, s32[8]{0:T(128)} %stack.144.block_spots_ref, bf16[256,1024]{1,0:T(8,128)(2,1)} %copy-done.49, ...), custom_call_target="tpu_custom_call" | custom-call | flops 4294967296 | bytes 1048576 | tf_op jit(solution)/shard_map/pallas_call | solution.py:512
  533.3 3.9 collective-permute-start.59
  540.0 5.3 collective-permute-done.57
  560.8 8.7 %collective-permute-done.63 = bf16[128,768]{1,0:T(8,128)(2,1)S(1)} collective-permute-done((bf16[128,768]{1,0:T(8,128)(2,1)S(1)}, bf16[128,768]{1,0:T(8,128)(2,1)S(1)}, u32[]{:S(2)}, u32[]{:S(2)}) %collective-permute-start.63) | collective-permute-done | bytes 196640 | tf_op jit(solution)/shard_map/ppermute | solution.py:90
  569.5 5.2 collective-permute-done.60.refs_3_
  (340 shorter events, 172.2 us)
Async XLA Ops:
  7.2 160.0 %all-gather.5.cloned.1.call-start = ((), (), s32[]{:S(2)}) async-start(), calls=%async_computation.4 | async-start | bytes 7864320 | tf_op jit(solution)/shard_map/all_gather | solution.py:564
  11.8 25.1 %collective-permute-start.4 = (bf16[4,128,768]{2,1,0:T(8,128)(2,1)}, bf16[4,128,768]{2,1,0:T(8,128)(2,1)S(1)}, u32[]{:S(2)}, u32[]{:S(2)}) collective-permute-start(bf16[4,128,768]{2,1,0:T(8,128)(2,1)} %get-tuple-element.166), channel_id=1, source_target_pairs={{0,4},{4,0},{1,5},{5,1},{2,6},{6,2},{3,7},{7,3},{8,12},{12,8},{9,1... | collective-permute-start | bytes 2359304 | tf_op jit(solution)/shard_map/ppermute | solution.py:44
  38.3 252.1 %all-gather.7.cloned.1.call-start = ((), (), s32[]{:S(2)}) async-start(), calls=%async_computation.5 | async-start | bytes 7864320 | tf_op jit(solution)/shard_map/all_gather | solution.py:564
  52.5 21.8 %collective-permute-start.13 = (bf16[256,1024]{1,0:T(8,128)(2,1)S(1)}, bf16[256,1024]{1,0:T(8,128)(2,1)S(1)}, u32[]{:S(2)}, u32[]{:S(2)}) collective-permute-start(bf16[256,1024]{1,0:T(8,128)(2,1)S(1)} %get-tuple-element.208.refs_1_), channel_id=1, source_target_pairs={{0,2},{2,0},{1,3},{3,1},{4,6},{6,4},{5,7},{7,5},{8,10},{10,8},{9,1... | collective-permute-start | bytes 1572872 | tf_op jit(solution)/shard_map/ppermute | solution.py:44
  98.5 39.9 %collective-permute-start.24 = (bf16[4,128,768]{2,1,0:T(8,128)(2,1)}, bf16[4,128,768]{2,1,0:T(8,128)(2,1)}, u32[]{:S(2)}, u32[]{:S(2)}) collective-permute-start(bf16[4,128,768]{2,1,0:T(8,128)(2,1)} %get-tuple-element.213), channel_id=1, source_target_pairs={{0,4},{4,0},{1,5},{5,1},{2,6},{6,2},{3,7},{7,3},{8,12},{12,8},{9,1... | collective-permute-start | bytes 2359304 | tf_op jit(solution)/shard_map/ppermute | solution.py:44
  104.5 33.9 %collective-permute-start.22 = (bf16[256,1024]{1,0:T(8,128)(2,1)S(1)}, bf16[256,1024]{1,0:T(8,128)(2,1)S(1)}, u32[]{:S(2)}, u32[]{:S(2)}) collective-permute-start(bf16[256,1024]{1,0:T(8,128)(2,1)S(1)} %multiply_convert_fusion.2.refs_0_), channel_id=1, source_target_pairs={{0,2},{2,0},{1,3},{3,1},{4,6},{6,4},{5,7},{7,5},{8,10},{10,8},{9,1... | collective-permute-start | bytes 1572872 | tf_op jit(solution)/shard_map/ppermute | solution.py:44
  105.1 33.3 %collective-permute-start.21 = (bf16[256,1024]{1,0:T(8,128)(2,1)S(1)}, bf16[256,1024]{1,0:T(8,128)(2,1)S(1)}, u32[]{:S(2)}, u32[]{:S(2)}) collective-permute-start(bf16[256,1024]{1,0:T(8,128)(2,1)S(1)} %multiply_convert_fusion.2.refs_0_), channel_id=1, source_target_pairs={{0,4},{4,0},{1,5},{5,1},{2,6},{6,2},{3,7},{7,3},{8,12},{12,8},{9,1... | collective-permute-start | bytes 1572872 | tf_op jit(solution)/shard_map/ppermute | solution.py:44
  105.7 32.7 %collective-permute-start.20 = (bf16[256,1024]{1,0:T(8,128)(2,1)}, bf16[256,1024]{1,0:T(8,128)(2,1)}, u32[]{:S(2)}, u32[]{:S(2)}) collective-permute-start(bf16[256,1024]{1,0:T(8,128)(2,1)} %fusion.14), channel_id=1, source_target_pairs={{0,2},{2,0},{1,3},{3,1},{4,6},{6,4},{5,7},{7,5},{8,10},{10,8},{9,1... | collective-permute-start | bytes 1572872 | tf_op jit(solution)/shard_map/ppermute | solution.py:44
  110.5 22.3 %collective-permute-start.23 = (f32[16,2048]{1,0:T(8,128)}, f32[16,2048]{1,0:T(8,128)}, u32[]{:S(2)}, u32[]{:S(2)}) collective-permute-start(f32[16,2048]{1,0:T(8,128)} %reshape.192), channel_id=1, source_target_pairs={{0,4},{4,0},{1,5},{5,1},{2,6},{6,2},{3,7},{7,3},{8,12},{12,8},{9,1... | collective-permute-start | bytes 393224 | tf_op jit(solution)/shard_map/ppermute | solution.py:44
  159.7 256.8 %reduce-scatter.3.cloned.1.call-start = ((), (), s32[]{:S(2)}) async-start(), calls=%async_computation.2 | async-start | bytes 7864320 | tf_op jit(solution)/shard_map/reduce_scatter | solution.py:689
  160.0 62.7 %collective-permute-start.29 = (bf16[2,256,1024]{2,1,0:T(8,128)(2,1)S(1)}, bf16[2,256,1024]{2,1,0:T(8,128)(2,1)S(1)}, u32[]{:S(2)}, u32[]{:S(2)}) collective-permute-start(bf16[2,256,1024]{2,1,0:T(8,128)(2,1)S(1)} %shard_map.199.refs_0_), channel_id=1, source_target_pairs={{0,6},{2,4},{4,2},{6,0},{1,7},{3,5},{5,3},{7,1},{8,14},{10,12},{12... | collective-permute-start | bytes 3145736 | tf_op jit(solution)/shard_map/ppermute | solution.py:56
  161.5 61.2 %collective-permute-start.28 = (bf16[2,256,1024]{2,1,0:T(8,128)(2,1)S(1)}, bf16[2,256,1024]{2,1,0:T(8,128)(2,1)S(1)}, u32[]{:S(2)}, u32[]{:S(2)}) collective-permute-start(bf16[2,256,1024]{2,1,0:T(8,128)(2,1)S(1)} %shard_map.199.refs_0_), channel_id=1, source_target_pairs={{0,2},{2,0},{1,3},{3,1},{4,6},{6,4},{5,7},{7,5},{8,10},{10,8},{9,1... | collective-permute-start | bytes 3145736 | tf_op jit(solution)/shard_map/ppermute | solution.py:44
  163.0 59.7 %collective-permute-start.27 = (bf16[2,256,1024]{2,1,0:T(8,128)(2,1)S(1)}, bf16[2,256,1024]{2,1,0:T(8,128)(2,1)}, u32[]{:S(2)}, u32[]{:S(2)}) collective-permute-start(bf16[2,256,1024]{2,1,0:T(8,128)(2,1)S(1)} %shard_map.199.refs_0_), channel_id=1, source_target_pairs={{0,4},{4,0},{1,5},{5,1},{2,6},{6,2},{3,7},{7,3},{8,12},{12,8},{9,1... | collective-permute-start | bytes 3145736 | tf_op jit(solution)/shard_map/ppermute | solution.py:44
  290.4 254.9 %reduce-scatter.5.cloned.1.call-start = ((), (), s32[]{:S(2)}) async-start(), calls=%async_computation.3 | async-start | bytes 7864320 | tf_op jit(solution)/shard_map/reduce_scatter | solution.py:689
  355.2 61.2 %collective-permute-start.33 = (bf16[2,256,1024]{2,1,0:T(8,128)(2,1)S(1)}, bf16[2,256,1024]{2,1,0:T(8,128)(2,1)}, u32[]{:S(2)}, u32[]{:S(2)}) collective-permute-start(bf16[2,256,1024]{2,1,0:T(8,128)(2,1)S(1)} %get-tuple-element.241), channel_id=1, source_target_pairs={{0,4},{4,0},{1,5},{5,1},{2,6},{6,2},{3,7},{7,3},{8,12},{12,8},{9,1... | collective-permute-start | bytes 3145736 | tf_op jit(solution)/shard_map/ppermute | solution.py:44
  356.5 59.9 %collective-permute-start.34 = (bf16[2,256,1024]{2,1,0:T(8,128)(2,1)S(1)}, bf16[2,256,1024]{2,1,0:T(8,128)(2,1)}, u32[]{:S(2)}, u32[]{:S(2)}) collective-permute-start(bf16[2,256,1024]{2,1,0:T(8,128)(2,1)S(1)} %get-tuple-element.242), channel_id=1, source_target_pairs={{0,2},{2,0},{1,3},{3,1},{4,6},{6,4},{5,7},{7,5},{8,10},{10,8},{9,1... | collective-permute-start | bytes 3145736 | tf_op jit(solution)/shard_map/ppermute | solution.py:44
  356.7 59.7 %collective-permute-start.35 = (bf16[2,256,1024]{2,1,0:T(8,128)(2,1)S(1)}, bf16[2,256,1024]{2,1,0:T(8,128)(2,1)}, u32[]{:S(2)}, u32[]{:S(2)}) collective-permute-start(bf16[2,256,1024]{2,1,0:T(8,128)(2,1)S(1)} %pad_maximum_fusion.5), channel_id=1, source_target_pairs={{0,6},{2,4},{4,2},{6,0},{1,7},{3,5},{5,3},{7,1},{8,14},{10,12},{12... | collective-permute-start | bytes 3145736 | tf_op jit(solution)/shard_map/ppermute | solution.py:56
  438.3 24.5 %collective-permute-start.39 = (bf16[256,1024]{1,0:T(8,128)(2,1)S(1)}, bf16[256,1024]{1,0:T(8,128)(2,1)S(1)}, u32[]{:S(2)}, u32[]{:S(2)}) collective-permute-start(bf16[256,1024]{1,0:T(8,128)(2,1)S(1)} %get-tuple-element.258), channel_id=1, source_target_pairs={{0,4},{4,0},{1,5},{5,1},{2,6},{6,2},{3,7},{7,3},{8,12},{12,8},{9,1... | collective-permute-start | bytes 1572872 | tf_op jit(solution)/shard_map/ppermute | solution.py:44
  439.6 23.2 %collective-permute-start.40 = (bf16[256,1024]{1,0:T(8,128)(2,1)S(1)}, bf16[256,1024]{1,0:T(8,128)(2,1)}, u32[]{:S(2)}, u32[]{:S(2)}) collective-permute-start(bf16[256,1024]{1,0:T(8,128)(2,1)S(1)} %get-tuple-element.259), channel_id=1, source_target_pairs={{0,2},{2,0},{1,3},{3,1},{4,6},{6,4},{5,7},{7,5},{8,10},{10,8},{9,1... | collective-permute-start | bytes 1572872 | tf_op jit(solution)/shard_map/ppermute | solution.py:44
  439.9 25.3 %collective-permute-start.41 = (bf16[256,1024]{1,0:T(8,128)(2,1)S(1)}, bf16[256,1024]{1,0:T(8,128)(2,1)}, u32[]{:S(2)}, u32[]{:S(2)}) collective-permute-start(bf16[256,1024]{1,0:T(8,128)(2,1)S(1)} %get-tuple-element.260), channel_id=1, source_target_pairs={{0,6},{2,4},{4,2},{6,0},{1,7},{3,5},{5,3},{7,1},{8,14},{10,12},{12... | collective-permute-start | bytes 1572872 | tf_op jit(solution)/shard_map/ppermute | solution.py:56
  489.2 26.3 %collective-permute-start.48 = (bf16[256,1024]{1,0:T(8,128)(2,1)}, bf16[256,1024]{1,0:T(8,128)(2,1)S(1)}, u32[]{:S(2)}, u32[]{:S(2)}) collective-permute-start(bf16[256,1024]{1,0:T(8,128)(2,1)} %fusion.21), channel_id=1, source_target_pairs={{0,2},{2,0},{1,3},{3,1},{4,6},{6,4},{5,7},{7,5},{8,10},{10,8},{9,1... | collective-permute-start | bytes 1572872 | tf_op jit(solution)/shard_map/ppermute | solution.py:44
  489.6 26.0 %collective-permute-start.49 = (bf16[256,1024]{1,0:T(8,128)(2,1)}, bf16[256,1024]{1,0:T(8,128)(2,1)}, u32[]{:S(2)}, u32[]{:S(2)}) collective-permute-start(bf16[256,1024]{1,0:T(8,128)(2,1)} %get-tuple-element.280), channel_id=1, source_target_pairs={{0,4},{4,0},{1,5},{5,1},{2,6},{6,2},{3,7},{7,3},{8,12},{12,8},{9,1... | collective-permute-start | bytes 1572872 | tf_op jit(solution)/shard_map/ppermute | solution.py:44
  490.9 24.7 %collective-permute-start.50 = (bf16[256,1024]{1,0:T(8,128)(2,1)}, bf16[256,1024]{1,0:T(8,128)(2,1)}, u32[]{:S(2)}, u32[]{:S(2)}) collective-permute-start(bf16[256,1024]{1,0:T(8,128)(2,1)} %get-tuple-element.281), channel_id=1, source_target_pairs={{0,2},{2,0},{1,3},{3,1},{4,6},{6,4},{5,7},{7,5},{8,10},{10,8},{9,1... | collective-permute-start | bytes 1572872 | tf_op jit(solution)/shard_map/ppermute | solution.py:44
  545.3 24.2 %collective-permute-start.61 = (bf16[256,1024]{1,0:T(8,128)(2,1)}, bf16[256,1024]{1,0:T(8,128)(2,1)S(1)}, u32[]{:S(2)}, u32[]{:S(2)}) collective-permute-start(bf16[256,1024]{1,0:T(8,128)(2,1)} %get-tuple-element.307), channel_id=1, source_target_pairs={{0,6},{2,4},{4,2},{6,0},{1,7},{3,5},{5,3},{7,1},{8,14},{10,12},{12... | collective-permute-start | bytes 1572872 | tf_op jit(solution)/shard_map/ppermute | solution.py:56
  (111 other events, 834.2 us)
Sparse Core Ops, SparseCore 0:
  38.4 116.3 all-gather.4
  159.8 117.3 all-gather.6
  290.5 112.3 reduce-scatter.2
  416.6 112.3 reduce-scatter.4

commit v6 on v5

--- a/solution.py
+++ b/solution.py
@@ -10,7 +10,7 @@
 
 HD = 64
 E = 32
-CHUNKS = (4, 4)
+CHUNKS = (8, 8)
 
 EPSILON = 1e-06
 BF = jnp.bfloat16
@@ -133,27 +133,25 @@
 
 def pack_kernel(side_ref, gate_up_ref, down_ref, *rest):
     *outs, rows_scr = rest
-    blk = down_ref.shape[2]
+    hidden_local, blk = down_ref.shape[1:]
     offset = 0
     for mine_ref, theirs_ref in zip(outs[::2], outs[1::2]):
-        pairs = mine_ref.shape[0]
-        hidden_local = mine_ref.shape[2] // 6
+        count = mine_ref.shape[1] // (3 * hidden_local)
         for out_ref, half in ((theirs_ref, 1 - side_ref[0]), (mine_ref, side_ref[0])):
-            for p in range(pairs):
-                for i in range(2):
-                    expert = half * (E // 2) + 2 * (offset + p) + i
-                    rows_scr[...] = gate_up_ref[expert].astype(FP)
-                    for part in range(2):
-                        cols = slice((2 * part + i) * hidden_local, (2 * part + i + 1) * hidden_local)
-                        out_ref[p, :, cols] = rows_scr[pl.ds(part, blk, stride=2), :].astype(BF)
-                    cols = slice((4 + i) * hidden_local, (5 + i) * hidden_local)
-                    out_ref[p, :, cols] = down_ref[expert].astype(FP).T.astype(BF)
-        offset += pairs
+            for i in range(count):
+                expert = half * (E // 2) + offset + i
+                rows_scr[...] = gate_up_ref[expert].astype(FP)
+                values = [rows_scr[pl.ds(part, blk, stride=2), :] for part in range(2)]
+                values.append(down_ref[expert].astype(FP).T)
+                for part, value in enumerate(values):
+                    start = (part * count + i) * hidden_local
+                    out_ref[:, start : start + hidden_local] = value.astype(BF)
+        offset += count
 
 
 def pack_experts(side, w_gate_up, w_down):
     experts, blk, _, hidden_local = w_gate_up.shape
-    shapes = [jax.ShapeDtypeStruct((pairs, blk, 6 * hidden_local), BF) for pairs in CHUNKS]
+    shapes = [jax.ShapeDtypeStruct((blk, 3 * count * hidden_local), BF) for count in CHUNKS]
     outs = pl.pallas_call(
         pack_kernel,
         in_specs=[SMEM, VMEM, VMEM],
@@ -168,26 +166,26 @@
 
 def unpack_kernel(side_ref, *refs):
     *ins, gate_up_ref, down_ref = refs
-    blk = down_ref.shape[2]
+    hidden_local, blk = down_ref.shape[1:]
     offset = 0
     for kept_ref, got_ref in zip(ins[::2], ins[1::2]):
-        pairs = got_ref.shape[0]
-        hidden_local = got_ref.shape[2] // 6
+        count = got_ref.shape[1] // (3 * hidden_local)
         for mine, half in ((True, side_ref[0]), (False, 1 - side_ref[0])):
-            for p in range(pairs):
-                packed = (kept_ref[0, p] if mine else got_ref[p]).astype(FP)
-                for i in range(2):
-                    expert = half * (E // 2) + 2 * (offset + p) + i
-                    for part in range(2):
-                        cols = slice((2 * part + i) * hidden_local, (2 * part + i + 1) * hidden_local)
-                        gate_up_ref[expert, pl.ds(part, blk, stride=2), :] = packed[:, cols]
-                    down_ref[expert] = packed[:, (4 + i) * hidden_local : (5 + i) * hidden_local].T
-        offset += pairs
-
-
-def unpack_experts(side, shards):
-    blk, width = shards[0][1].shape[1:]
-    hidden_local = width // 6
+            for i in range(count):
+                expert = half * (E // 2) + offset + i
+                values = []
+                for part in range(3):
+                    start = (part * count + i) * hidden_local
+                    cols = slice(start, start + hidden_local)
+                    values.append((kept_ref[0, :, cols] if mine else got_ref[:, cols]).astype(FP))
+                for part in range(2):
+                    gate_up_ref[expert, pl.ds(part, blk, stride=2), :] = values[part]
+                down_ref[expert] = values[2].T
+        offset += count
+
+
+def unpack_experts(side, hidden_local, shards):
+    blk = shards[0][1].shape[0]
     operands = [array for shard in shards for array in shard]
     gate_up, down = pl.pallas_call(
         unpack_kernel,
@@ -226,14 +224,12 @@
     rest = list(rest)
     sums_in = [] if first else [rest.pop(0), rest.pop(0)]
     earlier_ref = None if start else rest.pop(0)
-    acc = rest.pop()
-    grads_ref = rest.pop()
-    sums_out = rest
+    sums_out, (grads_ref, acc, hidden_scr, pair_scr, sem) = rest[:-5], rest[-5:]
     step = pl.program_id(0)
-    blocks, pairs, blk, width = w_ref.shape
-    model_width = blocks * blk
-    half = width // 3
-    hidden_local = half // 2
+    blocks, blk, width = w_ref.shape
+    third = width // 3
+    hidden_local = third // CHUNKS[0]
+    part = min(2 * hidden_local, third)
 
     def spot(block):
         place = (block // 2) * 2 + (side_ref[0] + block % 2) % 2
@@ -241,44 +237,40 @@
 
     @pl.when(step == 0)
     def _():
-        if start:
-            acc[...] = jnp.zeros_like(acc)
-        else:
-            for p in range(pairs):
-                for block in range(blocks):
-                    acc[p, spot(block), :] = earlier_ref[block, p].astype(FP)
+        if not start:
+            pltpu.make_async_copy(earlier_ref, grads_ref, sem).start()
+        acc[...] = jnp.zeros_like(acc)
 
     x = jnp.concatenate([xa_ref[...], xb_ref[...]], axis=0)
     g = jnp.concatenate([ga_ref[...], gb_ref[...]], axis=0)
     gates = gate_ref[...].reshape(x.shape[0], gate_ref.shape[-1])
-    totals = [None, None]
-    for p in range(pairs):
-        weights = w_ref[:, p].reshape(model_width, width)
-        pre = dot_nn(x, weights[:, : 2 * half])
-        out_back = dot_nn(g, weights[:, 2 * half :])
-        gate = pre[:, :half]
-        up = pre[:, half:]
+    weights = w_ref.reshape(blocks * blk, width)
+    for p in range(0, third, part):
+        own, up_cols = slice(p, p + part), slice(third + p, third + p + part)
+        gate = dot_nn(x, weights[:, own])
+        up = dot_nn(x, weights[:, up_cols])
+        out_back = dot_nn(g, weights[:, 2 * third + p : 2 * third + p + part])
         sig = 0.5 + 0.5 * jnp.tanh(0.5 * gate)
         share = jnp.concatenate(
             [
                 jnp.broadcast_to(gates[:, i : i + 1], (x.shape[0], hidden_local))
-                for i in (column + 2 * p, column + 2 * p + 1)
+                for i in range(column + p // hidden_local, column + (p + part) // hidden_local)
             ],
             axis=1,
         )
         silu = gate * sig
-        hidden = (share * (silu * up)).astype(BF)
         hidden_grad = share * out_back
-        gate_grad = (hidden_grad * up * (sig + silu * (1.0 - sig))).astype(BF)
-        up_grad = (hidden_grad * silu).astype(BF)
-        pair_grad = jnp.concatenate([gate_grad, up_grad], axis=1)
-        terms = (
-            dot_nt(hidden, weights[:, 2 * half :]),
-            dot_nt(pair_grad, weights[:, : 2 * half]),
-        )
-        totals = [t if s is None else s + t for s, t in zip(totals, terms)]
-        acc[p, :, : 2 * half] += dot_tn(x, pair_grad)
-        acc[p, :, 2 * half :] += dot_tn(g, hidden)
+        hidden_scr[:, own] = (share * (silu * up)).astype(BF)
+        pair_scr[:, own] = (hidden_grad * up * (sig + silu * (1.0 - sig))).astype(BF)
+        pair_scr[:, up_cols] = (hidden_grad * silu).astype(BF)
+    hidden = hidden_scr[...]
+    pair_grad = pair_scr[...]
+    totals = [
+        dot_nt(hidden, weights[:, 2 * third :]),
+        dot_nt(pair_grad, weights[:, : 2 * third]),
+    ]
+    acc[:, : 2 * third] += dot_tn(x, pair_grad)
+    acc[:, 2 * third :] += dot_tn(g, hidden)
     if not first:
         totals = [s[...].reshape(t.shape) + t for s, t in zip(sums_in, totals)]
     if last:
@@ -292,15 +284,19 @@
 
     @pl.when(step == pl.num_programs(0) - 1)
     def _():
-        for p in range(pairs):
-            for block in range(blocks):
-                grads_ref[block, p] = acc[p, spot(block), :].astype(BF)
+        if not start:
+            pltpu.make_async_copy(earlier_ref, grads_ref, sem).wait()
+        for block in range(blocks):
+            value = acc[spot(block), :]
+            if not start:
+                value = value + grads_ref[block].astype(FP)
+            grads_ref[block] = value.astype(BF)
 
 
 def moe_chunk(side, rows_in, gates, weights, sums, earlier, micro, column, last):
     count, rows, model_width = rows_in[0].shape
     count //= 2
-    blocks, pairs, blk, width = weights.shape
+    blocks, blk, width = weights.shape
     once = pl.Buffered(1)
     tile = min(128, rows)
     parts = rows // tile
@@ -311,7 +307,7 @@
     gate_spec = pl.BlockSpec(
         (None, None, 2, tile, gates.shape[-1]), lambda i: (micro, i // parts, 0, i % parts, 0)
     )
-    whole = pl.BlockSpec(weights.shape, lambda i: (0, 0, 0, 0), pipeline_mode=once)
+    whole = pl.BlockSpec(weights.shape, lambda i: (0, 0, 0), pipeline_mode=once)
     first, start = sums is None, earlier is None
     operands = [side, *rows_in, *rows_in, gates, weights] + ([] if first else list(sums))
     operands += [] if start else [earlier]
@@ -326,9 +322,14 @@
         grid=(count * parts,),
         in_specs=[SMEM, x_half, x_half, g_half, g_half, gate_spec, whole]
         + ([] if first else [row, row])
-        + ([] if start else [whole]),
+        + ([] if start else [pl.BlockSpec(memory_space=pl.ANY)]),
         out_specs=out_specs + [whole],
-        scratch_shapes=[pltpu.VMEM((pairs, model_width, width), FP)],
+        scratch_shapes=[
+            pltpu.VMEM((model_width, width), FP),
+            pltpu.VMEM((2 * tile, width // 3), BF),
+            pltpu.VMEM((2 * tile, 2 * width // 3), BF),
+            pltpu.SemaphoreType.DMA,
+        ],
         out_shape=outs + [jax.ShapeDtypeStruct(weights.shape, BF)],
         input_output_aliases={} if first or last else {7: 0, 8: 1},
         compiler_params=pltpu.CompilerParams(vmem_limit_bytes=60 << 20),
@@ -653,7 +654,7 @@
     turn = after(side_at, shards[1])
     all_grads = []
     first_expert = 0
-    for chunk, pairs in enumerate(CHUNKS):
+    for chunk, count in enumerate(CHUNKS):
         last = chunk == len(CHUNKS) - 1
         grads = None
         for m in range(micro_count):
@@ -682,7 +683,7 @@
                 came = to_neighbours(along)
             else:
                 turn = after(side_at, *waited)
-        first_expert += 2 * pairs
+        first_expert += count
         all_grads.append(grads.reshape(depth, 2, *grads.shape[1:]))
 
     def reduce_grads(grads):
@@ -709,12 +710,17 @@
         *came, all_grads[1], sums[1][2], sums[1][3], *sums[1][:2], grad_shards[0]
     )
     grad_shards = [first_shard, reduce_grads(grads)]
-    outputs = [(middle[0] + sum_of(mixed_own, [c[1] for c in came])).astype(BF)]
+    first_came, first_mixed_own = came, mixed_own
     middle_grad, low, gain_moe = middle_back(0, own, [c[0] for c in came])
     shard_got = [swap(first_shard[1], "y")]
     across, near_rows = swap(low, "x"), swap(low, "c")
-    own, along = half_sums(kept, after(sent, low))
-    across, near_rows, *along = together(across, near_rows, *along)
+    last_mixed_sent, sent, _ = together(last_mixed_sent, sent, low)
+    own, along = half_sums(kept, sent)
+    mixed_own, mixed_along = half_sums(last_mixed_kept, last_mixed_sent)
+    across, near_rows, shard_got[0], *along = together(
+        across, near_rows, shard_got[0], *along, *mixed_along
+    )
+    along, mixed_along = along[:3], along[3:]
     far_rows = swap(across, "c")
     came = to_neighbours(along)
     results = backward(0, spots, [low, across, near_rows, far_rows], None)
@@ -726,44 +732,45 @@
     gain_moe = gain_moe + gain
     across, near_rows = swap(low, "x"), swap(low, "c")
     input_own, input_along = half_sums(kept, sent)
-    mixed_own, mixed_along = half_sums(last_mixed_kept, after(last_mixed_sent, low))
-    across, near_rows, *mixed_along, input_along, shard_got[0], outputs[0] = together(
-        across, near_rows, *mixed_along, *input_along, shard_got[0], outputs[0]
+    across, near_rows, input_along, *mixed_along = together(
+        across, near_rows, *input_along, *mixed_along
     )
     far_rows = swap(across, "c")
     input_came = swap(input_along, "x")
-    mixed_came = [swap(mixed_along[0], "y"), swap(mixed_along[1], "x")]
+    mixed_came = [swap(mixed_along[0], "y"), cross(mixed_along[2])]
     results = backward(1, spots, [low, across, near_rows, far_rows], earlier)
-    input_came, *mixed_came, grads_kept, grads_sent, kept, sent, gain = together(
-        input_came, *mixed_came, *results
-    )
+    input_came, (mixed_came, results, first_came) = together(
+        input_came, (mixed_came, results, first_came)
+    )
+    grads_kept, grads_sent, kept, sent, gain = results
 
     gains = jnp.concatenate([(gain_attn + gain)[0] / norm_attn, gain_moe]).reshape(16, -1)
+    grads_got = swap(grads_sent, "y")
     own, along = half_sums(kept, sent)
     first_input = input_back(0, middle_grads[0], input_own, input_came)
-    for axis in ("c", "x", "y"):
+    outputs = [(middle[0] + sum_of(first_mixed_own, [c[1] for c in first_came])).astype(BF)]
+    for axis in ("c", "x"):
         gains = gains + swap(gains, axis)
-    along, gains, first_input, grads_sent, diagonal = together(
-        along[0], gains, first_input, grads_sent, mixed_along[2]
-    )
-    input_came, grads_got = swap(along, "x"), swap(grads_sent, "y")
-    gains = sum_over_z(gains, depth).reshape(2, model_width)
-    input_came, grads_got, gains, last_shard, diagonal = together(
-        input_came, grads_got, gains, grad_shards[1], diagonal
-    )
+    gains, mixed_along = together(gains, mixed_along[1])
+    mixed_came.append(swap(mixed_along, "x"))
+    gains = sum_over_z(gains, depth)
+    along, gains, first_input, outputs[0], grads_got, last_shard, mixed_came[2] = together(
+        along[0], gains, first_input, outputs[0], grads_got, grad_shards[1], mixed_came[2]
+    )
+    input_came = swap(along, "x")
     shard_got.append(swap(last_shard[1], "y"))
-    diagonal = cross(diagonal)
     column = grads_kept + grads_got.astype(FP)
     pieces = along_z_sent(column, depth)
     last_input = input_back(1, middle_grads[1], own, input_came)
-    shard_got[1], diagonal, last_input, *pieces = together(
-        shard_got[1], diagonal, last_input, *pieces
-    )
+    outputs.append((middle[1] + sum_of(mixed_own, mixed_came)).astype(BF))
+    last_input, outputs[1], shard_got[1], gains, *pieces = together(
+        last_input, outputs[1], shard_got[1], gains, *pieces
+    )
+    gains = (gains + swap(gains, "y")).reshape(2, model_width)
     shard_pair, shard_down = unpack_experts(
-        side_at, list(zip([grad_shards[0], last_shard], shard_got))
+        side_at, w_down.shape[1], list(zip([grad_shards[0], last_shard], shard_got))
     )
     attn_shard = sum_of(column[0], pieces)
-    outputs.append((middle[1] + sum_of(mixed_own, [*mixed_came, diagonal])).astype(BF))
     input_grads = [first_input, last_input]
     return (
         jnp.stack(outputs),

time: 599 us -> 569 us (0.950)
  Pallas kernels: 303 us -> 283 us
  waiting for transfers between devices: 129 us -> 121 us
  local copies, waits for them, and re-layouts: 30.7 us -> 24.4 us
    pallas_call x4, Pallas kernels: 225 us -> 206 us  [moe_chunk(): pl.pallas_call(functools.partial(moe_kernel, first, last, start, column),...]
    unnamed x133 -> x127, local copies, waits for them, and re-layouts: 16.1 us -> 14.2 us
  transfers between devices with their start and end apart: 69 -> 69, of which waited for: 26 -> 24; matrix products, arithmetic and copies ran while one was open for 10% -> 11% of each run, Pallas kernels for 50% -> 50%
where the time goes in v6:
time: 569 us; the launch traced here: 565 us
  Pallas kernels  283 us (50%)
  waiting for transfers between devices  121 us (21%)
  starting transfers between devices  67.4 us (12%)
  other arithmetic  54.1 us (10%)
  local copies, waits for them, and re-layouts  24.4 us (4%)
  between operations  15 us (3%)
    pallas_call x4, Pallas kernels, moe_chunk(): pl.pallas_call(functools.partial(moe_kernel, first, last, start, column),...  206 us
    ppermute x51, waiting for transfers between devices, swap(): return lax.ppermute(value, axis, [(0, 1), (1, 0)])  88.8 us
    pallas_call x2, Pallas kernels, attn_backward(): pl.pallas_call(functools.partial(attn_backward_kernel, widths, first), in...  42.6 us
    ppermute x51, starting transfers between devices, swap(): return lax.ppermute(value, axis, [(0, 1), (1, 0)])  41.1 us
    pallas_call x2, Pallas kernels, attn_forward(): pl.pallas_call(functools.partial(attn_forward_kernel, widths, len(weights...  23.4 us
    unnamed x127, local copies, waits for them, and re-layouts  14.2 us
    ppermute x6, waiting for transfers between devices, cross(): return lax.ppermute(value, ('y', 'x'), [(i, 3 - i) for i in range(4)])  12.6 us
  transfers between devices with their start and end apart: 69, of which 24 were waited for; matrix products, arithmetic and copies ran while one was open for 11% of the time, Pallas kernels for 50%

profile of v6, /device:TPU:0, one launch (start us, length us, event | category | flops | bytes accessed | tf_op | source)
XLA Modules:
  0.0 565.1 jit_solution(3799922271982450396)
XLA Ops:
  28.9 10.3 %collective-permute-done.2.rest_7_ = bf16[128,768]{1,0:T(8,128)(2,1)} collective-permute-done((bf16[128,768]{1,0:T(8,128)(2,1)S(1)}, bf16[128,768]{1,0:T(8,128)(2,1)}, u32[]{:S(2)}, u32[]{:S(2)}) %collective-permute-start.2) | collective-permute-done | bytes 196640 | tf_op jit(solution)/shard_map/ppermute | solution.py:84
  45.0 5.9 %collective-permute-done.5.rest_8_ = bf16[128,768]{1,0:T(8,128)(2,1)S(1)} collective-permute-done((bf16[128,768]{1,0:T(8,128)(2,1)}, bf16[128,768]{1,0:T(8,128)(2,1)S(1)}, u32[]{:S(2)}, u32[]{:S(2)}) %collective-permute-start.5) | collective-permute-done | bytes 196640 | tf_op jit(solution)/shard_map/ppermute | solution.py:44
  59.3 3.7 collective-permute-done.8.rest_11_
  64.5 11.9 %shard_map.197 = (bf16[1024,512]{1,0:T(8,128)(2,1)}, bf16[1024,256]{1,0:T(8,128)(2,1)}, f32[2,256,1024]{2,1,0:T(8,128)}, bf16[2,256,1024]{2,1,0:T(8,128)(2,1)}, bf16[1024,768]{1,0:T(8,128)(2,1)}) custom-call(s32[4]{0:T(128)} %pad_add_fusion.spots_ref, s32[8]{0:T(128)} %stack.132.weight_spots_ref, bf16[256,1024]{1,0:T(8,128)(2,1)} %get-tuple-element.417.rest_0_.rest_4_, ...), custom_call_target="tpu_custom_call" | custom-call | flops 15032385536 | bytes 1048576 | tf_op jit(solution)/shard_map/pallas_call | solution.py:478
  88.2 11.5 %shard_map.198 = (bf16[1024,512]{1,0:T(8,128)(2,1)}, bf16[1024,256]{1,0:T(8,128)(2,1)}, f32[2,256,1024]{2,1,0:T(8,128)}, bf16[2,256,1024]{2,1,0:T(8,128)(2,1)}) custom-call(s32[4]{0:T(128)} %pad_add_fusion.spots_ref, s32[8]{0:T(128)} %stack.132.weight_spots_ref, bf16[256,1024]{1,0:T(8,128)(2,1)} %get-tuple-element.187.rest_0_.rest_4_, ...), custom_call_target="tpu_custom_call" | custom-call | flops 15032385536 | bytes 1048576 | tf_op jit(solution)/shard_map/pallas_call | solution.py:478
  112.8 23.6 %collective-permute-done.23 = f32[16,2048]{1,0:T(8,128)S(1)} collective-permute-done((f32[16,2048]{1,0:T(8,128)S(1)}, f32[16,2048]{1,0:T(8,128)S(1)}, u32[]{:S(2)}, u32[]{:S(2)}) %collective-permute-start.23) | collective-permute-done | bytes 131104 | tf_op jit(solution)/shard_map/ppermute | solution.py:44
  146.0 7.2 %collective-permute-done.25.refs_6_ = bf16[256,1024]{1,0:T(8,128)(2,1)} collective-permute-done((bf16[256,1024]{1,0:T(8,128)(2,1)S(1)}, bf16[256,1024]{1,0:T(8,128)(2,1)}, u32[]{:S(2)}, u32[]{:S(2)}) %collective-permute-start.25) | collective-permute-done | bytes 524320 | tf_op jit(solution)/shard_map/ppermute | solution.py:56
  154.3 3.5 shard_map.200.xa_ref.ga_ref
  161.8 3.6 collective-permute-done.26.xb_ref.gb_ref
  165.4 51.0 %shard_map.201 = (f32[4,2,256,1024]{3,2,1,0:T(8,128)}, f32[4,2,256,1024]{3,2,1,0:T(8,128)}, bf16[8,128,3072]{2,1,0:T(8,128)(2,1)}) custom-call(s32[1]{0:T(128)} %bitcast.1.side_ref, bf16[8,256,1024]{2,1,0:T(8,128)(2,1)} %shard_map.200.xa_ref.ga_ref, bf16[8,256,1024]{2,1,0:T(8,128)(2,1)} %collective-permute-done.26.xb_ref.gb_ref, ...), custom_call_target="tpu_custom_call" | custom-call | flops 6442450944 | bytes 1048576 | tf_op jit(solution)/shard_map/pallas_call | solution.py:320
  219.9 7.2 %collective-permute-done.30.xb_ref.gb_ref = bf16[8,256,1024]{2,1,0:T(8,128)(2,1)} collective-permute-done((bf16[8,256,1024]{2,1,0:T(8,128)(2,1)S(1)}, bf16[8,256,1024]{2,1,0:T(8,128)(2,1)}, u32[]{:S(2)}, u32[]{:S(2)}) %collective-permute-start.30) | collective-permute-done | bytes 4194336 | tf_op jit(solution)/shard_map/ppermute | solution.py:44
  227.1 51.4 %shard_map.203 = (f32[4,2,256,1024]{3,2,1,0:T(8,128)}, f32[4,2,256,1024]{3,2,1,0:T(8,128)}, bf16[8,128,3072]{2,1,0:T(8,128)(2,1)}) custom-call(s32[1]{0:T(128)} %bitcast.1.side_ref, bf16[8,256,1024]{2,1,0:T(8,128)(2,1)} %bitcast.182, bf16[8,256,1024]{2,1,0:T(8,128)(2,1)} %collective-permute-done.30.xb_ref.gb_ref, bf16[8,256,1024]{2,1,0:T(8,128)(2,1)} %bitcast.183, ...), custom_call_target="tpu_custom_call" | custom-call | flops 6442450944 | bytes 1048576 | tf_op jit(solution)/shard_map/pallas_call | solution.py:320
  278.6 51.3 %shard_map.204 = (f32[4,256,1024]{2,1,0:T(8,128)}, bf16[4,256,1024]{2,1,0:T(8,128)(2,1)}, f32[4,256,1024]{2,1,0:T(8,128)}, bf16[4,256,1024]{2,1,0:T(8,128)(2,1)}, bf16[8,128,3072]{2,1,0:T(8,128)(2,1)}) custom-call(s32[1]{0:T(128)} %bitcast.1.side_ref, bf16[8,256,1024]{2,1,0:T(8,128)(2,1)} %shard_map.200.xa_ref.ga_ref, ...), custom_call_target="tpu_custom_call" | custom-call | flops 6442450944 | bytes 1048576 | tf_op jit(solution)/shard_map/pallas_call | solution.py:320
  330.5 3.9 collective-permute-done.31
  344.8 52.3 %shard_map.205 = (f32[4,256,1024]{2,1,0:T(8,128)}, bf16[4,256,1024]{2,1,0:T(8,128)(2,1)}, f32[4,256,1024]{2,1,0:T(8,128)}, bf16[4,256,1024]{2,1,0:T(8,128)(2,1)}, bf16[8,128,3072]{2,1,0:T(8,128)(2,1)}) custom-call(s32[1]{0:T(128)} %bitcast.1.side_ref, bf16[8,256,1024]{2,1,0:T(8,128)(2,1)} %bitcast.184, ...), custom_call_target="tpu_custom_call" | custom-call | flops 6442450944 | bytes 1048576 | tf_op jit(solution)/shard_map/pallas_call | solution.py:320
  412.1 7.4 %collective-permute-done.37.rest_1_ = bf16[256,1024]{1,0:T(8,128)(2,1)} collective-permute-done((bf16[256,1024]{1,0:T(8,128)(2,1)S(1)}, bf16[256,1024]{1,0:T(8,128)(2,1)}, u32[]{:S(2)}, u32[]{:S(2)}) %collective-permute-start.37) | collective-permute-done | bytes 524320 | tf_op jit(solution)/shard_map/ppermute | solution.py:44
  419.6 3.7 collective-permute-done.39.refs_1_
  427.4 20.3 %shard_map.206 = (f32[1024,768]{1,0:T(8,128)}, f32[2,256,1024]{2,1,0:T(8,128)}, bf16[2,256,1024]{2,1,0:T(8,128)(2,1)}, f32[1,1024]{1,0:T(1,128)}) custom-call(s32[4]{0:T(128)} %pad_add_fusion.spots_ref, s32[8]{0:T(128)} %stack.144.block_spots_ref, bf16[256,1024]{1,0:T(8,128)(2,1)} %copy-done.42, bf16[256,1024]{1,0:T(8,128)(2,1)} %collective-permute-done.37.rest_1_, ...), custom_call_target="tpu_custom_call" | custom-call | flops 4294967296 | bytes 1048576 | tf_op jit(solution)/shard_map/pallas_call | solution.py:513
  456.4 12.1 %collective-permute-done.45.rest_1_ = bf16[256,1024]{1,0:T(8,128)(2,1)S(1)} collective-permute-done((bf16[256,1024]{1,0:T(8,128)(2,1)S(1)}, bf16[256,1024]{1,0:T(8,128)(2,1)S(1)}, u32[]{:S(2)}, u32[]{:S(2)}) %collective-permute-start.45) | collective-permute-done | bytes 524320 | tf_op jit(solution)/shard_map/ppermute | solution.py:44
  473.0 22.3 %shard_map.207 = (f32[4,128,768]{2,1,0:T(8,128)}, bf16[4,128,768]{2,1,0:T(8,128)(2,1)}, f32[2,256,1024]{2,1,0:T(8,128)}, bf16[2,256,1024]{2,1,0:T(8,128)(2,1)}, f32[1,1024]{1,0:T(1,128)}) custom-call(s32[4]{0:T(128)} %pad_add_fusion.spots_ref, s32[8]{0:T(128)} %stack.144.block_spots_ref, bf16[256,1024]{1,0:T(8,128)(2,1)} %copy-done.45, ...), custom_call_target="tpu_custom_call" | custom-call | flops 4294967296 | bytes 1048576 | tf_op jit(solution)/shard_map/pallas_call | solution.py:513
  502.2 3.5 collective-permute-start.55
  515.5 5.8 %collective-permute-done.58 = bf16[256,1024]{1,0:T(8,128)(2,1)S(1)} collective-permute-done((bf16[256,1024]{1,0:T(8,128)(2,1)S(1)}, bf16[256,1024]{1,0:T(8,128)(2,1)S(1)}, u32[]{:S(2)}, u32[]{:S(2)}) %collective-permute-start.58) | collective-permute-done | bytes 524320 | tf_op jit(solution)/shard_map/ppermute | solution.py:44
  526.0 3.5 collective-permute-start.63
  535.9 9.0 %collective-permute-done.62 = bf16[128,768]{1,0:T(8,128)(2,1)S(1)} collective-permute-done((bf16[128,768]{1,0:T(8,128)(2,1)S(1)}, bf16[128,768]{1,0:T(8,128)(2,1)S(1)}, u32[]{:S(2)}, u32[]{:S(2)}) %collective-permute-start.62) | collective-permute-done | bytes 196640 | tf_op jit(solution)/shard_map/ppermute | solution.py:90
  (334 shorter events, 164.2 us)
Async XLA Ops:
  7.2 158.2 %all-gather.5.cloned.1.call-start = ((), (), s32[]{:S(2)}) async-start(), calls=%async_computation.4 | async-start | bytes 7864320 | tf_op jit(solution)/shard_map/all_gather | solution.py:565
  12.1 27.4 %collective-permute-start.4 = (bf16[128,3072]{1,0:T(8,128)(2,1)S(1)}, bf16[128,3072]{1,0:T(8,128)(2,1)S(1)}, u32[]{:S(2)}, u32[]{:S(2)}) collective-permute-start(bf16[128,3072]{1,0:T(8,128)(2,1)S(1)} %get-tuple-element.171), channel_id=1, source_target_pairs={{0,4},{4,0},{1,5},{5,1},{2,6},{6,2},{3,7},{7,3},{8,12},{12,8},{9,1... | collective-permute-start | bytes 2359304 | tf_op jit(solution)/shard_map/ppermute | solution.py:44
  41.0 237.6 %all-gather.7.cloned.1.call-start = ((), (), s32[]{:S(2)}) async-start(), calls=%async_computation.5 | async-start | bytes 7864320 | tf_op jit(solution)/shard_map/all_gather | solution.py:565
  55.2 21.2 %collective-permute-start.13 = (bf16[256,1024]{1,0:T(8,128)(2,1)S(1)}, bf16[256,1024]{1,0:T(8,128)(2,1)S(1)}, u32[]{:S(2)}, u32[]{:S(2)}) collective-permute-start(bf16[256,1024]{1,0:T(8,128)(2,1)S(1)} %get-tuple-element.213.refs_1_), channel_id=1, source_target_pairs={{0,2},{2,0},{1,3},{3,1},{4,6},{6,4},{5,7},{7,5},{8,10},{10,8},{9,1... | collective-permute-start | bytes 1572872 | tf_op jit(solution)/shard_map/ppermute | solution.py:44
  102.1 36.4 %collective-permute-start.24 = (bf16[128,3072]{1,0:T(8,128)(2,1)}, bf16[128,3072]{1,0:T(8,128)(2,1)}, u32[]{:S(2)}, u32[]{:S(2)}) collective-permute-start(bf16[128,3072]{1,0:T(8,128)(2,1)} %copy-done.8), channel_id=1, source_target_pairs={{0,4},{4,0},{1,5},{5,1},{2,6},{6,2},{3,7},{7,3},{8,12},{12,8},{9,1... | collective-permute-start | bytes 2359304 | tf_op jit(solution)/shard_map/ppermute | solution.py:44
  108.3 30.2 %collective-permute-start.22 = (bf16[256,1024]{1,0:T(8,128)(2,1)S(1)}, bf16[256,1024]{1,0:T(8,128)(2,1)}, u32[]{:S(2)}, u32[]{:S(2)}) collective-permute-start(bf16[256,1024]{1,0:T(8,128)(2,1)S(1)} %multiply_convert_fusion.2.refs_0_), channel_id=1, source_target_pairs={{0,2},{2,0},{1,3},{3,1},{4,6},{6,4},{5,7},{7,5},{8,10},{10,8},{9,1... | collective-permute-start | bytes 1572872 | tf_op jit(solution)/shard_map/ppermute | solution.py:44
  109.4 29.2 %collective-permute-start.21 = (bf16[256,1024]{1,0:T(8,128)(2,1)S(1)}, bf16[256,1024]{1,0:T(8,128)(2,1)}, u32[]{:S(2)}, u32[]{:S(2)}) collective-permute-start(bf16[256,1024]{1,0:T(8,128)(2,1)S(1)} %multiply_convert_fusion.2.refs_0_), channel_id=1, source_target_pairs={{0,4},{4,0},{1,5},{5,1},{2,6},{6,2},{3,7},{7,3},{8,12},{12,8},{9,1... | collective-permute-start | bytes 1572872 | tf_op jit(solution)/shard_map/ppermute | solution.py:44
  110.0 28.5 %collective-permute-start.20 = (bf16[256,1024]{1,0:T(8,128)(2,1)}, bf16[256,1024]{1,0:T(8,128)(2,1)}, u32[]{:S(2)}, u32[]{:S(2)}) collective-permute-start(bf16[256,1024]{1,0:T(8,128)(2,1)} %fusion.14), channel_id=1, source_target_pairs={{0,2},{2,0},{1,3},{3,1},{4,6},{6,4},{5,7},{7,5},{8,10},{10,8},{9,1... | collective-permute-start | bytes 1572872 | tf_op jit(solution)/shard_map/ppermute | solution.py:44
  111.3 25.0 %collective-permute-start.23 = (f32[16,2048]{1,0:T(8,128)S(1)}, f32[16,2048]{1,0:T(8,128)S(1)}, u32[]{:S(2)}, u32[]{:S(2)}) collective-permute-start(f32[16,2048]{1,0:T(8,128)S(1)} %reshape.194), channel_id=1, source_target_pairs={{0,4},{4,0},{1,5},{5,1},{2,6},{6,2},{3,7},{7,3},{8,12},{12,8},{9,1... | collective-permute-start | bytes 393224 | tf_op jit(solution)/shard_map/ppermute | solution.py:44
  157.9 239.2 %reduce-scatter.3.cloned.1.call-start = ((), (), s32[]{:S(2)}) async-start(), calls=%async_computation.2 | async-start | bytes 7864320 | tf_op jit(solution)/shard_map/reduce_scatter | solution.py:690
  158.2 58.2 %collective-permute-start.29 = (bf16[2,256,1024]{2,1,0:T(8,128)(2,1)S(1)}, bf16[2,256,1024]{2,1,0:T(8,128)(2,1)S(1)}, u32[]{:S(2)}, u32[]{:S(2)}) collective-permute-start(bf16[2,256,1024]{2,1,0:T(8,128)(2,1)S(1)} %shard_map.199.refs_0_), channel_id=1, source_target_pairs={{0,6},{2,4},{4,2},{6,0},{1,7},{3,5},{5,3},{7,1},{8,14},{10,12},{12... | collective-permute-start | bytes 3145736 | tf_op jit(solution)/shard_map/ppermute | solution.py:56
  160.3 56.1 %collective-permute-start.28 = (bf16[2,256,1024]{2,1,0:T(8,128)(2,1)S(1)}, bf16[2,256,1024]{2,1,0:T(8,128)(2,1)S(1)}, u32[]{:S(2)}, u32[]{:S(2)}) collective-permute-start(bf16[2,256,1024]{2,1,0:T(8,128)(2,1)S(1)} %shard_map.199.refs_0_), channel_id=1, source_target_pairs={{0,2},{2,0},{1,3},{3,1},{4,6},{6,4},{5,7},{7,5},{8,10},{10,8},{9,1... | collective-permute-start | bytes 3145736 | tf_op jit(solution)/shard_map/ppermute | solution.py:44
  161.3 55.2 %collective-permute-start.27 = (bf16[2,256,1024]{2,1,0:T(8,128)(2,1)S(1)}, bf16[2,256,1024]{2,1,0:T(8,128)(2,1)}, u32[]{:S(2)}, u32[]{:S(2)}) collective-permute-start(bf16[2,256,1024]{2,1,0:T(8,128)(2,1)S(1)} %shard_map.199.refs_0_), channel_id=1, source_target_pairs={{0,4},{4,0},{1,5},{5,1},{2,6},{6,2},{3,7},{7,3},{8,12},{12,8},{9,1... | collective-permute-start | bytes 3145736 | tf_op jit(solution)/shard_map/ppermute | solution.py:44
  278.6 243.5 %reduce-scatter.5.cloned.1.call-start = ((), (), s32[]{:S(2)}) async-start(), calls=%async_computation.3 | async-start | bytes 7864320 | tf_op jit(solution)/shard_map/reduce_scatter | solution.py:690
  341.3 55.8 %collective-permute-start.33 = (bf16[2,256,1024]{2,1,0:T(8,128)(2,1)}, bf16[2,256,1024]{2,1,0:T(8,128)(2,1)S(1)}, u32[]{:S(2)}, u32[]{:S(2)}) collective-permute-start(bf16[2,256,1024]{2,1,0:T(8,128)(2,1)} %get-tuple-element.246), channel_id=1, source_target_pairs={{0,4},{4,0},{1,5},{5,1},{2,6},{6,2},{3,7},{7,3},{8,12},{12,8},{9,1... | collective-permute-start | bytes 3145736 | tf_op jit(solution)/shard_map/ppermute | solution.py:44
  342.7 54.4 %collective-permute-start.34 = (bf16[2,256,1024]{2,1,0:T(8,128)(2,1)}, bf16[2,256,1024]{2,1,0:T(8,128)(2,1)}, u32[]{:S(2)}, u32[]{:S(2)}) collective-permute-start(bf16[2,256,1024]{2,1,0:T(8,128)(2,1)} %get-tuple-element.247), channel_id=1, source_target_pairs={{0,2},{2,0},{1,3},{3,1},{4,6},{6,4},{5,7},{7,5},{8,10},{10,8},{9,1... | collective-permute-start | bytes 3145736 | tf_op jit(solution)/shard_map/ppermute | solution.py:44
  343.6 53.5 %collective-permute-start.35 = (bf16[2,256,1024]{2,1,0:T(8,128)(2,1)}, bf16[2,256,1024]{2,1,0:T(8,128)(2,1)}, u32[]{:S(2)}, u32[]{:S(2)}) collective-permute-start(bf16[2,256,1024]{2,1,0:T(8,128)(2,1)} %pad_maximum_fusion.5), channel_id=1, source_target_pairs={{0,6},{2,4},{4,2},{6,0},{1,7},{3,5},{5,3},{7,1},{8,14},{10,12},{12... | collective-permute-start | bytes 3145736 | tf_op jit(solution)/shard_map/ppermute | solution.py:56
  423.3 24.4 %collective-permute-start.41 = (bf16[256,1024]{1,0:T(8,128)(2,1)}, bf16[256,1024]{1,0:T(8,128)(2,1)}, u32[]{:S(2)}, u32[]{:S(2)}) collective-permute-start(bf16[256,1024]{1,0:T(8,128)(2,1)} %get-tuple-element.267), channel_id=1, source_target_pairs={{0,4},{4,0},{1,5},{5,1},{2,6},{6,2},{3,7},{7,3},{8,12},{12,8},{9,1... | collective-permute-start | bytes 1572872 | tf_op jit(solution)/shard_map/ppermute | solution.py:44
  424.6 23.0 %collective-permute-start.42 = (bf16[256,1024]{1,0:T(8,128)(2,1)}, bf16[256,1024]{1,0:T(8,128)(2,1)}, u32[]{:S(2)}, u32[]{:S(2)}) collective-permute-start(bf16[256,1024]{1,0:T(8,128)(2,1)} %get-tuple-element.268), channel_id=1, source_target_pairs={{0,2},{2,0},{1,3},{3,1},{4,6},{6,4},{5,7},{7,5},{8,10},{10,8},{9,1... | collective-permute-start | bytes 1572872 | tf_op jit(solution)/shard_map/ppermute | solution.py:44
  425.5 24.8 %collective-permute-start.43 = (bf16[256,1024]{1,0:T(8,128)(2,1)}, bf16[256,1024]{1,0:T(8,128)(2,1)}, u32[]{:S(2)}, u32[]{:S(2)}) collective-permute-start(bf16[256,1024]{1,0:T(8,128)(2,1)} %get-tuple-element.269), channel_id=1, source_target_pairs={{0,6},{2,4},{4,2},{6,0},{1,7},{3,5},{5,3},{7,1},{8,14},{10,12},{12... | collective-permute-start | bytes 1572872 | tf_op jit(solution)/shard_map/ppermute | solution.py:56
  468.6 26.7 %collective-permute-start.48 = (bf16[256,1024]{1,0:T(8,128)(2,1)}, bf16[256,1024]{1,0:T(8,128)(2,1)S(1)}, u32[]{:S(2)}, u32[]{:S(2)}) collective-permute-start(bf16[256,1024]{1,0:T(8,128)(2,1)} %fusion.21), channel_id=1, source_target_pairs={{0,2},{2,0},{1,3},{3,1},{4,6},{6,4},{5,7},{7,5},{8,10},{10,8},{9,1... | collective-permute-start | bytes 1572872 | tf_op jit(solution)/shard_map/ppermute | solution.py:44
  469.4 25.9 %collective-permute-start.49 = (bf16[256,1024]{1,0:T(8,128)(2,1)}, bf16[256,1024]{1,0:T(8,128)(2,1)}, u32[]{:S(2)}, u32[]{:S(2)}) collective-permute-start(bf16[256,1024]{1,0:T(8,128)(2,1)} %get-tuple-element.287), channel_id=1, source_target_pairs={{0,4},{4,0},{1,5},{5,1},{2,6},{6,2},{3,7},{7,3},{8,12},{12,8},{9,1... | collective-permute-start | bytes 1572872 | tf_op jit(solution)/shard_map/ppermute | solution.py:44
  471.0 24.3 %collective-permute-start.50 = (bf16[256,1024]{1,0:T(8,128)(2,1)}, bf16[256,1024]{1,0:T(8,128)(2,1)}, u32[]{:S(2)}, u32[]{:S(2)}) collective-permute-start(bf16[256,1024]{1,0:T(8,128)(2,1)} %get-tuple-element.288), channel_id=1, source_target_pairs={{0,6},{2,4},{4,2},{6,0},{1,7},{3,5},{5,3},{7,1},{8,14},{10,12},{12... | collective-permute-start | bytes 1572872 | tf_op jit(solution)/shard_map/ppermute | solution.py:56
  499.5 22.5 %collective-permute-start.57 = (bf16[4,128,768]{2,1,0:T(8,128)(2,1)}, bf16[4,128,768]{2,1,0:T(8,128)(2,1)}, u32[]{:S(2)}, u32[]{:S(2)}) collective-permute-start(bf16[4,128,768]{2,1,0:T(8,128)(2,1)} %get-tuple-element.309), channel_id=1, source_target_pairs={{0,4},{4,0},{1,5},{5,1},{2,6},{6,2},{3,7},{7,3},{8,12},{12,8},{9,1... | collective-permute-start | bytes 2359304 | tf_op jit(solution)/shard_map/ppermute | solution.py:44
  (108 other events, 826.6 us)
Sparse Core Ops, SparseCore 0:
  41.1 116.3 all-gather.4
  159.6 116.3 all-gather.6
  278.7 113.3 reduce-scatter.2
  398.2 113.3 reduce-scatter.4

commit v7 on v6

--- a/solution.py
+++ b/solution.py
@@ -365,10 +365,10 @@
     x_pieces, rest = rest[:4], rest[4:]
     w_pieces, rest = rest[:n_weights], rest[n_weights:]
     if n_weights > 1:
-        qkv_ref, heads_ref, kept_ref, sent_ref, w_ref, x_scr = rest
+        qkv_ref, heads_ref, kept_ref, sent_ref, lse_ref, w_ref, x_scr = rest
         place_rows(weight_spots_ref, w_pieces, w_ref)
     else:
-        qkv_ref, heads_ref, kept_ref, sent_ref, x_scr = rest
+        qkv_ref, heads_ref, kept_ref, sent_ref, lse_ref, x_scr = rest
         w_ref = w_pieces[0]
     place_rows(spots_ref, x_pieces, x_scr)
     rows = x_scr.shape[0]
@@ -389,8 +389,11 @@
             scores = jnp.where(col_pos <= row_pos, near, -1e30)
             if start:
                 scores = jnp.concatenate([dot_nt(query, keys[:start]), scores], axis=1)
-            exponent = jnp.exp(scores - jnp.max(scores, axis=-1, keepdims=True))
+            highest = jnp.max(scores, axis=-1, keepdims=True)
+            exponent = jnp.exp(scores - highest)
             total = jnp.sum(exponent, axis=-1, keepdims=True)
+            logs = jnp.broadcast_to(highest + jnp.log(total), (ratio * tile, 128))
+            lse_ref[pl.ds(kv * (rows // tile) + start // tile, 1), :] = logs.T[:1]
             probs = (exponent * (1.0 / total)).astype(BF)
             out = dot_nn(probs, values[:stop]).astype(BF)
             for r, c in enumerate(cols):
@@ -402,8 +405,8 @@
     q_width, kv_width = widths
     proj_width = q_width + 2 * kv_width
     dy_pieces, x_pieces, rest = rest[:4], rest[4:8], list(rest[8:])
-    qkv_ref, heads_ref, w_ref = rest[:3]
-    rest = rest[3:]
+    qkv_ref, heads_ref, lse_ref, w_ref = rest[:4]
+    rest = rest[4:]
     if first:
         grads_ref, kept_ref, sent_ref, gain_ref = rest[:4]
         rest = rest[4:]
@@ -436,8 +439,7 @@
             scores = jnp.where(key_pos <= row_pos, near, -1e30)
             if start:
                 scores = jnp.concatenate([dot_nt(keys[:start], query), scores], axis=0)
-            exponent = jnp.exp(scores - jnp.max(scores, axis=0, keepdims=True))
-            probs = exponent * (1.0 / jnp.sum(exponent, axis=0, keepdims=True))
+            probs = jnp.exp(scores - lse_ref[pl.ds(kv * (rows // tile) + start // tile, 1), :])
             prob_grad = dot_nt(values[:stop], out_grad)
             inner = jnp.sum(probs * prob_grad, axis=0, keepdims=True)
             score_grad = (probs * (prob_grad - inner)).astype(BF)
@@ -469,11 +471,14 @@
     rows, model_width = pieces[0].shape
     width = weights[0].shape[1]
     whole = len(weights) == 1
+    tile = min(256, 4 * rows)
+    stats = (widths[1] // HD * (4 * rows // tile), widths[0] // widths[1] * tile)
     outs = [
         jax.ShapeDtypeStruct((4 * rows, widths[0] + 2 * widths[1]), BF),
         jax.ShapeDtypeStruct((4 * rows, widths[0]), BF),
         jax.ShapeDtypeStruct((2, rows, model_width), FP),
         jax.ShapeDtypeStruct((2, rows, model_width), BF),
+        jax.ShapeDtypeStruct(stats, FP),
     ] + ([] if whole else [jax.ShapeDtypeStruct((model_width, width), BF)])
     results = pl.pallas_call(
         functools.partial(attn_forward_kernel, widths, len(weights)),
@@ -487,11 +492,11 @@
     return results if not whole else [*results, weights[0]]
 
 
-def attn_backward(spots, block_spots, dy, x, qkv, heads, weights, earlier, widths):
+def attn_backward(spots, block_spots, dy, x, qkv, heads, lse, weights, earlier, widths):
     rows, model_width = x[0].shape
     width = weights.shape[1]
     first = earlier is None
-    operands = [*dy, *x, qkv, heads, weights] + ([] if first else [earlier])
+    operands = [*dy, *x, qkv, heads, lse, weights] + ([] if first else [earlier])
     depth = block_spots.shape[0] // 2
     whole = (model_width, width)
     blocks = (depth, model_width // depth // 2, width)
@@ -517,7 +522,7 @@
         out_shape=outs,
         scratch_shapes=scratch,
         compiler_params=pltpu.CompilerParams(vmem_limit_bytes=58 << 20),
-        cost_estimate=cost(4 << 30),
+        cost_estimate=cost(1 << 24),
     )(spots, block_spots, *operands)
 
 
@@ -549,9 +554,9 @@
         [2 * lax.rem(place + r, depth) + s for s in (side, 1 - side) for r in range(depth)]
     ).astype(jnp.int32)
 
-    packed = pack_experts(side_at, w_gate_up, w_down)
-    packed_attn = pack_attn(after(w_query, packed[0][1]), w_key, w_value, w_out)
-    in_rows = after(block_input, packed_attn).astype(FP)
+    packed_attn = pack_attn(w_query, w_key, w_value, w_out)
+    packed = pack_experts(after(side_at, packed_attn), w_gate_up, w_down)
+    in_rows = after(block_input, packed[0][1]).astype(FP)
     normed_attn, scale_attn = row_norm(in_rows, norm_attn)
     normed = [normed_attn[m].astype(BF) for m in range(micro_count)]
     cots = [cotangent[m] for m in range(micro_count)]
@@ -588,9 +593,11 @@
 
     cot_diagonal = cross(cot)
     turn = after(spots, shards[0])
-    qkv, heads, kept, sent, whole = attn_forward(turn, weight_spots, attn_in[0], weights, widths)
+    qkv, heads, kept, sent, lse, whole = attn_forward(
+        turn, weight_spots, attn_in[0], weights, widths
+    )
     weights = [whole]
-    saved = [(qkv, heads)]
+    saved = [(qkv, heads, lse)]
     sent, cot_diagonal, cot_across, across = together(
         sent, cot_diagonal, cot_across, next_across
     )
@@ -599,16 +606,23 @@
     near_rows, far_rows = swap(normed[1], "c"), swap(across, "c")
     along = plus(kept[1], got[1]).astype(BF)
     own = plus(kept[0], got[0])
-    along, near_rows, far_rows, cot, theirs, turn = together(
-        along, near_rows, far_rows, cots[0], packed[1][1], spots
-    )
+    along, near_rows, far_rows, cot, turn = together(along, near_rows, far_rows, cots[0], spots)
     attn_in.append([normed[1], across, near_rows, far_rows])
 
-    came, cot_near = swap(along, "x"), swap(cot, "y")
-    theirs = swap(theirs, "y")
-    qkv, heads, kept, sent, _ = attn_forward(turn, weight_spots, attn_in[1], weights, widths)
-    saved.append((qkv, heads))
-    sent, came, cot_near = together(sent, came, cot_near)
+    expert_ids = jnp.arange(E, dtype=jnp.int32)[:, None, None, None]
+    gates = jnp.sum(jnp.where(routes == expert_ids, gate_weights, 0.0), axis=3)
+    gates = gates.reshape(2, E // 2, micro_count, 2, 2, rows_local)
+    gates = jnp.where(chip == 0, gates, gates[:, :, :, ::-1])
+    gates = jnp.where(core == 0, gates, gates[:, :, :, :, ::-1])
+    mine = lax.dynamic_index_in_dim(gates, side, 0, False)
+    other = lax.dynamic_index_in_dim(gates, 1 - side, 0, False)
+    other = after(other.reshape(E // 2, -1), along)
+    came, cot_near, gates_got = swap(along, "x"), swap(cot, "y"), swap(other, "y")
+    qkv, heads, kept, sent, lse, _ = attn_forward(
+        turn, weight_spots, attn_in[1], weights, widths
+    )
+    saved.append((qkv, heads, lse))
+    sent, came, cot_near, gates_got = together(sent, came, cot_near, gates_got)
 
     def moe_rows(middle):
         normed, scale = row_norm(middle, norm_moe)
@@ -622,36 +636,30 @@
     own = plus(kept[0], got[0])
     along, low = together(along, low)
 
-    came = swap(along, "x")
-    near, across = swap(low, "y"), swap(low, "x")
-    expert_ids = jnp.arange(E, dtype=jnp.int32)[:, None, None, None]
-    gates = jnp.sum(jnp.where(routes == expert_ids, gate_weights, 0.0), axis=3)
-    gates = gates.reshape(2, E // 2, micro_count, 2, 2, rows_local)
-    gates = jnp.where(chip == 0, gates, gates[:, :, :, ::-1])
-    gates = jnp.where(core == 0, gates, gates[:, :, :, :, ::-1])
-    mine = lax.dynamic_index_in_dim(gates, side, 0, False)
-    other = lax.dynamic_index_in_dim(gates, 1 - side, 0, False)
-    gates = jnp.stack([mine, swap(other.reshape(E // 2, -1), "y").reshape(mine.shape)])
+    near, across, diagonal = to_neighbours([low] * 3)
+    gates = jnp.stack([mine, gates_got.reshape(mine.shape)])
     gates = gates.transpose(2, 3, 0, 4, 5, 1).reshape(micro_count, 4, 2, rows_local, E // 2)
-    came, near, across, gates, theirs, low = together(came, near, across, gates, theirs, low)
-
-    diagonal = cross(low)
-    shards.append(shard_of(1, theirs))
-    chunk_weights.append(whole_of(shards[1]))
+    near, across, diagonal, gates, along, theirs = together(
+        near, across, diagonal, gates, along, packed[1][1]
+    )
+
+    came, theirs = swap(along, "x"), swap(theirs, "y")
+    blocks = stacked(
+        [normed[0], cots[0], near, cot_near, across, cot_across, diagonal, cot_diagonal]
+    )
+    experts_in = [(blocks, swap(blocks, "c"))]
+    came, theirs, blocks = together(came, theirs, blocks)
     middle.append(in_rows[1] + plus(own, came))
     low, scale = moe_rows(middle[1])
     normed.append(low)
     scale_moe.append(scale)
     pair = stacked([low, cots[1]])
-    diagonal, pair, _ = together(diagonal, pair, shards[1])
-    blocks = stacked(
-        [normed[0], cots[0], near, cot_near, across, cot_across, diagonal, cot_diagonal]
-    )
-    experts_in = [(blocks, swap(blocks, "c"))]
+    shards.append(shard_of(1, theirs))
+    chunk_weights.append(whole_of(shards[1]))
     neighbours = to_neighbours([pair] * 3)
 
     sums = [None] * micro_count
-    turn = after(side_at, shards[1])
+    turn = after(side_at, shards[1], pair)
     all_grads = []
     first_expert = 0
     for chunk, count in enumerate(CHUNKS):
@@ -712,19 +720,15 @@
     grad_shards = [first_shard, reduce_grads(grads)]
     first_came, first_mixed_own = came, mixed_own
     middle_grad, low, gain_moe = middle_back(0, own, [c[0] for c in came])
-    shard_got = [swap(first_shard[1], "y")]
     across, near_rows = swap(low, "x"), swap(low, "c")
     last_mixed_sent, sent, _ = together(last_mixed_sent, sent, low)
     own, along = half_sums(kept, sent)
     mixed_own, mixed_along = half_sums(last_mixed_kept, last_mixed_sent)
-    across, near_rows, shard_got[0], *along = together(
-        across, near_rows, shard_got[0], *along, *mixed_along
-    )
-    along, mixed_along = along[:3], along[3:]
+    came = to_neighbours(along)
+    across, near_rows, came[0], *mixed_along = together(across, near_rows, came[0], *mixed_along)
     far_rows = swap(across, "c")
-    came = to_neighbours(along)
     results = backward(0, spots, [low, across, near_rows, far_rows], None)
-    *came, earlier, kept, sent, gain_attn = together(*came, *results)
+    *came, earlier, kept, sent, gain_attn, first_shard = together(*came, *results, first_shard)
 
     middle_grads = [middle_grad]
     middle_grad, low, gain = middle_back(1, own, came)
@@ -732,8 +736,9 @@
     gain_moe = gain_moe + gain
     across, near_rows = swap(low, "x"), swap(low, "c")
     input_own, input_along = half_sums(kept, sent)
-    across, near_rows, input_along, *mixed_along = together(
-        across, near_rows, *input_along, *mixed_along
+    shard_got = [swap(first_shard[1], "y")]
+    across, near_rows, shard_got[0], input_along, *mixed_along = together(
+        across, near_rows, shard_got[0], *input_along, *mixed_along
     )
     far_rows = swap(across, "c")
     input_came = swap(input_along, "x")
@@ -749,17 +754,17 @@
     own, along = half_sums(kept, sent)
     first_input = input_back(0, middle_grads[0], input_own, input_came)
     outputs = [(middle[0] + sum_of(first_mixed_own, [c[1] for c in first_came])).astype(BF)]
-    for axis in ("c", "x"):
-        gains = gains + swap(gains, axis)
-    gains, mixed_along = together(gains, mixed_along[1])
-    mixed_came.append(swap(mixed_along, "x"))
-    gains = sum_over_z(gains, depth)
-    along, gains, first_input, outputs[0], grads_got, last_shard, mixed_came[2] = together(
-        along[0], gains, first_input, outputs[0], grads_got, grad_shards[1], mixed_came[2]
+    mixed_came.append(swap(mixed_along[1], "x"))
+    gains = sum_over_z(gains + swap(gains, "c"), depth)
+    gains, mixed_came[2] = together(gains, mixed_came[2])
+    gains = gains + swap(gains, "x")
+    column = grads_kept + grads_got.astype(FP)
+    along, gains, first_input, outputs[0], column, last_shard, mixed_own = together(
+        along[0], gains, first_input, outputs[0], column, grad_shards[1], mixed_own
     )
     input_came = swap(along, "x")
-    shard_got.append(swap(last_shard[1], "y"))
-    column = grads_kept + grads_got.astype(FP)
+    last_sent, column = together(last_shard[1], column)
+    shard_got.append(swap(last_sent, "y"))
     pieces = along_z_sent(column, depth)
     last_input = input_back(1, middle_grads[1], own, input_came)
     outputs.append((middle[1] + sum_of(mixed_own, mixed_came)).astype(BF))

time: 569 us -> 559 us (0.982)
  other arithmetic: 54.1 us -> 46.6 us
    ppermute x2, waiting for transfers between devices: 0.01 us -> 6.32 us  [sum_over_z(): value = value + lax.ppermute(value, 'z', pairs)]
    unnamed x127 -> x139, local copies, waits for them, and re-layouts: 14.2 us -> 12.9 us
  transfers between devices with their start and end apart: 69 -> 69, of which waited for: 24 -> 28; matrix products, arithmetic and copies ran while one was open for 11% -> 10% of each run, Pallas kernels for 50% -> 50%
where the time goes in v7:
time: 559 us; the launch traced here: 555 us
  Pallas kernels  280 us (50%)
  waiting for transfers between devices  125 us (22%)
  starting transfers between devices  63.7 us (11%)
  other arithmetic  46.6 us (8%)
  local copies, waits for them, and re-layouts  24.8 us (4%)
  between operations  14.9 us (3%)
    pallas_call x4, Pallas kernels, moe_chunk(): pl.pallas_call(functools.partial(moe_kernel, first, last, start, column),...  206 us
    ppermute x51, waiting for transfers between devices, swap(): return lax.ppermute(value, axis, [(0, 1), (1, 0)])  86.7 us
    pallas_call x2, Pallas kernels, attn_backward(): pl.pallas_call(functools.partial(attn_backward_kernel, widths, first), in...  39.9 us
    ppermute x51, starting transfers between devices, swap(): return lax.ppermute(value, axis, [(0, 1), (1, 0)])  35.8 us
    pallas_call x2, Pallas kernels, attn_forward(): pl.pallas_call(functools.partial(attn_forward_kernel, widths, len(weights...  23.1 us
    unnamed x139, local copies, waits for them, and re-layouts  12.9 us
  transfers between devices with their start and end apart: 69, of which 28 were waited for; matrix products, arithmetic and copies ran while one was open for 10% of the time, Pallas kernels for 50%

profile of v7, /device:TPU:0, one launch (start us, length us, event | category | flops | bytes accessed | tf_op | source)
XLA Modules:
  0.0 555.2 jit_solution(2248124728156902388)
XLA Ops:
  23.5 10.5 %collective-permute-done.2.rest_7_ = bf16[128,768]{1,0:T(8,128)(2,1)} collective-permute-done((bf16[128,768]{1,0:T(8,128)(2,1)}, bf16[128,768]{1,0:T(8,128)(2,1)}, u32[]{:S(2)}, u32[]{:S(2)}) %collective-permute-start.2) | collective-permute-done | bytes 196640 | tf_op jit(solution)/shard_map/ppermute | solution.py:84
  41.0 5.9 %collective-permute-done.5.rest_8_ = bf16[128,768]{1,0:T(8,128)(2,1)S(1)} collective-permute-done((bf16[128,768]{1,0:T(8,128)(2,1)}, bf16[128,768]{1,0:T(8,128)(2,1)S(1)}, u32[]{:S(2)}, u32[]{:S(2)}) %collective-permute-start.5) | collective-permute-done | bytes 196640 | tf_op jit(solution)/shard_map/ppermute | solution.py:44
  61.1 11.7 %shard_map.197 = (bf16[1024,512]{1,0:T(8,128)(2,1)}, bf16[1024,256]{1,0:T(8,128)(2,1)}, f32[2,256,1024]{2,1,0:T(8,128)}, bf16[2,256,1024]{2,1,0:T(8,128)(2,1)}, ...) custom-call(s32[4]{0:T(128)} %pad_add_fusion.spots_ref, s32[8]{0:T(128)} %stack.132.weight_spots_ref, ...), custom_call_target="tpu_custom_call" | custom-call | flops 15032385536 | bytes 1048576 | tf_op jit(solution)/shard_map/pallas_call | solution.py:483
  84.5 11.4 %shard_map.198 = (bf16[1024,512]{1,0:T(8,128)(2,1)}, bf16[1024,256]{1,0:T(8,128)(2,1)}, f32[2,256,1024]{2,1,0:T(8,128)}, bf16[2,256,1024]{2,1,0:T(8,128)(2,1)}, f32[8,512]{1,0:T(8,128)}) custom-call(s32[4]{0:T(128)} %pad_add_fusion.spots_ref, s32[8]{0:T(128)} %stack.132.weight_spots_ref, bf16[256,1024]{1,0:T(8,128)(2,1)} %copy-done.43, ...), custom_call_target="tpu_custom_call" | custom-call | flops 15032385536 | bytes 1048576 | tf_op jit(solution)/shard_map/pallas_call | solution.py:483
  95.9 4.0 collective-permute-done.18.refs_3_
  113.2 6.6 %collective-permute-done.23.refs_6_ = bf16[256,1024]{1,0:T(8,128)(2,1)} collective-permute-done((bf16[256,1024]{1,0:T(8,128)(2,1)S(1)}, bf16[256,1024]{1,0:T(8,128)(2,1)}, u32[]{:S(2)}, u32[]{:S(2)}) %collective-permute-start.23) | collective-permute-done | bytes 524320 | tf_op jit(solution)/shard_map/ppermute | solution.py:56
  119.9 10.6 %collective-permute-done.22.refs_4_ = bf16[256,1024]{1,0:T(8,128)(2,1)} collective-permute-done((bf16[256,1024]{1,0:T(8,128)(2,1)S(1)}, bf16[256,1024]{1,0:T(8,128)(2,1)}, u32[]{:S(2)}, u32[]{:S(2)}) %collective-permute-start.22) | collective-permute-done | bytes 524320 | tf_op jit(solution)/shard_map/ppermute | solution.py:44
  132.4 3.6 shard_map.199.xa_ref.ga_ref
  136.1 9.6 %collective-permute-done.24 = bf16[256,1024]{1,0:T(8,128)(2,1)S(1)} collective-permute-done((bf16[256,1024]{1,0:T(8,128)(2,1)}, bf16[256,1024]{1,0:T(8,128)(2,1)S(1)}, u32[]{:S(2)}, u32[]{:S(2)}) %collective-permute-start.24) | collective-permute-done | bytes 524320 | tf_op jit(solution)/shard_map/ppermute | solution.py:44
  145.6 4.4 collective-permute-done.25
  158.8 51.2 %shard_map.201 = (f32[4,2,256,1024]{3,2,1,0:T(8,128)}, f32[4,2,256,1024]{3,2,1,0:T(8,128)}, bf16[8,128,3072]{2,1,0:T(8,128)(2,1)}) custom-call(s32[1]{0:T(128)} %bitcast.1.side_ref, bf16[8,256,1024]{2,1,0:T(8,128)(2,1)} %shard_map.199.xa_ref.ga_ref, bf16[8,256,1024]{2,1,0:T(8,128)(2,1)} %collective-permute-done.26.xb_ref.gb_ref, ...), custom_call_target="tpu_custom_call" | custom-call | flops 6442450944 | bytes 1048576 | tf_op jit(solution)/shard_map/pallas_call | solution.py:320
  213.4 7.3 %collective-permute-done.30.xb_ref.gb_ref = bf16[8,256,1024]{2,1,0:T(8,128)(2,1)} collective-permute-done((bf16[8,256,1024]{2,1,0:T(8,128)(2,1)S(1)}, bf16[8,256,1024]{2,1,0:T(8,128)(2,1)}, u32[]{:S(2)}, u32[]{:S(2)}) %collective-permute-start.30) | collective-permute-done | bytes 4194336 | tf_op jit(solution)/shard_map/ppermute | solution.py:44
  220.7 51.4 %shard_map.203 = (f32[4,2,256,1024]{3,2,1,0:T(8,128)}, f32[4,2,256,1024]{3,2,1,0:T(8,128)}, bf16[8,128,3072]{2,1,0:T(8,128)(2,1)}) custom-call(s32[1]{0:T(128)} %bitcast.1.side_ref, bf16[8,256,1024]{2,1,0:T(8,128)(2,1)} %bitcast.172, bf16[8,256,1024]{2,1,0:T(8,128)(2,1)} %collective-permute-done.30.xb_ref.gb_ref, bf16[8,256,1024]{2,1,0:T(8,128)(2,1)} %bitcast.173, ...), custom_call_target="tpu_custom_call" | custom-call | flops 6442450944 | bytes 1048576 | tf_op jit(solution)/shard_map/pallas_call | solution.py:320
  272.2 51.3 %shard_map.204 = (f32[4,256,1024]{2,1,0:T(8,128)}, bf16[4,256,1024]{2,1,0:T(8,128)(2,1)}, f32[4,256,1024]{2,1,0:T(8,128)}, bf16[4,256,1024]{2,1,0:T(8,128)(2,1)}, bf16[8,128,3072]{2,1,0:T(8,128)(2,1)}) custom-call(s32[1]{0:T(128)} %bitcast.1.side_ref, bf16[8,256,1024]{2,1,0:T(8,128)(2,1)} %shard_map.199.xa_ref.ga_ref, ...), custom_call_target="tpu_custom_call" | custom-call | flops 6442450944 | bytes 1048576 | tf_op jit(solution)/shard_map/pallas_call | solution.py:320
  324.0 3.9 collective-permute-done.31
  337.3 52.2 %shard_map.205 = (f32[4,256,1024]{2,1,0:T(8,128)}, bf16[4,256,1024]{2,1,0:T(8,128)(2,1)}, f32[4,256,1024]{2,1,0:T(8,128)}, bf16[4,256,1024]{2,1,0:T(8,128)(2,1)}, bf16[8,128,3072]{2,1,0:T(8,128)(2,1)}) custom-call(s32[1]{0:T(128)} %bitcast.1.side_ref, bf16[8,256,1024]{2,1,0:T(8,128)(2,1)} %bitcast.174, ...), custom_call_target="tpu_custom_call" | custom-call | flops 6442450944 | bytes 1048576 | tf_op jit(solution)/shard_map/pallas_call | solution.py:320
  403.9 5.7 %collective-permute-done.37.rest_1_ = bf16[256,1024]{1,0:T(8,128)(2,1)} collective-permute-done((bf16[256,1024]{1,0:T(8,128)(2,1)S(1)}, bf16[256,1024]{1,0:T(8,128)(2,1)}, u32[]{:S(2)}, u32[]{:S(2)}) %collective-permute-start.37) | collective-permute-done | bytes 524320 | tf_op jit(solution)/shard_map/ppermute | solution.py:44
  409.6 4.9 collective-permute-done.39
  418.7 19.0 %shard_map.206 = (f32[1024,768]{1,0:T(8,128)}, f32[2,256,1024]{2,1,0:T(8,128)}, bf16[2,256,1024]{2,1,0:T(8,128)(2,1)}, f32[1,1024]{1,0:T(1,128)}) custom-call(s32[4]{0:T(128)} %pad_add_fusion.spots_ref, s32[8]{0:T(128)} %stack.144.block_spots_ref, bf16[256,1024]{1,0:T(8,128)(2,1)} %copy-done.40, bf16[256,1024]{1,0:T(8,128)(2,1)} %collective-permute-done.37.rest_1_, ...), custom_call_target="tpu_custom_call" | custom-call | flops 16777216 | bytes 1048576 | tf_op jit(solution)/shard_map/pallas_call | solution.py:518
  447.7 12.3 %collective-permute-done.44.rest_1_ = bf16[256,1024]{1,0:T(8,128)(2,1)S(1)} collective-permute-done((bf16[256,1024]{1,0:T(8,128)(2,1)S(1)}, bf16[256,1024]{1,0:T(8,128)(2,1)S(1)}, u32[]{:S(2)}, u32[]{:S(2)}) %collective-permute-start.44) | collective-permute-done | bytes 524320 | tf_op jit(solution)/shard_map/ppermute | solution.py:44
  465.2 20.9 %shard_map.207 = (f32[4,128,768]{2,1,0:T(8,128)}, bf16[4,128,768]{2,1,0:T(8,128)(2,1)}, f32[2,256,1024]{2,1,0:T(8,128)}, bf16[2,256,1024]{2,1,0:T(8,128)(2,1)}, f32[1,1024]{1,0:T(1,128)}) custom-call(s32[4]{0:T(128)} %pad_add_fusion.spots_ref, s32[8]{0:T(128)} %stack.144.block_spots_ref, bf16[256,1024]{1,0:T(8,128)(2,1)} %copy-done.42, ...), custom_call_target="tpu_custom_call" | custom-call | flops 16777216 | bytes 1048576 | tf_op jit(solution)/shard_map/pallas_call | solution.py:518
  490.9 3.6 collective-permute-start.54
  494.5 5.0 collective-permute-done.54
  525.0 10.6 %collective-permute-done.62 = bf16[128,768]{1,0:T(8,128)(2,1)S(1)} collective-permute-done((bf16[128,768]{1,0:T(8,128)(2,1)S(1)}, bf16[128,768]{1,0:T(8,128)(2,1)S(1)}, u32[]{:S(2)}, u32[]{:S(2)}) %collective-permute-start.62) | collective-permute-done | bytes 196640 | tf_op jit(solution)/shard_map/ppermute | solution.py:90
  (347 shorter events, 162.8 us)
Async XLA Ops:
  7.2 151.6 %all-gather.5.cloned.1.call-start = ((), (), s32[]{:S(2)}) async-start(), calls=%async_computation.4 | async-start | bytes 7864320 | tf_op jit(solution)/shard_map/all_gather | solution.py:570
  11.8 22.6 %collective-permute-start.4 = (bf16[128,3072]{1,0:T(8,128)(2,1)S(1)}, bf16[128,3072]{1,0:T(8,128)(2,1)}, u32[]{:S(2)}, u32[]{:S(2)}) collective-permute-start(bf16[128,3072]{1,0:T(8,128)(2,1)S(1)} %get-tuple-element.176), channel_id=1, source_target_pairs={{0,4},{4,0},{1,5},{5,1},{2,6},{6,2},{3,7},{7,3},{8,12},{12,8},{9,1... | collective-permute-start | bytes 2359304 | tf_op jit(solution)/shard_map/ppermute | solution.py:44
  37.0 235.2 %all-gather.7.cloned.1.call-start = ((), (), s32[]{:S(2)}) async-start(), calls=%async_computation.5 | async-start | bytes 7864320 | tf_op jit(solution)/shard_map/all_gather | solution.py:570
  38.7 21.0 %collective-permute-start.10 = (bf16[256,1024]{1,0:T(8,128)(2,1)}, bf16[256,1024]{1,0:T(8,128)(2,1)}, u32[]{:S(2)}, u32[]{:S(2)}) collective-permute-start(bf16[256,1024]{1,0:T(8,128)(2,1)} %collective-permute-done.3.rest_1_.rest_5_), channel_id=1, source_target_pairs={{0,1},{1,0},{2,3},{3,2},{4,5},{5,4},{6,7},{7,6},{8,9},{9,8},{10,11... | collective-permute-start | bytes 1572872 | tf_op jit(solution)/shard_map/ppermute | solution.py:44
  51.2 21.7 %collective-permute-start.13 = (bf16[256,1024]{1,0:T(8,128)(2,1)S(1)}, bf16[256,1024]{1,0:T(8,128)(2,1)S(1)}, u32[]{:S(2)}, u32[]{:S(2)}) collective-permute-start(bf16[256,1024]{1,0:T(8,128)(2,1)S(1)} %get-tuple-element.216.refs_1_), channel_id=1, source_target_pairs={{0,2},{2,0},{1,3},{3,1},{4,6},{6,4},{5,7},{7,5},{8,10},{10,8},{9,1... | collective-permute-start | bytes 1572872 | tf_op jit(solution)/shard_map/ppermute | solution.py:44
  105.5 24.9 %collective-permute-start.22 = (bf16[256,1024]{1,0:T(8,128)(2,1)S(1)}, bf16[256,1024]{1,0:T(8,128)(2,1)}, u32[]{:S(2)}, u32[]{:S(2)}) collective-permute-start(bf16[256,1024]{1,0:T(8,128)(2,1)S(1)} %multiply_convert_fusion.2.refs_0_), channel_id=1, source_target_pairs={{0,2},{2,0},{1,3},{3,1},{4,6},{6,4},{5,7},{7,5},{8,10},{10,8},{9,1... | collective-permute-start | bytes 1572872 | tf_op jit(solution)/shard_map/ppermute | solution.py:44
  107.0 23.4 %collective-permute-start.21 = (bf16[256,1024]{1,0:T(8,128)(2,1)S(1)}, bf16[256,1024]{1,0:T(8,128)(2,1)}, u32[]{:S(2)}, u32[]{:S(2)}) collective-permute-start(bf16[256,1024]{1,0:T(8,128)(2,1)S(1)} %multiply_convert_fusion.2.refs_0_), channel_id=1, source_target_pairs={{0,4},{4,0},{1,5},{5,1},{2,6},{6,2},{3,7},{7,3},{8,12},{12,8},{9,1... | collective-permute-start | bytes 1572872 | tf_op jit(solution)/shard_map/ppermute | solution.py:44
  136.0 22.8 %collective-permute-start.26 = (bf16[8,256,1024]{2,1,0:T(8,128)(2,1)}, bf16[8,256,1024]{2,1,0:T(8,128)(2,1)}, u32[]{:S(2)}, u32[]{:S(2)}) collective-permute-start(bf16[8,256,1024]{2,1,0:T(8,128)(2,1)} %shard_map.199.xa_ref.ga_ref), channel_id=1, source_target_pairs={{0,1},{1,0},{2,3},{3,2},{4,5},{5,4},{6,7},{7,6},{8,9},{9,8},{10,11... | collective-permute-start | bytes 12582920 | tf_op jit(solution)/shard_map/ppermute | solution.py:44
  151.5 238.1 %reduce-scatter.3.cloned.1.call-start = ((), (), s32[]{:S(2)}) async-start(), calls=%async_computation.2 | async-start | bytes 7864320 | tf_op jit(solution)/shard_map/reduce_scatter | solution.py:698
  155.2 54.8 %collective-permute-start.29 = (bf16[2,256,1024]{2,1,0:T(8,128)(2,1)S(1)}, bf16[2,256,1024]{2,1,0:T(8,128)(2,1)S(1)}, u32[]{:S(2)}, u32[]{:S(2)}) collective-permute-start(bf16[2,256,1024]{2,1,0:T(8,128)(2,1)S(1)} %shard_map.200.refs_0_), channel_id=1, source_target_pairs={{0,6},{2,4},{4,2},{6,0},{1,7},{3,5},{5,3},{7,1},{8,14},{10,12},{12... | collective-permute-start | bytes 3145736 | tf_op jit(solution)/shard_map/ppermute | solution.py:56
  156.7 53.3 %collective-permute-start.28 = (bf16[2,256,1024]{2,1,0:T(8,128)(2,1)S(1)}, bf16[2,256,1024]{2,1,0:T(8,128)(2,1)S(1)}, u32[]{:S(2)}, u32[]{:S(2)}) collective-permute-start(bf16[2,256,1024]{2,1,0:T(8,128)(2,1)S(1)} %shard_map.200.refs_0_), channel_id=1, source_target_pairs={{0,2},{2,0},{1,3},{3,1},{4,6},{6,4},{5,7},{7,5},{8,10},{10,8},{9,1... | collective-permute-start | bytes 3145736 | tf_op jit(solution)/shard_map/ppermute | solution.py:44
  158.3 51.8 %collective-permute-start.27 = (bf16[2,256,1024]{2,1,0:T(8,128)(2,1)S(1)}, bf16[2,256,1024]{2,1,0:T(8,128)(2,1)}, u32[]{:S(2)}, u32[]{:S(2)}) collective-permute-start(bf16[2,256,1024]{2,1,0:T(8,128)(2,1)S(1)} %shard_map.200.refs_0_), channel_id=1, source_target_pairs={{0,4},{4,0},{1,5},{5,1},{2,6},{6,2},{3,7},{7,3},{8,12},{12,8},{9,1... | collective-permute-start | bytes 3145736 | tf_op jit(solution)/shard_map/ppermute | solution.py:44
  272.1 239.1 %reduce-scatter.5.cloned.1.call-start = ((), (), s32[]{:S(2)}) async-start(), calls=%async_computation.3 | async-start | bytes 7864320 | tf_op jit(solution)/shard_map/reduce_scatter | solution.py:698
  333.8 55.7 %collective-permute-start.33 = (bf16[2,256,1024]{2,1,0:T(8,128)(2,1)}, bf16[2,256,1024]{2,1,0:T(8,128)(2,1)}, u32[]{:S(2)}, u32[]{:S(2)}) collective-permute-start(bf16[2,256,1024]{2,1,0:T(8,128)(2,1)} %get-tuple-element.251), channel_id=1, source_target_pairs={{0,4},{4,0},{1,5},{5,1},{2,6},{6,2},{3,7},{7,3},{8,12},{12,8},{9,1... | collective-permute-start | bytes 3145736 | tf_op jit(solution)/shard_map/ppermute | solution.py:44
  335.2 54.4 %collective-permute-start.34 = (bf16[2,256,1024]{2,1,0:T(8,128)(2,1)}, bf16[2,256,1024]{2,1,0:T(8,128)(2,1)}, u32[]{:S(2)}, u32[]{:S(2)}) collective-permute-start(bf16[2,256,1024]{2,1,0:T(8,128)(2,1)} %get-tuple-element.252), channel_id=1, source_target_pairs={{0,2},{2,0},{1,3},{3,1},{4,6},{6,4},{5,7},{7,5},{8,10},{10,8},{9,1... | collective-permute-start | bytes 3145736 | tf_op jit(solution)/shard_map/ppermute | solution.py:44
  335.3 54.2 %collective-permute-start.35 = (bf16[2,256,1024]{2,1,0:T(8,128)(2,1)S(1)}, bf16[2,256,1024]{2,1,0:T(8,128)(2,1)}, u32[]{:S(2)}, u32[]{:S(2)}) collective-permute-start(bf16[2,256,1024]{2,1,0:T(8,128)(2,1)S(1)} %pad_maximum_fusion.5), channel_id=1, source_target_pairs={{0,6},{2,4},{4,2},{6,0},{1,7},{3,5},{5,3},{7,1},{8,14},{10,12},{12... | collective-permute-start | bytes 3145736 | tf_op jit(solution)/shard_map/ppermute | solution.py:56
  414.5 23.2 %collective-permute-start.42 = (bf16[256,1024]{1,0:T(8,128)(2,1)}, bf16[256,1024]{1,0:T(8,128)(2,1)S(1)}, u32[]{:S(2)}, u32[]{:S(2)}) collective-permute-start(bf16[256,1024]{1,0:T(8,128)(2,1)} %get-tuple-element.408), channel_id=1, source_target_pairs={{0,6},{2,4},{4,2},{6,0},{1,7},{3,5},{5,3},{7,1},{8,14},{10,12},{12... | collective-permute-start | bytes 1572872 | tf_op jit(solution)/shard_map/ppermute | solution.py:56
  415.6 25.5 %collective-permute-start.41 = (bf16[256,1024]{1,0:T(8,128)(2,1)}, bf16[256,1024]{1,0:T(8,128)(2,1)}, u32[]{:S(2)}, u32[]{:S(2)}) collective-permute-start(bf16[256,1024]{1,0:T(8,128)(2,1)} %get-tuple-element.409), channel_id=1, source_target_pairs={{0,2},{2,0},{1,3},{3,1},{4,6},{6,4},{5,7},{7,5},{8,10},{10,8},{9,1... | collective-permute-start | bytes 1572872 | tf_op jit(solution)/shard_map/ppermute | solution.py:44
  460.4 25.7 %collective-permute-start.48 = (bf16[256,1024]{1,0:T(8,128)(2,1)}, bf16[256,1024]{1,0:T(8,128)(2,1)S(1)}, u32[]{:S(2)}, u32[]{:S(2)}) collective-permute-start(bf16[256,1024]{1,0:T(8,128)(2,1)} %fusion.17), channel_id=1, source_target_pairs={{0,2},{2,0},{1,3},{3,1},{4,6},{6,4},{5,7},{7,5},{8,10},{10,8},{9,1... | collective-permute-start | bytes 1572872 | tf_op jit(solution)/shard_map/ppermute | solution.py:44
  460.8 25.3 %collective-permute-start.49 = (bf16[256,1024]{1,0:T(8,128)(2,1)}, bf16[256,1024]{1,0:T(8,128)(2,1)}, u32[]{:S(2)}, u32[]{:S(2)}) collective-permute-start(bf16[256,1024]{1,0:T(8,128)(2,1)} %get-tuple-element.292), channel_id=1, source_target_pairs={{0,4},{4,0},{1,5},{5,1},{2,6},{6,2},{3,7},{7,3},{8,12},{12,8},{9,1... | collective-permute-start | bytes 1572872 | tf_op jit(solution)/shard_map/ppermute | solution.py:44
  461.8 25.3 %collective-permute-start.50 = (bf16[256,1024]{1,0:T(8,128)(2,1)}, bf16[256,1024]{1,0:T(8,128)(2,1)}, u32[]{:S(2)}, u32[]{:S(2)}) collective-permute-start(bf16[256,1024]{1,0:T(8,128)(2,1)} %get-tuple-element.293), channel_id=1, source_target_pairs={{0,6},{2,4},{4,2},{6,0},{1,7},{3,5},{5,3},{7,1},{8,14},{10,12},{12... | collective-permute-start | bytes 1572872 | tf_op jit(solution)/shard_map/ppermute | solution.py:56
  463.9 40.1 %collective-permute-start.56 = (bf16[256,1024]{1,0:T(8,128)(2,1)}, bf16[256,1024]{1,0:T(8,128)(2,1)}, u32[]{:S(2)}, u32[]{:S(2)}) collective-permute-start(bf16[256,1024]{1,0:T(8,128)(2,1)} %get-tuple-element.309), channel_id=1, source_target_pairs={{0,2},{2,0},{1,3},{3,1},{4,6},{6,4},{5,7},{7,5},{8,10},{10,8},{9,1... | collective-permute-start | bytes 1572872 | tf_op jit(solution)/shard_map/ppermute | solution.py:44
  487.9 20.8 %collective-permute-start.58 = (bf16[4,128,768]{2,1,0:T(8,128)(2,1)}, bf16[4,128,768]{2,1,0:T(8,128)(2,1)S(1)}, u32[]{:S(2)}, u32[]{:S(2)}) collective-permute-start(bf16[4,128,768]{2,1,0:T(8,128)(2,1)} %get-tuple-element.316), channel_id=1, source_target_pairs={{0,4},{4,0},{1,5},{5,1},{2,6},{6,2},{3,7},{7,3},{8,12},{12,8},{9,1... | collective-permute-start | bytes 2359304 | tf_op jit(solution)/shard_map/ppermute | solution.py:44
  489.0 21.0 %collective-permute-start.52 = (bf16[2,256,1024]{2,1,0:T(8,128)(2,1)}, bf16[2,256,1024]{2,1,0:T(8,128)(2,1)S(1)}, u32[]{:S(2)}, u32[]{:S(2)}) collective-permute-start(bf16[2,256,1024]{2,1,0:T(8,128)(2,1)} %get-tuple-element.306), channel_id=1, source_target_pairs={{0,1},{1,0},{2,3},{3,2},{4,5},{5,4},{6,7},{7,6},{8,9},{9,8},{10,11... | collective-permute-start | bytes 3145736 | tf_op jit(solution)/shard_map/ppermute | solution.py:44
  (114 other events, 1025.7 us)
Sparse Core Ops, SparseCore 0:
  37.1 116.3 all-gather.4
  155.1 113.8 all-gather.6
  272.2 112.6 reduce-scatter.2
  389.8 112.7 reduce-scatter.4

commit v8 on v7

--- a/solution.py
+++ b/solution.py
@@ -404,20 +404,19 @@
 def attn_backward_kernel(widths, first, spots_ref, block_spots_ref, *rest):
     q_width, kv_width = widths
     proj_width = q_width + 2 * kv_width
-    dy_pieces, x_pieces, rest = rest[:4], rest[4:8], list(rest[8:])
+    dy_pieces, rest = rest[:4], list(rest[4:])
+    x_pieces = [] if first else [rest.pop(0) for _ in range(4)]
     qkv_ref, heads_ref, lse_ref, w_ref = rest[:4]
     rest = rest[4:]
+    x_scr = gain_ref = None
     if first:
-        grads_ref, kept_ref, sent_ref, gain_ref = rest[:4]
-        rest = rest[4:]
+        proj_grad_ref, kept_ref, sent_ref, dy_scr, head_grad_ref, key_acc, value_acc = rest
     else:
         earlier_ref, grads_kept_ref, grads_sent_ref, kept_ref, sent_ref, gain_ref = rest[:6]
-        grads_ref = rest[6]
-        rest = rest[7:]
-    dy_scr, x_scr, head_grad_ref, proj_grad_ref, key_acc, value_acc = rest
+        grads_ref, dy_scr, x_scr, head_grad_ref, proj_grad_ref, key_acc, value_acc = rest[6:]
+        place_rows(spots_ref, x_pieces, x_scr)
     place_rows(spots_ref, dy_pieces, dy_scr)
-    place_rows(spots_ref, x_pieces, x_scr)
-    rows = x_scr.shape[0]
+    rows = dy_scr.shape[0]
     ratio = q_width // kv_width
     tile = min(256, rows)
     head_grad_ref[...] = dot_nn(dy_scr[...], w_ref[:, proj_width:]).astype(BF)
@@ -451,20 +450,44 @@
         proj_grad_ref[:, key_cols] = key_acc[...].astype(BF)
         proj_grad_ref[:, value_cols] = value_acc[...].astype(BF)
     product_rows(spots_ref, proj_grad_ref, w_ref[:, :proj_width], kept_ref, sent_ref, x_scr, gain_ref)
+    if first:
+        return
+    grads_ref[:, :proj_width] = earlier_ref[:, :proj_width] + dot_tn(x_scr[...], proj_grad_ref[...])
+    grads_ref[:, proj_width:] = earlier_ref[:, proj_width:] + dot_tn(dy_scr[...], heads_ref[...])
+    depth, blk, _ = grads_kept_ref.shape
+    for r in range(depth):
+        here = pl.ds(pl.multiple_of(block_spots_ref[r] * blk, blk), blk)
+        grads_kept_ref[r] = grads_ref[here, :]
+        here = pl.ds(pl.multiple_of(block_spots_ref[depth + r] * blk, blk), blk)
+        grads_sent_ref[r] = grads_ref[here, :].astype(BF)
+
+
+def attn_weights_kernel(proj_width, spots_ref, *rest):
+    dy_pieces, x_pieces, rest = rest[:4], rest[4:8], rest[8:]
+    heads_ref, proj_grad_ref, w_ref, grads_ref, gain_ref, dy_scr, x_scr = rest
+    place_rows(spots_ref, dy_pieces, dy_scr)
+    place_rows(spots_ref, x_pieces, x_scr)
     proj_part = dot_tn(x_scr[...], proj_grad_ref[...])
-    out_part = dot_tn(dy_scr[...], heads_ref[...])
-    if first:
-        grads_ref[:, :proj_width] = proj_part
-        grads_ref[:, proj_width:] = out_part
-    else:
-        grads_ref[:, :proj_width] = earlier_ref[:, :proj_width] + proj_part
-        grads_ref[:, proj_width:] = earlier_ref[:, proj_width:] + out_part
-        depth, blk, _ = grads_kept_ref.shape
-        for r in range(depth):
-            here = pl.ds(pl.multiple_of(block_spots_ref[r] * blk, blk), blk)
-            grads_kept_ref[r] = grads_ref[here, :]
-            here = pl.ds(pl.multiple_of(block_spots_ref[depth + r] * blk, blk), blk)
-            grads_sent_ref[r] = grads_ref[here, :].astype(BF)
+    grads_ref[:, :proj_width] = proj_part
+    grads_ref[:, proj_width:] = dot_tn(dy_scr[...], heads_ref[...])
+    products = proj_part * w_ref[:, :proj_width].astype(FP)
+    gain_ref[...] = jnp.sum(products, axis=1, keepdims=True)
+
+
+def attn_weights(spots, dy, x, heads, proj_grad, weights):
+    rows, model_width = x[0].shape
+    return pl.pallas_call(
+        functools.partial(attn_weights_kernel, proj_grad.shape[1]),
+        in_specs=[SMEM] + [VMEM] * 11,
+        out_specs=[VMEM] * 2,
+        out_shape=[
+            jax.ShapeDtypeStruct((model_width, weights.shape[1]), FP),
+            jax.ShapeDtypeStruct((model_width, 1), FP),
+        ],
+        scratch_shapes=[pltpu.VMEM((4 * rows, model_width), BF)] * 2,
+        compiler_params=pltpu.CompilerParams(vmem_limit_bytes=56 << 20),
+        cost_estimate=cost(4 << 30),
+    )(spots, *dy, *x, heads, proj_grad, weights)
 
 
 def attn_forward(spots, weight_spots, pieces, weights, widths):
@@ -496,25 +519,23 @@
     rows, model_width = x[0].shape
     width = weights.shape[1]
     first = earlier is None
-    operands = [*dy, *x, qkv, heads, lse, weights] + ([] if first else [earlier])
+    operands = [*dy] + ([] if first else [*x]) + [qkv, heads, lse, weights]
+    operands += [] if first else [earlier]
     depth = block_spots.shape[0] // 2
     whole = (model_width, width)
     blocks = (depth, model_width // depth // 2, width)
-    scratch = [
-        pltpu.VMEM((4 * rows, model_width), BF),
-        pltpu.VMEM((4 * rows, model_width), BF),
-        pltpu.VMEM(heads.shape, BF),
-        pltpu.VMEM(qkv.shape, BF),
-        pltpu.VMEM((4 * rows, HD), FP),
-        pltpu.VMEM((4 * rows, HD), FP),
-    ]
+    placed = pltpu.VMEM((4 * rows, model_width), BF)
+    proj_shape = (4 * rows, widths[0] + 2 * widths[1])
+    sums = [pltpu.VMEM((4 * rows, HD), FP)] * 2
+    outs = [jax.ShapeDtypeStruct((2, rows, model_width), t) for t in (FP, BF)]
     if first:
-        outs = [jax.ShapeDtypeStruct(whole, FP)]
+        outs = [jax.ShapeDtypeStruct(proj_shape, BF)] + outs
+        scratch = [placed, pltpu.VMEM(heads.shape, BF), *sums]
     else:
-        outs = [jax.ShapeDtypeStruct(blocks, FP), jax.ShapeDtypeStruct(blocks, BF)]
-        scratch = [pltpu.VMEM(whole, FP)] + scratch
-    outs += [jax.ShapeDtypeStruct((2, rows, model_width), t) for t in (FP, BF)]
-    outs += [jax.ShapeDtypeStruct((1, model_width), FP)]
+        outs = [jax.ShapeDtypeStruct(blocks, FP), jax.ShapeDtypeStruct(blocks, BF)] + outs
+        outs += [jax.ShapeDtypeStruct((1, model_width), FP)]
+        scratch = [pltpu.VMEM(whole, FP), placed, placed, pltpu.VMEM(heads.shape, BF)]
+        scratch += [pltpu.VMEM(proj_shape, BF), *sums]
     return pl.pallas_call(
         functools.partial(attn_backward_kernel, widths, first),
         in_specs=[SMEM] * 2 + [VMEM] * len(operands),
@@ -725,10 +746,14 @@
     own, along = half_sums(kept, sent)
     mixed_own, mixed_along = half_sums(last_mixed_kept, last_mixed_sent)
     came = to_neighbours(along)
-    across, near_rows, came[0], *mixed_along = together(across, near_rows, came[0], *mixed_along)
+    across, near_rows, came[:2], mixed_along = together(across, near_rows, came[:2], mixed_along)
     far_rows = swap(across, "c")
-    results = backward(0, spots, [low, across, near_rows, far_rows], None)
-    *came, earlier, kept, sent, gain_attn, first_shard = together(*came, *results, first_shard)
+    rows = [low, across, near_rows, far_rows]
+    results = backward(0, spots, rows, None)
+    *came, proj_grad, kept, sent, first_shard = together(*came, *results, first_shard)
+    earlier, gain_attn = attn_weights(
+        spots, rows, attn_in[0], saved[0][1], proj_grad, weights[0]
+    )
 
     middle_grads = [middle_grad]
     middle_grad, low, gain = middle_back(1, own, came)
@@ -737,19 +762,19 @@
     across, near_rows = swap(low, "x"), swap(low, "c")
     input_own, input_along = half_sums(kept, sent)
     shard_got = [swap(first_shard[1], "y")]
-    across, near_rows, shard_got[0], input_along, *mixed_along = together(
-        across, near_rows, shard_got[0], *input_along, *mixed_along
+    across, near_rows, shard_got[0], input_along, earlier, *mixed_along = together(
+        across, near_rows, shard_got[0], *input_along, earlier, *mixed_along
     )
     far_rows = swap(across, "c")
     input_came = swap(input_along, "x")
     mixed_came = [swap(mixed_along[0], "y"), cross(mixed_along[2])]
     results = backward(1, spots, [low, across, near_rows, far_rows], earlier)
-    input_came, (mixed_came, results, first_came) = together(
-        input_came, (mixed_came, results, first_came)
+    input_came, gain_attn, (mixed_came, results, first_came) = together(
+        input_came, gain_attn, (mixed_came, results, first_came)
     )
     grads_kept, grads_sent, kept, sent, gain = results
 
-    gains = jnp.concatenate([(gain_attn + gain)[0] / norm_attn, gain_moe]).reshape(16, -1)
+    gains = jnp.concatenate([(gain_attn[:, 0] + gain[0]) / norm_attn, gain_moe]).reshape(16, -1)
     grads_got = swap(grads_sent, "y")
     own, along = half_sums(kept, sent)
     first_input = input_back(0, middle_grads[0], input_own, input_came)

time: 559 us -> 560 us (level)
  waiting for transfers between devices: 125 us -> 117 us
    pallas_call x0 -> x1, Pallas kernels: none -> 7.24 us  [attn_weights(): pl.pallas_call(functools.partial(attn_weights_kernel, proj_grad.shape[1])...]
    unnamed x139 -> x143, local copies, waits for them, and re-layouts: 12.9 us -> 14.6 us
  transfers between devices with their start and end apart: 69 -> 69, of which waited for: 28 -> 27; matrix products, arithmetic and copies ran while one was open for 10% -> 10% of each run, Pallas kernels for 50% -> 50%
where the time goes in v8:
time: 560 us; the launch traced here: 557 us
  Pallas kernels  284 us (51%)
  waiting for transfers between devices  117 us (21%)
  starting transfers between devices  65.3 us (12%)
  other arithmetic  48.4 us (9%)
  local copies, waits for them, and re-layouts  27.7 us (5%)
  between operations  14.9 us (3%)
    pallas_call x4, Pallas kernels, moe_chunk(): pl.pallas_call(functools.partial(moe_kernel, first, last, start, column),...  206 us
    ppermute x51, waiting for transfers between devices, swap(): return lax.ppermute(value, axis, [(0, 1), (1, 0)])  84.2 us
    ppermute x51, starting transfers between devices, swap(): return lax.ppermute(value, axis, [(0, 1), (1, 0)])  36.2 us
    pallas_call x2, Pallas kernels, attn_backward(): pl.pallas_call(functools.partial(attn_backward_kernel, widths, first), in...  36 us
    pallas_call x2, Pallas kernels, attn_forward(): pl.pallas_call(functools.partial(attn_forward_kernel, widths, len(weights...  23.1 us
    unnamed x143, local copies, waits for them, and re-layouts  14.6 us
  transfers between devices with their start and end apart: 69, of which 27 were waited for; matrix products, arithmetic and copies ran while one was open for 10% of the time, Pallas kernels for 50%

profile of v8, /device:TPU:0, one launch (start us, length us, event | category | flops | bytes accessed | tf_op | source)
XLA Modules:
  0.0 557.0 jit_solution(6544540476205336947)
XLA Ops:
  23.5 10.5 %collective-permute-done.2.rest_7_ = bf16[128,768]{1,0:T(8,128)(2,1)} collective-permute-done((bf16[128,768]{1,0:T(8,128)(2,1)}, bf16[128,768]{1,0:T(8,128)(2,1)}, u32[]{:S(2)}, u32[]{:S(2)}) %collective-permute-start.2) | collective-permute-done | bytes 196640 | tf_op jit(solution)/shard_map/ppermute | solution.py:84
  41.0 5.9 %collective-permute-done.5.rest_8_ = bf16[128,768]{1,0:T(8,128)(2,1)S(1)} collective-permute-done((bf16[128,768]{1,0:T(8,128)(2,1)}, bf16[128,768]{1,0:T(8,128)(2,1)S(1)}, u32[]{:S(2)}, u32[]{:S(2)}) %collective-permute-start.5) | collective-permute-done | bytes 196640 | tf_op jit(solution)/shard_map/ppermute | solution.py:44
  55.4 3.5 collective-permute-done.8.rest_11_
  61.2 11.7 %shard_map.197 = (bf16[1024,512]{1,0:T(8,128)(2,1)}, bf16[1024,256]{1,0:T(8,128)(2,1)}, f32[2,256,1024]{2,1,0:T(8,128)}, bf16[2,256,1024]{2,1,0:T(8,128)(2,1)}, ...) custom-call(s32[4]{0:T(128)} %pad_add_fusion.spots_ref, s32[8]{0:T(128)} %stack.132.weight_spots_ref, ...), custom_call_target="tpu_custom_call" | custom-call | flops 15032385536 | bytes 1048576 | tf_op jit(solution)/shard_map/pallas_call | solution.py:506
  84.5 11.4 %shard_map.198 = (bf16[1024,512]{1,0:T(8,128)(2,1)}, bf16[1024,256]{1,0:T(8,128)(2,1)}, f32[2,256,1024]{2,1,0:T(8,128)}, bf16[2,256,1024]{2,1,0:T(8,128)(2,1)}, f32[8,512]{1,0:T(8,128)}) custom-call(s32[4]{0:T(128)} %pad_add_fusion.spots_ref, s32[8]{0:T(128)} %stack.132.weight_spots_ref, bf16[256,1024]{1,0:T(8,128)(2,1)} %copy-done.42, ...), custom_call_target="tpu_custom_call" | custom-call | flops 15032385536 | bytes 1048576 | tf_op jit(solution)/shard_map/pallas_call | solution.py:506
  95.9 4.0 collective-permute-done.18.refs_3_
  113.4 6.6 %collective-permute-done.23.refs_6_ = bf16[256,1024]{1,0:T(8,128)(2,1)} collective-permute-done((bf16[256,1024]{1,0:T(8,128)(2,1)S(1)}, bf16[256,1024]{1,0:T(8,128)(2,1)}, u32[]{:S(2)}, u32[]{:S(2)}) %collective-permute-start.23) | collective-permute-done | bytes 524320 | tf_op jit(solution)/shard_map/ppermute | solution.py:56
  120.0 10.5 %collective-permute-done.22.refs_4_ = bf16[256,1024]{1,0:T(8,128)(2,1)} collective-permute-done((bf16[256,1024]{1,0:T(8,128)(2,1)S(1)}, bf16[256,1024]{1,0:T(8,128)(2,1)}, u32[]{:S(2)}, u32[]{:S(2)}) %collective-permute-start.22) | collective-permute-done | bytes 524320 | tf_op jit(solution)/shard_map/ppermute | solution.py:44
  132.4 3.6 shard_map.199.xa_ref.ga_ref
  136.1 9.6 %collective-permute-done.24 = bf16[256,1024]{1,0:T(8,128)(2,1)S(1)} collective-permute-done((bf16[256,1024]{1,0:T(8,128)(2,1)}, bf16[256,1024]{1,0:T(8,128)(2,1)S(1)}, u32[]{:S(2)}, u32[]{:S(2)}) %collective-permute-start.24) | collective-permute-done | bytes 524320 | tf_op jit(solution)/shard_map/ppermute | solution.py:44
  145.7 4.4 collective-permute-done.25
  158.9 51.2 %shard_map.201 = (f32[4,2,256,1024]{3,2,1,0:T(8,128)}, f32[4,2,256,1024]{3,2,1,0:T(8,128)}, bf16[8,128,3072]{2,1,0:T(8,128)(2,1)}) custom-call(s32[1]{0:T(128)} %bitcast.1.side_ref, bf16[8,256,1024]{2,1,0:T(8,128)(2,1)} %shard_map.199.xa_ref.ga_ref, bf16[8,256,1024]{2,1,0:T(8,128)(2,1)} %collective-permute-done.26.xb_ref.gb_ref, ...), custom_call_target="tpu_custom_call" | custom-call | flops 6442450944 | bytes 1048576 | tf_op jit(solution)/shard_map/pallas_call | solution.py:320
  213.5 7.3 %collective-permute-done.30.xb_ref.gb_ref = bf16[8,256,1024]{2,1,0:T(8,128)(2,1)} collective-permute-done((bf16[8,256,1024]{2,1,0:T(8,128)(2,1)S(1)}, bf16[8,256,1024]{2,1,0:T(8,128)(2,1)}, u32[]{:S(2)}, u32[]{:S(2)}) %collective-permute-start.30) | collective-permute-done | bytes 4194336 | tf_op jit(solution)/shard_map/ppermute | solution.py:44
  220.8 51.4 %shard_map.203 = (f32[4,2,256,1024]{3,2,1,0:T(8,128)}, f32[4,2,256,1024]{3,2,1,0:T(8,128)}, bf16[8,128,3072]{2,1,0:T(8,128)(2,1)}) custom-call(s32[1]{0:T(128)} %bitcast.1.side_ref, bf16[8,256,1024]{2,1,0:T(8,128)(2,1)} %bitcast.172, bf16[8,256,1024]{2,1,0:T(8,128)(2,1)} %collective-permute-done.30.xb_ref.gb_ref, bf16[8,256,1024]{2,1,0:T(8,128)(2,1)} %bitcast.173, ...), custom_call_target="tpu_custom_call" | custom-call | flops 6442450944 | bytes 1048576 | tf_op jit(solution)/shard_map/pallas_call | solution.py:320
  272.3 51.3 %shard_map.204 = (f32[4,256,1024]{2,1,0:T(8,128)}, bf16[4,256,1024]{2,1,0:T(8,128)(2,1)}, f32[4,256,1024]{2,1,0:T(8,128)}, bf16[4,256,1024]{2,1,0:T(8,128)(2,1)}, bf16[8,128,3072]{2,1,0:T(8,128)(2,1)}) custom-call(s32[1]{0:T(128)} %bitcast.1.side_ref, bf16[8,256,1024]{2,1,0:T(8,128)(2,1)} %shard_map.199.xa_ref.ga_ref, ...), custom_call_target="tpu_custom_call" | custom-call | flops 6442450944 | bytes 1048576 | tf_op jit(solution)/shard_map/pallas_call | solution.py:320
  324.1 3.9 collective-permute-done.31
  337.4 52.2 %shard_map.205 = (f32[4,256,1024]{2,1,0:T(8,128)}, bf16[4,256,1024]{2,1,0:T(8,128)(2,1)}, f32[4,256,1024]{2,1,0:T(8,128)}, bf16[4,256,1024]{2,1,0:T(8,128)(2,1)}, bf16[8,128,3072]{2,1,0:T(8,128)(2,1)}) custom-call(s32[1]{0:T(128)} %bitcast.1.side_ref, bf16[8,256,1024]{2,1,0:T(8,128)(2,1)} %bitcast.174, ...), custom_call_target="tpu_custom_call" | custom-call | flops 6442450944 | bytes 1048576 | tf_op jit(solution)/shard_map/pallas_call | solution.py:320
  404.1 5.9 %collective-permute-done.37.rest_1_ = bf16[256,1024]{1,0:T(8,128)(2,1)S(1)} collective-permute-done((bf16[256,1024]{1,0:T(8,128)(2,1)S(1)}, bf16[256,1024]{1,0:T(8,128)(2,1)S(1)}, u32[]{:S(2)}, u32[]{:S(2)}) %collective-permute-start.37) | collective-permute-done | bytes 524320 | tf_op jit(solution)/shard_map/ppermute | solution.py:44
  410.1 10.8 %collective-permute-done.40 = bf16[256,1024]{1,0:T(8,128)(2,1)S(1)} collective-permute-done((bf16[256,1024]{1,0:T(8,128)(2,1)S(1)}, bf16[256,1024]{1,0:T(8,128)(2,1)S(1)}, u32[]{:S(2)}, u32[]{:S(2)}) %collective-permute-start.40) | collective-permute-done | bytes 524320 | tf_op jit(solution)/shard_map/ppermute | solution.py:44
  424.4 15.2 %shard_map.206 = (bf16[1024,512]{1,0:T(8,128)(2,1)}, f32[2,256,1024]{2,1,0:T(8,128)}, bf16[2,256,1024]{2,1,0:T(8,128)(2,1)}) custom-call(s32[4]{0:T(128)} %pad_add_fusion.spots_ref, s32[8]{0:T(128)} %stack.144.block_spots_ref, bf16[256,1024]{1,0:T(8,128)(2,1)} %copy-done.34, bf16[256,1024]{1,0:T(8,128)(2,1)} %copy-done.48, bf16[256,1024]{1,0:T(8,128)(2,1)} %copy-done.47, ...), custom_call_target="tpu_custom_call" | custom-call | flops 16777216 | bytes 1048576 | tf_op jit(solution)/shard_map/pallas_call | solution.py:539
  446.8 7.2 %shard_map.207 = (f32[1024,768]{1,0:T(8,128)}, f32[1024,1]{1,0:T(8,128)}) custom-call(s32[4]{0:T(128)} %pad_add_fusion.spots_ref, bf16[256,1024]{1,0:T(8,128)(2,1)} %copy-done.34, bf16[256,1024]{1,0:T(8,128)(2,1)} %copy-done.48, bf16[256,1024]{1,0:T(8,128)(2,1)} %copy-done.47, bf16[256,1024]{1,0:T(8,128)(2,1)} %copy-done.53, bf16[256,1024]{1,0:T(8,128)(2,1)} %copy-done.56, ...), custom_call_target="tpu_custom_call" | custom-call | flops 4294967296 | bytes 1048576 | tf_op jit(solution)/shard_map/pallas_call | solution.py:479
  455.0 4.8 collective-permute-done.44.rest_1_
  465.6 20.8 %shard_map.208 = (f32[4,128,768]{2,1,0:T(8,128)}, bf16[4,128,768]{2,1,0:T(8,128)(2,1)}, f32[2,256,1024]{2,1,0:T(8,128)}, bf16[2,256,1024]{2,1,0:T(8,128)(2,1)}, f32[1,1024]{1,0:T(1,128)}) custom-call(s32[4]{0:T(128)} %pad_add_fusion.spots_ref, s32[8]{0:T(128)} %stack.144.block_spots_ref, bf16[256,1024]{1,0:T(8,128)(2,1)} %copy-done.41, ...), custom_call_target="tpu_custom_call" | custom-call | flops 16777216 | bytes 1048576 | tf_op jit(solution)/shard_map/pallas_call | solution.py:539
  527.5 9.9 %collective-permute-done.62 = bf16[128,768]{1,0:T(8,128)(2,1)S(1)} collective-permute-done((bf16[128,768]{1,0:T(8,128)(2,1)S(1)}, bf16[128,768]{1,0:T(8,128)(2,1)S(1)}, u32[]{:S(2)}, u32[]{:S(2)}) %collective-permute-start.62) | collective-permute-done | bytes 196640 | tf_op jit(solution)/shard_map/ppermute | solution.py:90
  (352 shorter events, 168.5 us)
Async XLA Ops:
  7.2 151.7 %all-gather.5.cloned.1.call-start = ((), (), s32[]{:S(2)}) async-start(), calls=%async_computation.4 | async-start | bytes 7864320 | tf_op jit(solution)/shard_map/all_gather | solution.py:591
  11.8 22.6 %collective-permute-start.4 = (bf16[128,3072]{1,0:T(8,128)(2,1)S(1)}, bf16[128,3072]{1,0:T(8,128)(2,1)}, u32[]{:S(2)}, u32[]{:S(2)}) collective-permute-start(bf16[128,3072]{1,0:T(8,128)(2,1)S(1)} %get-tuple-element.179), channel_id=1, source_target_pairs={{0,4},{4,0},{1,5},{5,1},{2,6},{6,2},{3,7},{7,3},{8,12},{12,8},{9,1... | collective-permute-start | bytes 2359304 | tf_op jit(solution)/shard_map/ppermute | solution.py:44
  37.0 235.3 %all-gather.7.cloned.1.call-start = ((), (), s32[]{:S(2)}) async-start(), calls=%async_computation.5 | async-start | bytes 7864320 | tf_op jit(solution)/shard_map/all_gather | solution.py:591
  38.2 20.7 %collective-permute-start.11 = (bf16[256,1024]{1,0:T(8,128)(2,1)S(1)}, bf16[256,1024]{1,0:T(8,128)(2,1)S(1)}, u32[]{:S(2)}, u32[]{:S(2)}) collective-permute-start(bf16[256,1024]{1,0:T(8,128)(2,1)S(1)} %get-tuple-element.194.rest_0_.rest_4_), channel_id=1, source_target_pairs={{0,2},{2,0},{1,3},{3,1},{4,6},{6,4},{5,7},{7,5},{8,10},{10,8},{9,1... | collective-permute-start | bytes 1572872 | tf_op jit(solution)/shard_map/ppermute | solution.py:44
  38.8 21.0 %collective-permute-start.10 = (bf16[256,1024]{1,0:T(8,128)(2,1)}, bf16[256,1024]{1,0:T(8,128)(2,1)}, u32[]{:S(2)}, u32[]{:S(2)}) collective-permute-start(bf16[256,1024]{1,0:T(8,128)(2,1)} %collective-permute-done.3.rest_1_.rest_5_), channel_id=1, source_target_pairs={{0,1},{1,0},{2,3},{3,2},{4,5},{5,4},{6,7},{7,6},{8,9},{9,8},{10,11... | collective-permute-start | bytes 1572872 | tf_op jit(solution)/shard_map/ppermute | solution.py:44
  51.2 21.7 %collective-permute-start.13 = (bf16[256,1024]{1,0:T(8,128)(2,1)S(1)}, bf16[256,1024]{1,0:T(8,128)(2,1)S(1)}, u32[]{:S(2)}, u32[]{:S(2)}) collective-permute-start(bf16[256,1024]{1,0:T(8,128)(2,1)S(1)} %get-tuple-element.219.refs_1_), channel_id=1, source_target_pairs={{0,2},{2,0},{1,3},{3,1},{4,6},{6,4},{5,7},{7,5},{8,10},{10,8},{9,1... | collective-permute-start | bytes 1572872 | tf_op jit(solution)/shard_map/ppermute | solution.py:44
  105.6 24.9 %collective-permute-start.22 = (bf16[256,1024]{1,0:T(8,128)(2,1)S(1)}, bf16[256,1024]{1,0:T(8,128)(2,1)}, u32[]{:S(2)}, u32[]{:S(2)}) collective-permute-start(bf16[256,1024]{1,0:T(8,128)(2,1)S(1)} %multiply_convert_fusion.2.refs_0_), channel_id=1, source_target_pairs={{0,2},{2,0},{1,3},{3,1},{4,6},{6,4},{5,7},{7,5},{8,10},{10,8},{9,1... | collective-permute-start | bytes 1572872 | tf_op jit(solution)/shard_map/ppermute | solution.py:44
  107.2 23.4 %collective-permute-start.21 = (bf16[256,1024]{1,0:T(8,128)(2,1)S(1)}, bf16[256,1024]{1,0:T(8,128)(2,1)}, u32[]{:S(2)}, u32[]{:S(2)}) collective-permute-start(bf16[256,1024]{1,0:T(8,128)(2,1)S(1)} %multiply_convert_fusion.2.refs_0_), channel_id=1, source_target_pairs={{0,4},{4,0},{1,5},{5,1},{2,6},{6,2},{3,7},{7,3},{8,12},{12,8},{9,1... | collective-permute-start | bytes 1572872 | tf_op jit(solution)/shard_map/ppermute | solution.py:44
  136.1 22.8 %collective-permute-start.26 = (bf16[8,256,1024]{2,1,0:T(8,128)(2,1)}, bf16[8,256,1024]{2,1,0:T(8,128)(2,1)}, u32[]{:S(2)}, u32[]{:S(2)}) collective-permute-start(bf16[8,256,1024]{2,1,0:T(8,128)(2,1)} %shard_map.199.xa_ref.ga_ref), channel_id=1, source_target_pairs={{0,1},{1,0},{2,3},{3,2},{4,5},{5,4},{6,7},{7,6},{8,9},{9,8},{10,11... | collective-permute-start | bytes 12582920 | tf_op jit(solution)/shard_map/ppermute | solution.py:44
  151.6 238.1 %reduce-scatter.3.cloned.1.call-start = ((), (), s32[]{:S(2)}) async-start(), calls=%async_computation.2 | async-start | bytes 7864320 | tf_op jit(solution)/shard_map/reduce_scatter | solution.py:719
  155.3 54.8 %collective-permute-start.29 = (bf16[2,256,1024]{2,1,0:T(8,128)(2,1)S(1)}, bf16[2,256,1024]{2,1,0:T(8,128)(2,1)S(1)}, u32[]{:S(2)}, u32[]{:S(2)}) collective-permute-start(bf16[2,256,1024]{2,1,0:T(8,128)(2,1)S(1)} %shard_map.200.refs_0_), channel_id=1, source_target_pairs={{0,6},{2,4},{4,2},{6,0},{1,7},{3,5},{5,3},{7,1},{8,14},{10,12},{12... | collective-permute-start | bytes 3145736 | tf_op jit(solution)/shard_map/ppermute | solution.py:56
  156.8 53.3 %collective-permute-start.28 = (bf16[2,256,1024]{2,1,0:T(8,128)(2,1)S(1)}, bf16[2,256,1024]{2,1,0:T(8,128)(2,1)S(1)}, u32[]{:S(2)}, u32[]{:S(2)}) collective-permute-start(bf16[2,256,1024]{2,1,0:T(8,128)(2,1)S(1)} %shard_map.200.refs_0_), channel_id=1, source_target_pairs={{0,2},{2,0},{1,3},{3,1},{4,6},{6,4},{5,7},{7,5},{8,10},{10,8},{9,1... | collective-permute-start | bytes 3145736 | tf_op jit(solution)/shard_map/ppermute | solution.py:44
  158.4 51.8 %collective-permute-start.27 = (bf16[2,256,1024]{2,1,0:T(8,128)(2,1)S(1)}, bf16[2,256,1024]{2,1,0:T(8,128)(2,1)}, u32[]{:S(2)}, u32[]{:S(2)}) collective-permute-start(bf16[2,256,1024]{2,1,0:T(8,128)(2,1)S(1)} %shard_map.200.refs_0_), channel_id=1, source_target_pairs={{0,4},{4,0},{1,5},{5,1},{2,6},{6,2},{3,7},{7,3},{8,12},{12,8},{9,1... | collective-permute-start | bytes 3145736 | tf_op jit(solution)/shard_map/ppermute | solution.py:44
  272.2 240.9 %reduce-scatter.5.cloned.1.call-start = ((), (), s32[]{:S(2)}) async-start(), calls=%async_computation.3 | async-start | bytes 7864320 | tf_op jit(solution)/shard_map/reduce_scatter | solution.py:719
  333.9 55.7 %collective-permute-start.33 = (bf16[2,256,1024]{2,1,0:T(8,128)(2,1)}, bf16[2,256,1024]{2,1,0:T(8,128)(2,1)}, u32[]{:S(2)}, u32[]{:S(2)}) collective-permute-start(bf16[2,256,1024]{2,1,0:T(8,128)(2,1)} %get-tuple-element.254), channel_id=1, source_target_pairs={{0,4},{4,0},{1,5},{5,1},{2,6},{6,2},{3,7},{7,3},{8,12},{12,8},{9,1... | collective-permute-start | bytes 3145736 | tf_op jit(solution)/shard_map/ppermute | solution.py:44
  335.3 54.4 %collective-permute-start.34 = (bf16[2,256,1024]{2,1,0:T(8,128)(2,1)}, bf16[2,256,1024]{2,1,0:T(8,128)(2,1)}, u32[]{:S(2)}, u32[]{:S(2)}) collective-permute-start(bf16[2,256,1024]{2,1,0:T(8,128)(2,1)} %get-tuple-element.255), channel_id=1, source_target_pairs={{0,2},{2,0},{1,3},{3,1},{4,6},{6,4},{5,7},{7,5},{8,10},{10,8},{9,1... | collective-permute-start | bytes 3145736 | tf_op jit(solution)/shard_map/ppermute | solution.py:44
  335.4 54.2 %collective-permute-start.35 = (bf16[2,256,1024]{2,1,0:T(8,128)(2,1)S(1)}, bf16[2,256,1024]{2,1,0:T(8,128)(2,1)}, u32[]{:S(2)}, u32[]{:S(2)}) collective-permute-start(bf16[2,256,1024]{2,1,0:T(8,128)(2,1)S(1)} %pad_maximum_fusion.5), channel_id=1, source_target_pairs={{0,6},{2,4},{4,2},{6,0},{1,7},{3,5},{5,3},{7,1},{8,14},{10,12},{12... | collective-permute-start | bytes 3145736 | tf_op jit(solution)/shard_map/ppermute | solution.py:56
  400.4 20.5 %collective-permute-start.40 = (bf16[256,1024]{1,0:T(8,128)(2,1)S(1)}, bf16[256,1024]{1,0:T(8,128)(2,1)S(1)}, u32[]{:S(2)}, u32[]{:S(2)}) collective-permute-start(bf16[256,1024]{1,0:T(8,128)(2,1)S(1)} %get-tuple-element.415), channel_id=1, source_target_pairs={{0,2},{2,0},{1,3},{3,1},{4,6},{6,4},{5,7},{7,5},{8,10},{10,8},{9,1... | collective-permute-start | bytes 1572872 | tf_op jit(solution)/shard_map/ppermute | solution.py:44
  460.5 25.9 %collective-permute-start.48 = (bf16[256,1024]{1,0:T(8,128)(2,1)}, bf16[256,1024]{1,0:T(8,128)(2,1)S(1)}, u32[]{:S(2)}, u32[]{:S(2)}) collective-permute-start(bf16[256,1024]{1,0:T(8,128)(2,1)} %fusion.17), channel_id=1, source_target_pairs={{0,2},{2,0},{1,3},{3,1},{4,6},{6,4},{5,7},{7,5},{8,10},{10,8},{9,1... | collective-permute-start | bytes 1572872 | tf_op jit(solution)/shard_map/ppermute | solution.py:44
  462.1 25.5 %collective-permute-start.49 = (bf16[256,1024]{1,0:T(8,128)(2,1)}, bf16[256,1024]{1,0:T(8,128)(2,1)S(1)}, u32[]{:S(2)}, u32[]{:S(2)}) collective-permute-start(bf16[256,1024]{1,0:T(8,128)(2,1)} %get-tuple-element.298), channel_id=1, source_target_pairs={{0,4},{4,0},{1,5},{5,1},{2,6},{6,2},{3,7},{7,3},{8,12},{12,8},{9,1... | collective-permute-start | bytes 1572872 | tf_op jit(solution)/shard_map/ppermute | solution.py:44
  462.7 24.9 %collective-permute-start.50 = (bf16[256,1024]{1,0:T(8,128)(2,1)S(1)}, bf16[256,1024]{1,0:T(8,128)(2,1)}, u32[]{:S(2)}, u32[]{:S(2)}) collective-permute-start(bf16[256,1024]{1,0:T(8,128)(2,1)S(1)} %copy-done.46), channel_id=1, source_target_pairs={{0,6},{2,4},{4,2},{6,0},{1,7},{3,5},{5,3},{7,1},{8,14},{10,12},{12... | collective-permute-start | bytes 1572872 | tf_op jit(solution)/shard_map/ppermute | solution.py:56
  464.0 41.6 %collective-permute-start.56 = (bf16[256,1024]{1,0:T(8,128)(2,1)}, bf16[256,1024]{1,0:T(8,128)(2,1)}, u32[]{:S(2)}, u32[]{:S(2)}) collective-permute-start(bf16[256,1024]{1,0:T(8,128)(2,1)} %get-tuple-element.315), channel_id=1, source_target_pairs={{0,2},{2,0},{1,3},{3,1},{4,6},{6,4},{5,7},{7,5},{8,10},{10,8},{9,1... | collective-permute-start | bytes 1572872 | tf_op jit(solution)/shard_map/ppermute | solution.py:44
  490.5 20.2 %collective-permute-start.58 = (bf16[4,128,768]{2,1,0:T(8,128)(2,1)}, bf16[4,128,768]{2,1,0:T(8,128)(2,1)S(1)}, u32[]{:S(2)}, u32[]{:S(2)}) collective-permute-start(bf16[4,128,768]{2,1,0:T(8,128)(2,1)} %get-tuple-element.322), channel_id=1, source_target_pairs={{0,4},{4,0},{1,5},{5,1},{2,6},{6,2},{3,7},{7,3},{8,12},{12,8},{9,1... | collective-permute-start | bytes 2359304 | tf_op jit(solution)/shard_map/ppermute | solution.py:44
  491.2 20.8 %collective-permute-start.52 = (bf16[2,256,1024]{2,1,0:T(8,128)(2,1)}, bf16[2,256,1024]{2,1,0:T(8,128)(2,1)S(1)}, u32[]{:S(2)}, u32[]{:S(2)}) collective-permute-start(bf16[2,256,1024]{2,1,0:T(8,128)(2,1)} %get-tuple-element.312), channel_id=1, source_target_pairs={{0,1},{1,0},{2,3},{3,2},{4,5},{5,4},{6,7},{7,6},{8,9},{9,8},{10,11... | collective-permute-start | bytes 3145736 | tf_op jit(solution)/shard_map/ppermute | solution.py:44
  (116 other events, 1033.5 us)
Sparse Core Ops, SparseCore 0:
  37.1 116.3 all-gather.4
  155.1 113.9 all-gather.6
  272.3 112.5 reduce-scatter.2
  389.9 112.7 reduce-scatter.4

commit v9 on v8

--- a/solution.py
+++ b/solution.py
@@ -374,7 +374,7 @@
     rows = x_scr.shape[0]
     proj_width = q_width + 2 * kv_width
     ratio = q_width // kv_width
-    tile = min(256, rows)
+    tile = min(512, rows)
     qkv_ref[...] = dot_nn(x_scr[...], w_ref[:, :proj_width]).astype(BF)
     for kv in range(kv_width // HD):
         keys = qkv_ref[:, q_width + kv * HD : q_width + (kv + 1) * HD]
@@ -418,7 +418,7 @@
     place_rows(spots_ref, dy_pieces, dy_scr)
     rows = dy_scr.shape[0]
     ratio = q_width // kv_width
-    tile = min(256, rows)
+    tile = min(512, rows)
     head_grad_ref[...] = dot_nn(dy_scr[...], w_ref[:, proj_width:]).astype(BF)
     for kv in range(kv_width // HD):
         key_cols = slice(q_width + kv * HD, q_width + (kv + 1) * HD)
@@ -494,7 +494,7 @@
     rows, model_width = pieces[0].shape
     width = weights[0].shape[1]
     whole = len(weights) == 1
-    tile = min(256, 4 * rows)
+    tile = min(512, 4 * rows)
     stats = (widths[1] // HD * (4 * rows // tile), widths[0] // widths[1] * tile)
     outs = [
         jax.ShapeDtypeStruct((4 * rows, widths[0] + 2 * widths[1]), BF),

time: 560 us -> 562 us (level)
  no operation moved by 1% of the time
where the time goes in v9:
time: 562 us; the launch traced here: 559 us
  Pallas kernels  285 us (51%)
  waiting for transfers between devices  116 us (21%)
  starting transfers between devices  66.7 us (12%)
  other arithmetic  48.6 us (9%)
  local copies, waits for them, and re-layouts  27.4 us (5%)
  between operations  15 us (3%)
    pallas_call x4, Pallas kernels, moe_chunk(): pl.pallas_call(functools.partial(moe_kernel, first, last, start, column),...  206 us
    ppermute x51, waiting for transfers between devices, swap(): return lax.ppermute(value, axis, [(0, 1), (1, 0)])  84 us
    pallas_call x2, Pallas kernels, attn_backward(): pl.pallas_call(functools.partial(attn_backward_kernel, widths, first), in...  37.9 us
    ppermute x51, starting transfers between devices, swap(): return lax.ppermute(value, axis, [(0, 1), (1, 0)])  36.8 us
    pallas_call x2, Pallas kernels, attn_forward(): pl.pallas_call(functools.partial(attn_forward_kernel, widths, len(weights...  22.5 us
    unnamed x143, local copies, waits for them, and re-layouts  14.4 us
  transfers between devices with their start and end apart: 69, of which 27 were waited for; matrix products, arithmetic and copies ran while one was open for 10% of the time, Pallas kernels for 50%

profile of v9, /device:TPU:0, one launch (start us, length us, event | category | flops | bytes accessed | tf_op | source)
XLA Modules:
  0.0 559.0 jit_solution(4455363953853776165)
XLA Ops:
  23.5 10.5 %collective-permute-done.2.rest_7_ = bf16[128,768]{1,0:T(8,128)(2,1)} collective-permute-done((bf16[128,768]{1,0:T(8,128)(2,1)}, bf16[128,768]{1,0:T(8,128)(2,1)}, u32[]{:S(2)}, u32[]{:S(2)}) %collective-permute-start.2) | collective-permute-done | bytes 196640 | tf_op jit(solution)/shard_map/ppermute | solution.py:84
  41.0 5.9 %collective-permute-done.5.rest_8_ = bf16[128,768]{1,0:T(8,128)(2,1)S(1)} collective-permute-done((bf16[128,768]{1,0:T(8,128)(2,1)}, bf16[128,768]{1,0:T(8,128)(2,1)S(1)}, u32[]{:S(2)}, u32[]{:S(2)}) %collective-permute-start.5) | collective-permute-done | bytes 196640 | tf_op jit(solution)/shard_map/ppermute | solution.py:44
  61.2 11.2 %shard_map.197 = (bf16[1024,512]{1,0:T(8,128)(2,1)}, bf16[1024,256]{1,0:T(8,128)(2,1)}, f32[2,256,1024]{2,1,0:T(8,128)}, bf16[2,256,1024]{2,1,0:T(8,128)(2,1)}, ...) custom-call(s32[4]{0:T(128)} %pad_add_fusion.spots_ref, s32[8]{0:T(128)} %stack.132.weight_spots_ref, ...), custom_call_target="tpu_custom_call" | custom-call | flops 15032385536 | bytes 1048576 | tf_op jit(solution)/shard_map/pallas_call | solution.py:506
  84.5 11.2 %shard_map.198 = (bf16[1024,512]{1,0:T(8,128)(2,1)}, bf16[1024,256]{1,0:T(8,128)(2,1)}, f32[2,256,1024]{2,1,0:T(8,128)}, bf16[2,256,1024]{2,1,0:T(8,128)(2,1)}, f32[4,1024]{1,0:T(4,128)}) custom-call(s32[4]{0:T(128)} %pad_add_fusion.spots_ref, s32[8]{0:T(128)} %stack.132.weight_spots_ref, bf16[256,1024]{1,0:T(8,128)(2,1)} %copy-done.42, ...), custom_call_target="tpu_custom_call" | custom-call | flops 15032385536 | bytes 1048576 | tf_op jit(solution)/shard_map/pallas_call | solution.py:506
  95.8 4.1 collective-permute-done.18.refs_3_
  113.4 6.6 %collective-permute-done.23.refs_6_ = bf16[256,1024]{1,0:T(8,128)(2,1)} collective-permute-done((bf16[256,1024]{1,0:T(8,128)(2,1)S(1)}, bf16[256,1024]{1,0:T(8,128)(2,1)}, u32[]{:S(2)}, u32[]{:S(2)}) %collective-permute-start.23) | collective-permute-done | bytes 524320 | tf_op jit(solution)/shard_map/ppermute | solution.py:56
  120.0 10.5 %collective-permute-done.22.refs_4_ = bf16[256,1024]{1,0:T(8,128)(2,1)} collective-permute-done((bf16[256,1024]{1,0:T(8,128)(2,1)S(1)}, bf16[256,1024]{1,0:T(8,128)(2,1)}, u32[]{:S(2)}, u32[]{:S(2)}) %collective-permute-start.22) | collective-permute-done | bytes 524320 | tf_op jit(solution)/shard_map/ppermute | solution.py:44
  132.4 3.6 shard_map.199.xa_ref.ga_ref
  136.1 9.6 %collective-permute-done.24 = bf16[256,1024]{1,0:T(8,128)(2,1)S(1)} collective-permute-done((bf16[256,1024]{1,0:T(8,128)(2,1)}, bf16[256,1024]{1,0:T(8,128)(2,1)S(1)}, u32[]{:S(2)}, u32[]{:S(2)}) %collective-permute-start.24) | collective-permute-done | bytes 524320 | tf_op jit(solution)/shard_map/ppermute | solution.py:44
  145.7 4.4 collective-permute-done.25
  158.9 51.2 %shard_map.201 = (f32[4,2,256,1024]{3,2,1,0:T(8,128)}, f32[4,2,256,1024]{3,2,1,0:T(8,128)}, bf16[8,128,3072]{2,1,0:T(8,128)(2,1)}) custom-call(s32[1]{0:T(128)} %bitcast.1.side_ref, bf16[8,256,1024]{2,1,0:T(8,128)(2,1)} %shard_map.199.xa_ref.ga_ref, bf16[8,256,1024]{2,1,0:T(8,128)(2,1)} %collective-permute-done.26.xb_ref.gb_ref, ...), custom_call_target="tpu_custom_call" | custom-call | flops 6442450944 | bytes 1048576 | tf_op jit(solution)/shard_map/pallas_call | solution.py:320
  213.5 7.3 %collective-permute-done.30.xb_ref.gb_ref = bf16[8,256,1024]{2,1,0:T(8,128)(2,1)} collective-permute-done((bf16[8,256,1024]{2,1,0:T(8,128)(2,1)S(1)}, bf16[8,256,1024]{2,1,0:T(8,128)(2,1)}, u32[]{:S(2)}, u32[]{:S(2)}) %collective-permute-start.30) | collective-permute-done | bytes 4194336 | tf_op jit(solution)/shard_map/ppermute | solution.py:44
  220.8 51.4 %shard_map.203 = (f32[4,2,256,1024]{3,2,1,0:T(8,128)}, f32[4,2,256,1024]{3,2,1,0:T(8,128)}, bf16[8,128,3072]{2,1,0:T(8,128)(2,1)}) custom-call(s32[1]{0:T(128)} %bitcast.1.side_ref, bf16[8,256,1024]{2,1,0:T(8,128)(2,1)} %bitcast.172, bf16[8,256,1024]{2,1,0:T(8,128)(2,1)} %collective-permute-done.30.xb_ref.gb_ref, bf16[8,256,1024]{2,1,0:T(8,128)(2,1)} %bitcast.173, ...), custom_call_target="tpu_custom_call" | custom-call | flops 6442450944 | bytes 1048576 | tf_op jit(solution)/shard_map/pallas_call | solution.py:320
  272.3 51.3 %shard_map.204 = (f32[4,256,1024]{2,1,0:T(8,128)}, bf16[4,256,1024]{2,1,0:T(8,128)(2,1)}, f32[4,256,1024]{2,1,0:T(8,128)}, bf16[4,256,1024]{2,1,0:T(8,128)(2,1)}, bf16[8,128,3072]{2,1,0:T(8,128)(2,1)}) custom-call(s32[1]{0:T(128)} %bitcast.1.side_ref, bf16[8,256,1024]{2,1,0:T(8,128)(2,1)} %shard_map.199.xa_ref.ga_ref, ...), custom_call_target="tpu_custom_call" | custom-call | flops 6442450944 | bytes 1048576 | tf_op jit(solution)/shard_map/pallas_call | solution.py:320
  324.1 3.9 collective-permute-done.31
  337.4 52.2 %shard_map.205 = (f32[4,256,1024]{2,1,0:T(8,128)}, bf16[4,256,1024]{2,1,0:T(8,128)(2,1)}, f32[4,256,1024]{2,1,0:T(8,128)}, bf16[4,256,1024]{2,1,0:T(8,128)(2,1)}, bf16[8,128,3072]{2,1,0:T(8,128)(2,1)}) custom-call(s32[1]{0:T(128)} %bitcast.1.side_ref, bf16[8,256,1024]{2,1,0:T(8,128)(2,1)} %bitcast.174, ...), custom_call_target="tpu_custom_call" | custom-call | flops 6442450944 | bytes 1048576 | tf_op jit(solution)/shard_map/pallas_call | solution.py:320
  404.1 6.0 %collective-permute-done.37.rest_1_ = bf16[256,1024]{1,0:T(8,128)(2,1)S(1)} collective-permute-done((bf16[256,1024]{1,0:T(8,128)(2,1)S(1)}, bf16[256,1024]{1,0:T(8,128)(2,1)S(1)}, u32[]{:S(2)}, u32[]{:S(2)}) %collective-permute-start.37) | collective-permute-done | bytes 524320 | tf_op jit(solution)/shard_map/ppermute | solution.py:44
  410.1 10.8 %collective-permute-done.40 = bf16[256,1024]{1,0:T(8,128)(2,1)S(1)} collective-permute-done((bf16[256,1024]{1,0:T(8,128)(2,1)S(1)}, bf16[256,1024]{1,0:T(8,128)(2,1)S(1)}, u32[]{:S(2)}, u32[]{:S(2)}) %collective-permute-start.40) | collective-permute-done | bytes 524320 | tf_op jit(solution)/shard_map/ppermute | solution.py:44
  424.4 16.8 %shard_map.206 = (bf16[1024,512]{1,0:T(8,128)(2,1)}, f32[2,256,1024]{2,1,0:T(8,128)}, bf16[2,256,1024]{2,1,0:T(8,128)(2,1)}) custom-call(s32[4]{0:T(128)} %pad_add_fusion.spots_ref, s32[8]{0:T(128)} %stack.144.block_spots_ref, bf16[256,1024]{1,0:T(8,128)(2,1)} %copy-done.34, bf16[256,1024]{1,0:T(8,128)(2,1)} %copy-done.48, bf16[256,1024]{1,0:T(8,128)(2,1)} %copy-done.47, ...), custom_call_target="tpu_custom_call" | custom-call | flops 16777216 | bytes 1048576 | tf_op jit(solution)/shard_map/pallas_call | solution.py:539
  448.4 7.3 %shard_map.207 = (f32[1024,768]{1,0:T(8,128)}, f32[1024,1]{1,0:T(8,128)}) custom-call(s32[4]{0:T(128)} %pad_add_fusion.spots_ref, bf16[256,1024]{1,0:T(8,128)(2,1)} %copy-done.34, bf16[256,1024]{1,0:T(8,128)(2,1)} %copy-done.48, bf16[256,1024]{1,0:T(8,128)(2,1)} %copy-done.47, bf16[256,1024]{1,0:T(8,128)(2,1)} %copy-done.53, bf16[256,1024]{1,0:T(8,128)(2,1)} %copy-done.56, ...), custom_call_target="tpu_custom_call" | custom-call | flops 4294967296 | bytes 1048576 | tf_op jit(solution)/shard_map/pallas_call | solution.py:479
  456.7 4.8 collective-permute-done.44.rest_1_
  467.2 21.1 %shard_map.208 = (f32[4,128,768]{2,1,0:T(8,128)}, bf16[4,128,768]{2,1,0:T(8,128)(2,1)}, f32[2,256,1024]{2,1,0:T(8,128)}, bf16[2,256,1024]{2,1,0:T(8,128)(2,1)}, f32[1,1024]{1,0:T(1,128)}) custom-call(s32[4]{0:T(128)} %pad_add_fusion.spots_ref, s32[8]{0:T(128)} %stack.144.block_spots_ref, bf16[256,1024]{1,0:T(8,128)(2,1)} %copy-done.41, ...), custom_call_target="tpu_custom_call" | custom-call | flops 16777216 | bytes 1048576 | tf_op jit(solution)/shard_map/pallas_call | solution.py:539
  500.3 3.6 collective-permute-start.55
  529.2 9.9 %collective-permute-done.62 = bf16[128,768]{1,0:T(8,128)(2,1)S(1)} collective-permute-done((bf16[128,768]{1,0:T(8,128)(2,1)S(1)}, bf16[128,768]{1,0:T(8,128)(2,1)S(1)}, u32[]{:S(2)}, u32[]{:S(2)}) %collective-permute-start.62) | collective-permute-done | bytes 196640 | tf_op jit(solution)/shard_map/ppermute | solution.py:90
  (352 shorter events, 168.9 us)
Async XLA Ops:
  7.2 151.7 %all-gather.5.cloned.1.call-start = ((), (), s32[]{:S(2)}) async-start(), calls=%async_computation.4 | async-start | bytes 7864320 | tf_op jit(solution)/shard_map/all_gather | solution.py:591
  11.8 22.6 %collective-permute-start.4 = (bf16[128,3072]{1,0:T(8,128)(2,1)S(1)}, bf16[128,3072]{1,0:T(8,128)(2,1)}, u32[]{:S(2)}, u32[]{:S(2)}) collective-permute-start(bf16[128,3072]{1,0:T(8,128)(2,1)S(1)} %get-tuple-element.179), channel_id=1, source_target_pairs={{0,4},{4,0},{1,5},{5,1},{2,6},{6,2},{3,7},{7,3},{8,12},{12,8},{9,1... | collective-permute-start | bytes 2359304 | tf_op jit(solution)/shard_map/ppermute | solution.py:44
  37.0 235.3 %all-gather.7.cloned.1.call-start = ((), (), s32[]{:S(2)}) async-start(), calls=%async_computation.5 | async-start | bytes 7864320 | tf_op jit(solution)/shard_map/all_gather | solution.py:591
  38.2 20.7 %collective-permute-start.11 = (bf16[256,1024]{1,0:T(8,128)(2,1)S(1)}, bf16[256,1024]{1,0:T(8,128)(2,1)S(1)}, u32[]{:S(2)}, u32[]{:S(2)}) collective-permute-start(bf16[256,1024]{1,0:T(8,128)(2,1)S(1)} %get-tuple-element.194.rest_0_.rest_4_), channel_id=1, source_target_pairs={{0,2},{2,0},{1,3},{3,1},{4,6},{6,4},{5,7},{7,5},{8,10},{10,8},{9,1... | collective-permute-start | bytes 1572872 | tf_op jit(solution)/shard_map/ppermute | solution.py:44
  38.8 21.0 %collective-permute-start.10 = (bf16[256,1024]{1,0:T(8,128)(2,1)}, bf16[256,1024]{1,0:T(8,128)(2,1)}, u32[]{:S(2)}, u32[]{:S(2)}) collective-permute-start(bf16[256,1024]{1,0:T(8,128)(2,1)} %collective-permute-done.3.rest_1_.rest_5_), channel_id=1, source_target_pairs={{0,1},{1,0},{2,3},{3,2},{4,5},{5,4},{6,7},{7,6},{8,9},{9,8},{10,11... | collective-permute-start | bytes 1572872 | tf_op jit(solution)/shard_map/ppermute | solution.py:44
  51.2 21.2 %collective-permute-start.13 = (bf16[256,1024]{1,0:T(8,128)(2,1)S(1)}, bf16[256,1024]{1,0:T(8,128)(2,1)S(1)}, u32[]{:S(2)}, u32[]{:S(2)}) collective-permute-start(bf16[256,1024]{1,0:T(8,128)(2,1)S(1)} %get-tuple-element.219.refs_1_), channel_id=1, source_target_pairs={{0,2},{2,0},{1,3},{3,1},{4,6},{6,4},{5,7},{7,5},{8,10},{10,8},{9,1... | collective-permute-start | bytes 1572872 | tf_op jit(solution)/shard_map/ppermute | solution.py:44
  105.6 24.9 %collective-permute-start.22 = (bf16[256,1024]{1,0:T(8,128)(2,1)S(1)}, bf16[256,1024]{1,0:T(8,128)(2,1)}, u32[]{:S(2)}, u32[]{:S(2)}) collective-permute-start(bf16[256,1024]{1,0:T(8,128)(2,1)S(1)} %multiply_convert_fusion.2.refs_0_), channel_id=1, source_target_pairs={{0,2},{2,0},{1,3},{3,1},{4,6},{6,4},{5,7},{7,5},{8,10},{10,8},{9,1... | collective-permute-start | bytes 1572872 | tf_op jit(solution)/shard_map/ppermute | solution.py:44
  107.2 23.4 %collective-permute-start.21 = (bf16[256,1024]{1,0:T(8,128)(2,1)S(1)}, bf16[256,1024]{1,0:T(8,128)(2,1)}, u32[]{:S(2)}, u32[]{:S(2)}) collective-permute-start(bf16[256,1024]{1,0:T(8,128)(2,1)S(1)} %multiply_convert_fusion.2.refs_0_), channel_id=1, source_target_pairs={{0,4},{4,0},{1,5},{5,1},{2,6},{6,2},{3,7},{7,3},{8,12},{12,8},{9,1... | collective-permute-start | bytes 1572872 | tf_op jit(solution)/shard_map/ppermute | solution.py:44
  136.1 22.8 %collective-permute-start.26 = (bf16[8,256,1024]{2,1,0:T(8,128)(2,1)}, bf16[8,256,1024]{2,1,0:T(8,128)(2,1)}, u32[]{:S(2)}, u32[]{:S(2)}) collective-permute-start(bf16[8,256,1024]{2,1,0:T(8,128)(2,1)} %shard_map.199.xa_ref.ga_ref), channel_id=1, source_target_pairs={{0,1},{1,0},{2,3},{3,2},{4,5},{5,4},{6,7},{7,6},{8,9},{9,8},{10,11... | collective-permute-start | bytes 12582920 | tf_op jit(solution)/shard_map/ppermute | solution.py:44
  151.6 238.1 %reduce-scatter.3.cloned.1.call-start = ((), (), s32[]{:S(2)}) async-start(), calls=%async_computation.2 | async-start | bytes 7864320 | tf_op jit(solution)/shard_map/reduce_scatter | solution.py:719
  155.3 54.8 %collective-permute-start.29 = (bf16[2,256,1024]{2,1,0:T(8,128)(2,1)S(1)}, bf16[2,256,1024]{2,1,0:T(8,128)(2,1)S(1)}, u32[]{:S(2)}, u32[]{:S(2)}) collective-permute-start(bf16[2,256,1024]{2,1,0:T(8,128)(2,1)S(1)} %shard_map.200.refs_0_), channel_id=1, source_target_pairs={{0,6},{2,4},{4,2},{6,0},{1,7},{3,5},{5,3},{7,1},{8,14},{10,12},{12... | collective-permute-start | bytes 3145736 | tf_op jit(solution)/shard_map/ppermute | solution.py:56
  156.8 53.3 %collective-permute-start.28 = (bf16[2,256,1024]{2,1,0:T(8,128)(2,1)S(1)}, bf16[2,256,1024]{2,1,0:T(8,128)(2,1)S(1)}, u32[]{:S(2)}, u32[]{:S(2)}) collective-permute-start(bf16[2,256,1024]{2,1,0:T(8,128)(2,1)S(1)} %shard_map.200.refs_0_), channel_id=1, source_target_pairs={{0,2},{2,0},{1,3},{3,1},{4,6},{6,4},{5,7},{7,5},{8,10},{10,8},{9,1... | collective-permute-start | bytes 3145736 | tf_op jit(solution)/shard_map/ppermute | solution.py:44
  158.4 51.8 %collective-permute-start.27 = (bf16[2,256,1024]{2,1,0:T(8,128)(2,1)S(1)}, bf16[2,256,1024]{2,1,0:T(8,128)(2,1)}, u32[]{:S(2)}, u32[]{:S(2)}) collective-permute-start(bf16[2,256,1024]{2,1,0:T(8,128)(2,1)S(1)} %shard_map.200.refs_0_), channel_id=1, source_target_pairs={{0,4},{4,0},{1,5},{5,1},{2,6},{6,2},{3,7},{7,3},{8,12},{12,8},{9,1... | collective-permute-start | bytes 3145736 | tf_op jit(solution)/shard_map/ppermute | solution.py:44
  272.2 242.6 %reduce-scatter.5.cloned.1.call-start = ((), (), s32[]{:S(2)}) async-start(), calls=%async_computation.3 | async-start | bytes 7864320 | tf_op jit(solution)/shard_map/reduce_scatter | solution.py:719
  333.9 55.7 %collective-permute-start.33 = (bf16[2,256,1024]{2,1,0:T(8,128)(2,1)}, bf16[2,256,1024]{2,1,0:T(8,128)(2,1)}, u32[]{:S(2)}, u32[]{:S(2)}) collective-permute-start(bf16[2,256,1024]{2,1,0:T(8,128)(2,1)} %get-tuple-element.254), channel_id=1, source_target_pairs={{0,4},{4,0},{1,5},{5,1},{2,6},{6,2},{3,7},{7,3},{8,12},{12,8},{9,1... | collective-permute-start | bytes 3145736 | tf_op jit(solution)/shard_map/ppermute | solution.py:44
  335.3 54.4 %collective-permute-start.34 = (bf16[2,256,1024]{2,1,0:T(8,128)(2,1)}, bf16[2,256,1024]{2,1,0:T(8,128)(2,1)}, u32[]{:S(2)}, u32[]{:S(2)}) collective-permute-start(bf16[2,256,1024]{2,1,0:T(8,128)(2,1)} %get-tuple-element.255), channel_id=1, source_target_pairs={{0,2},{2,0},{1,3},{3,1},{4,6},{6,4},{5,7},{7,5},{8,10},{10,8},{9,1... | collective-permute-start | bytes 3145736 | tf_op jit(solution)/shard_map/ppermute | solution.py:44
  335.4 54.3 %collective-permute-start.35 = (bf16[2,256,1024]{2,1,0:T(8,128)(2,1)S(1)}, bf16[2,256,1024]{2,1,0:T(8,128)(2,1)}, u32[]{:S(2)}, u32[]{:S(2)}) collective-permute-start(bf16[2,256,1024]{2,1,0:T(8,128)(2,1)S(1)} %pad_maximum_fusion.5), channel_id=1, source_target_pairs={{0,6},{2,4},{4,2},{6,0},{1,7},{3,5},{5,3},{7,1},{8,14},{10,12},{12... | collective-permute-start | bytes 3145736 | tf_op jit(solution)/shard_map/ppermute | solution.py:56
  400.4 20.5 %collective-permute-start.40 = (bf16[256,1024]{1,0:T(8,128)(2,1)S(1)}, bf16[256,1024]{1,0:T(8,128)(2,1)S(1)}, u32[]{:S(2)}, u32[]{:S(2)}) collective-permute-start(bf16[256,1024]{1,0:T(8,128)(2,1)S(1)} %get-tuple-element.415), channel_id=1, source_target_pairs={{0,2},{2,0},{1,3},{3,1},{4,6},{6,4},{5,7},{7,5},{8,10},{10,8},{9,1... | collective-permute-start | bytes 1572872 | tf_op jit(solution)/shard_map/ppermute | solution.py:44
  462.1 26.2 %collective-permute-start.48 = (bf16[256,1024]{1,0:T(8,128)(2,1)}, bf16[256,1024]{1,0:T(8,128)(2,1)S(1)}, u32[]{:S(2)}, u32[]{:S(2)}) collective-permute-start(bf16[256,1024]{1,0:T(8,128)(2,1)} %fusion.17), channel_id=1, source_target_pairs={{0,2},{2,0},{1,3},{3,1},{4,6},{6,4},{5,7},{7,5},{8,10},{10,8},{9,1... | collective-permute-start | bytes 1572872 | tf_op jit(solution)/shard_map/ppermute | solution.py:44
  463.7 25.5 %collective-permute-start.49 = (bf16[256,1024]{1,0:T(8,128)(2,1)}, bf16[256,1024]{1,0:T(8,128)(2,1)S(1)}, u32[]{:S(2)}, u32[]{:S(2)}) collective-permute-start(bf16[256,1024]{1,0:T(8,128)(2,1)} %get-tuple-element.298), channel_id=1, source_target_pairs={{0,4},{4,0},{1,5},{5,1},{2,6},{6,2},{3,7},{7,3},{8,12},{12,8},{9,1... | collective-permute-start | bytes 1572872 | tf_op jit(solution)/shard_map/ppermute | solution.py:44
  464.3 24.9 %collective-permute-start.50 = (bf16[256,1024]{1,0:T(8,128)(2,1)S(1)}, bf16[256,1024]{1,0:T(8,128)(2,1)}, u32[]{:S(2)}, u32[]{:S(2)}) collective-permute-start(bf16[256,1024]{1,0:T(8,128)(2,1)S(1)} %copy-done.46), channel_id=1, source_target_pairs={{0,6},{2,4},{4,2},{6,0},{1,7},{3,5},{5,3},{7,1},{8,14},{10,12},{12... | collective-permute-start | bytes 1572872 | tf_op jit(solution)/shard_map/ppermute | solution.py:56
  465.6 41.3 %collective-permute-start.56 = (bf16[256,1024]{1,0:T(8,128)(2,1)}, bf16[256,1024]{1,0:T(8,128)(2,1)}, u32[]{:S(2)}, u32[]{:S(2)}) collective-permute-start(bf16[256,1024]{1,0:T(8,128)(2,1)} %get-tuple-element.315), channel_id=1, source_target_pairs={{0,2},{2,0},{1,3},{3,1},{4,6},{6,4},{5,7},{7,5},{8,10},{10,8},{9,1... | collective-permute-start | bytes 1572872 | tf_op jit(solution)/shard_map/ppermute | solution.py:44
  492.1 20.2 %collective-permute-start.58 = (bf16[4,128,768]{2,1,0:T(8,128)(2,1)}, bf16[4,128,768]{2,1,0:T(8,128)(2,1)S(1)}, u32[]{:S(2)}, u32[]{:S(2)}) collective-permute-start(bf16[4,128,768]{2,1,0:T(8,128)(2,1)} %get-tuple-element.322), channel_id=1, source_target_pairs={{0,4},{4,0},{1,5},{5,1},{2,6},{6,2},{3,7},{7,3},{8,12},{12,8},{9,1... | collective-permute-start | bytes 2359304 | tf_op jit(solution)/shard_map/ppermute | solution.py:44
  492.8 20.8 %collective-permute-start.52 = (bf16[2,256,1024]{2,1,0:T(8,128)(2,1)}, bf16[2,256,1024]{2,1,0:T(8,128)(2,1)S(1)}, u32[]{:S(2)}, u32[]{:S(2)}) collective-permute-start(bf16[2,256,1024]{2,1,0:T(8,128)(2,1)} %get-tuple-element.312), channel_id=1, source_target_pairs={{0,1},{1,0},{2,3},{3,2},{4,5},{5,4},{6,7},{7,6},{8,9},{9,8},{10,11... | collective-permute-start | bytes 3145736 | tf_op jit(solution)/shard_map/ppermute | solution.py:44
  (116 other events, 1041.8 us)
Sparse Core Ops, SparseCore 0:
  37.1 116.3 all-gather.4
  155.1 113.9 all-gather.6
  272.3 112.5 reduce-scatter.2
  389.9 112.7 reduce-scatter.4
